TPU v7x, 32 devices: a whole 2x2x4 slice. The times are simulated.
32 devices in a mesh: parts: 2 (over x), genome: 8 (over z, y), reads: 2 (over core).
Axes of the slice: x: 2, y: 2, z: 4, core: 2. Of those that a mesh axis runs over, the one named last changes fastest.
Arguments:
- likelihood: bfloat16 [32, 64, 256, 128], P(('parts', 'reads'), 'genome'), parts along dimension 0, may hold values from 0.0099487305 to 1
- block_ids: int32 [32, 64], P(('parts', 'reads'), 'genome'), parts along dimension 0, may hold values from 0 to 191, as said below
- slot_valid: int32 [32, 64], P(('parts', 'reads'), 'genome'), parts along dimension 0, may hold values from 0 to 1, as said below
- start_weights: float32 [49152], P(('parts', 'genome', 'reads')), parts along dimension 0, may hold values from 0.5 to 2
Outputs:
- abundance: float32 [49152], P(('parts', 'genome', 'reads')), parts along dimension 0
There are 2 independent parts, one for each index of `parts`. A program takes and returns all parts, laid end to end along the dimension named above; each array names one. Nothing has to cross between parts.
Inputs may be any that keep to these rules, and one draw needn't show every extreme that they name: `block_ids`: the 64 genome blocks of one read block are distinct. `slot_valid`: within each read block, the valid slots among the 8 slots held by one index of genome come first; slot 0 of every read block is valid.
All inputs are finite; a program needn't handle non-finite values.
Results may differ from a plain program's by a relative error of at most 0.0003.
Values sent between devices are 32-bit elements; how exact they have to be, the bound alone decides.
No kernel may reach another device: no remote copies, remote signals or barrier semaphores. Data moves between devices by JAX's collectives and lax.ppermute only.
A program may use at most 64 MiB of HBM per device.

v0:
```python
import jax
import jax.numpy as jnp
from jax import lax
from jax.sharding import PartitionSpec as P

ITERS = 2


def local_counts(full, likelihood, block_ids, slot_valid):
    cols = likelihood.shape[3]
    blocks = full.shape[0] // cols
    table = full.reshape(blocks, cols)
    picked = table[block_ids] * slot_valid.astype(jnp.float32)[:, :, None]
    lik_float = likelihood.astype(jnp.float32)
    row_part = jnp.sum(lik_float * picked[:, :, None, :], axis=(1, 3))
    row_total = lax.psum(row_part, "genome")
    inverse = 1.0 / row_total
    contrib = picked * jnp.sum(lik_float * inverse[:, None, :, None], axis=2)
    flat_ids = block_ids.reshape(-1)
    one_hot = (flat_ids[None, :] == jnp.arange(blocks, dtype=jnp.int32)[:, None]).astype(
        jnp.float32
    )
    summed = jnp.dot(
        one_hot,
        contrib.reshape(-1, cols),
        preferred_element_type=jnp.float32,
        precision=lax.Precision.HIGHEST,
    )
    return summed.reshape(blocks * cols)


def local(likelihood, block_ids, slot_valid, start_weights):
    full = lax.all_gather(start_weights, ("genome", "reads"), axis=0, tiled=True)
    total_reads = likelihood.shape[0] * lax.axis_size("reads") * likelihood.shape[2]
    scale = full.shape[0] / total_reads
    owned = start_weights
    for step in range(ITERS):
        partial_value = local_counts(full, likelihood, block_ids, slot_valid)
        owned = (
            lax.psum_scatter(partial_value, ("genome", "reads"), scatter_dimension=0, tiled=True)
            * scale
        )
        if step + 1 < ITERS:
            full = lax.all_gather(owned, ("genome", "reads"), axis=0, tiled=True)
    return owned


def solution(mesh):
    placed = (
        P(("parts", "reads"), "genome", None, None),
        P(("parts", "reads"), "genome"),
        P(("parts", "reads"), "genome"),
        P(("parts", "genome", "reads")),
    )
    return jax.shard_map(
        local,
        mesh=mesh,
        in_specs=placed,
        out_specs=P(("parts", "genome", "reads")),
        check_vma=False,
    )
```

profile of v0, /device:TPU:0, one launch (start us, length us, event | category | flops | bytes accessed | tf_op | source)
XLA Modules:
  0.0 284.8 jit_solution(6398667421512296714)
XLA Ops:
  6.5 0.7 compare_select_fusion
  7.2 0.8 eq.8
  8.0 0.1 reshape.37
  8.1 0.7 reshape.57
  8.8 23.3 %all-gather = f32[16,1,1536]{2,1,0:T(1,128)S(1)} all-gather(f32[1,1,1536]{2,1,0:T(1,128)S(1)} %reshape.57), channel_id=1, replica_groups=mesh['parts'=2,'genome'=8,'reads'=2] {'genome','reads'}, dimensions={0}, use_global_device_ids=true | all-gather | bytes 104448 | tf_op jit(solution)/shard_map/all_gather | solution.py:33
  32.1 0.7 convert_element_type.4
  32.8 0.1 mul.78
  32.9 0.6 gather_fusion
  33.5 0.1 bitcast_multiply_fusion.5
  33.6 3.1 %fusion = f32[8,256]{1,0:T(8,128)S(1)} fusion(bf16[8,8,256,128]{3,2,1,0:T(8,128)(2,1)} %param.4, f32[8,8,128]{2,1,0:T(8,128)S(1)} %bitcast_multiply_fusion.5), kind=kLoop, calls=%fused_computation.6 | loop fusion | flops 6289408 | bytes 4235264 | tf_op jit(solution)/shard_map/reduce_sum | solution.py:15
  36.7 17.4 %psum.14 = f32[8,256]{1,0:T(8,128)S(1)} all-reduce(f32[8,256]{1,0:T(8,128)S(1)} %fusion), channel_id=1, replica_groups=mesh['parts'=2,'genome'=8,'reads'=2] {'genome'}, use_global_device_ids=true, to_apply=%region_1.0 | all-reduce | flops 2048 | bytes 16384 | tf_op jit(solution)/shard_map/psum | solution.py:16
  54.1 3.5 %fusion.1 = f32[8,8,128]{2,1,0:T(8,128)S(1)} fusion(bf16[8,8,256,128]{3,2,1,0:T(8,128)(2,1)} %param.4, f32[8,256]{1,0:T(8,128)S(1)} %broadcast_divide_fusion.1), kind=kLoop, calls=%fused_computation.7 | loop fusion | flops 6283264 | bytes 4235264 | tf_op jit(solution)/shard_map/reduce_sum | solution.py:18
  57.6 0.9 convolution_bitcast_fusion.1
  58.6 0.6 dynamic-slice
  59.8 84.7 %all-reduce.5.cloned.1.call-done = f32[24576]{0:T(1024)} async-done(((f32[24576]{0:T(1024)}), f32[24576]{0:T(1024)}) %all-reduce.5.cloned.1.call-update) | async-done | bytes 98320
  144.5 0.8 dynamic-slice_multiply_fusion.1
  145.3 19.7 %all-gather.1 = f32[16,1,1536]{2,1,0:T(1,128)S(1)} all-gather(f32[1,1,1536]{2,1,0:T(1,128)S(1)} %reshape.59), channel_id=1, replica_groups=mesh['parts'=2,'genome'=8,'reads'=2] {'genome','reads'}, dimensions={0}, use_global_device_ids=true | all-gather | bytes 104448 | tf_op jit(solution)/shard_map/all_gather | solution.py:44
  165.0 0.6 gather_fusion.1
  165.6 3.1 %fusion.2 = f32[8,256]{1,0:T(8,128)S(1)} fusion(bf16[8,8,256,128]{3,2,1,0:T(8,128)(2,1)} %param.4, f32[8,8,128]{2,1,0:T(8,128)S(1)} %bitcast_multiply_fusion.2), kind=kLoop, calls=%fused_computation.8 | loop fusion | flops 6289408 | bytes 4235264 | tf_op jit(solution)/shard_map/reduce_sum | solution.py:15
  168.7 17.4 %psum.15 = f32[8,256]{1,0:T(8,128)S(1)} all-reduce(f32[8,256]{1,0:T(8,128)S(1)} %fusion.2), channel_id=1, replica_groups=mesh['parts'=2,'genome'=8,'reads'=2] {'genome'}, use_global_device_ids=true, to_apply=%region_5.0 | all-reduce | flops 2048 | bytes 16384 | tf_op jit(solution)/shard_map/psum | solution.py:16
  186.1 3.5 %fusion.3 = f32[8,8,128]{2,1,0:T(8,128)S(1)} fusion(bf16[8,8,256,128]{3,2,1,0:T(8,128)(2,1)} %param.4, f32[8,256]{1,0:T(8,128)S(1)} %broadcast_divide_fusion), kind=kLoop, calls=%fused_computation.9 | loop fusion | flops 6283264 | bytes 4235264 | tf_op jit(solution)/shard_map/reduce_sum | solution.py:18
  189.7 0.9 convolution_bitcast_fusion
  190.6 86.0 %all-reduce.7.cloned.1.call-done = f32[24576]{0:T(1024)} async-done(((f32[24576]{0:T(1024)}), f32[24576]{0:T(1024)}) %all-reduce.7.cloned.1.call-update) | async-done | bytes 98320
  276.6 1.4 dynamic-slice_multiply_fusion
  (11 shorter events, 0.2 us)
Async XLA Ops:
  6.5 138.0 %all-reduce.5.cloned.1.call-start = ((), (), s32[]{:S(2)}) async-start(), calls=%async_computation | async-start | bytes 196608
  33.6 25.0 %copy-start = (u32[32]{0:T(128)S(1)}, u32[32]{0:T(128)}, u32[]{:S(2)}) copy-start(u32[32]{0:T(128)} %constant.12) | copy-start | bytes 388
  58.5 218.1 %all-reduce.7.cloned.1.call-start = ((), (), s32[]{:S(2)}) async-start(), calls=%async_computation.1 | async-start | bytes 196608
Sparse Core Ops, SparseCore 0:
  58.6 85.8 all-reduce.4
  190.7 85.8 all-reduce.6
where the time goes:
time: 285 us
  waiting for transfers between devices  171 us (60%)
  blocking collectives  77.8 us (27%)
  other arithmetic  16.9 us (6%)
  between operations  14.1 us (5%)
  local copies, waits for them, and re-layouts  3.42 us (1%)
    unnamed x4, waiting for transfers between devices  171 us
    psum x2, blocking collectives, local_counts(): row_total = lax.psum(row_part, 'genome')  34.8 us
    all_gather x1, blocking collectives, local(): lax.all_gather(start_weights, ('genome', 'reads'), axis=0, tiled=True)  23.3 us
    all_gather x1, blocking collectives, local(): full = lax.all_gather(owned, ('genome', 'reads'), axis=0, tiled=True)  19.7 us
    reduce_sum x2, other arithmetic, local_counts(): contrib = picked * jnp.sum(lik_float * inverse[:, None, :, None], axis=2)  7.02 us
    reduce_sum x2, other arithmetic, local_counts(): row_part = jnp.sum(lik_float * picked[:, :, None, :], axis=(1, 3))  6.17 us
  transfers between devices with their start and end apart: 2, of which 2 were waited for; matrix products, arithmetic and copies ran while one was open for 0% of the time, Pallas kernels for 0%

commit v1 on v0

v1 whole, which is shorter than its diff:
```python
import jax
import jax.numpy as jnp
from jax import lax
from jax.sharding import PartitionSpec as P

ITERS = 2
ALL = ("genome", "reads")


def spread(x, axes):
    n = lax.axis_size(axes)
    sent = jnp.broadcast_to(x[None], (n,) + x.shape)
    return lax.all_to_all(sent, axes, 0, 0, tiled=True)


def sum_genome_steps(x):
    n = lax.axis_size("genome")
    hop = 1
    while hop < n:
        pairs = [(i, i ^ hop) for i in range(n)]
        x = x + lax.ppermute(x, "genome", pairs)
        hop *= 2
    return x


def sum_genome_direct(x):
    return jnp.sum(spread(x, "genome"), axis=0)


def local_counts(table, likelihood, block_ids, slot_valid, sum_genome):
    blocks, cols = table.shape
    picked = table[block_ids] * slot_valid.astype(jnp.float32)[:, :, None]
    lik_float = likelihood.astype(jnp.float32)
    row_part = jnp.sum(lik_float * picked[:, :, None, :], axis=(1, 3))
    row_total = sum_genome(row_part)
    inverse = 1.0 / row_total
    contrib = picked * jnp.sum(lik_float * inverse[:, None, :, None], axis=2)
    flat_ids = block_ids.reshape(-1)
    one_hot = (flat_ids[None, :] == jnp.arange(blocks, dtype=jnp.int32)[:, None]).astype(
        jnp.float32
    )
    return jnp.dot(
        one_hot,
        contrib.reshape(-1, cols),
        preferred_element_type=jnp.float32,
        precision=lax.Precision.HIGHEST,
    )


def local(likelihood, block_ids, slot_valid, start_weights):
    cols = likelihood.shape[3]
    n = lax.axis_size(ALL)
    owned = start_weights.reshape(-1, cols)
    own_blocks = owned.shape[0]
    blocks = own_blocks * n
    total_reads = likelihood.shape[0] * lax.axis_size("reads") * likelihood.shape[2]
    scale = blocks * cols / total_reads
    for step in range(ITERS):
        table = spread(owned, ALL).reshape(blocks, cols)
        summer = sum_genome_steps if step == 0 else sum_genome_direct
        counts = local_counts(table, likelihood, block_ids, slot_valid, summer)
        parts = lax.all_to_all(counts.reshape(n, own_blocks, cols), ALL, 0, 0, tiled=True)
        owned = jnp.sum(parts, axis=0) * scale
    return owned.reshape(-1)


def solution(mesh):
    placed = (
        P(("parts", "reads"), "genome", None, None),
        P(("parts", "reads"), "genome"),
        P(("parts", "reads"), "genome"),
        P(("parts", "genome", "reads")),
    )
    return jax.shard_map(
        local,
        mesh=mesh,
        in_specs=placed,
        out_specs=P(("parts", "genome", "reads")),
        check_vma=False,
    )
```

time: 285 us -> 85.9 us (0.30)
  waiting for transfers between devices: 171 us -> 17.6 us
  blocking collectives: 77.8 us -> 40.9 us
  between operations: 14.1 us -> 0.12 us
  starting transfers between devices: 0.04 us -> 7.88 us
    unnamed x4 -> x0, waiting for transfers between devices: 171 us -> none
    all_gather x2 -> x0, blocking collectives: 43 us -> none  [the longest x1 23.3 us: local(): lax.all_gather(start_weights, ('genome', 'reads'), axis=0, tiled=True)]
    all_to_all x0 -> x4, blocking collectives: none -> 40.9 us  [the longest x2 21 us: local(): lax.all_to_all(counts.reshape(n, own_blocks, cols), ALL, 0, 0, tiled=True)]
    psum x2 -> x0, blocking collectives: 34.8 us -> none  [local_counts(): row_total = lax.psum(row_part, 'genome')]
    ppermute x0 -> x3, waiting for transfers between devices: none -> 11.1 us  [sum_genome_steps(): x = x + lax.ppermute(x, 'genome', pairs)]
    all_to_all x0 -> x1, starting transfers between devices: none -> 7.39 us  [spread(): return lax.all_to_all(sent, axes, 0, 0, tiled=True)]
    all_to_all x0 -> x1, waiting for transfers between devices: none -> 6.47 us  [spread(): return lax.all_to_all(sent, axes, 0, 0, tiled=True)]
  transfers between devices with their start and end apart: 2 -> 4, of which waited for: 2 -> 4; matrix products, arithmetic and copies ran while one was open for 0% -> 2% of each run, Pallas kernels for 0% -> 0%
where the time goes in v1:
time: 85.9 us; the launch traced here: 85.3 us
  blocking collectives  40.9 us (48%)
  waiting for transfers between devices  17.6 us (20%)
  other arithmetic  15.5 us (18%)
  starting transfers between devices  7.88 us (9%)
  local copies, waits for them, and re-layouts  2.83 us (3%)
    all_to_all x2, blocking collectives, local(): lax.all_to_all(counts.reshape(n, own_blocks, cols), ALL, 0, 0, tiled=True)  21 us
    all_to_all x2, blocking collectives, spread(): return lax.all_to_all(sent, axes, 0, 0, tiled=True)  19.8 us
    ppermute x3, waiting for transfers between devices, sum_genome_steps(): x = x + lax.ppermute(x, 'genome', pairs)  11.1 us
    all_to_all x1, starting transfers between devices, spread(): return lax.all_to_all(sent, axes, 0, 0, tiled=True)  7.39 us
    reduce_sum x2, other arithmetic, local_counts(): contrib = picked * jnp.sum(lik_float * inverse[:, None, :, None], axis=2)  7.02 us
    all_to_all x1, waiting for transfers between devices, spread(): return lax.all_to_all(sent, axes, 0, 0, tiled=True)  6.47 us
    reduce_sum x2, other arithmetic, local_counts(): row_part = jnp.sum(lik_float * picked[:, :, None, :], axis=(1, 3))  6.16 us
  transfers between devices with their start and end apart: 4, of which 4 were waited for; matrix products, arithmetic and copies ran while one was open for 2% of the time, Pallas kernels for 0%

profile of v1, /device:TPU:0, one launch (start us, length us, event | category | flops | bytes accessed | tf_op | source)
XLA Modules:
  0.0 85.3 jit_solution(11314237852405566704)
XLA Ops:
  0.0 1.4 %broadcast_in_dim.11 = f32[16,12,128]{2,1,0:T(8,128)} broadcast(f32[12,128]{1,0:T(8,128)} %bitcast.23), dimensions={1,2} | broadcast | bytes 104448 | tf_op jit(solution)/shard_map/broadcast_in_dim | solution.py:12
  1.4 7.4 %all-to-all-start = ((f32[16,12,128]{2,1,0:T(8,128)}), f32[16,12,128]{2,1,0:T(8,128)S(1)}, u32[]{:S(2)}, u32[]{:S(2)}) async-start(f32[16,12,128]{2,1,0:T(8,128)} %broadcast_in_dim.11), calls=%async_computation | async-start | bytes 262144 | tf_op jit(solution)/shard_map/all_to_all | solution.py:13
  8.8 0.7 compare_select_fusion
  9.4 0.7 convert_element_type.4
  10.2 6.5 %all-to-all-done = f32[16,12,128]{2,1,0:T(8,128)S(1)} async-done(((f32[16,12,128]{2,1,0:T(8,128)}), f32[16,12,128]{2,1,0:T(8,128)S(1)}, u32[]{:S(2)}, u32[]{:S(2)}) %all-to-all-start) | async-done | bytes 98336 | tf_op jit(solution)/shard_map/all_to_all | solution.py:13
  16.7 0.6 gather_fusion
  17.4 3.1 %fusion = f32[8,256]{1,0:T(8,128)S(1)} fusion(bf16[8,8,256,128]{3,2,1,0:T(8,128)(2,1)} %param.4, f32[8,8,128]{2,1,0:T(8,128)S(1)} %bitcast_multiply_fusion.5), kind=kLoop, calls=%fused_computation.6 | loop fusion | flops 6289408 | bytes 4235264 | tf_op jit(solution)/shard_map/reduce_sum | solution.py:34
  20.5 3.6 %collective-permute-done = f32[8,256]{1,0:T(8,128)S(1)} collective-permute-done((f32[8,256]{1,0:T(8,128)S(1)}, f32[8,256]{1,0:T(8,128)S(1)}, u32[]{:S(2)}, u32[]{:S(2)}) %collective-permute-start) | collective-permute-done | bytes 8224 | tf_op jit(solution)/shard_map/ppermute | solution.py:21
  24.2 0.1 eq.35
  24.3 3.6 %collective-permute-done.1 = f32[8,256]{1,0:T(8,128)S(1)} collective-permute-done((f32[8,256]{1,0:T(8,128)S(1)}, f32[8,256]{1,0:T(8,128)S(1)}, u32[]{:S(2)}, u32[]{:S(2)}) %collective-permute-start.1) | collective-permute-done | bytes 8224 | tf_op jit(solution)/shard_map/ppermute | solution.py:21
  27.8 0.4 collective-permute-start.2
  28.3 0.1 broadcast_compare_fusion
  28.4 3.9 %collective-permute-done.2 = f32[8,256]{1,0:T(8,128)S(1)} collective-permute-done((f32[8,256]{1,0:T(8,128)S(1)}, f32[8,256]{1,0:T(8,128)S(1)}, u32[]{:S(2)}, u32[]{:S(2)}) %collective-permute-start.2) | collective-permute-done | bytes 8224 | tf_op jit(solution)/shard_map/ppermute | solution.py:21
  32.4 3.5 %fusion.1 = f32[8,8,128]{2,1,0:T(8,128)S(1)} fusion(bf16[8,8,256,128]{3,2,1,0:T(8,128)(2,1)} %param.4, f32[8,256]{1,0:T(8,128)S(1)} %add_divide_fusion), kind=kLoop, calls=%fused_computation.7 | loop fusion | flops 6283264 | bytes 4235264 | tf_op jit(solution)/shard_map/reduce_sum | solution.py:37
  35.9 0.3 fusion.6
  36.2 10.5 %all_to_all.25 = f32[16,12,128]{2,1,0:T(8,128)S(1)} all-to-all(f32[16,12,128]{2,1,0:T(8,128)S(1)} %fusion.6), channel_id=1, replica_groups=mesh['parts'=2,'genome'=8,'reads'=2] {'genome','reads'}, dimensions={0} | all-to-all | bytes 196608 | tf_op jit(solution)/shard_map/all_to_all | solution.py:62
  46.8 10.5 %all_to_all.26 = f32[16,12,128]{2,1,0:T(8,128)S(1)} all-to-all(f32[16,12,128]{2,1,0:T(8,128)S(1)} %broadcast_in_dim.13), channel_id=1, replica_groups=mesh['parts'=2,'genome'=8,'reads'=2] {'genome','reads'}, dimensions={0} | all-to-all | bytes 196608 | tf_op jit(solution)/shard_map/all_to_all | solution.py:13
  57.3 0.6 gather_fusion.1
  58.0 3.1 %fusion.2 = f32[8,256]{1,0:T(8,128)S(1)} fusion(bf16[8,8,256,128]{3,2,1,0:T(8,128)(2,1)} %param.4, f32[8,8,128]{2,1,0:T(8,128)S(1)} %bitcast_multiply_fusion.2), kind=kLoop, calls=%fused_computation.8 | loop fusion | flops 6289408 | bytes 4235264 | tf_op jit(solution)/shard_map/reduce_sum | solution.py:34
  61.1 9.3 %all_to_all.27 = f32[8,8,256]{2,1,0:T(8,128)S(1)} all-to-all(f32[8,8,256]{2,1,0:T(8,128)S(1)} %broadcast_in_dim.14), channel_id=1, replica_groups=mesh['parts'=2,'genome'=8,'reads'=2] {'genome'}, dimensions={0} | all-to-all | bytes 131072 | tf_op jit(solution)/shard_map/all_to_all | solution.py:13
  70.4 3.5 %fusion.3 = f32[8,8,128]{2,1,0:T(8,128)S(1)} fusion(bf16[8,8,256,128]{3,2,1,0:T(8,128)(2,1)} %param.4, f32[8,256]{1,0:T(8,128)S(1)} %broadcast_divide_fusion), kind=kLoop, calls=%fused_computation.9 | loop fusion | flops 6283264 | bytes 4235264 | tf_op jit(solution)/shard_map/reduce_sum | solution.py:37
  73.9 0.3 fusion.4
  74.2 10.5 %all_to_all.28 = f32[16,12,128]{2,1,0:T(8,128)S(1)} all-to-all(f32[16,12,128]{2,1,0:T(8,128)S(1)} %fusion.4), channel_id=1, replica_groups=mesh['parts'=2,'genome'=8,'reads'=2] {'genome','reads'}, dimensions={0} | all-to-all | bytes 196608 | tf_op jit(solution)/shard_map/all_to_all | solution.py:62
  84.7 0.6 multiply_bitcast_fusion
  (22 shorter events, 0.5 us)
Async XLA Ops:
  0.0 24.2 %copy-start = (s32[8,8]{1,0:T(8,128)S(1)}, s32[8,8]{1,0:T(8,128)}, u32[]{:S(2)}) copy-start(s32[8,8]{1,0:T(8,128)} %param.5) | copy-start | bytes 772
  1.4 15.3 %all-to-all-start = ((f32[16,12,128]{2,1,0:T(8,128)}), f32[16,12,128]{2,1,0:T(8,128)S(1)}, u32[]{:S(2)}, u32[]{:S(2)}) async-start(f32[16,12,128]{2,1,0:T(8,128)} %broadcast_in_dim.11), calls=%async_computation | async-start | bytes 262144 | tf_op jit(solution)/shard_map/all_to_all | solution.py:13
  20.5 3.7 %collective-permute-start = (f32[8,256]{1,0:T(8,128)S(1)}, f32[8,256]{1,0:T(8,128)S(1)}, u32[]{:S(2)}, u32[]{:S(2)}) collective-permute-start(f32[8,256]{1,0:T(8,128)S(1)} %fusion), channel_id=1, source_target_pairs={{0,2},{2,0},{4,6},{6,4},{8,10},{10,8},{12,14},{14,12},{1,3},{3,1},... | collective-permute-start | bytes 24584 | tf_op jit(solution)/shard_map/ppermute | solution.py:21
  24.2 3.7 %collective-permute-start.1 = (f32[8,256]{1,0:T(8,128)S(1)}, f32[8,256]{1,0:T(8,128)S(1)}, u32[]{:S(2)}, u32[]{:S(2)}) collective-permute-start(f32[8,256]{1,0:T(8,128)S(1)} %add.19), channel_id=1, source_target_pairs={{0,4},{2,6},{4,0},{6,2},{8,12},{10,14},{12,8},{14,10},{1,5},{3,7},... | collective-permute-start | bytes 24584 | tf_op jit(solution)/shard_map/ppermute | solution.py:21
  27.8 4.5 %collective-permute-start.2 = (f32[8,256]{1,0:T(8,128)S(1)}, f32[8,256]{1,0:T(8,128)S(1)}, u32[]{:S(2)}, u32[]{:S(2)}) collective-permute-start(f32[8,256]{1,0:T(8,128)S(1)} %add.20), channel_id=1, source_target_pairs={{0,8},{2,10},{4,12},{6,14},{8,0},{10,2},{12,4},{14,6},{1,9},{3,11}... | collective-permute-start | bytes 24584 | tf_op jit(solution)/shard_map/ppermute | solution.py:21

commit v2 on v1

v2 whole, which is shorter than its diff:
```python
import jax
import jax.numpy as jnp
from jax import lax
from jax.sharding import PartitionSpec as P

ITERS = 2
ALL = ("genome", "reads")


def radices(n):
    out = []
    while n > 1:
        r = 4 if n % 4 == 0 else 2
        out.append(r)
        n //= r
    return out


def swap(x, axes, k):
    n = lax.axis_size(axes)
    return lax.ppermute(x, axes, [(i, i ^ k) for i in range(n)])


def tree_sum(parts):
    while len(parts) > 1:
        parts = [a + b for a, b in zip(parts[::2], parts[1::2])] + (
            [parts[-1]] if len(parts) % 2 else []
        )
    return parts[0]


def position(k, n):
    place = 0
    for r in radices(n):
        n //= r
        place = place + (k % r) * n
        k = k // r
    return place


def scatter_sum(x, axes):
    stride = 1
    for r in radices(lax.axis_size(axes)):
        rows = x.shape[0] // r
        parts = [x[j * rows : (j + 1) * rows] for j in range(r)]
        x = tree_sum([parts[0]] + [swap(parts[j], axes, j * stride) for j in range(1, r)])
        stride *= r
    return x


def gather(x, axes):
    stride = lax.axis_size(axes)
    for r in radices(stride)[::-1]:
        stride //= r
        x = jnp.concatenate([x] + [swap(x, axes, j * stride) for j in range(1, r)], axis=0)
    return x


def sum_all(x, axes):
    n = lax.axis_size(axes)
    stride = 1
    for r in radices(n)[::-1]:
        x = tree_sum([x] + [swap(x, axes, j * stride) for j in range(1, r)])
        stride *= r
    return x


def local(likelihood, block_ids, slot_valid, start_weights):
    cols = likelihood.shape[3]
    n = lax.axis_size(ALL)
    me = lax.axis_index(ALL)
    owned = start_weights.reshape(-1, cols)
    own_blocks = owned.shape[0]
    blocks = own_blocks * n
    total_reads = likelihood.shape[0] * lax.axis_size("reads") * likelihood.shape[2]
    scale = blocks * cols / total_reads
    place = position((block_ids // own_blocks) ^ me, n) * own_blocks + block_ids % own_blocks
    valid = slot_valid.astype(jnp.float32)[:, :, None]
    one_hot = (
        place.reshape(-1)[None, :] == jnp.arange(blocks, dtype=jnp.int32)[:, None]
    ).astype(jnp.float32)
    lik_float = likelihood.astype(jnp.float32)
    for step in range(ITERS):
        table = gather(owned, ALL)
        picked = table[place] * valid
        row_part = jnp.sum(lik_float * picked[:, :, None, :], axis=(1, 3))
        inverse = 1.0 / sum_all(row_part, "genome")
        contrib = picked * jnp.sum(lik_float * inverse[:, None, :, None], axis=2)
        counts = jnp.dot(
            one_hot,
            contrib.reshape(-1, cols),
            preferred_element_type=jnp.float32,
            precision=lax.Precision.HIGHEST,
        )
        owned = scatter_sum(counts, ALL) * scale
    return owned.reshape(-1)


def solution(mesh):
    placed = (
        P(("parts", "reads"), "genome", None, None),
        P(("parts", "reads"), "genome"),
        P(("parts", "reads"), "genome"),
        P(("parts", "genome", "reads")),
    )
    return jax.shard_map(
        local,
        mesh=mesh,
        in_specs=placed,
        out_specs=P(("parts", "genome", "reads")),
        check_vma=False,
    )
```

time: 85.9 us -> 81.5 us (0.949)
  blocking collectives: 40.9 us -> 0 us
  starting transfers between devices: 7.88 us -> 38.5 us
  waiting for transfers between devices: 17.6 us -> 25.5 us
  other arithmetic: 15.5 us -> 14 us
    all_to_all x4 -> x0, blocking collectives: 40.9 us -> none  [the longest x2 21 us: local(): lax.all_to_all(counts.reshape(n, own_blocks, cols), ALL, 0, 0, tiled=True)]
    ppermute x3 -> x32, starting transfers between devices: 0.5 us -> 38.5 us  [swap(): return lax.ppermute(x, axes, [(i, i ^ k) for i in range(n)])]
    ppermute x3 -> x32, waiting for transfers between devices: 11.1 us -> 25.5 us  [swap(): return lax.ppermute(x, axes, [(i, i ^ k) for i in range(n)])]
    all_to_all x1 -> x0, starting transfers between devices: 7.39 us -> none  [spread(): return lax.all_to_all(sent, axes, 0, 0, tiled=True)]
    all_to_all x1 -> x0, waiting for transfers between devices: 6.47 us -> none  [spread(): return lax.all_to_all(sent, axes, 0, 0, tiled=True)]
    reduce_sum x7 -> x4, other arithmetic: 13.2 us -> 11.1 us  [the longest x2 6.31 us: local(): row_part = jnp.sum(lik_float * picked[:, :, None, :], axis=(1, 3))]
    broadcast_in_dim x4 -> x1, local copies, waits for them, and re-layouts: 1.45 us -> 0.08 us  [local(): picked = table[place] * valid]
    concatenate x0 -> x2, local copies, waits for them, and re-layouts: none -> 1.05 us  [gather(): jnp.concatenate([x] + [swap(x, axes, j * stride) for j in range(1, r)], a...]
  transfers between devices with their start and end apart: 4 -> 32, of which waited for: 4 -> 26; matrix products, arithmetic and copies ran while one was open for 2% -> 2% of each run, Pallas kernels for 0% -> 0%
where the time goes in v2:
time: 81.5 us; the launch traced here: 81.2 us
  starting transfers between devices  38.5 us (47%)
  waiting for transfers between devices  25.5 us (31%)
  other arithmetic  14 us (17%)
  local copies, waits for them, and re-layouts  2.51 us (3%)
    ppermute x32, starting transfers between devices, swap(): return lax.ppermute(x, axes, [(i, i ^ k) for i in range(n)])  38.5 us
    ppermute x32, waiting for transfers between devices, swap(): return lax.ppermute(x, axes, [(i, i ^ k) for i in range(n)])  25.5 us
    reduce_sum x2, other arithmetic, local(): row_part = jnp.sum(lik_float * picked[:, :, None, :], axis=(1, 3))  6.31 us
    reduce_sum x2, other arithmetic, local(): contrib = picked * jnp.sum(lik_float * inverse[:, None, :, None], axis=2)  4.81 us
  transfers between devices with their start and end apart: 32, of which 26 were waited for; matrix products, arithmetic and copies ran while one was open for 2% of the time, Pallas kernels for 0%

profile of v2, /device:TPU:0, one launch (start us, length us, event | category | flops | bytes accessed | tf_op | source)
XLA Modules:
  0.0 81.2 jit_solution(6475637503056810074)
XLA Ops:
  0.0 5.0 %collective-permute-start.2 = (f32[12,128]{1,0:T(8,128)}, f32[12,128]{1,0:T(8,128)S(1)}, u32[]{:S(2)}, u32[]{:S(2)}) collective-permute-start(f32[12,128]{1,0:T(8,128)} %bitcast.13), channel_id=1, source_target_pairs={{0,12},{1,13},{2,14},{3,15},{4,8},{5,9},{6,10},{7,11},{8,4},{9,5},... | collective-permute-start | bytes 18440 | tf_op jit(solution)/shard_map/ppermute | solution.py:21
  6.9 2.9 %collective-permute-done.1 = f32[12,128]{1,0:T(8,128)S(1)} collective-permute-done((f32[12,128]{1,0:T(8,128)}, f32[12,128]{1,0:T(8,128)S(1)}, u32[]{:S(2)}, u32[]{:S(2)}) %collective-permute-start.1) | collective-permute-done | bytes 6176 | tf_op jit(solution)/shard_map/ppermute | solution.py:21
  10.5 1.6 %collective-permute-start.4 = (f32[48,128]{1,0:T(8,128)S(1)}, f32[48,128]{1,0:T(8,128)S(1)}, u32[]{:S(2)}, u32[]{:S(2)}) collective-permute-start(f32[48,128]{1,0:T(8,128)S(1)} %pad_maximum_fusion), channel_id=1, source_target_pairs={{0,2},{1,3},{2,0},{3,1},{4,6},{5,7},{6,4},{7,5},{8,10},{9,11},{10,... | collective-permute-start | bytes 73736 | tf_op jit(solution)/shard_map/ppermute | solution.py:21
  16.0 3.1 %fusion = f32[8,256]{1,0:T(8,128)S(1)} fusion(bf16[8,8,256,128]{3,2,1,0:T(8,128)(2,1)} %param.4, f32[8,8,128]{2,1,0:T(8,128)S(1)} %bitcast_multiply_fusion.5), kind=kLoop, calls=%fused_computation.6 | loop fusion | flops 6289408 | bytes 4235264 | tf_op jit(solution)/shard_map/reduce_sum | solution.py:86
  19.1 1.6 %collective-permute-start.6 = (f32[8,256]{1,0:T(8,128)S(1)}, f32[8,256]{1,0:T(8,128)S(1)}, u32[]{:S(2)}, u32[]{:S(2)}) collective-permute-start(f32[8,256]{1,0:T(8,128)S(1)} %fusion), channel_id=1, source_target_pairs={{0,2},{2,0},{4,6},{6,4},{8,10},{10,8},{12,14},{14,12},{1,3},{3,1},... | collective-permute-start | bytes 24584 | tf_op jit(solution)/shard_map/ppermute | solution.py:21
  20.6 2.1 %collective-permute-done.6 = f32[8,256]{1,0:T(8,128)S(1)} collective-permute-done((f32[8,256]{1,0:T(8,128)S(1)}, f32[8,256]{1,0:T(8,128)S(1)}, u32[]{:S(2)}, u32[]{:S(2)}) %collective-permute-start.6) | collective-permute-done | bytes 8224 | tf_op jit(solution)/shard_map/ppermute | solution.py:21
  22.8 1.5 %collective-permute-start.9 = (f32[8,256]{1,0:T(8,128)S(1)}, f32[8,256]{1,0:T(8,128)S(1)}, u32[]{:S(2)}, u32[]{:S(2)}) collective-permute-start(f32[8,256]{1,0:T(8,128)S(1)} %add.96), channel_id=1, source_target_pairs={{0,12},{2,14},{4,8},{6,10},{8,4},{10,6},{12,0},{14,2},{1,13},{3,15... | collective-permute-start | bytes 24584 | tf_op jit(solution)/shard_map/ppermute | solution.py:21
  24.8 2.4 %collective-permute-start.7 = (f32[8,256]{1,0:T(8,128)S(1)}, f32[8,256]{1,0:T(8,128)S(1)}, u32[]{:S(2)}, u32[]{:S(2)}) collective-permute-start(f32[8,256]{1,0:T(8,128)S(1)} %add.96), channel_id=1, source_target_pairs={{0,4},{2,6},{4,0},{6,2},{8,12},{10,14},{12,8},{14,10},{1,5},{3,7},... | collective-permute-start | bytes 24584 | tf_op jit(solution)/shard_map/ppermute | solution.py:21
  28.9 3.5 %fusion.1 = f32[8,8,128]{2,1,0:T(8,128)S(1)} fusion(bf16[8,8,256,128]{3,2,1,0:T(8,128)(2,1)} %param.4, f32[8,256]{1,0:T(8,128)S(1)} %add_divide_fusion.1), kind=kLoop, calls=%fused_computation.7 | loop fusion | flops 6283264 | bytes 4235264 | tf_op jit(solution)/shard_map/reduce_sum | solution.py:88
  32.8 1.6 %collective-permute-start.11 = (f32[48,128]{1,0:T(8,128)S(1)}, f32[48,128]{1,0:T(8,128)S(1)}, u32[]{:S(2)}, u32[]{:S(2)}) collective-permute-start(f32[48,128]{1,0:T(8,128)S(1)} %get-tuple-element.11), channel_id=1, source_target_pairs={{0,2},{1,3},{2,0},{3,1},{4,6},{5,7},{6,4},{7,5},{8,10},{9,11},{10,... | collective-permute-start | bytes 73736 | tf_op jit(solution)/shard_map/ppermute | solution.py:21
  34.6 1.6 %collective-permute-done.12 = f32[48,128]{1,0:T(8,128)S(1)} collective-permute-done((f32[48,128]{1,0:T(8,128)S(1)}, f32[48,128]{1,0:T(8,128)S(1)}, u32[]{:S(2)}, u32[]{:S(2)}) %collective-permute-start.12) | collective-permute-done | bytes 24608 | tf_op jit(solution)/shard_map/ppermute | solution.py:21
  36.7 2.6 %collective-permute-start.15 = (f32[12,128]{1,0:T(8,128)S(1)}, f32[12,128]{1,0:T(8,128)S(1)}, u32[]{:S(2)}, u32[]{:S(2)}) collective-permute-start(f32[12,128]{1,0:T(8,128)S(1)} %get-tuple-element.16), channel_id=1, source_target_pairs={{0,12},{1,13},{2,14},{3,15},{4,8},{5,9},{6,10},{7,11},{8,4},{9,5},... | collective-permute-start | bytes 18440 | tf_op jit(solution)/shard_map/ppermute | solution.py:21
  42.2 1.6 %collective-permute-done.14 = f32[12,128]{1,0:T(8,128)S(1)} collective-permute-done((f32[12,128]{1,0:T(8,128)S(1)}, f32[12,128]{1,0:T(8,128)S(1)}, u32[]{:S(2)}, u32[]{:S(2)}) %collective-permute-start.14) | collective-permute-done | bytes 6176 | tf_op jit(solution)/shard_map/ppermute | solution.py:21
  46.3 2.0 %collective-permute-start.16 = (f32[12,128]{1,0:T(8,128)S(1)}, f32[12,128]{1,0:T(8,128)S(1)}, u32[]{:S(2)}, u32[]{:S(2)}) collective-permute-start(f32[12,128]{1,0:T(8,128)S(1)} %fusion.18), channel_id=1, source_target_pairs={{0,4},{1,5},{2,6},{3,7},{4,0},{5,1},{6,2},{7,3},{8,12},{9,13},{10,... | collective-permute-start | bytes 18440 | tf_op jit(solution)/shard_map/ppermute | solution.py:21
  50.0 1.6 %collective-permute-start.20 = (f32[48,128]{1,0:T(8,128)S(1)}, f32[48,128]{1,0:T(8,128)S(1)}, u32[]{:S(2)}, u32[]{:S(2)}) collective-permute-start(f32[48,128]{1,0:T(8,128)S(1)} %pad_maximum_fusion.1), channel_id=1, source_target_pairs={{0,2},{1,3},{2,0},{3,1},{4,6},{5,7},{6,4},{7,5},{8,10},{9,11},{10,... | collective-permute-start | bytes 73736 | tf_op jit(solution)/shard_map/ppermute | solution.py:21
  51.9 1.6 %collective-permute-done.21 = f32[48,128]{1,0:T(8,128)S(1)} collective-permute-done((f32[48,128]{1,0:T(8,128)S(1)}, f32[48,128]{1,0:T(8,128)S(1)}, u32[]{:S(2)}, u32[]{:S(2)}) %collective-permute-start.21) | collective-permute-done | bytes 24608 | tf_op jit(solution)/shard_map/ppermute | solution.py:21
  54.8 3.2 %fusion.2 = f32[8,256]{1,0:T(8,128)S(1)} fusion(bf16[8,8,256,128]{3,2,1,0:T(8,128)(2,1)} %param.4, f32[8,8,128]{2,1,0:T(8,128)S(1)} %bitcast_multiply_fusion.2), kind=kLoop, calls=%fused_computation.8 | loop fusion | flops 6289408 | bytes 4235264 | tf_op jit(solution)/shard_map/reduce_sum | solution.py:86
  58.0 1.6 %collective-permute-start.22 = (f32[8,256]{1,0:T(8,128)S(1)}, f32[8,256]{1,0:T(8,128)S(1)}, u32[]{:S(2)}, u32[]{:S(2)}) collective-permute-start(f32[8,256]{1,0:T(8,128)S(1)} %fusion.2), channel_id=1, source_target_pairs={{0,2},{2,0},{4,6},{6,4},{8,10},{10,8},{12,14},{14,12},{1,3},{3,1},... | collective-permute-start | bytes 24584 | tf_op jit(solution)/shard_map/ppermute | solution.py:21
  59.6 2.1 %collective-permute-done.22 = f32[8,256]{1,0:T(8,128)S(1)} collective-permute-done((f32[8,256]{1,0:T(8,128)S(1)}, f32[8,256]{1,0:T(8,128)S(1)}, u32[]{:S(2)}, u32[]{:S(2)}) %collective-permute-start.22) | collective-permute-done | bytes 8224 | tf_op jit(solution)/shard_map/ppermute | solution.py:21
  61.7 2.5 %collective-permute-start.25 = (f32[8,256]{1,0:T(8,128)S(1)}, f32[8,256]{1,0:T(8,128)S(1)}, u32[]{:S(2)}, u32[]{:S(2)}) collective-permute-start(f32[8,256]{1,0:T(8,128)S(1)} %add.106), channel_id=1, source_target_pairs={{0,12},{2,14},{4,8},{6,10},{8,4},{10,6},{12,0},{14,2},{1,13},{3,15... | collective-permute-start | bytes 24584 | tf_op jit(solution)/shard_map/ppermute | solution.py:21
  67.2 1.6 %collective-permute-done.24 = f32[8,256]{1,0:T(8,128)S(1)} collective-permute-done((f32[8,256]{1,0:T(8,128)S(1)}, f32[8,256]{1,0:T(8,128)S(1)}, u32[]{:S(2)}, u32[]{:S(2)}) %collective-permute-start.24) | collective-permute-done | bytes 8224 | tf_op jit(solution)/shard_map/ppermute | solution.py:21
  70.5 1.6 %collective-permute-start.27 = (f32[48,128]{1,0:T(8,128)S(1)}, f32[48,128]{1,0:T(8,128)S(1)}, u32[]{:S(2)}, u32[]{:S(2)}) collective-permute-start(f32[48,128]{1,0:T(8,128)S(1)} %get-tuple-element.8), channel_id=1, source_target_pairs={{0,2},{1,3},{2,0},{3,1},{4,6},{5,7},{6,4},{7,5},{8,10},{9,11},{10,... | collective-permute-start | bytes 73736 | tf_op jit(solution)/shard_map/ppermute | solution.py:21
  72.4 1.6 %collective-permute-done.28 = f32[48,128]{1,0:T(8,128)S(1)} collective-permute-done((f32[48,128]{1,0:T(8,128)S(1)}, f32[48,128]{1,0:T(8,128)S(1)}, u32[]{:S(2)}, u32[]{:S(2)}) %collective-permute-start.28) | collective-permute-done | bytes 24608 | tf_op jit(solution)/shard_map/ppermute | solution.py:21
  76.9 2.0 %collective-permute-start.29 = (f32[12,128]{1,0:T(8,128)S(1)}, f32[12,128]{1,0:T(8,128)S(1)}, u32[]{:S(2)}, u32[]{:S(2)}) collective-permute-start(f32[12,128]{1,0:T(8,128)S(1)} %get-tuple-element.15), channel_id=1, source_target_pairs={{0,4},{1,5},{2,6},{3,7},{4,0},{5,1},{6,2},{7,3},{8,12},{9,13},{10,... | collective-permute-start | bytes 18440 | tf_op jit(solution)/shard_map/ppermute | solution.py:21
  (74 shorter events, 28.6 us)
Async XLA Ops:
  0.0 6.9 %collective-permute-start.2 = (f32[12,128]{1,0:T(8,128)}, f32[12,128]{1,0:T(8,128)S(1)}, u32[]{:S(2)}, u32[]{:S(2)}) collective-permute-start(f32[12,128]{1,0:T(8,128)} %bitcast.13), channel_id=1, source_target_pairs={{0,12},{1,13},{2,14},{3,15},{4,8},{5,9},{6,10},{7,11},{8,4},{9,5},... | collective-permute-start | bytes 18440 | tf_op jit(solution)/shard_map/ppermute | solution.py:21
  5.0 4.8 %collective-permute-start.1 = (f32[12,128]{1,0:T(8,128)}, f32[12,128]{1,0:T(8,128)S(1)}, u32[]{:S(2)}, u32[]{:S(2)}) collective-permute-start(f32[12,128]{1,0:T(8,128)} %bitcast.14), channel_id=1, source_target_pairs={{0,8},{1,9},{2,10},{3,11},{4,12},{5,13},{6,14},{7,15},{8,0},{9,1},... | collective-permute-start | bytes 18440 | tf_op jit(solution)/shard_map/ppermute | solution.py:21
  5.1 4.8 %collective-permute-start = (f32[12,128]{1,0:T(8,128)}, f32[12,128]{1,0:T(8,128)S(1)}, u32[]{:S(2)}, u32[]{:S(2)}) collective-permute-start(f32[12,128]{1,0:T(8,128)} %bitcast.15), channel_id=1, source_target_pairs={{0,4},{1,5},{2,6},{3,7},{4,0},{5,1},{6,2},{7,3},{8,12},{9,13},{10,... | collective-permute-start | bytes 18440 | tf_op jit(solution)/shard_map/ppermute | solution.py:21
  10.5 3.9 %collective-permute-start.4 = (f32[48,128]{1,0:T(8,128)S(1)}, f32[48,128]{1,0:T(8,128)S(1)}, u32[]{:S(2)}, u32[]{:S(2)}) collective-permute-start(f32[48,128]{1,0:T(8,128)S(1)} %pad_maximum_fusion), channel_id=1, source_target_pairs={{0,2},{1,3},{2,0},{3,1},{4,6},{5,7},{6,4},{7,5},{8,10},{9,11},{10,... | collective-permute-start | bytes 73736 | tf_op jit(solution)/shard_map/ppermute | solution.py:21
  19.1 3.7 %collective-permute-start.6 = (f32[8,256]{1,0:T(8,128)S(1)}, f32[8,256]{1,0:T(8,128)S(1)}, u32[]{:S(2)}, u32[]{:S(2)}) collective-permute-start(f32[8,256]{1,0:T(8,128)S(1)} %fusion), channel_id=1, source_target_pairs={{0,2},{2,0},{4,6},{6,4},{8,10},{10,8},{12,14},{14,12},{1,3},{3,1},... | collective-permute-start | bytes 24584 | tf_op jit(solution)/shard_map/ppermute | solution.py:21
  22.8 5.4 %collective-permute-start.9 = (f32[8,256]{1,0:T(8,128)S(1)}, f32[8,256]{1,0:T(8,128)S(1)}, u32[]{:S(2)}, u32[]{:S(2)}) collective-permute-start(f32[8,256]{1,0:T(8,128)S(1)} %add.96), channel_id=1, source_target_pairs={{0,12},{2,14},{4,8},{6,10},{8,4},{10,6},{12,0},{14,2},{1,13},{3,15... | collective-permute-start | bytes 24584 | tf_op jit(solution)/shard_map/ppermute | solution.py:21
  24.3 4.6 %collective-permute-start.8 = (f32[8,256]{1,0:T(8,128)S(1)}, f32[8,256]{1,0:T(8,128)S(1)}, u32[]{:S(2)}, u32[]{:S(2)}) collective-permute-start(f32[8,256]{1,0:T(8,128)S(1)} %add.96), channel_id=1, source_target_pairs={{0,8},{2,10},{4,12},{6,14},{8,0},{10,2},{12,4},{14,6},{1,9},{3,11}... | collective-permute-start | bytes 24584 | tf_op jit(solution)/shard_map/ppermute | solution.py:21
  24.8 4.1 %collective-permute-start.7 = (f32[8,256]{1,0:T(8,128)S(1)}, f32[8,256]{1,0:T(8,128)S(1)}, u32[]{:S(2)}, u32[]{:S(2)}) collective-permute-start(f32[8,256]{1,0:T(8,128)S(1)} %add.96), channel_id=1, source_target_pairs={{0,4},{2,6},{4,0},{6,2},{8,12},{10,14},{12,8},{14,10},{1,5},{3,7},... | collective-permute-start | bytes 24584 | tf_op jit(solution)/shard_map/ppermute | solution.py:21
  32.8 3.9 %collective-permute-start.11 = (f32[48,128]{1,0:T(8,128)S(1)}, f32[48,128]{1,0:T(8,128)S(1)}, u32[]{:S(2)}, u32[]{:S(2)}) collective-permute-start(f32[48,128]{1,0:T(8,128)S(1)} %get-tuple-element.11), channel_id=1, source_target_pairs={{0,2},{1,3},{2,0},{3,1},{4,6},{5,7},{6,4},{7,5},{8,10},{9,11},{10,... | collective-permute-start | bytes 73736 | tf_op jit(solution)/shard_map/ppermute | solution.py:21
  36.7 5.5 %collective-permute-start.15 = (f32[12,128]{1,0:T(8,128)S(1)}, f32[12,128]{1,0:T(8,128)S(1)}, u32[]{:S(2)}, u32[]{:S(2)}) collective-permute-start(f32[12,128]{1,0:T(8,128)S(1)} %get-tuple-element.16), channel_id=1, source_target_pairs={{0,12},{1,13},{2,14},{3,15},{4,8},{5,9},{6,10},{7,11},{8,4},{9,5},... | collective-permute-start | bytes 18440 | tf_op jit(solution)/shard_map/ppermute | solution.py:21
  39.2 4.6 %collective-permute-start.14 = (f32[12,128]{1,0:T(8,128)S(1)}, f32[12,128]{1,0:T(8,128)S(1)}, u32[]{:S(2)}, u32[]{:S(2)}) collective-permute-start(f32[12,128]{1,0:T(8,128)S(1)} %get-tuple-element.17), channel_id=1, source_target_pairs={{0,8},{1,9},{2,10},{3,11},{4,12},{5,13},{6,14},{7,15},{8,0},{9,1},... | collective-permute-start | bytes 18440 | tf_op jit(solution)/shard_map/ppermute | solution.py:21
  40.1 3.7 %collective-permute-start.13 = (f32[12,128]{1,0:T(8,128)S(1)}, f32[12,128]{1,0:T(8,128)S(1)}, u32[]{:S(2)}, u32[]{:S(2)}) collective-permute-start(f32[12,128]{1,0:T(8,128)S(1)} %get-tuple-element.18), channel_id=1, source_target_pairs={{0,4},{1,5},{2,6},{3,7},{4,0},{5,1},{6,2},{7,3},{8,12},{9,13},{10,... | collective-permute-start | bytes 18440 | tf_op jit(solution)/shard_map/ppermute | solution.py:21
  43.9 5.4 %collective-permute-start.18 = (f32[12,128]{1,0:T(8,128)S(1)}, f32[12,128]{1,0:T(8,128)S(1)}, u32[]{:S(2)}, u32[]{:S(2)}) collective-permute-start(f32[12,128]{1,0:T(8,128)S(1)} %fusion.18), channel_id=1, source_target_pairs={{0,12},{1,13},{2,14},{3,15},{4,8},{5,9},{6,10},{7,11},{8,4},{9,5},... | collective-permute-start | bytes 18440 | tf_op jit(solution)/shard_map/ppermute | solution.py:21
  45.3 4.5 %collective-permute-start.17 = (f32[12,128]{1,0:T(8,128)S(1)}, f32[12,128]{1,0:T(8,128)S(1)}, u32[]{:S(2)}, u32[]{:S(2)}) collective-permute-start(f32[12,128]{1,0:T(8,128)S(1)} %fusion.18), channel_id=1, source_target_pairs={{0,8},{1,9},{2,10},{3,11},{4,12},{5,13},{6,14},{7,15},{8,0},{9,1},... | collective-permute-start | bytes 18440 | tf_op jit(solution)/shard_map/ppermute | solution.py:21
  46.3 3.7 %collective-permute-start.16 = (f32[12,128]{1,0:T(8,128)S(1)}, f32[12,128]{1,0:T(8,128)S(1)}, u32[]{:S(2)}, u32[]{:S(2)}) collective-permute-start(f32[12,128]{1,0:T(8,128)S(1)} %fusion.18), channel_id=1, source_target_pairs={{0,4},{1,5},{2,6},{3,7},{4,0},{5,1},{6,2},{7,3},{8,12},{9,13},{10,... | collective-permute-start | bytes 18440 | tf_op jit(solution)/shard_map/ppermute | solution.py:21
  50.0 3.9 %collective-permute-start.20 = (f32[48,128]{1,0:T(8,128)S(1)}, f32[48,128]{1,0:T(8,128)S(1)}, u32[]{:S(2)}, u32[]{:S(2)}) collective-permute-start(f32[48,128]{1,0:T(8,128)S(1)} %pad_maximum_fusion.1), channel_id=1, source_target_pairs={{0,2},{1,3},{2,0},{3,1},{4,6},{5,7},{6,4},{7,5},{8,10},{9,11},{10,... | collective-permute-start | bytes 73736 | tf_op jit(solution)/shard_map/ppermute | solution.py:21
  58.0 3.7 %collective-permute-start.22 = (f32[8,256]{1,0:T(8,128)S(1)}, f32[8,256]{1,0:T(8,128)S(1)}, u32[]{:S(2)}, u32[]{:S(2)}) collective-permute-start(f32[8,256]{1,0:T(8,128)S(1)} %fusion.2), channel_id=1, source_target_pairs={{0,2},{2,0},{4,6},{6,4},{8,10},{10,8},{12,14},{14,12},{1,3},{3,1},... | collective-permute-start | bytes 24584 | tf_op jit(solution)/shard_map/ppermute | solution.py:21
  61.7 5.4 %collective-permute-start.25 = (f32[8,256]{1,0:T(8,128)S(1)}, f32[8,256]{1,0:T(8,128)S(1)}, u32[]{:S(2)}, u32[]{:S(2)}) collective-permute-start(f32[8,256]{1,0:T(8,128)S(1)} %add.106), channel_id=1, source_target_pairs={{0,12},{2,14},{4,8},{6,10},{8,4},{10,6},{12,0},{14,2},{1,13},{3,15... | collective-permute-start | bytes 24584 | tf_op jit(solution)/shard_map/ppermute | solution.py:21
  64.2 4.5 %collective-permute-start.24 = (f32[8,256]{1,0:T(8,128)S(1)}, f32[8,256]{1,0:T(8,128)S(1)}, u32[]{:S(2)}, u32[]{:S(2)}) collective-permute-start(f32[8,256]{1,0:T(8,128)S(1)} %add.106), channel_id=1, source_target_pairs={{0,8},{2,10},{4,12},{6,14},{8,0},{10,2},{12,4},{14,6},{1,9},{3,11}... | collective-permute-start | bytes 24584 | tf_op jit(solution)/shard_map/ppermute | solution.py:21
  65.2 3.7 %collective-permute-start.23 = (f32[8,256]{1,0:T(8,128)S(1)}, f32[8,256]{1,0:T(8,128)S(1)}, u32[]{:S(2)}, u32[]{:S(2)}) collective-permute-start(f32[8,256]{1,0:T(8,128)S(1)} %add.106), channel_id=1, source_target_pairs={{0,4},{2,6},{4,0},{6,2},{8,12},{10,14},{12,8},{14,10},{1,5},{3,7},... | collective-permute-start | bytes 24584 | tf_op jit(solution)/shard_map/ppermute | solution.py:21
  70.5 3.9 %collective-permute-start.27 = (f32[48,128]{1,0:T(8,128)S(1)}, f32[48,128]{1,0:T(8,128)S(1)}, u32[]{:S(2)}, u32[]{:S(2)}) collective-permute-start(f32[48,128]{1,0:T(8,128)S(1)} %get-tuple-element.8), channel_id=1, source_target_pairs={{0,2},{1,3},{2,0},{3,1},{4,6},{5,7},{6,4},{7,5},{8,10},{9,11},{10,... | collective-permute-start | bytes 73736 | tf_op jit(solution)/shard_map/ppermute | solution.py:21
  74.4 5.5 %collective-permute-start.31 = (f32[12,128]{1,0:T(8,128)S(1)}, f32[12,128]{1,0:T(8,128)S(1)}, u32[]{:S(2)}, u32[]{:S(2)}) collective-permute-start(f32[12,128]{1,0:T(8,128)S(1)} %get-tuple-element.13), channel_id=1, source_target_pairs={{0,12},{1,13},{2,14},{3,15},{4,8},{5,9},{6,10},{7,11},{8,4},{9,5},... | collective-permute-start | bytes 18440 | tf_op jit(solution)/shard_map/ppermute | solution.py:21
  75.9 4.5 %collective-permute-start.30 = (f32[12,128]{1,0:T(8,128)S(1)}, f32[12,128]{1,0:T(8,128)S(1)}, u32[]{:S(2)}, u32[]{:S(2)}) collective-permute-start(f32[12,128]{1,0:T(8,128)S(1)} %get-tuple-element.14), channel_id=1, source_target_pairs={{0,8},{1,9},{2,10},{3,11},{4,12},{5,13},{6,14},{7,15},{8,0},{9,1},... | collective-permute-start | bytes 18440 | tf_op jit(solution)/shard_map/ppermute | solution.py:21
  76.9 3.7 %collective-permute-start.29 = (f32[12,128]{1,0:T(8,128)S(1)}, f32[12,128]{1,0:T(8,128)S(1)}, u32[]{:S(2)}, u32[]{:S(2)}) collective-permute-start(f32[12,128]{1,0:T(8,128)S(1)} %get-tuple-element.15), channel_id=1, source_target_pairs={{0,4},{1,5},{2,6},{3,7},{4,0},{5,1},{6,2},{7,3},{8,12},{9,13},{10,... | collective-permute-start | bytes 18440 | tf_op jit(solution)/shard_map/ppermute | solution.py:21
  (9 other events, 37.3 us)

commit v3 on v2

v3 whole, which is shorter than its diff:
```python
import jax
import jax.numpy as jnp
from jax import lax
from jax.experimental import pallas as pl
from jax.experimental.pallas import tpu as pltpu
from jax.sharding import PartitionSpec as P

ITERS = 2
ALL = ("genome", "reads")
TERMS = 16


def radices(n):
    out = []
    while n > 1:
        r = 4 if n % 4 == 0 else 2
        out.append(r)
        n //= r
    return out


def swap(x, axes, k):
    n = lax.axis_size(axes)
    return lax.ppermute(x, axes, [(i, i ^ k) for i in range(n)])


def tree_sum(parts):
    while len(parts) > 1:
        parts = [a + b for a, b in zip(parts[::2], parts[1::2])] + (
            [parts[-1]] if len(parts) % 2 else []
        )
    return parts[0]


def position(k, n):
    place = 0
    for r in radices(n):
        n //= r
        place = place + (k % r) * n
        k = k // r
    return place


def scatter_sum(x, axes):
    stride = 1
    for r in radices(lax.axis_size(axes)):
        rows = x.shape[0] // r
        parts = [x[j * rows : (j + 1) * rows] for j in range(r)]
        x = tree_sum([parts[0]] + [swap(parts[j], axes, j * stride) for j in range(1, r)])
        stride *= r
    return x


def gather_high(x, axes):
    stride = lax.axis_size(axes)
    for r in radices(stride)[:0:-1]:
        stride //= r
        x = jnp.concatenate([x] + [swap(x, axes, j * stride) for j in range(1, r)], axis=0)
    return x


def spread(x, axes):
    n = lax.axis_size(axes)
    sent = jnp.broadcast_to(x[None], (n,) + x.shape)
    return lax.all_to_all(sent, axes, 0, 0, tiled=True)


def dot_exact(a, b):
    return jnp.dot(
        a, b, preferred_element_type=jnp.float32, precision=lax.Precision.HIGHEST
    )


def split(row):
    x = jnp.broadcast_to(row, (TERMS, row.shape[1]))
    hi = x.astype(jnp.bfloat16).astype(jnp.float32)
    rest = x - hi
    mid = rest.astype(jnp.bfloat16).astype(jnp.float32)
    low = rest - mid
    at = lax.broadcasted_iota(jnp.int32, x.shape, 0)
    out = jnp.where(at == 0, hi, jnp.where(at == 1, mid, jnp.where(at == 2, low, 0.0)))
    return out.astype(jnp.bfloat16)


def row_kernel(picked_ref, lik_ref, out_ref):
    read_blocks, slots, reads, cols = lik_ref.shape
    for b in range(read_blocks):
        total = None
        for s in range(0, slots, 2):
            at = b * slots + s
            left = jnp.concatenate(
                [split(picked_ref[at : at + 1, :]), split(picked_ref[at + 1 : at + 2, :])], axis=1
            )
            right = jnp.concatenate([lik_ref[b, s], lik_ref[b, s + 1]], axis=1)
            part = lax.dot_general(
                left, right, (((1,), (1,)), ((), ())), preferred_element_type=jnp.float32
            )
            total = part if total is None else total + part
        out_ref[b : b + 1, :] = jnp.sum(total, axis=0, keepdims=True)


def col_kernel(parts_ref, picked_ref, lik_ref, out_ref, inverse_ref):
    read_blocks, slots, reads, cols = lik_ref.shape
    total = parts_ref[0]
    for i in range(1, parts_ref.shape[0]):
        total = total + parts_ref[i]
    inverse_ref[...] = 1.0 / total
    for b in range(read_blocks):
        left = split(inverse_ref[b : b + 1, :])
        for s in range(0, slots, 2):
            at = b * slots + s
            right = jnp.concatenate([lik_ref[b, s], lik_ref[b, s + 1]], axis=1)
            part = jnp.dot(left, right, preferred_element_type=jnp.float32)
            summed = jnp.sum(part, axis=0, keepdims=True)
            out_ref[at : at + 1, :] = picked_ref[at : at + 1, :] * summed[:, :cols]
            out_ref[at + 1 : at + 2, :] = picked_ref[at + 1 : at + 2, :] * summed[:, cols:]


def call(kernel, shape, scratch, *operands):
    vmem = pl.BlockSpec(memory_space=pltpu.VMEM)
    return pl.pallas_call(
        kernel,
        out_shape=jax.ShapeDtypeStruct(shape, jnp.float32),
        in_specs=[vmem] * len(operands),
        out_specs=vmem,
        scratch_shapes=scratch,
        compiler_params=pltpu.CompilerParams(vmem_limit_bytes=40 * 2**20),
    )(*operands)


def local(likelihood, block_ids, slot_valid, start_weights):
    read_blocks, slots, reads, cols = likelihood.shape
    n = lax.axis_size(ALL)
    me = lax.axis_index(ALL)
    near = radices(n)[0]
    own_weights = start_weights.reshape(-1, cols)
    own_blocks = own_weights.shape[0]
    blocks = own_blocks * n
    all_slots = read_blocks * slots
    total_reads = read_blocks * lax.axis_size("reads") * reads
    scale = blocks * cols / total_reads
    likelihood = pltpu.with_memory_space_constraint(likelihood, pltpu.VMEM)

    ids = block_ids.reshape(-1)
    valid = slot_valid.reshape(-1)
    owner = position((ids // own_blocks) ^ me, n)

    id_rows = -(-all_slots // cols)
    rows = -(-(own_blocks + id_rows) // 8) * 8
    coded = jnp.where(valid > 0, ids, -1).astype(jnp.float32)
    coded = jnp.pad(coded, (0, id_rows * cols - all_slots)).reshape(id_rows, cols)
    sent = jnp.pad(
        jnp.concatenate([own_weights, coded], axis=0), ((0, rows - own_blocks - id_rows), (0, 0))
    )
    far = gather_high(sent, ALL)
    full = jnp.concatenate([far] + [swap(far, ALL, j) for j in range(1, near)], axis=0)
    every = full.reshape(near, n // near, rows, cols)
    known = every[:, :, own_blocks : own_blocks + id_rows].reshape(near, n // near, -1)
    known = known[:, :, :all_slots]
    wanted = known[:, 0].reshape(-1)
    given = known[0].reshape(-1)
    match = ((wanted[:, None] == given[None, :]) & (wanted[:, None] >= 0)).astype(jnp.float32)

    place = jnp.where(valid > 0, owner * rows + ids % own_blocks, -1)
    pick = (place[:, None] == jnp.arange(n * rows, dtype=jnp.int32)[None, :]).astype(jnp.float32)
    picked = dot_exact(pick, full)

    for step in range(ITERS):
        row_part = call(row_kernel, (read_blocks, reads), [], picked, likelihood)
        row_parts = spread(row_part, "genome")
        contrib = call(
            col_kernel,
            (all_slots, cols),
            [pltpu.VMEM((read_blocks, reads), jnp.float32)],
            row_parts,
            picked,
            likelihood,
        )
        if step + 1 < ITERS:
            sums = dot_exact(match, gather_high(contrib, ALL))
            parts = [sums[j * all_slots : (j + 1) * all_slots] for j in range(near)]
            picked = scale * tree_sum(
                [parts[0]] + [swap(parts[j], ALL, j) for j in range(1, near)]
            )

    place = owner * own_blocks + ids % own_blocks
    count = (jnp.arange(blocks, dtype=jnp.int32)[:, None] == place[None, :]).astype(jnp.float32)
    return (scatter_sum(dot_exact(count, contrib), ALL) * scale).reshape(-1)


def solution(mesh):
    placed = (
        P(("parts", "reads"), "genome", None, None),
        P(("parts", "reads"), "genome"),
        P(("parts", "reads"), "genome"),
        P(("parts", "genome", "reads")),
    )
    return jax.shard_map(
        local,
        mesh=mesh,
        in_specs=placed,
        out_specs=P(("parts", "genome", "reads")),
        check_vma=False,
    )
```

time: 81.5 us -> 73.8 us (0.906)
  starting transfers between devices: 38.5 us -> 23.6 us
  other arithmetic: 14 us -> 2.08 us
  blocking collectives: 0 us -> 10.8 us
  local copies, waits for them, and re-layouts: 2.51 us -> 8.3 us
  Pallas kernels: 0 us -> 3.75 us
  waiting for transfers between devices: 25.5 us -> 24 us
    ppermute x32 -> x18, starting transfers between devices: 38.5 us -> 20.2 us  [swap(): return lax.ppermute(x, axes, [(i, i ^ k) for i in range(n)])]
    reduce_sum x4 -> x0, other arithmetic: 11.1 us -> none  [the longest x2 6.31 us: local(): row_part = jnp.sum(lik_float * picked[:, :, None, :], axis=(1, 3))]
    all_to_all x0 -> x1, blocking collectives: none -> 10.8 us  [spread(): return lax.all_to_all(sent, axes, 0, 0, tiled=True)]
    ppermute x32 -> x18, waiting for transfers between devices: 25.5 us -> 17.3 us  [swap(): return lax.ppermute(x, axes, [(i, i ^ k) for i in range(n)])]
    all_to_all x0 -> x1, waiting for transfers between devices: none -> 6.72 us  [spread(): return lax.all_to_all(sent, axes, 0, 0, tiled=True)]
    unnamed x2 -> x11, local copies, waits for them, and re-layouts: 0.01 us -> 6.57 us
    pallas_call x0 -> x4, Pallas kernels: none -> 3.75 us  [call(): pl.pallas_call(kernel, out_shape=jax.ShapeDtypeStruct(shape, jnp.float32)...]
    all_to_all x0 -> x1, starting transfers between devices: none -> 3.35 us  [spread(): return lax.all_to_all(sent, axes, 0, 0, tiled=True)]
  transfers between devices with their start and end apart: 32 -> 19, of which waited for: 26 -> 12; matrix products, arithmetic and copies ran while one was open for 2% -> 0% of each run, Pallas kernels for 0% -> 0%
where the time goes in v3:
time: 73.8 us; the launch traced here: 73.4 us
  waiting for transfers between devices  24 us (33%)
  starting transfers between devices  23.6 us (32%)
  blocking collectives  10.8 us (15%)
  local copies, waits for them, and re-layouts  8.3 us (11%)
  Pallas kernels  3.75 us (5%)
  other arithmetic  2.08 us (3%)
    ppermute x18, starting transfers between devices, swap(): return lax.ppermute(x, axes, [(i, i ^ k) for i in range(n)])  20.2 us
    ppermute x18, waiting for transfers between devices, swap(): return lax.ppermute(x, axes, [(i, i ^ k) for i in range(n)])  17.3 us
    all_to_all x1, blocking collectives, spread(): return lax.all_to_all(sent, axes, 0, 0, tiled=True)  10.8 us
    all_to_all x1, waiting for transfers between devices, spread(): return lax.all_to_all(sent, axes, 0, 0, tiled=True)  6.72 us
    unnamed x11, local copies, waits for them, and re-layouts  6.57 us
    pallas_call x4, Pallas kernels, call(): pl.pallas_call(kernel, out_shape=jax.ShapeDtypeStruct(shape, jnp.float32)...  3.75 us
    all_to_all x1, starting transfers between devices, spread(): return lax.all_to_all(sent, axes, 0, 0, tiled=True)  3.35 us
  transfers between devices with their start and end apart: 19, of which 12 were waited for; matrix products, arithmetic and copies ran while one was open for 0% of the time, Pallas kernels for 0%

profile of v3, /device:TPU:0, one launch (start us, length us, event | category | flops | bytes accessed | tf_op | source)
XLA Modules:
  0.0 73.4 jit_solution(5858295060278039310)
XLA Ops:
  2.3 3.0 %collective-permute-start = (f32[16,128]{1,0:T(8,128)S(1)}, f32[16,128]{1,0:T(8,128)S(1)}, u32[]{:S(2)}, u32[]{:S(2)}) collective-permute-start(f32[16,128]{1,0:T(8,128)S(1)} %get-tuple-element.8), channel_id=1, source_target_pairs={{0,4},{1,5},{2,6},{3,7},{4,0},{5,1},{6,2},{7,3},{8,12},{9,13},{10,... | collective-permute-start | bytes 24584 | tf_op jit(solution)/shard_map/ppermute | solution.py:24
  5.4 2.6 %collective-permute-start.1 = (f32[16,128]{1,0:T(8,128)S(1)}, f32[16,128]{1,0:T(8,128)S(1)}, u32[]{:S(2)}, u32[]{:S(2)}) collective-permute-start(f32[16,128]{1,0:T(8,128)S(1)} %get-tuple-element.8), channel_id=1, source_target_pairs={{0,8},{1,9},{2,10},{3,11},{4,12},{5,13},{6,14},{7,15},{8,0},{9,1},... | collective-permute-start | bytes 24584 | tf_op jit(solution)/shard_map/ppermute | solution.py:24
  7.9 2.0 %collective-permute-done.1 = f32[16,128]{1,0:T(8,128)S(1)} collective-permute-done((f32[16,128]{1,0:T(8,128)S(1)}, f32[16,128]{1,0:T(8,128)S(1)}, u32[]{:S(2)}, u32[]{:S(2)}) %collective-permute-start.1) | collective-permute-done | bytes 8224 | tf_op jit(solution)/shard_map/ppermute | solution.py:24
  9.9 3.5 %collective-permute-done.2 = f32[16,128]{1,0:T(8,128)S(1)} collective-permute-done((f32[16,128]{1,0:T(8,128)S(1)}, f32[16,128]{1,0:T(8,128)S(1)}, u32[]{:S(2)}, u32[]{:S(2)}) %collective-permute-start.2) | collective-permute-done | bytes 8224 | tf_op jit(solution)/shard_map/ppermute | solution.py:24
  13.4 1.5 %collective-permute-start.4 = (f32[64,128]{1,0:T(8,128)S(1)}, f32[64,128]{1,0:T(8,128)S(1)}, u32[]{:S(2)}, u32[]{:S(2)}) collective-permute-start(f32[64,128]{1,0:T(8,128)S(1)} %pad_maximum_fusion), channel_id=1, source_target_pairs={{0,2},{1,3},{2,0},{3,1},{4,6},{5,7},{6,4},{7,5},{8,10},{9,11},{10,... | collective-permute-start | bytes 98312 | tf_op jit(solution)/shard_map/ppermute | solution.py:24
  15.3 2.0 %collective-permute-done.4 = f32[64,128]{1,0:T(8,128)S(1)} collective-permute-done((f32[64,128]{1,0:T(8,128)S(1)}, f32[64,128]{1,0:T(8,128)S(1)}, u32[]{:S(2)}, u32[]{:S(2)}) %collective-permute-start.4) | collective-permute-done | bytes 32800 | tf_op jit(solution)/shard_map/ppermute | solution.py:24
  17.3 0.9 %collective-permute-done.5 = f32[64,128]{1,0:T(8,128)S(1)} collective-permute-done((f32[64,128]{1,0:T(8,128)S(1)}, f32[64,128]{1,0:T(8,128)S(1)}, u32[]{:S(2)}, u32[]{:S(2)}) %collective-permute-start.5) | collective-permute-done | bytes 32800 | tf_op jit(solution)/shard_map/ppermute | solution.py:24
  18.5 2.2 %copy-done = bf16[8,8,256,128]{3,2,1,0:T(8,128)(2,1)S(1)} copy-done((bf16[8,8,256,128]{3,2,1,0:T(8,128)(2,1)S(1)}, bf16[8,8,256,128]{3,2,1,0:T(8,128)(2,1)}, u32[]{:S(2)}) %copy-start) | copy-done | bytes 4194328
  20.7 1.2 %shard_map.46 = f32[8,256]{1,0:T(8,128)S(1)} custom-call(f32[64,128]{1,0:T(8,128)S(1)} %fusion.14.picked_ref, bf16[8,8,256,128]{3,2,1,0:T(8,128)(2,1)S(1)} %copy-done), custom_call_target="tpu_custom_call" | custom-call | tf_op jit(solution)/shard_map/pallas_call | solution.py:121
  22.5 3.3 %all-to-all-start = ((f32[8,8,256]{2,1,0:T(8,128)}), f32[8,8,256]{2,1,0:T(8,128)S(1)}, u32[]{:S(2)}, u32[]{:S(2)}) async-start(f32[8,8,256]{2,1,0:T(8,128)} %broadcast_in_dim.7), calls=%async_computation | async-start | bytes 131072 | tf_op jit(solution)/shard_map/all_to_all | solution.py:65
  26.0 6.7 %all-to-all-done.parts_ref = f32[8,8,256]{2,1,0:T(8,128)S(1)} async-done(((f32[8,8,256]{2,1,0:T(8,128)}), f32[8,8,256]{2,1,0:T(8,128)S(1)}, u32[]{:S(2)}, u32[]{:S(2)}) %all-to-all-start) | async-done | bytes 65568 | tf_op jit(solution)/shard_map/all_to_all | solution.py:65
  32.7 2.2 %copy-done.1 = bf16[8,8,256,128]{3,2,1,0:T(8,128)(2,1)S(1)} copy-done((bf16[8,8,256,128]{3,2,1,0:T(8,128)(2,1)S(1)}, bf16[8,8,256,128]{3,2,1,0:T(8,128)(2,1)}, u32[]{:S(2)}) %copy-start.1) | copy-done | bytes 4194328
  36.2 1.1 %collective-permute-start.7 = (f32[64,128]{1,0:T(8,128)S(1)}, f32[64,128]{1,0:T(8,128)S(1)}, u32[]{:S(2)}, u32[]{:S(2)}) collective-permute-start(f32[64,128]{1,0:T(8,128)S(1)} %shard_map.47), channel_id=1, source_target_pairs={{0,8},{1,9},{2,10},{3,11},{4,12},{5,13},{6,14},{7,15},{8,0},{9,1},... | collective-permute-start | bytes 98312 | tf_op jit(solution)/shard_map/ppermute | solution.py:24
  37.3 2.7 %collective-permute-start.6 = (f32[64,128]{1,0:T(8,128)S(1)}, f32[64,128]{1,0:T(8,128)S(1)}, u32[]{:S(2)}, u32[]{:S(2)}) collective-permute-start(f32[64,128]{1,0:T(8,128)S(1)} %shard_map.47), channel_id=1, source_target_pairs={{0,4},{1,5},{2,6},{3,7},{4,0},{5,1},{6,2},{7,3},{8,12},{9,13},{10,... | collective-permute-start | bytes 98312 | tf_op jit(solution)/shard_map/ppermute | solution.py:24
  40.1 1.2 %collective-permute-done.8 = f32[64,128]{1,0:T(8,128)S(1)} collective-permute-done((f32[64,128]{1,0:T(8,128)S(1)}, f32[64,128]{1,0:T(8,128)S(1)}, u32[]{:S(2)}, u32[]{:S(2)}) %collective-permute-start.8) | collective-permute-done | bytes 32800 | tf_op jit(solution)/shard_map/ppermute | solution.py:24
  43.1 1.1 %collective-permute-start.11 = (f32[64,128]{1,0:T(8,128)S(1)}, f32[64,128]{1,0:T(8,128)S(1)}, u32[]{:S(2)}, u32[]{:S(2)}) collective-permute-start(f32[64,128]{1,0:T(8,128)S(1)} %get-tuple-element.9), channel_id=1, source_target_pairs={{0,3},{1,2},{2,1},{3,0},{4,7},{5,6},{6,5},{7,4},{8,11},{9,10},{10,... | collective-permute-start | bytes 98312 | tf_op jit(solution)/shard_map/ppermute | solution.py:24
  44.2 2.3 %collective-permute-done.10 = f32[64,128]{1,0:T(8,128)S(1)} collective-permute-done((f32[64,128]{1,0:T(8,128)S(1)}, f32[64,128]{1,0:T(8,128)S(1)}, u32[]{:S(2)}, u32[]{:S(2)}) %collective-permute-start.10) | collective-permute-done | bytes 32800 | tf_op jit(solution)/shard_map/ppermute | solution.py:24
  46.8 2.2 %copy-done.2 = bf16[8,8,256,128]{3,2,1,0:T(8,128)(2,1)S(1)} copy-done((bf16[8,8,256,128]{3,2,1,0:T(8,128)(2,1)S(1)}, bf16[8,8,256,128]{3,2,1,0:T(8,128)(2,1)}, u32[]{:S(2)}) %copy-start.2) | copy-done | bytes 4194328
  49.0 1.2 %shard_map.48 = f32[8,256]{1,0:T(8,128)S(1)} custom-call(f32[64,128]{1,0:T(8,128)S(1)} %fusion.17.picked_ref, bf16[8,8,256,128]{3,2,1,0:T(8,128)(2,1)S(1)} %copy-done.2), custom_call_target="tpu_custom_call" | custom-call | tf_op jit(solution)/shard_map/pallas_call | solution.py:121
  50.2 10.8 %all_to_all.10.parts_ref = f32[8,8,256]{2,1,0:T(8,128)S(1)} all-to-all(f32[8,8,256]{2,1,0:T(8,128)S(1)} %broadcast_in_dim.8), channel_id=1, replica_groups=mesh['parts'=2,'genome'=8,'reads'=2] {'genome'}, dimensions={0} | all-to-all | bytes 131072 | tf_op jit(solution)/shard_map/all_to_all | solution.py:65
  62.4 1.4 %collective-permute-start.14 = (f32[48,128]{1,0:T(8,128)S(1)}, f32[48,128]{1,0:T(8,128)S(1)}, u32[]{:S(2)}, u32[]{:S(2)}) collective-permute-start(f32[48,128]{1,0:T(8,128)S(1)} %get-tuple-element.12), channel_id=1, source_target_pairs={{0,3},{1,2},{2,1},{3,0},{4,7},{5,6},{6,5},{7,4},{8,11},{9,10},{10,... | collective-permute-start | bytes 73736 | tf_op jit(solution)/shard_map/ppermute | solution.py:24
  63.8 2.1 %collective-permute-done.13 = f32[48,128]{1,0:T(8,128)S(1)} collective-permute-done((f32[48,128]{1,0:T(8,128)S(1)}, f32[48,128]{1,0:T(8,128)S(1)}, u32[]{:S(2)}, u32[]{:S(2)}) %collective-permute-start.13) | collective-permute-done | bytes 24608 | tf_op jit(solution)/shard_map/ppermute | solution.py:24
  67.3 3.1 %collective-permute-start.17 = (f32[12,128]{1,0:T(8,128)S(1)}, f32[12,128]{1,0:T(8,128)S(1)}, u32[]{:S(2)}, u32[]{:S(2)}) collective-permute-start(f32[12,128]{1,0:T(8,128)S(1)} %get-tuple-element.15), channel_id=1, source_target_pairs={{0,12},{1,13},{2,14},{3,15},{4,8},{5,9},{6,10},{7,11},{8,4},{9,5},... | collective-permute-start | bytes 18440 | tf_op jit(solution)/shard_map/ppermute | solution.py:24
  71.1 1.6 %collective-permute-done.17 = f32[12,128]{1,0:T(8,128)S(1)} collective-permute-done((f32[12,128]{1,0:T(8,128)S(1)}, f32[12,128]{1,0:T(8,128)S(1)}, u32[]{:S(2)}, u32[]{:S(2)}) %collective-permute-start.17) | collective-permute-done | bytes 6176 | tf_op jit(solution)/shard_map/ppermute | solution.py:24
  (56 shorter events, 11.1 us)
Async XLA Ops:
  2.3 5.6 %collective-permute-start = (f32[16,128]{1,0:T(8,128)S(1)}, f32[16,128]{1,0:T(8,128)S(1)}, u32[]{:S(2)}, u32[]{:S(2)}) collective-permute-start(f32[16,128]{1,0:T(8,128)S(1)} %get-tuple-element.8), channel_id=1, source_target_pairs={{0,4},{1,5},{2,6},{3,7},{4,0},{5,1},{6,2},{7,3},{8,12},{9,13},{10,... | collective-permute-start | bytes 24584 | tf_op jit(solution)/shard_map/ppermute | solution.py:24
  5.4 4.5 %collective-permute-start.1 = (f32[16,128]{1,0:T(8,128)S(1)}, f32[16,128]{1,0:T(8,128)S(1)}, u32[]{:S(2)}, u32[]{:S(2)}) collective-permute-start(f32[16,128]{1,0:T(8,128)S(1)} %get-tuple-element.8), channel_id=1, source_target_pairs={{0,8},{1,9},{2,10},{3,11},{4,12},{5,13},{6,14},{7,15},{8,0},{9,1},... | collective-permute-start | bytes 24584 | tf_op jit(solution)/shard_map/ppermute | solution.py:24
  7.9 5.4 %collective-permute-start.2 = (f32[16,128]{1,0:T(8,128)S(1)}, f32[16,128]{1,0:T(8,128)S(1)}, u32[]{:S(2)}, u32[]{:S(2)}) collective-permute-start(f32[16,128]{1,0:T(8,128)S(1)} %get-tuple-element.8), channel_id=1, source_target_pairs={{0,12},{1,13},{2,14},{3,15},{4,8},{5,9},{6,10},{7,11},{8,4},{9,5},... | collective-permute-start | bytes 24584 | tf_op jit(solution)/shard_map/ppermute | solution.py:24
  13.4 1.9 %collective-permute-start.3 = (f32[64,128]{1,0:T(8,128)S(1)}, f32[64,128]{1,0:T(8,128)S(1)}, u32[]{:S(2)}, u32[]{:S(2)}) collective-permute-start(f32[64,128]{1,0:T(8,128)S(1)} %pad_maximum_fusion), channel_id=1, source_target_pairs={{0,1},{1,0},{2,3},{3,2},{4,5},{5,4},{6,7},{7,6},{8,9},{9,8},{10,11... | collective-permute-start | bytes 98312 | tf_op jit(solution)/shard_map/ppermute | solution.py:24
  13.4 3.9 %collective-permute-start.4 = (f32[64,128]{1,0:T(8,128)S(1)}, f32[64,128]{1,0:T(8,128)S(1)}, u32[]{:S(2)}, u32[]{:S(2)}) collective-permute-start(f32[64,128]{1,0:T(8,128)S(1)} %pad_maximum_fusion), channel_id=1, source_target_pairs={{0,2},{1,3},{2,0},{3,1},{4,6},{5,7},{6,4},{7,5},{8,10},{9,11},{10,... | collective-permute-start | bytes 98312 | tf_op jit(solution)/shard_map/ppermute | solution.py:24
  14.9 3.3 %collective-permute-start.5 = (f32[64,128]{1,0:T(8,128)S(1)}, f32[64,128]{1,0:T(8,128)S(1)}, u32[]{:S(2)}, u32[]{:S(2)}) collective-permute-start(f32[64,128]{1,0:T(8,128)S(1)} %pad_maximum_fusion), channel_id=1, source_target_pairs={{0,3},{1,2},{2,1},{3,0},{4,7},{5,6},{6,5},{7,4},{8,11},{9,10},{10,... | collective-permute-start | bytes 98312 | tf_op jit(solution)/shard_map/ppermute | solution.py:24
  18.5 2.2 %copy-start = (bf16[8,8,256,128]{3,2,1,0:T(8,128)(2,1)S(1)}, bf16[8,8,256,128]{3,2,1,0:T(8,128)(2,1)}, u32[]{:S(2)}) copy-start(bf16[8,8,256,128]{3,2,1,0:T(8,128)(2,1)} %lik_ref.7) | copy-start | bytes 12582916
  22.5 10.2 %all-to-all-start = ((f32[8,8,256]{2,1,0:T(8,128)}), f32[8,8,256]{2,1,0:T(8,128)S(1)}, u32[]{:S(2)}, u32[]{:S(2)}) async-start(f32[8,8,256]{2,1,0:T(8,128)} %broadcast_in_dim.7), calls=%async_computation | async-start | bytes 131072 | tf_op jit(solution)/shard_map/all_to_all | solution.py:65
  32.7 2.2 %copy-start.1 = (bf16[8,8,256,128]{3,2,1,0:T(8,128)(2,1)S(1)}, bf16[8,8,256,128]{3,2,1,0:T(8,128)(2,1)}, u32[]{:S(2)}) copy-start(bf16[8,8,256,128]{3,2,1,0:T(8,128)(2,1)} %lik_ref.7) | copy-start | bytes 12582916
  35.6 5.8 %collective-permute-start.8 = (f32[64,128]{1,0:T(8,128)S(1)}, f32[64,128]{1,0:T(8,128)S(1)}, u32[]{:S(2)}, u32[]{:S(2)}) collective-permute-start(f32[64,128]{1,0:T(8,128)S(1)} %shard_map.47), channel_id=1, source_target_pairs={{0,12},{1,13},{2,14},{3,15},{4,8},{5,9},{6,10},{7,11},{8,4},{9,5},... | collective-permute-start | bytes 98312 | tf_op jit(solution)/shard_map/ppermute | solution.py:24
  36.2 5.2 %collective-permute-start.7 = (f32[64,128]{1,0:T(8,128)S(1)}, f32[64,128]{1,0:T(8,128)S(1)}, u32[]{:S(2)}, u32[]{:S(2)}) collective-permute-start(f32[64,128]{1,0:T(8,128)S(1)} %shard_map.47), channel_id=1, source_target_pairs={{0,8},{1,9},{2,10},{3,11},{4,12},{5,13},{6,14},{7,15},{8,0},{9,1},... | collective-permute-start | bytes 98312 | tf_op jit(solution)/shard_map/ppermute | solution.py:24
  37.3 4.6 %collective-permute-start.6 = (f32[64,128]{1,0:T(8,128)S(1)}, f32[64,128]{1,0:T(8,128)S(1)}, u32[]{:S(2)}, u32[]{:S(2)}) collective-permute-start(f32[64,128]{1,0:T(8,128)S(1)} %shard_map.47), channel_id=1, source_target_pairs={{0,4},{1,5},{2,6},{3,7},{4,0},{5,1},{6,2},{7,3},{8,12},{9,13},{10,... | collective-permute-start | bytes 98312 | tf_op jit(solution)/shard_map/ppermute | solution.py:24
  42.3 1.9 %collective-permute-start.9 = (f32[64,128]{1,0:T(8,128)S(1)}, f32[64,128]{1,0:T(8,128)S(1)}, u32[]{:S(2)}, u32[]{:S(2)}) collective-permute-start(f32[64,128]{1,0:T(8,128)S(1)} %get-tuple-element.11), channel_id=1, source_target_pairs={{0,1},{1,0},{2,3},{3,2},{4,5},{5,4},{6,7},{7,6},{8,9},{9,8},{10,11... | collective-permute-start | bytes 98312 | tf_op jit(solution)/shard_map/ppermute | solution.py:24
  42.4 4.2 %collective-permute-start.10 = (f32[64,128]{1,0:T(8,128)S(1)}, f32[64,128]{1,0:T(8,128)S(1)}, u32[]{:S(2)}, u32[]{:S(2)}) collective-permute-start(f32[64,128]{1,0:T(8,128)S(1)} %get-tuple-element.10), channel_id=1, source_target_pairs={{0,2},{1,3},{2,0},{3,1},{4,6},{5,7},{6,4},{7,5},{8,10},{9,11},{10,... | collective-permute-start | bytes 98312 | tf_op jit(solution)/shard_map/ppermute | solution.py:24
  43.1 3.7 %collective-permute-start.11 = (f32[64,128]{1,0:T(8,128)S(1)}, f32[64,128]{1,0:T(8,128)S(1)}, u32[]{:S(2)}, u32[]{:S(2)}) collective-permute-start(f32[64,128]{1,0:T(8,128)S(1)} %get-tuple-element.9), channel_id=1, source_target_pairs={{0,3},{1,2},{2,1},{3,0},{4,7},{5,6},{6,5},{7,4},{8,11},{9,10},{10,... | collective-permute-start | bytes 98312 | tf_op jit(solution)/shard_map/ppermute | solution.py:24
  46.8 2.2 %copy-start.2 = (bf16[8,8,256,128]{3,2,1,0:T(8,128)(2,1)S(1)}, bf16[8,8,256,128]{3,2,1,0:T(8,128)(2,1)}, u32[]{:S(2)}) copy-start(bf16[8,8,256,128]{3,2,1,0:T(8,128)(2,1)} %lik_ref.7) | copy-start | bytes 12582916
  61.9 1.9 %collective-permute-start.12 = (f32[48,128]{1,0:T(8,128)S(1)}, f32[48,128]{1,0:T(8,128)S(1)}, u32[]{:S(2)}, u32[]{:S(2)}) collective-permute-start(f32[48,128]{1,0:T(8,128)S(1)} %get-tuple-element.14), channel_id=1, source_target_pairs={{0,1},{1,0},{2,3},{3,2},{4,5},{5,4},{6,7},{7,6},{8,9},{9,8},{10,11... | collective-permute-start | bytes 73736 | tf_op jit(solution)/shard_map/ppermute | solution.py:24
  62.0 4.0 %collective-permute-start.13 = (f32[48,128]{1,0:T(8,128)S(1)}, f32[48,128]{1,0:T(8,128)S(1)}, u32[]{:S(2)}, u32[]{:S(2)}) collective-permute-start(f32[48,128]{1,0:T(8,128)S(1)} %get-tuple-element.13), channel_id=1, source_target_pairs={{0,2},{1,3},{2,0},{3,1},{4,6},{5,7},{6,4},{7,5},{8,10},{9,11},{10,... | collective-permute-start | bytes 73736 | tf_op jit(solution)/shard_map/ppermute | solution.py:24
  62.4 3.5 %collective-permute-start.14 = (f32[48,128]{1,0:T(8,128)S(1)}, f32[48,128]{1,0:T(8,128)S(1)}, u32[]{:S(2)}, u32[]{:S(2)}) collective-permute-start(f32[48,128]{1,0:T(8,128)S(1)} %get-tuple-element.12), channel_id=1, source_target_pairs={{0,3},{1,2},{2,1},{3,0},{4,7},{5,6},{6,5},{7,4},{8,11},{9,10},{10,... | collective-permute-start | bytes 73736 | tf_op jit(solution)/shard_map/ppermute | solution.py:24
  66.0 4.5 %collective-permute-start.15 = (f32[12,128]{1,0:T(8,128)S(1)}, f32[12,128]{1,0:T(8,128)S(1)}, u32[]{:S(2)}, u32[]{:S(2)}) collective-permute-start(f32[12,128]{1,0:T(8,128)S(1)} %get-tuple-element.17), channel_id=1, source_target_pairs={{0,4},{1,5},{2,6},{3,7},{4,0},{5,1},{6,2},{7,3},{8,12},{9,13},{10,... | collective-permute-start | bytes 18440 | tf_op jit(solution)/shard_map/ppermute | solution.py:24
  66.6 4.5 %collective-permute-start.16 = (f32[12,128]{1,0:T(8,128)S(1)}, f32[12,128]{1,0:T(8,128)S(1)}, u32[]{:S(2)}, u32[]{:S(2)}) collective-permute-start(f32[12,128]{1,0:T(8,128)S(1)} %get-tuple-element.16), channel_id=1, source_target_pairs={{0,8},{1,9},{2,10},{3,11},{4,12},{5,13},{6,14},{7,15},{8,0},{9,1},... | collective-permute-start | bytes 18440 | tf_op jit(solution)/shard_map/ppermute | solution.py:24
  67.3 5.4 %collective-permute-start.17 = (f32[12,128]{1,0:T(8,128)S(1)}, f32[12,128]{1,0:T(8,128)S(1)}, u32[]{:S(2)}, u32[]{:S(2)}) collective-permute-start(f32[12,128]{1,0:T(8,128)S(1)} %get-tuple-element.15), channel_id=1, source_target_pairs={{0,12},{1,13},{2,14},{3,15},{4,8},{5,9},{6,10},{7,11},{8,4},{9,5},... | collective-permute-start | bytes 18440 | tf_op jit(solution)/shard_map/ppermute | solution.py:24

commit v4 on v3

--- a/solution.py
+++ b/solution.py
@@ -32,37 +32,17 @@
     return parts[0]
 
 
-def position(k, n):
-    place = 0
-    for r in radices(n):
-        n //= r
-        place = place + (k % r) * n
-        k = k // r
-    return place
-
-
-def scatter_sum(x, axes):
-    stride = 1
-    for r in radices(lax.axis_size(axes)):
-        rows = x.shape[0] // r
-        parts = [x[j * rows : (j + 1) * rows] for j in range(r)]
-        x = tree_sum([parts[0]] + [swap(parts[j], axes, j * stride) for j in range(1, r)])
-        stride *= r
-    return x
-
-
-def gather_high(x, axes):
-    stride = lax.axis_size(axes)
-    for r in radices(stride)[:0:-1]:
-        stride //= r
-        x = jnp.concatenate([x] + [swap(x, axes, j * stride) for j in range(1, r)], axis=0)
-    return x
-
-
-def spread(x, axes):
+def far_groups(axes, near):
     n = lax.axis_size(axes)
-    sent = jnp.broadcast_to(x[None], (n,) + x.shape)
-    return lax.all_to_all(sent, axes, 0, 0, tiled=True)
+    return [list(range(i, n, near)) for i in range(near)]
+
+
+def spread(x, axes, near):
+    count = lax.axis_size(axes) // near
+    sent = jnp.broadcast_to(x[None], (count,) + x.shape)
+    return lax.all_to_all(
+        sent, axes, 0, 0, tiled=True, axis_index_groups=far_groups(axes, near)
+    )
 
 
 def dot_exact(a, b):
@@ -116,6 +96,40 @@
             out_ref[at + 1 : at + 2, :] = picked_ref[at + 1 : at + 2, :] * summed[:, cols:]
 
 
+def pack_kernel(weights_ref, ids_ref, valid_ref, out_ref, wide_ref):
+    own_blocks = weights_ref.shape[0]
+    read_blocks, slots = ids_ref.shape
+    wide_ref[...] = jnp.zeros_like(wide_ref)
+    coded = jnp.where(valid_ref[...] > 0, ids_ref[...], -1)
+    wide_ref[:, :slots] = coded.astype(jnp.float32)
+    rolled = pltpu.roll(wide_ref[...], 0, 1, stride=slots, stride_axis=0)
+    out_ref[...] = jnp.zeros_like(out_ref)
+    out_ref[:own_blocks, :] = weights_ref[...]
+    out_ref[own_blocks : own_blocks + 1, :] = jnp.sum(rolled, axis=0, keepdims=True)
+
+
+def load_kernel(source_ref, out_ref, sems):
+    copies = [
+        pltpu.make_async_copy(source_ref.at[b], out_ref.at[b], sems.at[b])
+        for b in range(out_ref.shape[0])
+    ]
+    for copy in copies:
+        copy.start()
+    for copy in copies:
+        copy.wait()
+
+
+def load(x):
+    return pl.pallas_call(
+        load_kernel,
+        out_shape=pltpu.VMEM(x.shape, x.dtype),
+        in_specs=[pl.BlockSpec(memory_space=pl.ANY)],
+        out_specs=pl.BlockSpec(memory_space=pltpu.VMEM),
+        scratch_shapes=[pltpu.SemaphoreType.DMA((x.shape[0],))],
+        compiler_params=pltpu.CompilerParams(vmem_limit_bytes=16 * 2**20),
+    )(x)
+
+
 def call(kernel, shape, scratch, *operands):
     vmem = pl.BlockSpec(memory_space=pltpu.VMEM)
     return pl.pallas_call(
@@ -124,7 +138,7 @@
         in_specs=[vmem] * len(operands),
         out_specs=vmem,
         scratch_shapes=scratch,
-        compiler_params=pltpu.CompilerParams(vmem_limit_bytes=40 * 2**20),
+        compiler_params=pltpu.CompilerParams(vmem_limit_bytes=16 * 2**20),
     )(*operands)
 
 
@@ -133,51 +147,55 @@
     n = lax.axis_size(ALL)
     me = lax.axis_index(ALL)
     near = radices(n)[0]
+    far = n // near
     own_weights = start_weights.reshape(-1, cols)
     own_blocks = own_weights.shape[0]
     blocks = own_blocks * n
     all_slots = read_blocks * slots
     total_reads = read_blocks * lax.axis_size("reads") * reads
     scale = blocks * cols / total_reads
-    likelihood = pltpu.with_memory_space_constraint(likelihood, pltpu.VMEM)
+    held = load(pltpu.with_memory_space_constraint(likelihood, pltpu.HBM))
+
+    rows = -(-(own_blocks + 1) // 8) * 8
+    sent = call(
+        pack_kernel,
+        (rows, cols),
+        [pltpu.VMEM((read_blocks, cols), jnp.float32)],
+        own_weights,
+        block_ids,
+        slot_valid,
+    )
+    column = spread(sent, ALL, near).reshape(far * rows, cols)
+    full = jnp.concatenate([column] + [swap(column, ALL, j) for j in range(1, near)], axis=0)
 
     ids = block_ids.reshape(-1)
     valid = slot_valid.reshape(-1)
-    owner = position((ids // own_blocks) ^ me, n)
-
-    id_rows = -(-all_slots // cols)
-    rows = -(-(own_blocks + id_rows) // 8) * 8
-    coded = jnp.where(valid > 0, ids, -1).astype(jnp.float32)
-    coded = jnp.pad(coded, (0, id_rows * cols - all_slots)).reshape(id_rows, cols)
-    sent = jnp.pad(
-        jnp.concatenate([own_weights, coded], axis=0), ((0, rows - own_blocks - id_rows), (0, 0))
-    )
-    far = gather_high(sent, ALL)
-    full = jnp.concatenate([far] + [swap(far, ALL, j) for j in range(1, near)], axis=0)
-    every = full.reshape(near, n // near, rows, cols)
-    known = every[:, :, own_blocks : own_blocks + id_rows].reshape(near, n // near, -1)
-    known = known[:, :, :all_slots]
-    wanted = known[:, 0].reshape(-1)
-    given = known[0].reshape(-1)
-    match = ((wanted[:, None] == given[None, :]) & (wanted[:, None] >= 0)).astype(jnp.float32)
-
+    owner = ids // own_blocks
+    owner = ((owner % near) ^ (me % near)) * far + owner // near
     place = jnp.where(valid > 0, owner * rows + ids % own_blocks, -1)
     pick = (place[:, None] == jnp.arange(n * rows, dtype=jnp.int32)[None, :]).astype(jnp.float32)
     picked = dot_exact(pick, full)
 
+    known = full.reshape(near, far, rows, cols)[:, :, own_blocks, :all_slots]
+    wanted = lax.dynamic_index_in_dim(known, me // near, 1, keepdims=False).reshape(-1)
+    given = known[0].reshape(-1)
+    match = ((wanted[:, None] == given[None, :]) & (wanted[:, None] >= 0)).astype(jnp.float32)
+
     for step in range(ITERS):
-        row_part = call(row_kernel, (read_blocks, reads), [], picked, likelihood)
-        row_parts = spread(row_part, "genome")
+        row_part = call(row_kernel, (read_blocks, reads), [], picked, held)
+        row_part = row_part + swap(row_part, "genome", 1)
+        row_parts = spread(row_part, "genome", 2)
         contrib = call(
             col_kernel,
             (all_slots, cols),
             [pltpu.VMEM((read_blocks, reads), jnp.float32)],
             row_parts,
             picked,
-            likelihood,
+            held,
         )
         if step + 1 < ITERS:
-            sums = dot_exact(match, gather_high(contrib, ALL))
+            column = spread(contrib, ALL, near).reshape(far * all_slots, cols)
+            sums = dot_exact(match, column)
             parts = [sums[j * all_slots : (j + 1) * all_slots] for j in range(near)]
             picked = scale * tree_sum(
                 [parts[0]] + [swap(parts[j], ALL, j) for j in range(1, near)]
@@ -185,7 +203,19 @@
 
     place = owner * own_blocks + ids % own_blocks
     count = (jnp.arange(blocks, dtype=jnp.int32)[:, None] == place[None, :]).astype(jnp.float32)
-    return (scatter_sum(dot_exact(count, contrib), ALL) * scale).reshape(-1)
+    counts = dot_exact(count, contrib)
+    share = far * own_blocks
+    parts = [counts[j * share : (j + 1) * share] for j in range(near)]
+    counts = tree_sum([parts[0]] + [swap(parts[j], ALL, j) for j in range(1, near)])
+    counts = lax.all_to_all(
+        counts.reshape(far, own_blocks, cols),
+        ALL,
+        0,
+        0,
+        tiled=True,
+        axis_index_groups=far_groups(ALL, near),
+    )
+    return (jnp.sum(counts, axis=0) * scale).reshape(-1)
 
 
 def solution(mesh):

time: 73.8 us -> 84.4 us (1.14)
  blocking collectives: 10.8 us -> 16.2 us
  local copies, waits for them, and re-layouts: 8.3 us -> 13 us
  Pallas kernels: 3.75 us -> 6.05 us
  starting transfers between devices: 23.6 us -> 21.8 us
  waiting for transfers between devices: 24 us -> 23 us
    ppermute x18 -> x11, starting transfers between devices: 20.2 us -> 8.87 us  [swap(): return lax.ppermute(x, axes, [(i, i ^ k) for i in range(n)])]
    all_to_all x1 -> x3, starting transfers between devices: 3.35 us -> 12.9 us  [spread(): lax.all_to_all(sent, axes, 0, 0, tiled=True, axis_index_groups=far_groups...]
    ppermute x18 -> x11, waiting for transfers between devices: 17.3 us -> 8.5 us  [swap(): return lax.ppermute(x, axes, [(i, i ^ k) for i in range(n)])]
    all_to_all x1 -> x3, waiting for transfers between devices: 6.72 us -> 14.5 us  [spread(): lax.all_to_all(sent, axes, 0, 0, tiled=True, axis_index_groups=far_groups...]
    all_to_all x1 -> x2, blocking collectives: 10.8 us -> 16.2 us  [the longest x1 8.13 us: spread(): lax.all_to_all(sent, axes, 0, 0, tiled=True, axis_index_groups=far_groups...]
    unnamed x11 -> x14, local copies, waits for them, and re-layouts: 6.57 us -> 10.6 us
    pallas_call x0 -> x1, Pallas kernels: none -> 2.21 us  [load(): pl.pallas_call(load_kernel, out_shape=pltpu.VMEM(x.shape, x.dtype), in_sp...]
    broadcast_in_dim x2 -> x4, local copies, waits for them, and re-layouts: 0.64 us -> 1.89 us  [spread(): sent = jnp.broadcast_to(x[None], (count,) + x.shape)]
  transfers between devices with their start and end apart: 19 -> 14, of which waited for: 12 -> 9; matrix products, arithmetic and copies ran while one was open for 0% -> 3% of each run, Pallas kernels for 0% -> 3%
where the time goes in v4:
time: 84.4 us; the launch traced here: 83.7 us
  waiting for transfers between devices  23 us (27%)
  starting transfers between devices  21.8 us (26%)
  blocking collectives  16.2 us (19%)
  local copies, waits for them, and re-layouts  13 us (15%)
  Pallas kernels  6.05 us (7%)
  other arithmetic  2.76 us (3%)
    all_to_all x3, waiting for transfers between devices, spread(): lax.all_to_all(sent, axes, 0, 0, tiled=True, axis_index_groups=far_groups...  14.5 us
    all_to_all x3, starting transfers between devices, spread(): lax.all_to_all(sent, axes, 0, 0, tiled=True, axis_index_groups=far_groups...  12.9 us
    unnamed x14, local copies, waits for them, and re-layouts  10.6 us
    ppermute x11, starting transfers between devices, swap(): return lax.ppermute(x, axes, [(i, i ^ k) for i in range(n)])  8.87 us
    ppermute x11, waiting for transfers between devices, swap(): return lax.ppermute(x, axes, [(i, i ^ k) for i in range(n)])  8.5 us
    all_to_all x1, blocking collectives, spread(): lax.all_to_all(sent, axes, 0, 0, tiled=True, axis_index_groups=far_groups...  8.13 us
    all_to_all x1, blocking collectives, local(): lax.all_to_all(counts.reshape(far, own_blocks, cols), ALL, 0, 0, tiled=Tr...  8.04 us
    pallas_call x5, Pallas kernels, call(): pl.pallas_call(kernel, out_shape=jax.ShapeDtypeStruct(shape, jnp.float32)...  3.83 us
  transfers between devices with their start and end apart: 14, of which 9 were waited for; matrix products, arithmetic and copies ran while one was open for 3% of the time, Pallas kernels for 3%

profile of v4, /device:TPU:0, one launch (start us, length us, event | category | flops | bytes accessed | tf_op | source)
XLA Modules:
  0.0 83.7 jit_solution(1511348205635509859)
XLA Ops:
  2.8 6.3 %all-to-all-start = ((f32[4,16,128]{2,1,0:T(8,128)}), f32[4,16,128]{2,1,0:T(8,128)S(1)}, u32[]{:S(2)}, u32[]{:S(2)}) async-start(f32[4,16,128]{2,1,0:T(8,128)} %broadcast_in_dim.10), calls=%async_computation | async-start | bytes 65536 | tf_op jit(solution)/shard_map/all_to_all | solution.py:43
  11.5 3.2 %all-to-all-done = f32[4,16,128]{2,1,0:T(8,128)S(1)} async-done(((f32[4,16,128]{2,1,0:T(8,128)}), f32[4,16,128]{2,1,0:T(8,128)S(1)}, u32[]{:S(2)}, u32[]{:S(2)}) %all-to-all-start) | async-done | bytes 32800 | tf_op jit(solution)/shard_map/all_to_all | solution.py:43
  14.8 1.6 %collective-permute-start.1 = (f32[64,128]{1,0:T(8,128)S(1)}, f32[64,128]{1,0:T(8,128)S(1)}, u32[]{:S(2)}, u32[]{:S(2)}) collective-permute-start(f32[64,128]{1,0:T(8,128)S(1)} %bitcast.13), channel_id=1, source_target_pairs={{0,2},{1,3},{2,0},{3,1},{4,6},{5,7},{6,4},{7,5},{8,10},{9,11},{10,... | collective-permute-start | bytes 98312 | tf_op jit(solution)/shard_map/ppermute | solution.py:24
  16.6 2.2 %shard_map.47.lik_ref = bf16[8,8,256,128]{3,2,1,0:T(8,128)(2,1)S(1)} custom-call(bf16[8,8,256,128]{3,2,1,0:T(8,128)(2,1)} %source_ref.1), custom_call_target="tpu_custom_call" | custom-call | tf_op jit(solution)/shard_map/pallas_call | solution.py:123
  18.8 1.9 %copy-done = bf16[8,8,256,128]{3,2,1,0:T(8,128)(2,1)} copy-done((bf16[8,8,256,128]{3,2,1,0:T(8,128)(2,1)}, bf16[8,8,256,128]{3,2,1,0:T(8,128)(2,1)S(1)}, u32[]{:S(2)}) %copy-start) | copy-done | bytes 4194328
  21.0 2.2 %copy-done.1 = bf16[8,8,256,128]{3,2,1,0:T(8,128)(2,1)S(1)} copy-done((bf16[8,8,256,128]{3,2,1,0:T(8,128)(2,1)S(1)}, bf16[8,8,256,128]{3,2,1,0:T(8,128)(2,1)}, u32[]{:S(2)}) %copy-start.1) | copy-done | bytes 4194328
  23.2 1.2 %shard_map.48 = f32[8,256]{1,0:T(8,128)S(1)} custom-call(f32[64,128]{1,0:T(8,128)S(1)} %fusion.7.picked_ref, bf16[8,8,256,128]{3,2,1,0:T(8,128)(2,1)S(1)} %copy-done.1), custom_call_target="tpu_custom_call" | custom-call | tf_op jit(solution)/shard_map/pallas_call | solution.py:135
  24.4 1.6 %collective-permute-start.3 = (f32[8,256]{1,0:T(8,128)S(1)}, f32[8,256]{1,0:T(8,128)S(1)}, u32[]{:S(2)}, u32[]{:S(2)}) collective-permute-start(f32[8,256]{1,0:T(8,128)S(1)} %shard_map.48), channel_id=1, source_target_pairs={{0,2},{2,0},{4,6},{6,4},{8,10},{10,8},{12,14},{14,12},{1,3},{3,1},... | collective-permute-start | bytes 24584 | tf_op jit(solution)/shard_map/ppermute | solution.py:24
  26.0 2.1 %collective-permute-done.3 = f32[8,256]{1,0:T(8,128)S(1)} collective-permute-done((f32[8,256]{1,0:T(8,128)S(1)}, f32[8,256]{1,0:T(8,128)S(1)}, u32[]{:S(2)}, u32[]{:S(2)}) %collective-permute-start.3) | collective-permute-done | bytes 8224 | tf_op jit(solution)/shard_map/ppermute | solution.py:24
  28.8 3.3 %all-to-all-start.1 = ((f32[4,8,256]{2,1,0:T(8,128)}), f32[4,8,256]{2,1,0:T(8,128)S(1)}, u32[]{:S(2)}, u32[]{:S(2)}) async-start(f32[4,8,256]{2,1,0:T(8,128)} %broadcast_in_dim.11), calls=%async_computation.1 | async-start | bytes 65536 | tf_op jit(solution)/shard_map/all_to_all | solution.py:43
  32.3 5.4 %all-to-all-done.1.parts_ref = f32[4,8,256]{2,1,0:T(8,128)S(1)} async-done(((f32[4,8,256]{2,1,0:T(8,128)}), f32[4,8,256]{2,1,0:T(8,128)S(1)}, u32[]{:S(2)}, u32[]{:S(2)}) %all-to-all-start.1) | async-done | bytes 32800 | tf_op jit(solution)/shard_map/all_to_all | solution.py:43
  37.7 2.2 %copy-done.2 = bf16[8,8,256,128]{3,2,1,0:T(8,128)(2,1)S(1)} copy-done((bf16[8,8,256,128]{3,2,1,0:T(8,128)(2,1)S(1)}, bf16[8,8,256,128]{3,2,1,0:T(8,128)(2,1)}, u32[]{:S(2)}) %copy-start.2) | copy-done | bytes 4194328
  41.2 3.3 %all-to-all-start.2 = ((f32[4,64,128]{2,1,0:T(8,128)}), f32[4,64,128]{2,1,0:T(8,128)S(1)}, u32[]{:S(2)}, u32[]{:S(2)}) async-start(f32[4,64,128]{2,1,0:T(8,128)} %broadcast_in_dim.12), calls=%async_computation.2 | async-start | bytes 262144 | tf_op jit(solution)/shard_map/all_to_all | solution.py:43
  44.5 5.9 %all-to-all-done.2 = f32[4,64,128]{2,1,0:T(8,128)S(1)} async-done(((f32[4,64,128]{2,1,0:T(8,128)}), f32[4,64,128]{2,1,0:T(8,128)S(1)}, u32[]{:S(2)}, u32[]{:S(2)}) %all-to-all-start.2) | async-done | bytes 131104 | tf_op jit(solution)/shard_map/all_to_all | solution.py:43
  50.8 1.6 %collective-permute-start.5 = (f32[64,128]{1,0:T(8,128)S(1)}, f32[64,128]{1,0:T(8,128)S(1)}, u32[]{:S(2)}, u32[]{:S(2)}) collective-permute-start(f32[64,128]{1,0:T(8,128)S(1)} %get-tuple-element.8), channel_id=1, source_target_pairs={{0,2},{1,3},{2,0},{3,1},{4,6},{5,7},{6,4},{7,5},{8,10},{9,11},{10,... | collective-permute-start | bytes 98312 | tf_op jit(solution)/shard_map/ppermute | solution.py:24
  52.7 1.8 %collective-permute-done.6 = f32[64,128]{1,0:T(8,128)S(1)} collective-permute-done((f32[64,128]{1,0:T(8,128)S(1)}, f32[64,128]{1,0:T(8,128)S(1)}, u32[]{:S(2)}, u32[]{:S(2)}) %collective-permute-start.6) | collective-permute-done | bytes 32800 | tf_op jit(solution)/shard_map/ppermute | solution.py:24
  54.9 2.2 %copy-done.3 = bf16[8,8,256,128]{3,2,1,0:T(8,128)(2,1)S(1)} copy-done((bf16[8,8,256,128]{3,2,1,0:T(8,128)(2,1)S(1)}, bf16[8,8,256,128]{3,2,1,0:T(8,128)(2,1)}, u32[]{:S(2)}) %copy-start.3) | copy-done | bytes 4194328
  57.1 1.2 %shard_map.50 = f32[8,256]{1,0:T(8,128)S(1)} custom-call(f32[64,128]{1,0:T(8,128)S(1)} %fusion.10.picked_ref, bf16[8,8,256,128]{3,2,1,0:T(8,128)(2,1)S(1)} %copy-done.3), custom_call_target="tpu_custom_call" | custom-call | tf_op jit(solution)/shard_map/pallas_call | solution.py:135
  58.3 1.6 %collective-permute-start.7 = (f32[8,256]{1,0:T(8,128)S(1)}, f32[8,256]{1,0:T(8,128)S(1)}, u32[]{:S(2)}, u32[]{:S(2)}) collective-permute-start(f32[8,256]{1,0:T(8,128)S(1)} %shard_map.50), channel_id=1, source_target_pairs={{0,2},{2,0},{4,6},{6,4},{8,10},{10,8},{12,14},{14,12},{1,3},{3,1},... | collective-permute-start | bytes 24584 | tf_op jit(solution)/shard_map/ppermute | solution.py:24
  59.9 2.1 %collective-permute-done.7 = f32[8,256]{1,0:T(8,128)S(1)} collective-permute-done((f32[8,256]{1,0:T(8,128)S(1)}, f32[8,256]{1,0:T(8,128)S(1)}, u32[]{:S(2)}, u32[]{:S(2)}) %collective-permute-start.7) | collective-permute-done | bytes 8224 | tf_op jit(solution)/shard_map/ppermute | solution.py:24
  62.0 8.1 %all_to_all.25.parts_ref = f32[4,8,256]{2,1,0:T(8,128)S(1)} all-to-all(f32[4,8,256]{2,1,0:T(8,128)S(1)} %broadcast_in_dim.13), channel_id=1, replica_groups={{0,4,8,12},{2,6,10,14},{1,5,9,13},{3,7,11,15},{16,20,24,28},{18,22,26,3..., dimensions={0} | all-to-all | bytes 65536 | tf_op jit(solution)/shard_map/all_to_all | solution.py:43
  71.1 1.6 %collective-permute-start.9 = (f32[48,128]{1,0:T(8,128)S(1)}, f32[48,128]{1,0:T(8,128)S(1)}, u32[]{:S(2)}, u32[]{:S(2)}) collective-permute-start(f32[48,128]{1,0:T(8,128)S(1)} %get-tuple-element.11), channel_id=1, source_target_pairs={{0,2},{1,3},{2,0},{3,1},{4,6},{5,7},{6,4},{7,5},{8,10},{9,11},{10,... | collective-permute-start | bytes 73736 | tf_op jit(solution)/shard_map/ppermute | solution.py:24
  73.0 1.6 %collective-permute-done.10 = f32[48,128]{1,0:T(8,128)S(1)} collective-permute-done((f32[48,128]{1,0:T(8,128)S(1)}, f32[48,128]{1,0:T(8,128)S(1)}, u32[]{:S(2)}, u32[]{:S(2)}) %collective-permute-start.10) | collective-permute-done | bytes 24608 | tf_op jit(solution)/shard_map/ppermute | solution.py:24
  75.0 8.0 %all_to_all.26 = f32[4,12,128]{2,1,0:T(8,128)S(1)} all-to-all(f32[4,12,128]{2,1,0:T(8,128)S(1)} %reshape.164), channel_id=1, replica_groups={{0,4,8,12},{1,5,9,13},{2,6,10,14},{3,7,11,15},{16,20,24,28},{17,21,25,2..., dimensions={0} | all-to-all | bytes 49152 | tf_op jit(solution)/shard_map/all_to_all | solution.py:210
  (58 shorter events, 11.3 us)
Async XLA Ops:
  0.0 0.7 copy-start.4
  0.7 0.7 copy-start.5
  1.4 0.7 copy-start.6
  2.8 12.0 %all-to-all-start = ((f32[4,16,128]{2,1,0:T(8,128)}), f32[4,16,128]{2,1,0:T(8,128)S(1)}, u32[]{:S(2)}, u32[]{:S(2)}) async-start(f32[4,16,128]{2,1,0:T(8,128)} %broadcast_in_dim.10), calls=%async_computation | async-start | bytes 65536 | tf_op jit(solution)/shard_map/all_to_all | solution.py:43
  14.7 6.0 %collective-permute-start.2 = (f32[64,128]{1,0:T(8,128)S(1)}, f32[64,128]{1,0:T(8,128)S(1)}, u32[]{:S(2)}, u32[]{:S(2)}) collective-permute-start(f32[64,128]{1,0:T(8,128)S(1)} %bitcast.12), channel_id=1, source_target_pairs={{0,3},{1,2},{2,1},{3,0},{4,7},{5,6},{6,5},{7,4},{8,11},{9,10},{10,... | collective-permute-start | bytes 98312 | tf_op jit(solution)/shard_map/ppermute | solution.py:24
  14.8 6.0 %collective-permute-start.1 = (f32[64,128]{1,0:T(8,128)S(1)}, f32[64,128]{1,0:T(8,128)S(1)}, u32[]{:S(2)}, u32[]{:S(2)}) collective-permute-start(f32[64,128]{1,0:T(8,128)S(1)} %bitcast.13), channel_id=1, source_target_pairs={{0,2},{1,3},{2,0},{3,1},{4,6},{5,7},{6,4},{7,5},{8,10},{9,11},{10,... | collective-permute-start | bytes 98312 | tf_op jit(solution)/shard_map/ppermute | solution.py:24
  16.3 4.5 %collective-permute-start = (f32[64,128]{1,0:T(8,128)S(1)}, f32[64,128]{1,0:T(8,128)S(1)}, u32[]{:S(2)}, u32[]{:S(2)}) collective-permute-start(f32[64,128]{1,0:T(8,128)S(1)} %bitcast.14), channel_id=1, source_target_pairs={{0,1},{1,0},{2,3},{3,2},{4,5},{5,4},{6,7},{7,6},{8,9},{9,8},{10,11... | collective-permute-start | bytes 98312 | tf_op jit(solution)/shard_map/ppermute | solution.py:24
  18.8 2.0 %copy-start = (bf16[8,8,256,128]{3,2,1,0:T(8,128)(2,1)}, bf16[8,8,256,128]{3,2,1,0:T(8,128)(2,1)S(1)}, u32[]{:S(2)}) copy-start(bf16[8,8,256,128]{3,2,1,0:T(8,128)(2,1)S(1)} %shard_map.47.lik_ref) | copy-start | bytes 12582916
  21.0 2.2 %copy-start.1 = (bf16[8,8,256,128]{3,2,1,0:T(8,128)(2,1)S(1)}, bf16[8,8,256,128]{3,2,1,0:T(8,128)(2,1)}, u32[]{:S(2)}) copy-start(bf16[8,8,256,128]{3,2,1,0:T(8,128)(2,1)} %copy-done) | copy-start | bytes 12582916
  24.4 3.7 %collective-permute-start.3 = (f32[8,256]{1,0:T(8,128)S(1)}, f32[8,256]{1,0:T(8,128)S(1)}, u32[]{:S(2)}, u32[]{:S(2)}) collective-permute-start(f32[8,256]{1,0:T(8,128)S(1)} %shard_map.48), channel_id=1, source_target_pairs={{0,2},{2,0},{4,6},{6,4},{8,10},{10,8},{12,14},{14,12},{1,3},{3,1},... | collective-permute-start | bytes 24584 | tf_op jit(solution)/shard_map/ppermute | solution.py:24
  28.8 8.9 %all-to-all-start.1 = ((f32[4,8,256]{2,1,0:T(8,128)}), f32[4,8,256]{2,1,0:T(8,128)S(1)}, u32[]{:S(2)}, u32[]{:S(2)}) async-start(f32[4,8,256]{2,1,0:T(8,128)} %broadcast_in_dim.11), calls=%async_computation.1 | async-start | bytes 65536 | tf_op jit(solution)/shard_map/all_to_all | solution.py:43
  37.7 2.2 %copy-start.2 = (bf16[8,8,256,128]{3,2,1,0:T(8,128)(2,1)S(1)}, bf16[8,8,256,128]{3,2,1,0:T(8,128)(2,1)}, u32[]{:S(2)}) copy-start(bf16[8,8,256,128]{3,2,1,0:T(8,128)(2,1)} %copy-done) | copy-start | bytes 12582916
  41.2 9.2 %all-to-all-start.2 = ((f32[4,64,128]{2,1,0:T(8,128)}), f32[4,64,128]{2,1,0:T(8,128)S(1)}, u32[]{:S(2)}, u32[]{:S(2)}) async-start(f32[4,64,128]{2,1,0:T(8,128)} %broadcast_in_dim.12), calls=%async_computation.2 | async-start | bytes 262144 | tf_op jit(solution)/shard_map/all_to_all | solution.py:43
  50.7 3.7 %collective-permute-start.6 = (f32[64,128]{1,0:T(8,128)S(1)}, f32[64,128]{1,0:T(8,128)S(1)}, u32[]{:S(2)}, u32[]{:S(2)}) collective-permute-start(f32[64,128]{1,0:T(8,128)S(1)} %get-tuple-element.7), channel_id=1, source_target_pairs={{0,3},{1,2},{2,1},{3,0},{4,7},{5,6},{6,5},{7,4},{8,11},{9,10},{10,... | collective-permute-start | bytes 98312 | tf_op jit(solution)/shard_map/ppermute | solution.py:24
  50.8 4.0 %collective-permute-start.5 = (f32[64,128]{1,0:T(8,128)S(1)}, f32[64,128]{1,0:T(8,128)S(1)}, u32[]{:S(2)}, u32[]{:S(2)}) collective-permute-start(f32[64,128]{1,0:T(8,128)S(1)} %get-tuple-element.8), channel_id=1, source_target_pairs={{0,2},{1,3},{2,0},{3,1},{4,6},{5,7},{6,4},{7,5},{8,10},{9,11},{10,... | collective-permute-start | bytes 98312 | tf_op jit(solution)/shard_map/ppermute | solution.py:24
  52.4 2.4 %collective-permute-start.4 = (f32[64,128]{1,0:T(8,128)S(1)}, f32[64,128]{1,0:T(8,128)S(1)}, u32[]{:S(2)}, u32[]{:S(2)}) collective-permute-start(f32[64,128]{1,0:T(8,128)S(1)} %get-tuple-element.9), channel_id=1, source_target_pairs={{0,1},{1,0},{2,3},{3,2},{4,5},{5,4},{6,7},{7,6},{8,9},{9,8},{10,11... | collective-permute-start | bytes 98312 | tf_op jit(solution)/shard_map/ppermute | solution.py:24
  54.9 2.2 %copy-start.3 = (bf16[8,8,256,128]{3,2,1,0:T(8,128)(2,1)S(1)}, bf16[8,8,256,128]{3,2,1,0:T(8,128)(2,1)}, u32[]{:S(2)}) copy-start(bf16[8,8,256,128]{3,2,1,0:T(8,128)(2,1)} %copy-done) | copy-start | bytes 12582916
  58.3 3.7 %collective-permute-start.7 = (f32[8,256]{1,0:T(8,128)S(1)}, f32[8,256]{1,0:T(8,128)S(1)}, u32[]{:S(2)}, u32[]{:S(2)}) collective-permute-start(f32[8,256]{1,0:T(8,128)S(1)} %shard_map.50), channel_id=1, source_target_pairs={{0,2},{2,0},{4,6},{6,4},{8,10},{10,8},{12,14},{14,12},{1,3},{3,1},... | collective-permute-start | bytes 24584 | tf_op jit(solution)/shard_map/ppermute | solution.py:24
  71.0 3.5 %collective-permute-start.10 = (f32[48,128]{1,0:T(8,128)S(1)}, f32[48,128]{1,0:T(8,128)S(1)}, u32[]{:S(2)}, u32[]{:S(2)}) collective-permute-start(f32[48,128]{1,0:T(8,128)S(1)} %get-tuple-element.10), channel_id=1, source_target_pairs={{0,3},{1,2},{2,1},{3,0},{4,7},{5,6},{6,5},{7,4},{8,11},{9,10},{10,... | collective-permute-start | bytes 73736 | tf_op jit(solution)/shard_map/ppermute | solution.py:24
  71.1 3.9 %collective-permute-start.9 = (f32[48,128]{1,0:T(8,128)S(1)}, f32[48,128]{1,0:T(8,128)S(1)}, u32[]{:S(2)}, u32[]{:S(2)}) collective-permute-start(f32[48,128]{1,0:T(8,128)S(1)} %get-tuple-element.11), channel_id=1, source_target_pairs={{0,2},{1,3},{2,0},{3,1},{4,6},{5,7},{6,4},{7,5},{8,10},{9,11},{10,... | collective-permute-start | bytes 73736 | tf_op jit(solution)/shard_map/ppermute | solution.py:24
  72.7 2.3 %collective-permute-start.8 = (f32[48,128]{1,0:T(8,128)S(1)}, f32[48,128]{1,0:T(8,128)S(1)}, u32[]{:S(2)}, u32[]{:S(2)}) collective-permute-start(f32[48,128]{1,0:T(8,128)S(1)} %get-tuple-element.12), channel_id=1, source_target_pairs={{0,1},{1,0},{2,3},{3,2},{4,5},{5,4},{6,7},{7,6},{8,9},{9,8},{10,11... | collective-permute-start | bytes 73736 | tf_op jit(solution)/shard_map/ppermute | solution.py:24

commit v5 on v3

v5 whole, which is shorter than its diff:
```python
import jax
import jax.numpy as jnp
from jax import lax
from jax.experimental import pallas as pl
from jax.experimental.pallas import tpu as pltpu
from jax.sharding import PartitionSpec as P

ITERS = 2
ALL = ("genome", "reads")
TERMS = 16
ID_ROWS = 8
LANES = 128
VMEM = pl.BlockSpec(memory_space=pltpu.VMEM)
ANY = pl.BlockSpec(memory_space=pl.ANY)


def radices(n):
    out = []
    while n > 1:
        r = 4 if n % 4 == 0 else 2
        out.append(r)
        n //= r
    return out


def swap(x, axes, k):
    n = lax.axis_size(axes)
    return lax.ppermute(x, axes, [(i, i ^ k) for i in range(n)])


def position(k, n):
    place = 0
    for r in radices(n):
        n //= r
        place = place + (k % r) * n
        k = k // r
    return place


def gather_far(x, axes):
    parts = [x]
    stride = lax.axis_size(axes)
    for r in radices(stride)[:0:-1]:
        stride //= r
        sent = parts[0] if len(parts) == 1 else jnp.concatenate(parts, axis=0)
        parts = [sent] + [swap(sent, axes, j * stride) for j in range(1, r)]
    return parts


def dot(a, b, dims=(((1,), (0,)), ((), ()))):
    return lax.dot_general(a, b, dims, preferred_element_type=jnp.float32)


def terms(x):
    hi = x.astype(jnp.bfloat16)
    rest = x - hi.astype(jnp.float32)
    mid = rest.astype(jnp.bfloat16)
    return hi, mid, (rest - mid.astype(jnp.float32)).astype(jnp.bfloat16)


def select_rows(hot, x):
    hi, mid, low = terms(x)
    hot = hot.astype(jnp.bfloat16)
    return dot(hot, hi) + dot(hot, mid) + dot(hot, low)


def split(row):
    x = jnp.broadcast_to(row, (TERMS, row.shape[1]))
    hi = x.astype(jnp.bfloat16).astype(jnp.float32)
    rest = x - hi
    mid = rest.astype(jnp.bfloat16).astype(jnp.float32)
    low = rest - mid
    at = lax.broadcasted_iota(jnp.int32, x.shape, 0)
    out = jnp.where(at == 0, hi, jnp.where(at == 1, mid, jnp.where(at == 2, low, 0.0)))
    return out.astype(jnp.bfloat16)


def down(row):
    return jnp.transpose(jnp.broadcast_to(row, (LANES, LANES)))


def hot_rows(values, count):
    column = down(values)
    blocks = []
    for start in range(0, count, LANES):
        width = min(LANES, count - start)
        lane = lax.broadcasted_iota(jnp.int32, (LANES, width), 1).astype(jnp.float32) + start
        blocks.append((column[:, :width] == lane).astype(jnp.float32))
    return blocks[0] if len(blocks) == 1 else jnp.concatenate(blocks, axis=1)


def prepare_kernel(own_blocks, lik_ref, ids_ref, valid_ref, held_ref, info_ref, ids, valid, wide, sems):
    read_blocks, slots = ids.shape
    copies = [
        pltpu.make_async_copy(ids_ref, ids, sems.at[0]),
        pltpu.make_async_copy(valid_ref, valid, sems.at[1]),
    ]
    held = [
        pltpu.make_async_copy(lik_ref.at[b], held_ref.at[b], sems.at[2 + b])
        for b in range(held_ref.shape[0])
    ]
    for copy in copies + held:
        copy.start()
    for copy in copies:
        copy.wait()
    n = lax.axis_size(ALL)
    near = radices(n)[0]
    far = n // near
    me = lax.axis_index("genome") * lax.axis_size("reads") + lax.axis_index("reads")
    lane = lax.broadcasted_iota(jnp.int32, wide.shape, 1)
    wide[...] = jnp.zeros_like(wide)
    wide[:, :slots] = jnp.where(valid[...] > 0, ids[...], -1).astype(jnp.float32)
    flat = jnp.sum(
        pltpu.roll(wide[...], 0, 1, stride=slots, stride_axis=0), axis=0, keepdims=True
    )
    flat = jnp.where(lane[:1] < read_blocks * slots, flat, -1.0)
    owner = ((flat + 0.5) * (1.0 / own_blocks)).astype(jnp.int32)
    inside = flat.astype(jnp.int32) - owner * own_blocks
    away = owner ^ me
    place = position(away, n)
    place = (place // far) * near_rows(far, own_blocks) + (place % far) * own_blocks + inside
    place = jnp.where(flat < 0, -1, place).astype(jnp.float32)
    row = lax.broadcasted_iota(jnp.int32, info_ref.shape, 0)
    info_ref[...] = jnp.where(row == 0, flat, jnp.where(row == 1, place, 0.0))
    for copy in held:
        copy.wait()


def join_kernel(*refs):
    out_ref = refs[-1]
    at = 0
    for ref in refs[:-1]:
        out_ref[at : at + ref.shape[0], :] = ref[...]
        at += ref.shape[0]
    if at < out_ref.shape[0]:
        out_ref[at:, :] = jnp.zeros((out_ref.shape[0] - at, out_ref.shape[1]), jnp.float32)


def near_rows(far, own_blocks):
    return -(-(far * own_blocks + ID_ROWS) // 16) * 16


def row_sums(picked_ref, lik_ref, out_ref):
    read_blocks, slots, reads, cols = lik_ref.shape
    for b in range(read_blocks):
        total = None
        for s in range(0, slots, 2):
            at = b * slots + s
            left = jnp.concatenate(
                [split(picked_ref[at : at + 1, :]), split(picked_ref[at + 1 : at + 2, :])], axis=1
            )
            right = jnp.concatenate([lik_ref[b, s], lik_ref[b, s + 1]], axis=1)
            part = dot(left, right, (((1,), (1,)), ((), ())))
            total = part if total is None else total + part
        row = jnp.sum(total, axis=0, keepdims=True)
        for i in range(out_ref.shape[0]):
            out_ref[i, b : b + 1, :] = row


def first_row_kernel(near, info_ref, *refs):
    pieces, (lik_ref, out_ref, picked_ref) = refs[:near], refs[near:]
    table = jnp.concatenate([piece[...] for piece in pieces], axis=0)
    hot = hot_rows(info_ref[1:2, :], table.shape[0])
    picked_ref[...] = select_rows(hot[: picked_ref.shape[0]], table)
    row_sums(picked_ref, lik_ref, out_ref)


def next_row_kernel(near, scale, *refs):
    parts, (lik_ref, out_ref, picked_ref) = refs[:near], refs[near:]
    total = parts[0][...]
    for part in parts[1:]:
        total = total + part[...]
    picked_ref[...] = total * scale
    row_sums(picked_ref, lik_ref, out_ref)


def column_sums(parts_ref, picked_ref, lik_ref, contrib_ref, inverse_ref):
    read_blocks, slots, reads, cols = lik_ref.shape
    total = parts_ref[0]
    for i in range(1, parts_ref.shape[0]):
        total = total + parts_ref[i]
    inverse_ref[...] = 1.0 / total
    for b in range(read_blocks):
        left = split(inverse_ref[b : b + 1, :])
        for s in range(0, slots, 2):
            at = b * slots + s
            right = jnp.concatenate([lik_ref[b, s], lik_ref[b, s + 1]], axis=1)
            summed = jnp.sum(dot(left, right), axis=0, keepdims=True)
            contrib_ref[at : at + 1, :] = picked_ref[at : at + 1, :] * summed[:, :cols]
            contrib_ref[at + 1 : at + 2, :] = picked_ref[at + 1 : at + 2, :] * summed[:, cols:]


def column_kernel(info_ref, parts_ref, picked_ref, lik_ref, out_ref, inverse_ref):
    column_sums(parts_ref, picked_ref, lik_ref, out_ref, inverse_ref)
    out_ref[picked_ref.shape[0] :, :] = info_ref[...]


def last_column_kernel(info_ref, parts_ref, picked_ref, lik_ref, out_ref, inverse_ref, contrib_ref):
    column_sums(parts_ref, picked_ref, lik_ref, contrib_ref, inverse_ref)
    owners, own_blocks, cols = out_ref.shape
    all_slots = contrib_ref.shape[0]
    block = lax.broadcasted_iota(jnp.int32, (owners * own_blocks, all_slots), 0)
    hot = (block.astype(jnp.float32) == info_ref[0:1, :all_slots]).astype(jnp.float32)
    counts = select_rows(hot, contrib_ref[...])
    for i in range(owners):
        out_ref[i] = counts[i * own_blocks : (i + 1) * own_blocks, :]


def wanted_kernel(near, all_slots, pieces, *refs):
    given_refs, wanted, outs = refs[:pieces], refs[pieces : pieces + near], refs[pieces + near :]
    rows = all_slots + ID_ROWS
    half = LANES // 2
    lane = lax.broadcasted_iota(jnp.int32, (1, LANES), 1)
    ids, values = [], []
    for ref in given_refs:
        for at in range(0, ref.shape[0], rows):
            ids.append(ref[at + all_slots : at + all_slots + 1, :])
            values.append(ref[at : at + all_slots, :])
    pairs = [
        jnp.where(lane < half, a, pltpu.roll(b, half, 1)) for a, b in zip(ids[::2], ids[1::2])
    ]
    given = terms(jnp.concatenate(values, axis=0))
    for ids_ref, out_ref in zip(wanted, outs):
        column = down(ids_ref[0:1, :])[:all_slots]
        hot = jnp.concatenate([(column == pair).astype(jnp.float32) for pair in pairs], axis=1)
        hot = hot.astype(jnp.bfloat16)
        out_ref[...] = dot(hot, given[0]) + dot(hot, given[1]) + dot(hot, given[2])


def call(kernel, outs, scratch, *operands):
    return pl.pallas_call(
        kernel,
        out_shape=[jax.ShapeDtypeStruct(shape, jnp.float32) for shape in outs],
        in_specs=[VMEM] * len(operands),
        out_specs=[VMEM] * len(outs),
        scratch_shapes=[pltpu.VMEM(shape, jnp.float32) for shape in scratch],
        compiler_params=pltpu.CompilerParams(vmem_limit_bytes=16 * 2**20),
    )(*operands)


def prepare(own_blocks, likelihood, block_ids, slot_valid):
    read_blocks, slots = block_ids.shape
    return pl.pallas_call(
        lambda *refs: prepare_kernel(own_blocks, *refs),
        out_shape=[
            pltpu.VMEM(likelihood.shape, likelihood.dtype),
            jax.ShapeDtypeStruct((ID_ROWS, LANES), jnp.float32),
        ],
        in_specs=[ANY] * 3,
        out_specs=[VMEM] * 2,
        scratch_shapes=[
            pltpu.VMEM((read_blocks, slots), jnp.int32),
            pltpu.VMEM((read_blocks, slots), jnp.int32),
            pltpu.VMEM((read_blocks, LANES), jnp.float32),
            pltpu.SemaphoreType.DMA((2 + read_blocks,)),
        ],
        compiler_params=pltpu.CompilerParams(vmem_limit_bytes=16 * 2**20),
    )(*[pltpu.with_memory_space_constraint(x, pltpu.HBM) for x in (likelihood, block_ids, slot_valid)])


def local(likelihood, block_ids, slot_valid, start_weights):
    read_blocks, slots, reads, cols = likelihood.shape
    n = lax.axis_size(ALL)
    chips = lax.axis_size("genome")
    near = radices(n)[0]
    far = n // near
    own_weights = start_weights.reshape(-1, cols)
    own_blocks = own_weights.shape[0]
    all_slots = read_blocks * slots
    total_reads = read_blocks * lax.axis_size("reads") * reads
    scale = n * own_blocks * cols / total_reads

    column = gather_far(own_weights, ALL)
    held, info = prepare(own_blocks, likelihood, block_ids, slot_valid)
    (sent,) = call(join_kernel, [(near_rows(far, own_blocks), cols)], [], *column, info)
    pieces = [sent] + [swap(sent, ALL, j) for j in range(1, near)]
    at = far * own_blocks
    wanted = [info] + [piece[at : at + ID_ROWS] for piece in pieces[1:]]

    row_shapes = [(chips, read_blocks, reads), (all_slots, cols)]
    inverse = (read_blocks, reads)
    for step in range(ITERS):
        if step == 0:
            row_parts, picked = call(
                lambda *refs: first_row_kernel(near, *refs), row_shapes, [], info, *pieces, held
            )
        else:
            row_parts, picked = call(
                lambda *refs: next_row_kernel(near, scale, *refs), row_shapes, [], *parts, held
            )
        row_parts = lax.all_to_all(row_parts, "genome", 0, 0, tiled=True)
        if step + 1 < ITERS:
            (contrib,) = call(
                column_kernel,
                [(all_slots + ID_ROWS, cols)],
                [inverse],
                info,
                row_parts,
                picked,
                held,
            )
            given = gather_far(contrib, ALL)
            sums = call(
                lambda *refs: wanted_kernel(near, all_slots, len(given), *refs),
                [(all_slots, cols)] * near,
                [],
                *given,
                *wanted,
            )
            parts = [sums[0]] + [swap(sums[j], ALL, j) for j in range(1, near)]
    (counts,) = call(
        last_column_kernel,
        [(n, own_blocks, cols)],
        [inverse, (all_slots, cols)],
        info,
        row_parts,
        picked,
        held,
    )
    counts = lax.all_to_all(counts, ALL, 0, 0, tiled=True)
    return (jnp.sum(counts, axis=0) * scale).reshape(-1)


def solution(mesh):
    placed = (
        P(("parts", "reads"), "genome", None, None),
        P(("parts", "reads"), "genome"),
        P(("parts", "reads"), "genome"),
        P(("parts", "genome", "reads")),
    )
    return jax.shard_map(
        local,
        mesh=mesh,
        in_specs=placed,
        out_specs=P(("parts", "genome", "reads")),
        check_vma=False,
    )
```

time: 73.8 us -> 62.5 us (0.85)
  blocking collectives: 10.8 us -> 32.2 us
  waiting for transfers between devices: 24 us -> 8.59 us
  starting transfers between devices: 23.6 us -> 14 us
  local copies, waits for them, and re-layouts: 8.3 us -> 0.01 us
  Pallas kernels: 3.75 us -> 6.76 us
  other arithmetic: 2.08 us -> 0.62 us
    all_to_all x1 -> x3, blocking collectives: 10.8 us -> 32.2 us  [the longest x2 21.7 us: local(): row_parts = lax.all_to_all(row_parts, 'genome', 0, 0, tiled=True)]
    ppermute x18 -> x12, waiting for transfers between devices: 17.3 us -> 8.59 us  [swap(): return lax.ppermute(x, axes, [(i, i ^ k) for i in range(n)])]
    all_to_all x1 -> x0, waiting for transfers between devices: 6.72 us -> none  [spread(): return lax.all_to_all(sent, axes, 0, 0, tiled=True)]
    unnamed x11 -> x2, local copies, waits for them, and re-layouts: 6.57 us -> 0.01 us
    ppermute x18 -> x12, starting transfers between devices: 20.2 us -> 14 us  [swap(): return lax.ppermute(x, axes, [(i, i ^ k) for i in range(n)])]
    all_to_all x1 -> x0, starting transfers between devices: 3.35 us -> none  [spread(): return lax.all_to_all(sent, axes, 0, 0, tiled=True)]
    pallas_call x4 -> x7, Pallas kernels: 3.75 us -> 6.76 us  [the longest x6 4.5 us: call(): pl.pallas_call(kernel, out_shape=[jax.ShapeDtypeStruct(shape, jnp.float32...]
    reshape x2 -> x0, local copies, waits for them, and re-layouts: 0.77 us -> none  [the longest x1 0.77 us: local(): ids = block_ids.reshape(-1)]
  transfers between devices with their start and end apart: 19 -> 12, of which waited for: 12 -> 7; matrix products, arithmetic and copies ran while one was open for 0% -> 0% of each run, Pallas kernels for 0% -> 4%
where the time goes in v5:
time: 62.5 us; the launch traced here: 62.2 us
  blocking collectives  32.2 us (52%)
  starting transfers between devices  14 us (22%)
  waiting for transfers between devices  8.59 us (14%)
  Pallas kernels  6.76 us (11%)
    all_to_all x2, blocking collectives, local(): row_parts = lax.all_to_all(row_parts, 'genome', 0, 0, tiled=True)  21.7 us
    ppermute x12, starting transfers between devices, swap(): return lax.ppermute(x, axes, [(i, i ^ k) for i in range(n)])  14 us
    all_to_all x1, blocking collectives, local(): counts = lax.all_to_all(counts, ALL, 0, 0, tiled=True)  10.5 us
    ppermute x12, waiting for transfers between devices, swap(): return lax.ppermute(x, axes, [(i, i ^ k) for i in range(n)])  8.59 us
    pallas_call x6, Pallas kernels, call(): pl.pallas_call(kernel, out_shape=[jax.ShapeDtypeStruct(shape, jnp.float32...  4.5 us
    pallas_call x1, Pallas kernels, prepare(): pl.pallas_call(lambda *refs: prepare_kernel(own_blocks, *refs), out_shape...  2.26 us
  transfers between devices with their start and end apart: 12, of which 7 were waited for; matrix products, arithmetic and copies ran while one was open for 0% of the time, Pallas kernels for 4%

profile of v5, /device:TPU:0, one launch (start us, length us, event | category | flops | bytes accessed | tf_op | source)
XLA Modules:
  0.0 62.2 jit_solution(8375706599752240062)
XLA Ops:
  0.0 5.0 %collective-permute-start.2 = (f32[12,128]{1,0:T(8,128)}, f32[12,128]{1,0:T(8,128)S(1)}, u32[]{:S(2)}, u32[]{:S(2)}) collective-permute-start(f32[12,128]{1,0:T(8,128)} %bitcast.3), channel_id=1, source_target_pairs={{0,12},{1,13},{2,14},{3,15},{4,8},{5,9},{6,10},{7,11},{8,4},{9,5},... | collective-permute-start | bytes 18440 | tf_op jit(solution)/shard_map/ppermute | solution.py:28
  5.1 0.6 %collective-permute-start = (f32[12,128]{1,0:T(8,128)}, f32[12,128]{1,0:T(8,128)S(1)}, u32[]{:S(2)}, u32[]{:S(2)}) collective-permute-start(f32[12,128]{1,0:T(8,128)} %bitcast.5), channel_id=1, source_target_pairs={{0,4},{1,5},{2,6},{3,7},{4,0},{5,1},{6,2},{7,3},{8,12},{9,13},{10,... | collective-permute-start | bytes 18440 | tf_op jit(solution)/shard_map/ppermute | solution.py:28
  5.7 2.3 %shard_map.46 = (bf16[8,8,256,128]{3,2,1,0:T(8,128)(2,1)S(1)}, f32[8,128]{1,0:T(8,128)S(1)}) custom-call(bf16[8,8,256,128]{3,2,1,0:T(8,128)(2,1)} %refs_0_.1, s32[8,8]{1,0:T(8,128)} %refs_1_.1, s32[8,8]{1,0:T(8,128)} %refs_2_.1), custom_call_target="tpu_custom_call" | custom-call | tf_op jit(solution)/shard_map/pallas_call | solution.py:243
  8.0 1.9 %collective-permute-done.1.refs_2_ = f32[12,128]{1,0:T(8,128)S(1)} collective-permute-done((f32[12,128]{1,0:T(8,128)}, f32[12,128]{1,0:T(8,128)S(1)}, u32[]{:S(2)}, u32[]{:S(2)}) %collective-permute-start.1) | collective-permute-done | bytes 6176 | tf_op jit(solution)/shard_map/ppermute | solution.py:28
  9.9 1.6 %collective-permute-start.4 = (f32[64,128]{1,0:T(8,128)S(1)}, f32[64,128]{1,0:T(8,128)S(1)}, u32[]{:S(2)}, u32[]{:S(2)}) collective-permute-start(f32[64,128]{1,0:T(8,128)S(1)} %shard_map.47.refs_1_), channel_id=1, source_target_pairs={{0,2},{1,3},{2,0},{3,1},{4,6},{5,7},{6,4},{7,5},{8,10},{9,11},{10,... | collective-permute-start | bytes 98312 | tf_op jit(solution)/shard_map/ppermute | solution.py:28
  11.8 1.8 %collective-permute-done.5.refs_4_ = f32[64,128]{1,0:T(8,128)S(1)} collective-permute-done((f32[64,128]{1,0:T(8,128)S(1)}, f32[64,128]{1,0:T(8,128)S(1)}, u32[]{:S(2)}, u32[]{:S(2)}) %collective-permute-start.5) | collective-permute-done | bytes 32800 | tf_op jit(solution)/shard_map/ppermute | solution.py:28
  13.5 0.4 collective-permute-done.4.refs_3_
  13.9 1.4 %shard_map.48 = (f32[8,8,256]{2,1,0:T(8,128)S(1)}, f32[64,128]{1,0:T(8,128)S(1)}) custom-call(f32[8,128]{1,0:T(8,128)S(1)} %get-tuple-element.15.refs_4_.refs_0_.info_ref, f32[64,128]{1,0:T(8,128)S(1)} %shard_map.47.refs_1_, f32[64,128]{1,0:T(8,128)S(1)} %collective-permute-done.3.refs_2_, f32[64,128]{1,0:T(8,128)S(1)} %collective-permute-done.4.refs_3_, ...), custom_call_target="tpu_custom_call" | custom-call | tf_op jit(solution)/shard_map/pallas_call | solution.py:231
  15.3 10.9 %all_to_all.15.parts_ref = f32[8,8,256]{2,1,0:T(8,128)S(1)} all-to-all(f32[8,8,256]{2,1,0:T(8,128)S(1)} %get-tuple-element.17), channel_id=1, replica_groups=mesh['parts'=2,'genome'=8,'reads'=2] {'genome'}, dimensions={0} | all-to-all | bytes 131072 | tf_op jit(solution)/shard_map/all_to_all | solution.py:291
  26.3 0.7 %shard_map.49.refs_0_ = f32[72,128]{1,0:T(8,128)S(1)} custom-call(f32[8,128]{1,0:T(8,128)S(1)} %get-tuple-element.15.refs_4_.refs_0_.info_ref, f32[8,8,256]{2,1,0:T(8,128)S(1)} %all_to_all.15.parts_ref, f32[64,128]{1,0:T(8,128)S(1)} %get-tuple-element.18.picked_ref, bf16[8,8,256,128]{3,2,1,0:T(8,128)(2,1)S(1)} %get-tuple-element.16.refs_5_.lik_ref.refs_4_), custom_call_target="tpu_custom_call" | custom-call | tf_op jit(solution)/shard_map/pallas_call | solution.py:231
  27.0 0.6 %collective-permute-start.8 = (f32[72,128]{1,0:T(8,128)S(1)}, f32[72,128]{1,0:T(8,128)S(1)}, u32[]{:S(2)}, u32[]{:S(2)}) collective-permute-start(f32[72,128]{1,0:T(8,128)S(1)} %shard_map.49.refs_0_), channel_id=1, source_target_pairs={{0,12},{1,13},{2,14},{3,15},{4,8},{5,9},{6,10},{7,11},{8,4},{9,5},... | collective-permute-start | bytes 110600 | tf_op jit(solution)/shard_map/ppermute | solution.py:28
  27.6 1.1 %collective-permute-start.7 = (f32[72,128]{1,0:T(8,128)S(1)}, f32[72,128]{1,0:T(8,128)S(1)}, u32[]{:S(2)}, u32[]{:S(2)}) collective-permute-start(f32[72,128]{1,0:T(8,128)S(1)} %shard_map.49.refs_0_), channel_id=1, source_target_pairs={{0,8},{1,9},{2,10},{3,11},{4,12},{5,13},{6,14},{7,15},{8,0},{9,1},... | collective-permute-start | bytes 110600 | tf_op jit(solution)/shard_map/ppermute | solution.py:28
  28.7 2.7 %collective-permute-start.6 = (f32[72,128]{1,0:T(8,128)S(1)}, f32[72,128]{1,0:T(8,128)S(1)}, u32[]{:S(2)}, u32[]{:S(2)}) collective-permute-start(f32[72,128]{1,0:T(8,128)S(1)} %shard_map.49.refs_0_), channel_id=1, source_target_pairs={{0,4},{1,5},{2,6},{3,7},{4,0},{5,1},{6,2},{7,3},{8,12},{9,13},{10,... | collective-permute-start | bytes 110600 | tf_op jit(solution)/shard_map/ppermute | solution.py:28
  31.4 1.4 %collective-permute-done.8.refs_3_ = f32[72,128]{1,0:T(8,128)S(1)} collective-permute-done((f32[72,128]{1,0:T(8,128)S(1)}, f32[72,128]{1,0:T(8,128)S(1)}, u32[]{:S(2)}, u32[]{:S(2)}) %collective-permute-start.8) | collective-permute-done | bytes 36896 | tf_op jit(solution)/shard_map/ppermute | solution.py:28
  32.8 0.5 collective-permute-done.6.refs_1_
  33.3 0.3 shard_map.50
  33.7 0.8 %collective-permute-start.10 = (f32[64,128]{1,0:T(8,128)S(1)}, f32[64,128]{1,0:T(8,128)S(1)}, u32[]{:S(2)}, u32[]{:S(2)}) collective-permute-start(f32[64,128]{1,0:T(8,128)S(1)} %get-tuple-element.21), channel_id=1, source_target_pairs={{0,2},{1,3},{2,0},{3,1},{4,6},{5,7},{6,4},{7,5},{8,10},{9,11},{10,... | collective-permute-start | bytes 98312 | tf_op jit(solution)/shard_map/ppermute | solution.py:28
  34.5 1.1 %collective-permute-start.11 = (f32[64,128]{1,0:T(8,128)S(1)}, f32[64,128]{1,0:T(8,128)S(1)}, u32[]{:S(2)}, u32[]{:S(2)}) collective-permute-start(f32[64,128]{1,0:T(8,128)S(1)} %get-tuple-element.22), channel_id=1, source_target_pairs={{0,3},{1,2},{2,1},{3,0},{4,7},{5,6},{6,5},{7,4},{8,11},{9,10},{10,... | collective-permute-start | bytes 98312 | tf_op jit(solution)/shard_map/ppermute | solution.py:28
  35.6 2.3 %collective-permute-done.10.refs_2_ = f32[64,128]{1,0:T(8,128)S(1)} collective-permute-done((f32[64,128]{1,0:T(8,128)S(1)}, f32[64,128]{1,0:T(8,128)S(1)}, u32[]{:S(2)}, u32[]{:S(2)}) %collective-permute-start.10) | collective-permute-done | bytes 32800 | tf_op jit(solution)/shard_map/ppermute | solution.py:28
  38.2 1.2 %shard_map.51 = (f32[8,8,256]{2,1,0:T(8,128)S(1)}, f32[64,128]{1,0:T(8,128)S(1)}) custom-call(f32[64,128]{1,0:T(8,128)S(1)} %get-tuple-element.19.refs_0_, f32[64,128]{1,0:T(8,128)S(1)} %collective-permute-done.9.refs_1_, f32[64,128]{1,0:T(8,128)S(1)} %collective-permute-done.10.refs_2_, f32[64,128]{1,0:T(8,128)S(1)} %collective-permute-done.11.refs_3_, ...), custom_call_target="tpu_custom_call" | custom-call | tf_op jit(solution)/shard_map/pallas_call | solution.py:231
  39.5 10.7 %all_to_all.16.parts_ref = f32[8,8,256]{2,1,0:T(8,128)S(1)} all-to-all(f32[8,8,256]{2,1,0:T(8,128)S(1)} %get-tuple-element.23), channel_id=1, replica_groups=mesh['parts'=2,'genome'=8,'reads'=2] {'genome'}, dimensions={0} | all-to-all | bytes 131072 | tf_op jit(solution)/shard_map/all_to_all | solution.py:291
  50.2 0.9 %shard_map.52 = f32[16,12,128]{2,1,0:T(8,128)S(1)} custom-call(f32[8,128]{1,0:T(8,128)S(1)} %get-tuple-element.15.refs_4_.refs_0_.info_ref, f32[8,8,256]{2,1,0:T(8,128)S(1)} %all_to_all.16.parts_ref, f32[64,128]{1,0:T(8,128)S(1)} %get-tuple-element.24.picked_ref, bf16[8,8,256,128]{3,2,1,0:T(8,128)(2,1)S(1)} %get-tuple-element.16.refs_5_.lik_ref.refs_4_), custom_call_target="tpu_custom_call" | custom-call | tf_op jit(solution)/shard_map/pallas_call | solution.py:231
  51.1 10.5 %all_to_all.17 = f32[16,12,128]{2,1,0:T(8,128)S(1)} all-to-all(f32[16,12,128]{2,1,0:T(8,128)S(1)} %shard_map.52), channel_id=1, replica_groups=mesh['parts'=2,'genome'=8,'reads'=2] {'genome','reads'}, dimensions={0} | all-to-all | bytes 196608 | tf_op jit(solution)/shard_map/all_to_all | solution.py:320
  61.6 0.6 multiply_bitcast_fusion
  (17 shorter events, 0.8 us)
Async XLA Ops:
  0.0 9.8 %copy-start = (f32[1536]{0:T(1024)S(1)}, f32[1536]{0:T(1024)}, u32[]{:S(2)}) copy-start(f32[1536]{0:T(1024)} %param.7) | copy-start | bytes 18436
  0.0 8.0 %collective-permute-start.2 = (f32[12,128]{1,0:T(8,128)}, f32[12,128]{1,0:T(8,128)S(1)}, u32[]{:S(2)}, u32[]{:S(2)}) collective-permute-start(f32[12,128]{1,0:T(8,128)} %bitcast.3), channel_id=1, source_target_pairs={{0,12},{1,13},{2,14},{3,15},{4,8},{5,9},{6,10},{7,11},{8,4},{9,5},... | collective-permute-start | bytes 18440 | tf_op jit(solution)/shard_map/ppermute | solution.py:28
  5.1 4.8 %collective-permute-start.1 = (f32[12,128]{1,0:T(8,128)}, f32[12,128]{1,0:T(8,128)S(1)}, u32[]{:S(2)}, u32[]{:S(2)}) collective-permute-start(f32[12,128]{1,0:T(8,128)} %bitcast.4), channel_id=1, source_target_pairs={{0,8},{1,9},{2,10},{3,11},{4,12},{5,13},{6,14},{7,15},{8,0},{9,1},... | collective-permute-start | bytes 18440 | tf_op jit(solution)/shard_map/ppermute | solution.py:28
  5.1 4.8 %collective-permute-start = (f32[12,128]{1,0:T(8,128)}, f32[12,128]{1,0:T(8,128)S(1)}, u32[]{:S(2)}, u32[]{:S(2)}) collective-permute-start(f32[12,128]{1,0:T(8,128)} %bitcast.5), channel_id=1, source_target_pairs={{0,4},{1,5},{2,6},{3,7},{4,0},{5,1},{6,2},{7,3},{8,12},{9,13},{10,... | collective-permute-start | bytes 18440 | tf_op jit(solution)/shard_map/ppermute | solution.py:28
  9.8 3.7 %collective-permute-start.5 = (f32[64,128]{1,0:T(8,128)S(1)}, f32[64,128]{1,0:T(8,128)S(1)}, u32[]{:S(2)}, u32[]{:S(2)}) collective-permute-start(f32[64,128]{1,0:T(8,128)S(1)} %shard_map.47.refs_1_), channel_id=1, source_target_pairs={{0,3},{1,2},{2,1},{3,0},{4,7},{5,6},{6,5},{7,4},{8,11},{9,10},{10,... | collective-permute-start | bytes 98312 | tf_op jit(solution)/shard_map/ppermute | solution.py:28
  9.9 4.0 %collective-permute-start.4 = (f32[64,128]{1,0:T(8,128)S(1)}, f32[64,128]{1,0:T(8,128)S(1)}, u32[]{:S(2)}, u32[]{:S(2)}) collective-permute-start(f32[64,128]{1,0:T(8,128)S(1)} %shard_map.47.refs_1_), channel_id=1, source_target_pairs={{0,2},{1,3},{2,0},{3,1},{4,6},{5,7},{6,4},{7,5},{8,10},{9,11},{10,... | collective-permute-start | bytes 98312 | tf_op jit(solution)/shard_map/ppermute | solution.py:28
  11.5 2.4 %collective-permute-start.3 = (f32[64,128]{1,0:T(8,128)S(1)}, f32[64,128]{1,0:T(8,128)S(1)}, u32[]{:S(2)}, u32[]{:S(2)}) collective-permute-start(f32[64,128]{1,0:T(8,128)S(1)} %shard_map.47.refs_1_), channel_id=1, source_target_pairs={{0,1},{1,0},{2,3},{3,2},{4,5},{5,4},{6,7},{7,6},{8,9},{9,8},{10,11... | collective-permute-start | bytes 98312 | tf_op jit(solution)/shard_map/ppermute | solution.py:28
  27.0 5.9 %collective-permute-start.8 = (f32[72,128]{1,0:T(8,128)S(1)}, f32[72,128]{1,0:T(8,128)S(1)}, u32[]{:S(2)}, u32[]{:S(2)}) collective-permute-start(f32[72,128]{1,0:T(8,128)S(1)} %shard_map.49.refs_0_), channel_id=1, source_target_pairs={{0,12},{1,13},{2,14},{3,15},{4,8},{5,9},{6,10},{7,11},{8,4},{9,5},... | collective-permute-start | bytes 110600 | tf_op jit(solution)/shard_map/ppermute | solution.py:28
  27.6 5.3 %collective-permute-start.7 = (f32[72,128]{1,0:T(8,128)S(1)}, f32[72,128]{1,0:T(8,128)S(1)}, u32[]{:S(2)}, u32[]{:S(2)}) collective-permute-start(f32[72,128]{1,0:T(8,128)S(1)} %shard_map.49.refs_0_), channel_id=1, source_target_pairs={{0,8},{1,9},{2,10},{3,11},{4,12},{5,13},{6,14},{7,15},{8,0},{9,1},... | collective-permute-start | bytes 110600 | tf_op jit(solution)/shard_map/ppermute | solution.py:28
  28.7 4.6 %collective-permute-start.6 = (f32[72,128]{1,0:T(8,128)S(1)}, f32[72,128]{1,0:T(8,128)S(1)}, u32[]{:S(2)}, u32[]{:S(2)}) collective-permute-start(f32[72,128]{1,0:T(8,128)S(1)} %shard_map.49.refs_0_), channel_id=1, source_target_pairs={{0,4},{1,5},{2,6},{3,7},{4,0},{5,1},{6,2},{7,3},{8,12},{9,13},{10,... | collective-permute-start | bytes 110600 | tf_op jit(solution)/shard_map/ppermute | solution.py:28
  33.7 1.9 %collective-permute-start.9 = (f32[64,128]{1,0:T(8,128)S(1)}, f32[64,128]{1,0:T(8,128)S(1)}, u32[]{:S(2)}, u32[]{:S(2)}) collective-permute-start(f32[64,128]{1,0:T(8,128)S(1)} %get-tuple-element.20), channel_id=1, source_target_pairs={{0,1},{1,0},{2,3},{3,2},{4,5},{5,4},{6,7},{7,6},{8,9},{9,8},{10,11... | collective-permute-start | bytes 98312 | tf_op jit(solution)/shard_map/ppermute | solution.py:28
  33.7 4.2 %collective-permute-start.10 = (f32[64,128]{1,0:T(8,128)S(1)}, f32[64,128]{1,0:T(8,128)S(1)}, u32[]{:S(2)}, u32[]{:S(2)}) collective-permute-start(f32[64,128]{1,0:T(8,128)S(1)} %get-tuple-element.21), channel_id=1, source_target_pairs={{0,2},{1,3},{2,0},{3,1},{4,6},{5,7},{6,4},{7,5},{8,10},{9,11},{10,... | collective-permute-start | bytes 98312 | tf_op jit(solution)/shard_map/ppermute | solution.py:28
  34.5 3.7 %collective-permute-start.11 = (f32[64,128]{1,0:T(8,128)S(1)}, f32[64,128]{1,0:T(8,128)S(1)}, u32[]{:S(2)}, u32[]{:S(2)}) collective-permute-start(f32[64,128]{1,0:T(8,128)S(1)} %get-tuple-element.22), channel_id=1, source_target_pairs={{0,3},{1,2},{2,1},{3,0},{4,7},{5,6},{6,5},{7,4},{8,11},{9,10},{10,... | collective-permute-start | bytes 98312 | tf_op jit(solution)/shard_map/ppermute | solution.py:28

commit v6 on v5

v6 whole, which is shorter than its diff:
```python
import jax
import jax.numpy as jnp
from jax import lax
from jax.experimental import pallas as pl
from jax.experimental.pallas import tpu as pltpu
from jax.sharding import PartitionSpec as P

ITERS = 2
ALL = ("genome", "reads")
TERMS = 16
ID_ROWS = 8
NEAR = 4
LANES = 128
VMEM = pl.BlockSpec(memory_space=pltpu.VMEM)
ANY = pl.BlockSpec(memory_space=pl.ANY)


def radices(n):
    out = []
    while n > 1:
        r = 4 if n % 4 == 0 else 2
        out.append(r)
        n //= r
    return out


def swap(x, k):
    return lax.ppermute(x, ALL, [(i, i ^ k) for i in range(lax.axis_size(ALL))])


def near_swaps(parts):
    return [parts[0]] + [swap(parts[j], j) for j in range(1, len(parts))]


def far_radices():
    return radices(lax.axis_size(ALL) // NEAR)


def far_swaps(first, second, r, stride):
    everyone = range(lax.axis_size(ALL))
    if r == 2:
        got = lax.ppermute(first, ALL, [(i, i ^ stride) for i in everyone if i % 2])
        return [got]
    pairs = [(i, i ^ (2 * stride if i % 2 else stride)) for i in everyone]
    got = lax.ppermute(first, ALL, pairs)
    pairs = [(i, i ^ (3 * stride)) for i in everyone if i % 2]
    return [got, lax.ppermute(second, ALL, pairs)]


def dot(a, b, dims=(((1,), (0,)), ((), ()))):
    return lax.dot_general(a, b, dims, preferred_element_type=jnp.float32)


def terms(x):
    hi = x.astype(jnp.bfloat16)
    rest = x - hi.astype(jnp.float32)
    mid = rest.astype(jnp.bfloat16)
    return hi, mid, (rest - mid.astype(jnp.float32)).astype(jnp.bfloat16)


def select_rows(hot, x):
    hi, mid, low = terms(x)
    hot = hot.astype(jnp.bfloat16)
    return dot(hot, hi) + dot(hot, mid) + dot(hot, low)


def split(row):
    x = jnp.broadcast_to(row, (TERMS, row.shape[1]))
    hi = x.astype(jnp.bfloat16).astype(jnp.float32)
    rest = x - hi
    mid = rest.astype(jnp.bfloat16).astype(jnp.float32)
    low = rest - mid
    at = lax.broadcasted_iota(jnp.int32, x.shape, 0)
    out = jnp.where(at == 0, hi, jnp.where(at == 1, mid, jnp.where(at == 2, low, 0.0)))
    return out.astype(jnp.bfloat16)


def down(row):
    return jnp.transpose(jnp.broadcast_to(row, (LANES, LANES)))


def hot_rows(values, count):
    column = down(values)
    blocks = []
    for start in range(0, count, LANES):
        width = min(LANES, count - start)
        lane = lax.broadcasted_iota(jnp.int32, (LANES, width), 1).astype(jnp.float32) + start
        blocks.append((column[:, :width] == lane).astype(jnp.float32))
    return blocks[0] if len(blocks) == 1 else jnp.concatenate(blocks, axis=1)


def on_core_0():
    return lax.axis_index("reads") == 0


def far_place(owner, own_blocks):
    k = owner ^ (lax.axis_index("genome") * 2 + lax.axis_index("reads"))
    row = (owner % 2) * own_blocks
    size = 2 * own_blocks
    rest = k // NEAR
    half = 0 * rest
    radix = far_radices()
    for i, r in enumerate(radix):
        digit = rest % r
        rest = rest // r
        if i + 1 == len(radix):
            half = digit // (r // 2)
            digit = digit % (r // 2)
        row = row + digit * size
        size *= r
    return (k // 2) % 2 * 2 + (half ^ lax.axis_index("reads")), row


def near_rows(own_rows):
    return -(-(own_rows + ID_ROWS) // 16) * 16


def prepare_kernel(own_blocks, lik_ref, ids_ref, valid_ref, held_ref, info_ref, ids, valid, wide, sems):
    read_blocks, slots = ids.shape
    copies = [
        pltpu.make_async_copy(ids_ref, ids, sems.at[0]),
        pltpu.make_async_copy(valid_ref, valid, sems.at[1]),
    ]
    held = [
        pltpu.make_async_copy(lik_ref.at[b], held_ref.at[b], sems.at[2 + b])
        for b in range(held_ref.shape[0])
    ]
    for copy in copies + held:
        copy.start()
    for copy in copies:
        copy.wait()
    own_rows = lax.axis_size(ALL) // NEAR * own_blocks
    lane = lax.broadcasted_iota(jnp.int32, wide.shape, 1)
    wide[...] = jnp.zeros_like(wide)
    wide[:, :slots] = jnp.where(valid[...] > 0, ids[...], -1).astype(jnp.float32)
    flat = jnp.sum(
        pltpu.roll(wide[...], 0, 1, stride=slots, stride_axis=0), axis=0, keepdims=True
    )
    flat = jnp.where(lane[:1] < read_blocks * slots, flat, -1.0)
    block = jnp.maximum(flat, 0.0)
    owner = ((block + 0.5) * (1.0 / own_blocks)).astype(jnp.int32)
    inside = block.astype(jnp.int32) - owner * own_blocks
    piece, start = far_place(owner, own_blocks)
    picked = jnp.where(flat < 0, -1, piece * near_rows(own_rows) + start + inside)
    counted = jnp.where(flat < 0, -1, piece * own_rows + start + inside)
    row = lax.broadcasted_iota(jnp.int32, info_ref.shape, 0)
    info_ref[...] = jnp.where(
        row == 0,
        flat,
        jnp.where(
            row == 1, picked.astype(jnp.float32), jnp.where(row == 2, counted.astype(jnp.float32), 0.0)
        ),
    )
    for copy in held:
        copy.wait()


def chip_kernel(mine_ref, theirs_ref, out_ref):
    first = on_core_0()
    rows = mine_ref.shape[0]
    out_ref[:rows, :] = jnp.where(first, mine_ref[...], theirs_ref[...])
    out_ref[rows:, :] = jnp.where(first, theirs_ref[...], mine_ref[...])


def half_kernel(*refs):
    refs, out_ref = refs[:-1], refs[-1]
    rows = refs[0].shape[0]
    partners = 2 if len(refs) >= 3 and refs[2].shape == refs[0].shape else 1
    first = on_core_0()
    for i in range(partners):
        out_ref[i * rows : (i + 1) * rows, :] = jnp.where(first, refs[i][...], refs[i + 1][...])
    at = partners * rows
    for ref in refs[partners + 1 :]:
        out_ref[at : at + ref.shape[0], :] = ref[...]
        at += ref.shape[0]
    if at < out_ref.shape[0]:
        out_ref[at:, :] = jnp.zeros((out_ref.shape[0] - at, out_ref.shape[1]), jnp.float32)


def far_sum(first, x, *got):
    if len(got) == 1:
        return jnp.where(first, x, got[0])
    return got[0] + jnp.where(first, x, got[1])


def near_total_kernel(mine_ref, core_ref, chip_ref, both_ref, out_ref):
    rows = mine_ref.shape[0]
    out_ref[:rows, :] = mine_ref[...] + chip_ref[...]
    out_ref[rows:, :] = core_ref[...] + both_ref[...]


def far_total_kernel(x_ref, *refs):
    got, out_ref = refs[:-1], refs[-1]
    out_ref[...] = far_sum(on_core_0(), x_ref[...], *[ref[...] for ref in got])


def cross_kernel(mine_ref, theirs_ref, out_ref):
    rows = mine_ref.shape[0] // 2
    out_ref[:rows, :] = mine_ref[:rows, :] + theirs_ref[rows:, :]
    out_ref[rows:, :] = mine_ref[rows:, :] + theirs_ref[:rows, :]


def far_last_total_kernel(x_ref, *refs):
    got, (mine_ref, theirs_ref) = refs[:-2], refs[-2:]
    total = far_sum(on_core_0(), x_ref[...], *[ref[...] for ref in got])
    rows = mine_ref.shape[0]
    mine_ref[...] = total[:rows]
    theirs_ref[...] = total[rows:]


def near_counts_kernel(r, a_ref, b_ref, c_ref, d_ref, keep_ref, *outs):
    total = (a_ref[...] + b_ref[...]) + (c_ref[...] + d_ref[...])
    send_counts(r, total, keep_ref, *outs)


def send_counts(r, total, keep_ref, *outs):
    rows = keep_ref.shape[0]
    keep_ref[...] = total[:rows]
    if r == 4:
        outs[0][...] = jnp.where(on_core_0(), total[rows:], total[:rows])
        outs[1][...] = total[rows:]


def far_counts_kernel(x_ref, *refs):
    got, (mine_ref, theirs_ref) = refs[:-2], refs[-2:]
    first = on_core_0()
    total = far_sum(first, x_ref[...], *[ref[...] for ref in got])
    rows = mine_ref.shape[0]
    mine_ref[...] = jnp.where(first, total[:rows], total[rows:])
    theirs_ref[...] = jnp.where(first, total[rows:], total[:rows])


def next_counts_kernel(r, mine_ref, theirs_ref, keep_ref, *outs):
    send_counts(r, mine_ref[...] + theirs_ref[...], keep_ref, *outs)


def row_sums(picked_ref, lik_ref, out_ref):
    read_blocks, slots, reads, cols = lik_ref.shape
    for b in range(read_blocks):
        total = None
        for s in range(0, slots, 2):
            at = b * slots + s
            left = jnp.concatenate(
                [split(picked_ref[at : at + 1, :]), split(picked_ref[at + 1 : at + 2, :])], axis=1
            )
            right = jnp.concatenate([lik_ref[b, s], lik_ref[b, s + 1]], axis=1)
            part = dot(left, right, (((1,), (1,)), ((), ())))
            total = part if total is None else total + part
        out_ref[b : b + 1, :] = jnp.sum(total, axis=0, keepdims=True)


def first_row_kernel(info_ref, *refs):
    pieces, (lik_ref, out_ref, picked_ref) = refs[:NEAR], refs[NEAR:]
    table = jnp.concatenate([piece[...] for piece in pieces], axis=0)
    hot = hot_rows(info_ref[1:2, :], table.shape[0])
    picked_ref[...] = select_rows(hot[: picked_ref.shape[0]], table)
    row_sums(picked_ref, lik_ref, out_ref)


def next_row_kernel(scale, *refs):
    parts, (lik_ref, out_ref, picked_ref) = refs[:NEAR], refs[NEAR:]
    total = parts[0][...]
    for part in parts[1:]:
        total = total + part[...]
    picked_ref[...] = total * scale
    row_sums(picked_ref, lik_ref, out_ref)


def column_sums(mine_ref, theirs_ref, picked_ref, lik_ref, contrib_ref, inverse_ref):
    read_blocks, slots, reads, cols = lik_ref.shape
    inverse_ref[...] = 1.0 / (mine_ref[...] + theirs_ref[...])
    for b in range(read_blocks):
        left = split(inverse_ref[b : b + 1, :])
        for s in range(0, slots, 2):
            at = b * slots + s
            right = jnp.concatenate([lik_ref[b, s], lik_ref[b, s + 1]], axis=1)
            summed = jnp.sum(dot(left, right), axis=0, keepdims=True)
            contrib_ref[at : at + 1, :] = picked_ref[at : at + 1, :] * summed[:, :cols]
            contrib_ref[at + 1 : at + 2, :] = picked_ref[at + 1 : at + 2, :] * summed[:, cols:]


def column_kernel(info_ref, mine_ref, theirs_ref, picked_ref, lik_ref, out_ref, inverse_ref):
    column_sums(mine_ref, theirs_ref, picked_ref, lik_ref, out_ref, inverse_ref)
    out_ref[picked_ref.shape[0] :, :] = info_ref[...]


def last_column_kernel(info_ref, mine_ref, theirs_ref, picked_ref, lik_ref, *refs):
    outs, (inverse_ref, contrib_ref) = refs[:NEAR], refs[NEAR:]
    column_sums(mine_ref, theirs_ref, picked_ref, lik_ref, contrib_ref, inverse_ref)
    rows = outs[0].shape[0]
    all_slots = contrib_ref.shape[0]
    block = lax.broadcasted_iota(jnp.int32, (NEAR * rows, all_slots), 0)
    hot = (block.astype(jnp.float32) == info_ref[2:3, :all_slots]).astype(jnp.float32)
    counts = select_rows(hot, contrib_ref[...])
    for i in range(NEAR):
        outs[i][...] = counts[i * rows : (i + 1) * rows, :]


def wanted_kernel(all_slots, r, *refs):
    given, refs = refs[: r // 2 + 1], refs[r // 2 + 1 :]
    wanted, outs = refs[:NEAR], refs[NEAR:]
    rows = all_slots + ID_ROWS
    half = LANES // 2
    first = on_core_0()
    lane = lax.broadcasted_iota(jnp.int32, (1, LANES), 1)
    ids, values = [], []
    for i in range(r // 2):
        x = jnp.where(first, given[i][...], given[i + 1][...])
        for at in range(0, x.shape[0], rows):
            ids.append(x[at + all_slots : at + all_slots + 1, :])
            values.append(x[at : at + all_slots, :])
    pairs = [
        jnp.where(lane < half, a, pltpu.roll(b, half, 1)) for a, b in zip(ids[::2], ids[1::2])
    ]
    given = terms(jnp.concatenate(values, axis=0))
    for ids_ref, out_ref in zip(wanted, outs):
        column = down(ids_ref[0:1, :])[:all_slots]
        hot = jnp.concatenate([(column == pair).astype(jnp.float32) for pair in pairs], axis=1)
        hot = hot.astype(jnp.bfloat16)
        out_ref[...] = dot(hot, given[0]) + dot(hot, given[1]) + dot(hot, given[2])


def call(kernel, outs, scratch, *operands):
    return pl.pallas_call(
        kernel,
        out_shape=[jax.ShapeDtypeStruct(shape, jnp.float32) for shape in outs],
        in_specs=[VMEM] * len(operands),
        out_specs=[VMEM] * len(outs),
        scratch_shapes=[pltpu.VMEM(shape, jnp.float32) for shape in scratch],
        compiler_params=pltpu.CompilerParams(vmem_limit_bytes=16 * 2**20),
    )(*operands)


def prepare(own_blocks, likelihood, block_ids, slot_valid):
    read_blocks, slots = block_ids.shape
    return pl.pallas_call(
        lambda *refs: prepare_kernel(own_blocks, *refs),
        out_shape=[
            pltpu.VMEM(likelihood.shape, likelihood.dtype),
            jax.ShapeDtypeStruct((ID_ROWS, LANES), jnp.float32),
        ],
        in_specs=[ANY] * 3,
        out_specs=[VMEM] * 2,
        scratch_shapes=[
            pltpu.VMEM((read_blocks, slots), jnp.int32),
            pltpu.VMEM((read_blocks, slots), jnp.int32),
            pltpu.VMEM((read_blocks, LANES), jnp.float32),
            pltpu.SemaphoreType.DMA((2 + read_blocks,)),
        ],
        compiler_params=pltpu.CompilerParams(vmem_limit_bytes=16 * 2**20),
    )(*[pltpu.with_memory_space_constraint(x, pltpu.HBM) for x in (likelihood, block_ids, slot_valid)])


def far_gather(x):
    radix = far_radices()
    stride = NEAR
    for i, r in enumerate(radix):
        (x,) = call(chip_kernel, [(2 * x.shape[0], x.shape[1])], [], x, swap(x, 1))
        got = far_swaps(x, x, r, stride)
        stride *= r
        if i + 1 < len(radix):
            (x,) = call(half_kernel, [(r // 2 * x.shape[0], x.shape[1])], [], x, *got)
    return [x] + got


def total_rows(x):
    (x,) = call(near_total_kernel, [(2 * x.shape[0], x.shape[1])], [], *near_swaps([x] * NEAR))
    radix = far_radices()
    stride = NEAR
    for i, r in enumerate(radix):
        got = far_swaps(x, x, r, stride)
        stride *= r
        if i + 1 < len(radix):
            (x,) = call(far_total_kernel, [x.shape], [], x, *got)
            (x,) = call(cross_kernel, [x.shape], [], x, swap(x, 1))
    half = (x.shape[0] // 2, x.shape[1])
    mine, theirs = call(far_last_total_kernel, [half, half], [], x, *got)
    return mine, swap(theirs, 1)


def scatter_counts(parts):
    radix = far_radices()
    stride = NEAR
    for r in radix[:-1]:
        stride *= r
    rows, cols = parts[0].shape
    operands, kernel = near_swaps(parts), near_counts_kernel
    for r, before in zip(radix[::-1], radix[-2::-1] + [0]):
        rows = rows // (r // 2)
        outs = [(rows, cols)] * (3 if r == 4 else 1)
        kept, *sent = call(lambda *refs: kernel(r, *refs), outs, [], *operands)
        sent = sent or [kept, kept]
        got = far_swaps(*sent, r, stride)
        stride //= max(before, 1)
        rows //= 2
        mine, theirs = call(far_counts_kernel, [(rows, cols)] * 2, [], kept, *got)
        operands, kernel = [mine, swap(theirs, 1)], next_counts_kernel
    return operands


def local(likelihood, block_ids, slot_valid, start_weights):
    read_blocks, slots, reads, cols = likelihood.shape
    own_weights = start_weights.reshape(-1, cols)
    own_blocks = own_weights.shape[0]
    own_rows = lax.axis_size(ALL) // NEAR * own_blocks
    all_slots = read_blocks * slots
    total_reads = read_blocks * lax.axis_size("reads") * reads
    scale = lax.axis_size(ALL) * own_blocks * cols / total_reads

    column = far_gather(own_weights)
    held, info = prepare(own_blocks, likelihood, block_ids, slot_valid)
    (sent,) = call(half_kernel, [(near_rows(own_rows), cols)], [], *column, info)
    pieces = near_swaps([sent] * NEAR)
    wanted = [info] + [piece[own_rows : own_rows + ID_ROWS] for piece in pieces[1:]]

    outs = [(read_blocks, reads), (all_slots, cols)]
    inverse = (read_blocks, reads)
    row_part, picked = call(first_row_kernel, outs, [], info, *pieces, held)
    for step in range(ITERS - 1):
        totals = total_rows(row_part)
        (contrib,) = call(
            column_kernel, [(all_slots + ID_ROWS, cols)], [inverse], info, *totals, picked, held
        )
        given = far_gather(contrib)
        sums = call(
            lambda *refs: wanted_kernel(all_slots, far_radices()[-1], *refs),
            [(all_slots, cols)] * NEAR,
            [],
            *given,
            *wanted,
        )
        row_part, picked = call(
            lambda *refs: next_row_kernel(scale, *refs), outs, [], *near_swaps(sums), held
        )
    totals = total_rows(row_part)
    counts = call(
        last_column_kernel,
        [(own_rows, cols)] * NEAR,
        [inverse, (all_slots, cols)],
        info,
        *totals,
        picked,
        held,
    )
    mine, theirs = scatter_counts(counts)
    return ((mine + theirs) * scale).reshape(-1)


def solution(mesh):
    placed = (
        P(("parts", "reads"), "genome", None, None),
        P(("parts", "reads"), "genome"),
        P(("parts", "reads"), "genome"),
        P(("parts", "genome", "reads")),
    )
    return jax.shard_map(
        local,
        mesh=mesh,
        in_specs=placed,
        out_specs=P(("parts", "genome", "reads")),
        check_vma=False,
    )
```

time: 62.5 us -> 73.3 us (1.17)
  blocking collectives: 32.2 us -> 0 us
  waiting for transfers between devices: 8.59 us -> 32.8 us
  starting transfers between devices: 14 us -> 32 us
    all_to_all x3 -> x0, blocking collectives: 32.2 us -> none  [the longest x2 21.7 us: local(): row_parts = lax.all_to_all(row_parts, 'genome', 0, 0, tiled=True)]
    ppermute x12 -> x30, waiting for transfers between devices: 8.59 us -> 32.8 us  [the longest x20 18.8 us: swap(): return lax.ppermute(x, ALL, [(i, i ^ k) for i in range(lax.axis_size(ALL))])]
    ppermute x12 -> x30, starting transfers between devices: 14 us -> 32 us  [the longest x20 24.6 us: swap(): return lax.ppermute(x, ALL, [(i, i ^ k) for i in range(lax.axis_size(ALL))])]
    pallas_call x6 -> x14, Pallas kernels: 4.5 us -> 4.54 us  [call(): pl.pallas_call(kernel, out_shape=[jax.ShapeDtypeStruct(shape, jnp.float32...]
  transfers between devices with their start and end apart: 12 -> 30, of which waited for: 7 -> 19; matrix products, arithmetic and copies ran while one was open for 0% -> 0% of each run, Pallas kernels for 4% -> 3%
where the time goes in v6:
time: 73.3 us; the launch traced here: 73 us
  waiting for transfers between devices  32.8 us (45%)
  starting transfers between devices  32 us (44%)
  Pallas kernels  6.8 us (9%)
    ppermute x20, starting transfers between devices, swap(): return lax.ppermute(x, ALL, [(i, i ^ k) for i in range(lax.axis_size(ALL))])  24.6 us
    ppermute x20, waiting for transfers between devices, swap(): return lax.ppermute(x, ALL, [(i, i ^ k) for i in range(lax.axis_size(ALL))])  18.8 us
    ppermute x5, waiting for transfers between devices, far_swaps(): got = lax.ppermute(first, ALL, pairs)  13.9 us
    pallas_call x14, Pallas kernels, call(): pl.pallas_call(kernel, out_shape=[jax.ShapeDtypeStruct(shape, jnp.float32...  4.54 us
    ppermute x5, starting transfers between devices, far_swaps(): got = lax.ppermute(first, ALL, pairs)  4.12 us
    ppermute x5, starting transfers between devices, far_swaps(): return [got, lax.ppermute(second, ALL, pairs)]  3.29 us
    pallas_call x1, Pallas kernels, prepare(): pl.pallas_call(lambda *refs: prepare_kernel(own_blocks, *refs), out_shape...  2.26 us
  transfers between devices with their start and end apart: 30, of which 19 were waited for; matrix products, arithmetic and copies ran while one was open for 0% of the time, Pallas kernels for 3%

profile of v6, /device:TPU:0, one launch (start us, length us, event | category | flops | bytes accessed | tf_op | source)
XLA Modules:
  0.0 73.0 jit_solution(15621287187410989502)
XLA Ops:
  2.9 3.0 %collective-permute-start.1 = (f32[24,128]{1,0:T(8,128)S(1)}, f32[24,128]{1,0:T(8,128)S(1)}, u32[]{:S(2)}, u32[]{:S(2)}) collective-permute-start(f32[24,128]{1,0:T(8,128)S(1)} %shard_map.47.refs_0_), channel_id=1, source_target_pairs={{0,4},{1,9},{2,6},{3,11},{4,0},{5,13},{6,2},{7,15},{8,12},{9,1},{1... | collective-permute-start | bytes 36872 | tf_op jit(solution)/shard_map/ppermute | solution.py:45
  5.8 2.3 %shard_map.46 = (bf16[8,8,256,128]{3,2,1,0:T(8,128)(2,1)S(1)}, f32[8,128]{1,0:T(8,128)S(1)}) custom-call(bf16[8,8,256,128]{3,2,1,0:T(8,128)(2,1)} %refs_0_.1, s32[8,8]{1,0:T(8,128)} %refs_1_.1, s32[8,8]{1,0:T(8,128)} %refs_2_.1), custom_call_target="tpu_custom_call" | custom-call | tf_op jit(solution)/shard_map/pallas_call | solution.py:336
  8.1 5.4 %collective-permute-start.5 = (f32[64,128]{1,0:T(8,128)S(1)}, f32[64,128]{1,0:T(8,128)S(1)}, u32[]{:S(2)}, u32[]{:S(2)}) collective-permute-start(f32[64,128]{1,0:T(8,128)S(1)} %shard_map.48.refs_0_), channel_id=1, source_target_pairs={{0,3},{1,2},{2,1},{3,0},{4,7},{5,6},{6,5},{7,4},{8,11},{9,10},{10,... | collective-permute-start | bytes 98312 | tf_op jit(solution)/shard_map/ppermute | solution.py:28
  14.1 1.1 %collective-permute-done.5.refs_3_ = f32[64,128]{1,0:T(8,128)S(1)} collective-permute-done((f32[64,128]{1,0:T(8,128)S(1)}, f32[64,128]{1,0:T(8,128)S(1)}, u32[]{:S(2)}, u32[]{:S(2)}) %collective-permute-start.5) | collective-permute-done | bytes 32800 | tf_op jit(solution)/shard_map/ppermute | solution.py:28
  15.2 2.3 %collective-permute-done.4.refs_2_ = f32[64,128]{1,0:T(8,128)S(1)} collective-permute-done((f32[64,128]{1,0:T(8,128)S(1)}, f32[64,128]{1,0:T(8,128)S(1)}, u32[]{:S(2)}, u32[]{:S(2)}) %collective-permute-start.4) | collective-permute-done | bytes 32800 | tf_op jit(solution)/shard_map/ppermute | solution.py:28
  17.5 1.4 %shard_map.49 = (f32[8,256]{1,0:T(8,128)S(1)}, f32[64,128]{1,0:T(8,128)S(1)}) custom-call(f32[8,128]{1,0:T(8,128)S(1)} %get-tuple-element.28.refs_3_.info_ref, f32[64,128]{1,0:T(8,128)S(1)} %shard_map.48.refs_0_, f32[64,128]{1,0:T(8,128)S(1)} %collective-permute-done.3.refs_1_, f32[64,128]{1,0:T(8,128)S(1)} %collective-permute-done.4.refs_2_, ...), custom_call_target="tpu_custom_call" | custom-call | tf_op jit(solution)/shard_map/pallas_call | solution.py:324
  19.5 1.3 %collective-permute-start.6 = (f32[8,256]{1,0:T(8,128)S(1)}, f32[8,256]{1,0:T(8,128)S(1)}, u32[]{:S(2)}, u32[]{:S(2)}) collective-permute-start(f32[8,256]{1,0:T(8,128)S(1)} %get-tuple-element.30.mine_ref), channel_id=1, source_target_pairs={{0,1},{1,0},{2,3},{3,2},{4,5},{5,4},{6,7},{7,6},{8,9},{9,8},{10,11... | collective-permute-start | bytes 24584 | tf_op jit(solution)/shard_map/ppermute | solution.py:28
  20.8 1.2 %collective-permute-done.8.both_ref = f32[8,256]{1,0:T(8,128)S(1)} collective-permute-done((f32[8,256]{1,0:T(8,128)S(1)}, f32[8,256]{1,0:T(8,128)S(1)}, u32[]{:S(2)}, u32[]{:S(2)}) %collective-permute-start.8) | collective-permute-done | bytes 8224 | tf_op jit(solution)/shard_map/ppermute | solution.py:28
  23.4 3.7 %collective-permute-done.9.refs_0_ = f32[16,256]{1,0:T(8,128)S(1)} collective-permute-done((f32[16,256]{1,0:T(8,128)S(1)}, f32[16,256]{1,0:T(8,128)S(1)}, u32[]{:S(2)}, u32[]{:S(2)}) %collective-permute-start.9) | collective-permute-done | bytes 16416 | tf_op jit(solution)/shard_map/ppermute | solution.py:45
  27.1 1.5 %collective-permute-start.11 = (f32[8,256]{1,0:T(8,128)S(1)}, f32[8,256]{1,0:T(8,128)S(1)}, u32[]{:S(2)}, u32[]{:S(2)}) collective-permute-start(f32[8,256]{1,0:T(8,128)S(1)} %get-tuple-element.32), channel_id=1, source_target_pairs={{0,1},{1,0},{2,3},{3,2},{4,5},{5,4},{6,7},{7,6},{8,9},{9,8},{10,11... | collective-permute-start | bytes 24584 | tf_op jit(solution)/shard_map/ppermute | solution.py:28
  33.0 3.5 %collective-permute-done.13.refs_1_ = f32[144,128]{1,0:T(8,128)S(1)} collective-permute-done((f32[144,128]{1,0:T(8,128)S(1)}, f32[144,128]{1,0:T(8,128)S(1)}, u32[]{:S(2)}, u32[]{:S(2)}) %collective-permute-start.13) | collective-permute-done | bytes 73760 | tf_op jit(solution)/shard_map/ppermute | solution.py:45
  36.8 3.8 %collective-permute-start.15 = (f32[64,128]{1,0:T(8,128)S(1)}, f32[64,128]{1,0:T(8,128)S(1)}, u32[]{:S(2)}, u32[]{:S(2)}) collective-permute-start(f32[64,128]{1,0:T(8,128)S(1)} %get-tuple-element.35), channel_id=1, source_target_pairs={{0,1},{1,0},{2,3},{3,2},{4,5},{5,4},{6,7},{7,6},{8,9},{9,8},{10,11... | collective-permute-start | bytes 98312 | tf_op jit(solution)/shard_map/ppermute | solution.py:28
  40.6 1.5 %collective-permute-start.16 = (f32[64,128]{1,0:T(8,128)S(1)}, f32[64,128]{1,0:T(8,128)S(1)}, u32[]{:S(2)}, u32[]{:S(2)}) collective-permute-start(f32[64,128]{1,0:T(8,128)S(1)} %get-tuple-element.36), channel_id=1, source_target_pairs={{0,2},{1,3},{2,0},{3,1},{4,6},{5,7},{6,4},{7,5},{8,10},{9,11},{10,... | collective-permute-start | bytes 98312 | tf_op jit(solution)/shard_map/ppermute | solution.py:28
  42.1 2.4 %collective-permute-done.16.refs_2_ = f32[64,128]{1,0:T(8,128)S(1)} collective-permute-done((f32[64,128]{1,0:T(8,128)S(1)}, f32[64,128]{1,0:T(8,128)S(1)}, u32[]{:S(2)}, u32[]{:S(2)}) %collective-permute-start.16) | collective-permute-done | bytes 32800 | tf_op jit(solution)/shard_map/ppermute | solution.py:28
  44.5 1.2 %collective-permute-done.17.refs_3_ = f32[64,128]{1,0:T(8,128)S(1)} collective-permute-done((f32[64,128]{1,0:T(8,128)S(1)}, f32[64,128]{1,0:T(8,128)S(1)}, u32[]{:S(2)}, u32[]{:S(2)}) %collective-permute-start.17) | collective-permute-done | bytes 32800 | tf_op jit(solution)/shard_map/ppermute | solution.py:28
  45.7 1.2 %shard_map.55 = (f32[8,256]{1,0:T(8,128)S(1)}, f32[64,128]{1,0:T(8,128)S(1)}) custom-call(f32[64,128]{1,0:T(8,128)S(1)} %get-tuple-element.34.refs_0_, f32[64,128]{1,0:T(8,128)S(1)} %collective-permute-done.15.refs_1_, f32[64,128]{1,0:T(8,128)S(1)} %collective-permute-done.16.refs_2_, f32[64,128]{1,0:T(8,128)S(1)} %collective-permute-done.17.refs_3_, ...), custom_call_target="tpu_custom_call" | custom-call | tf_op jit(solution)/shard_map/pallas_call | solution.py:324
  47.4 1.3 %collective-permute-start.19 = (f32[8,256]{1,0:T(8,128)S(1)}, f32[8,256]{1,0:T(8,128)S(1)}, u32[]{:S(2)}, u32[]{:S(2)}) collective-permute-start(f32[8,256]{1,0:T(8,128)S(1)} %get-tuple-element.38.mine_ref), channel_id=1, source_target_pairs={{0,2},{1,3},{2,0},{3,1},{4,6},{5,7},{6,4},{7,5},{8,10},{9,11},{10,... | collective-permute-start | bytes 24584 | tf_op jit(solution)/shard_map/ppermute | solution.py:28
  48.9 1.2 %collective-permute-done.20.both_ref = f32[8,256]{1,0:T(8,128)S(1)} collective-permute-done((f32[8,256]{1,0:T(8,128)S(1)}, f32[8,256]{1,0:T(8,128)S(1)}, u32[]{:S(2)}, u32[]{:S(2)}) %collective-permute-start.20) | collective-permute-done | bytes 8224 | tf_op jit(solution)/shard_map/ppermute | solution.py:28
  51.8 3.7 %collective-permute-done.21.refs_0_ = f32[16,256]{1,0:T(8,128)S(1)} collective-permute-done((f32[16,256]{1,0:T(8,128)S(1)}, f32[16,256]{1,0:T(8,128)S(1)}, u32[]{:S(2)}, u32[]{:S(2)}) %collective-permute-start.21) | collective-permute-done | bytes 16416 | tf_op jit(solution)/shard_map/ppermute | solution.py:45
  55.5 2.5 %collective-permute-start.23 = (f32[8,256]{1,0:T(8,128)S(1)}, f32[8,256]{1,0:T(8,128)S(1)}, u32[]{:S(2)}, u32[]{:S(2)}) collective-permute-start(f32[8,256]{1,0:T(8,128)S(1)} %get-tuple-element.40), channel_id=1, source_target_pairs={{0,1},{1,0},{2,3},{3,2},{4,5},{5,4},{6,7},{7,6},{8,9},{9,8},{10,11... | collective-permute-start | bytes 24584 | tf_op jit(solution)/shard_map/ppermute | solution.py:28
  60.2 1.4 %collective-permute-start.25 = (f32[48,128]{1,0:T(8,128)S(1)}, f32[48,128]{1,0:T(8,128)S(1)}, u32[]{:S(2)}, u32[]{:S(2)}) collective-permute-start(f32[48,128]{1,0:T(8,128)S(1)} %get-tuple-element.44), channel_id=1, source_target_pairs={{0,2},{1,3},{2,0},{3,1},{4,6},{5,7},{6,4},{7,5},{8,10},{9,11},{10,... | collective-permute-start | bytes 73736 | tf_op jit(solution)/shard_map/ppermute | solution.py:28
  61.7 2.3 %collective-permute-done.25.refs_2_ = f32[48,128]{1,0:T(8,128)S(1)} collective-permute-done((f32[48,128]{1,0:T(8,128)S(1)}, f32[48,128]{1,0:T(8,128)S(1)}, u32[]{:S(2)}, u32[]{:S(2)}) %collective-permute-start.25) | collective-permute-done | bytes 24608 | tf_op jit(solution)/shard_map/ppermute | solution.py:28
  65.8 3.0 %collective-permute-done.27.refs_0_ = f32[24,128]{1,0:T(8,128)S(1)} collective-permute-done((f32[24,128]{1,0:T(8,128)S(1)}, f32[24,128]{1,0:T(8,128)S(1)}, u32[]{:S(2)}, u32[]{:S(2)}) %collective-permute-start.27) | collective-permute-done | bytes 12320 | tf_op jit(solution)/shard_map/ppermute | solution.py:45
  68.8 2.8 %collective-permute-start.29 = (f32[12,128]{1,0:T(8,128)S(1)}, f32[12,128]{1,0:T(8,128)S(1)}, u32[]{:S(2)}, u32[]{:S(2)}) collective-permute-start(f32[12,128]{1,0:T(8,128)S(1)} %get-tuple-element.50), channel_id=1, source_target_pairs={{0,1},{1,0},{2,3},{3,2},{4,5},{5,4},{6,7},{7,6},{8,9},{9,8},{10,11... | collective-permute-start | bytes 18440 | tf_op jit(solution)/shard_map/ppermute | solution.py:28
  (57 shorter events, 17.9 us)
Async XLA Ops:
  2.2 5.9 %collective-permute-start.2 = (f32[24,128]{1,0:T(8,128)S(1)}, f32[24,128]{1,0:T(8,128)S(1)}, u32[]{:S(2)}, u32[]{:S(2)}) collective-permute-start(f32[24,128]{1,0:T(8,128)S(1)} %shard_map.47.refs_0_), channel_id=1, source_target_pairs={{1,13},{3,15},{5,9},{7,11},{9,5},{11,7},{13,1},{15,3},{17,29},{19,... | collective-permute-start | bytes 36872 | tf_op jit(solution)/shard_map/ppermute | solution.py:47
  2.9 5.3 %collective-permute-start.1 = (f32[24,128]{1,0:T(8,128)S(1)}, f32[24,128]{1,0:T(8,128)S(1)}, u32[]{:S(2)}, u32[]{:S(2)}) collective-permute-start(f32[24,128]{1,0:T(8,128)S(1)} %shard_map.47.refs_0_), channel_id=1, source_target_pairs={{0,4},{1,9},{2,6},{3,11},{4,0},{5,13},{6,2},{7,15},{8,12},{9,1},{1... | collective-permute-start | bytes 36872 | tf_op jit(solution)/shard_map/ppermute | solution.py:45
  8.1 7.0 %collective-permute-start.5 = (f32[64,128]{1,0:T(8,128)S(1)}, f32[64,128]{1,0:T(8,128)S(1)}, u32[]{:S(2)}, u32[]{:S(2)}) collective-permute-start(f32[64,128]{1,0:T(8,128)S(1)} %shard_map.48.refs_0_), channel_id=1, source_target_pairs={{0,3},{1,2},{2,1},{3,0},{4,7},{5,6},{6,5},{7,4},{8,11},{9,10},{10,... | collective-permute-start | bytes 98312 | tf_op jit(solution)/shard_map/ppermute | solution.py:28
  13.6 3.9 %collective-permute-start.4 = (f32[64,128]{1,0:T(8,128)S(1)}, f32[64,128]{1,0:T(8,128)S(1)}, u32[]{:S(2)}, u32[]{:S(2)}) collective-permute-start(f32[64,128]{1,0:T(8,128)S(1)} %shard_map.48.refs_0_), channel_id=1, source_target_pairs={{0,2},{1,3},{2,0},{3,1},{4,6},{5,7},{6,4},{7,5},{8,10},{9,11},{10,... | collective-permute-start | bytes 98312 | tf_op jit(solution)/shard_map/ppermute | solution.py:28
  14.1 3.4 %collective-permute-start.3 = (f32[64,128]{1,0:T(8,128)S(1)}, f32[64,128]{1,0:T(8,128)S(1)}, u32[]{:S(2)}, u32[]{:S(2)}) collective-permute-start(f32[64,128]{1,0:T(8,128)S(1)} %shard_map.48.refs_0_), channel_id=1, source_target_pairs={{0,1},{1,0},{2,3},{3,2},{4,5},{5,4},{6,7},{7,6},{8,9},{9,8},{10,11... | collective-permute-start | bytes 98312 | tf_op jit(solution)/shard_map/ppermute | solution.py:28
  18.9 3.1 %collective-permute-start.8 = (f32[8,256]{1,0:T(8,128)S(1)}, f32[8,256]{1,0:T(8,128)S(1)}, u32[]{:S(2)}, u32[]{:S(2)}) collective-permute-start(f32[8,256]{1,0:T(8,128)S(1)} %get-tuple-element.30.mine_ref), channel_id=1, source_target_pairs={{0,3},{1,2},{2,1},{3,0},{4,7},{5,6},{6,5},{7,4},{8,11},{9,10},{10,... | collective-permute-start | bytes 24584 | tf_op jit(solution)/shard_map/ppermute | solution.py:28
  18.9 3.7 %collective-permute-start.7 = (f32[8,256]{1,0:T(8,128)S(1)}, f32[8,256]{1,0:T(8,128)S(1)}, u32[]{:S(2)}, u32[]{:S(2)}) collective-permute-start(f32[8,256]{1,0:T(8,128)S(1)} %get-tuple-element.30.mine_ref), channel_id=1, source_target_pairs={{0,2},{1,3},{2,0},{3,1},{4,6},{5,7},{6,4},{7,5},{8,10},{9,11},{10,... | collective-permute-start | bytes 24584 | tf_op jit(solution)/shard_map/ppermute | solution.py:28
  19.5 3.1 %collective-permute-start.6 = (f32[8,256]{1,0:T(8,128)S(1)}, f32[8,256]{1,0:T(8,128)S(1)}, u32[]{:S(2)}, u32[]{:S(2)}) collective-permute-start(f32[8,256]{1,0:T(8,128)S(1)} %get-tuple-element.30.mine_ref), channel_id=1, source_target_pairs={{0,1},{1,0},{2,3},{3,2},{4,5},{5,4},{6,7},{7,6},{8,9},{9,8},{10,11... | collective-permute-start | bytes 24584 | tf_op jit(solution)/shard_map/ppermute | solution.py:28
  23.3 3.8 %collective-permute-start.9 = (f32[16,256]{1,0:T(8,128)S(1)}, f32[16,256]{1,0:T(8,128)S(1)}, u32[]{:S(2)}, u32[]{:S(2)}) collective-permute-start(f32[16,256]{1,0:T(8,128)S(1)} %shard_map.50.x_ref), channel_id=1, source_target_pairs={{0,4},{1,9},{2,6},{3,11},{4,0},{5,13},{6,2},{7,15},{8,12},{9,1},{1... | collective-permute-start | bytes 49160 | tf_op jit(solution)/shard_map/ppermute | solution.py:45
  27.1 2.3 %collective-permute-start.11 = (f32[8,256]{1,0:T(8,128)S(1)}, f32[8,256]{1,0:T(8,128)S(1)}, u32[]{:S(2)}, u32[]{:S(2)}) collective-permute-start(f32[8,256]{1,0:T(8,128)S(1)} %get-tuple-element.32), channel_id=1, source_target_pairs={{0,1},{1,0},{2,3},{3,2},{4,5},{5,4},{6,7},{7,6},{8,9},{9,8},{10,11... | collective-permute-start | bytes 24584 | tf_op jit(solution)/shard_map/ppermute | solution.py:28
  32.1 4.4 %collective-permute-start.13 = (f32[144,128]{1,0:T(8,128)S(1)}, f32[144,128]{1,0:T(8,128)S(1)}, u32[]{:S(2)}, u32[]{:S(2)}) collective-permute-start(f32[144,128]{1,0:T(8,128)S(1)} %shard_map.53.refs_0_), channel_id=1, source_target_pairs={{0,4},{1,9},{2,6},{3,11},{4,0},{5,13},{6,2},{7,15},{8,12},{9,1},{1... | collective-permute-start | bytes 221192 | tf_op jit(solution)/shard_map/ppermute | solution.py:45
  36.8 5.3 %collective-permute-start.15 = (f32[64,128]{1,0:T(8,128)S(1)}, f32[64,128]{1,0:T(8,128)S(1)}, u32[]{:S(2)}, u32[]{:S(2)}) collective-permute-start(f32[64,128]{1,0:T(8,128)S(1)} %get-tuple-element.35), channel_id=1, source_target_pairs={{0,1},{1,0},{2,3},{3,2},{4,5},{5,4},{6,7},{7,6},{8,9},{9,8},{10,11... | collective-permute-start | bytes 98312 | tf_op jit(solution)/shard_map/ppermute | solution.py:28
  40.6 3.9 %collective-permute-start.16 = (f32[64,128]{1,0:T(8,128)S(1)}, f32[64,128]{1,0:T(8,128)S(1)}, u32[]{:S(2)}, u32[]{:S(2)}) collective-permute-start(f32[64,128]{1,0:T(8,128)S(1)} %get-tuple-element.36), channel_id=1, source_target_pairs={{0,2},{1,3},{2,0},{3,1},{4,6},{5,7},{6,4},{7,5},{8,10},{9,11},{10,... | collective-permute-start | bytes 98312 | tf_op jit(solution)/shard_map/ppermute | solution.py:28
  42.1 3.7 %collective-permute-start.17 = (f32[64,128]{1,0:T(8,128)S(1)}, f32[64,128]{1,0:T(8,128)S(1)}, u32[]{:S(2)}, u32[]{:S(2)}) collective-permute-start(f32[64,128]{1,0:T(8,128)S(1)} %get-tuple-element.37), channel_id=1, source_target_pairs={{0,3},{1,2},{2,1},{3,0},{4,7},{5,6},{6,5},{7,4},{8,11},{9,10},{10,... | collective-permute-start | bytes 98312 | tf_op jit(solution)/shard_map/ppermute | solution.py:28
  47.0 3.1 %collective-permute-start.20 = (f32[8,256]{1,0:T(8,128)S(1)}, f32[8,256]{1,0:T(8,128)S(1)}, u32[]{:S(2)}, u32[]{:S(2)}) collective-permute-start(f32[8,256]{1,0:T(8,128)S(1)} %get-tuple-element.38.mine_ref), channel_id=1, source_target_pairs={{0,3},{1,2},{2,1},{3,0},{4,7},{5,6},{6,5},{7,4},{8,11},{9,10},{10,... | collective-permute-start | bytes 24584 | tf_op jit(solution)/shard_map/ppermute | solution.py:28
  47.4 3.7 %collective-permute-start.19 = (f32[8,256]{1,0:T(8,128)S(1)}, f32[8,256]{1,0:T(8,128)S(1)}, u32[]{:S(2)}, u32[]{:S(2)}) collective-permute-start(f32[8,256]{1,0:T(8,128)S(1)} %get-tuple-element.38.mine_ref), channel_id=1, source_target_pairs={{0,2},{1,3},{2,0},{3,1},{4,6},{5,7},{6,4},{7,5},{8,10},{9,11},{10,... | collective-permute-start | bytes 24584 | tf_op jit(solution)/shard_map/ppermute | solution.py:28
  48.7 2.3 %collective-permute-start.18 = (f32[8,256]{1,0:T(8,128)S(1)}, f32[8,256]{1,0:T(8,128)S(1)}, u32[]{:S(2)}, u32[]{:S(2)}) collective-permute-start(f32[8,256]{1,0:T(8,128)S(1)} %get-tuple-element.38.mine_ref), channel_id=1, source_target_pairs={{0,1},{1,0},{2,3},{3,2},{4,5},{5,4},{6,7},{7,6},{8,9},{9,8},{10,11... | collective-permute-start | bytes 24584 | tf_op jit(solution)/shard_map/ppermute | solution.py:28
  51.7 3.8 %collective-permute-start.21 = (f32[16,256]{1,0:T(8,128)S(1)}, f32[16,256]{1,0:T(8,128)S(1)}, u32[]{:S(2)}, u32[]{:S(2)}) collective-permute-start(f32[16,256]{1,0:T(8,128)S(1)} %shard_map.56.x_ref), channel_id=1, source_target_pairs={{0,4},{1,9},{2,6},{3,11},{4,0},{5,13},{6,2},{7,15},{8,12},{9,1},{1... | collective-permute-start | bytes 49160 | tf_op jit(solution)/shard_map/ppermute | solution.py:45
  55.5 3.3 %collective-permute-start.23 = (f32[8,256]{1,0:T(8,128)S(1)}, f32[8,256]{1,0:T(8,128)S(1)}, u32[]{:S(2)}, u32[]{:S(2)}) collective-permute-start(f32[8,256]{1,0:T(8,128)S(1)} %get-tuple-element.40), channel_id=1, source_target_pairs={{0,1},{1,0},{2,3},{3,2},{4,5},{5,4},{6,7},{7,6},{8,9},{9,8},{10,11... | collective-permute-start | bytes 24584 | tf_op jit(solution)/shard_map/ppermute | solution.py:28
  60.2 3.8 %collective-permute-start.25 = (f32[48,128]{1,0:T(8,128)S(1)}, f32[48,128]{1,0:T(8,128)S(1)}, u32[]{:S(2)}, u32[]{:S(2)}) collective-permute-start(f32[48,128]{1,0:T(8,128)S(1)} %get-tuple-element.44), channel_id=1, source_target_pairs={{0,2},{1,3},{2,0},{3,1},{4,6},{5,7},{6,4},{7,5},{8,10},{9,11},{10,... | collective-permute-start | bytes 73736 | tf_op jit(solution)/shard_map/ppermute | solution.py:28
  61.6 3.4 %collective-permute-start.26 = (f32[48,128]{1,0:T(8,128)S(1)}, f32[48,128]{1,0:T(8,128)S(1)}, u32[]{:S(2)}, u32[]{:S(2)}) collective-permute-start(f32[48,128]{1,0:T(8,128)S(1)} %get-tuple-element.45), channel_id=1, source_target_pairs={{0,3},{1,2},{2,1},{3,0},{4,7},{5,6},{6,5},{7,4},{8,11},{9,10},{10,... | collective-permute-start | bytes 73736 | tf_op jit(solution)/shard_map/ppermute | solution.py:28
  65.0 3.8 %collective-permute-start.27 = (f32[24,128]{1,0:T(8,128)S(1)}, f32[24,128]{1,0:T(8,128)S(1)}, u32[]{:S(2)}, u32[]{:S(2)}) collective-permute-start(f32[24,128]{1,0:T(8,128)S(1)} %get-tuple-element.47), channel_id=1, source_target_pairs={{0,4},{1,9},{2,6},{3,11},{4,0},{5,13},{6,2},{7,15},{8,12},{9,1},{1... | collective-permute-start | bytes 36872 | tf_op jit(solution)/shard_map/ppermute | solution.py:45
  65.1 3.7 %collective-permute-start.28 = (f32[24,128]{1,0:T(8,128)S(1)}, f32[24,128]{1,0:T(8,128)S(1)}, u32[]{:S(2)}, u32[]{:S(2)}) collective-permute-start(f32[24,128]{1,0:T(8,128)S(1)} %get-tuple-element.48), channel_id=1, source_target_pairs={{1,13},{3,15},{5,9},{7,11},{9,5},{11,7},{13,1},{15,3},{17,29},{19,... | collective-permute-start | bytes 36872 | tf_op jit(solution)/shard_map/ppermute | solution.py:47
  68.8 3.6 %collective-permute-start.29 = (f32[12,128]{1,0:T(8,128)S(1)}, f32[12,128]{1,0:T(8,128)S(1)}, u32[]{:S(2)}, u32[]{:S(2)}) collective-permute-start(f32[12,128]{1,0:T(8,128)S(1)} %get-tuple-element.50), channel_id=1, source_target_pairs={{0,1},{1,0},{2,3},{3,2},{4,5},{5,4},{6,7},{7,6},{8,9},{9,8},{10,11... | collective-permute-start | bytes 18440 | tf_op jit(solution)/shard_map/ppermute | solution.py:28
  (7 other events, 8.5 us)

commit v7 on v5

--- a/solution.py
+++ b/solution.py
@@ -26,6 +26,10 @@
 def swap(x, axes, k):
     n = lax.axis_size(axes)
     return lax.ppermute(x, axes, [(i, i ^ k) for i in range(n)])
+
+
+def middle_first(n, k):
+    return [i ^ k for i in range(n)]
 
 
 def position(k, n):
@@ -195,15 +199,15 @@
     out_ref[picked_ref.shape[0] :, :] = info_ref[...]
 
 
-def last_column_kernel(info_ref, parts_ref, picked_ref, lik_ref, out_ref, inverse_ref, contrib_ref):
+def last_column_kernel(order, info_ref, parts_ref, picked_ref, lik_ref, out_ref, inverse_ref, contrib_ref):
     column_sums(parts_ref, picked_ref, lik_ref, contrib_ref, inverse_ref)
     owners, own_blocks, cols = out_ref.shape
     all_slots = contrib_ref.shape[0]
     block = lax.broadcasted_iota(jnp.int32, (owners * own_blocks, all_slots), 0)
     hot = (block.astype(jnp.float32) == info_ref[0:1, :all_slots]).astype(jnp.float32)
     counts = select_rows(hot, contrib_ref[...])
-    for i in range(owners):
-        out_ref[i] = counts[i * own_blocks : (i + 1) * own_blocks, :]
+    for i, owner in enumerate(order):
+        out_ref[i] = counts[owner * own_blocks : (owner + 1) * own_blocks, :]
 
 
 def wanted_kernel(near, all_slots, pieces, *refs):
@@ -288,7 +292,14 @@
             row_parts, picked = call(
                 lambda *refs: next_row_kernel(near, scale, *refs), row_shapes, [], *parts, held
             )
-        row_parts = lax.all_to_all(row_parts, "genome", 0, 0, tiled=True)
+        row_parts = lax.all_to_all(
+            row_parts,
+            "genome",
+            0,
+            0,
+            tiled=True,
+            axis_index_groups=[middle_first(chips, chips // 2)],
+        )
         if step + 1 < ITERS:
             (contrib,) = call(
                 column_kernel,
@@ -308,8 +319,9 @@
                 *wanted,
             )
             parts = [sums[0]] + [swap(sums[j], ALL, j) for j in range(1, near)]
+    order = middle_first(n, n // 2 + 1)
     (counts,) = call(
-        last_column_kernel,
+        lambda *refs: last_column_kernel(order, *refs),
         [(n, own_blocks, cols)],
         [inverse, (all_slots, cols)],
         info,
@@ -317,7 +329,7 @@
         picked,
         held,
     )
-    counts = lax.all_to_all(counts, ALL, 0, 0, tiled=True)
+    counts = lax.all_to_all(counts, ALL, 0, 0, tiled=True, axis_index_groups=[order])
     return (jnp.sum(counts, axis=0) * scale).reshape(-1)
 
 

time: 62.5 us -> 58.9 us (0.942)
  blocking collectives: 32.2 us -> 28.1 us
    all_to_all x3, blocking collectives: 32.2 us -> 28.1 us  [the longest x2 18.7 us: local(): lax.all_to_all(row_parts, 'genome', 0, 0, tiled=True, axis_index_groups=[...]
  transfers between devices with their start and end apart: 12 -> 12, of which waited for: 7 -> 6; matrix products, arithmetic and copies ran while one was open for 0% -> 0% of each run, Pallas kernels for 4% -> 4%
where the time goes in v7:
time: 58.9 us; the launch traced here: 58.6 us
  blocking collectives  28.1 us (48%)
  starting transfers between devices  14 us (24%)
  waiting for transfers between devices  9.08 us (15%)
  Pallas kernels  6.76 us (11%)
  other arithmetic  0.62 us (1%)
    all_to_all x2, blocking collectives, local(): lax.all_to_all(row_parts, 'genome', 0, 0, tiled=True, axis_index_groups=[...  18.7 us
    ppermute x12, starting transfers between devices, swap(): return lax.ppermute(x, axes, [(i, i ^ k) for i in range(n)])  14 us
    all_to_all x1, blocking collectives, local(): lax.all_to_all(counts, ALL, 0, 0, tiled=True, axis_index_groups=[order])  9.36 us
    ppermute x12, waiting for transfers between devices, swap(): return lax.ppermute(x, axes, [(i, i ^ k) for i in range(n)])  9.08 us
    pallas_call x6, Pallas kernels, call(): pl.pallas_call(kernel, out_shape=[jax.ShapeDtypeStruct(shape, jnp.float32...  4.5 us
    pallas_call x1, Pallas kernels, prepare(): pl.pallas_call(lambda *refs: prepare_kernel(own_blocks, *refs), out_shape...  2.26 us
  transfers between devices with their start and end apart: 12, of which 6 were waited for; matrix products, arithmetic and copies ran while one was open for 0% of the time, Pallas kernels for 4%

profile of v7, /device:TPU:0, one launch (start us, length us, event | category | flops | bytes accessed | tf_op | source)
XLA Modules:
  0.0 58.6 jit_solution(5236663932075899943)
XLA Ops:
  0.0 5.0 %collective-permute-start.2 = (f32[12,128]{1,0:T(8,128)}, f32[12,128]{1,0:T(8,128)S(1)}, u32[]{:S(2)}, u32[]{:S(2)}) collective-permute-start(f32[12,128]{1,0:T(8,128)} %bitcast.3), channel_id=1, source_target_pairs={{0,12},{1,13},{2,14},{3,15},{4,8},{5,9},{6,10},{7,11},{8,4},{9,5},... | collective-permute-start | bytes 18440 | tf_op jit(solution)/shard_map/ppermute | solution.py:28
  5.1 0.6 %collective-permute-start = (f32[12,128]{1,0:T(8,128)}, f32[12,128]{1,0:T(8,128)S(1)}, u32[]{:S(2)}, u32[]{:S(2)}) collective-permute-start(f32[12,128]{1,0:T(8,128)} %bitcast.5), channel_id=1, source_target_pairs={{0,4},{1,5},{2,6},{3,7},{4,0},{5,1},{6,2},{7,3},{8,12},{9,13},{10,... | collective-permute-start | bytes 18440 | tf_op jit(solution)/shard_map/ppermute | solution.py:28
  5.7 2.3 %shard_map.46 = (bf16[8,8,256,128]{3,2,1,0:T(8,128)(2,1)S(1)}, f32[8,128]{1,0:T(8,128)S(1)}) custom-call(bf16[8,8,256,128]{3,2,1,0:T(8,128)(2,1)} %refs_0_.1, s32[8,8]{1,0:T(8,128)} %refs_1_.1, s32[8,8]{1,0:T(8,128)} %refs_2_.1), custom_call_target="tpu_custom_call" | custom-call | tf_op jit(solution)/shard_map/pallas_call | solution.py:247
  8.0 1.9 %collective-permute-done.1.refs_2_ = f32[12,128]{1,0:T(8,128)S(1)} collective-permute-done((f32[12,128]{1,0:T(8,128)}, f32[12,128]{1,0:T(8,128)S(1)}, u32[]{:S(2)}, u32[]{:S(2)}) %collective-permute-start.1) | collective-permute-done | bytes 6176 | tf_op jit(solution)/shard_map/ppermute | solution.py:28
  9.9 1.6 %collective-permute-start.4 = (f32[64,128]{1,0:T(8,128)S(1)}, f32[64,128]{1,0:T(8,128)S(1)}, u32[]{:S(2)}, u32[]{:S(2)}) collective-permute-start(f32[64,128]{1,0:T(8,128)S(1)} %shard_map.47.refs_1_), channel_id=1, source_target_pairs={{0,2},{1,3},{2,0},{3,1},{4,6},{5,7},{6,4},{7,5},{8,10},{9,11},{10,... | collective-permute-start | bytes 98312 | tf_op jit(solution)/shard_map/ppermute | solution.py:28
  11.5 0.3 collective-permute-start.3
  11.8 1.8 %collective-permute-done.5.refs_4_ = f32[64,128]{1,0:T(8,128)S(1)} collective-permute-done((f32[64,128]{1,0:T(8,128)S(1)}, f32[64,128]{1,0:T(8,128)S(1)}, u32[]{:S(2)}, u32[]{:S(2)}) %collective-permute-start.5) | collective-permute-done | bytes 32800 | tf_op jit(solution)/shard_map/ppermute | solution.py:28
  13.5 0.4 collective-permute-done.4.refs_3_
  13.9 1.4 %shard_map.48 = (f32[8,8,256]{2,1,0:T(8,128)S(1)}, f32[64,128]{1,0:T(8,128)S(1)}) custom-call(f32[8,128]{1,0:T(8,128)S(1)} %get-tuple-element.15.refs_4_.refs_0_.info_ref, f32[64,128]{1,0:T(8,128)S(1)} %shard_map.47.refs_1_, f32[64,128]{1,0:T(8,128)S(1)} %collective-permute-done.3.refs_2_, f32[64,128]{1,0:T(8,128)S(1)} %collective-permute-done.4.refs_3_, ...), custom_call_target="tpu_custom_call" | custom-call | tf_op jit(solution)/shard_map/pallas_call | solution.py:235
  15.3 9.5 %all_to_all.15.parts_ref = f32[8,8,256]{2,1,0:T(8,128)S(1)} all-to-all(f32[8,8,256]{2,1,0:T(8,128)S(1)} %get-tuple-element.17), channel_id=1, replica_groups={{8,10,12,14,0,2,4,6},{9,11,13,15,1,3,5,7},{24,26,28,30,16,18,20,22},{25..., dimensions={0} | all-to-all | bytes 131072 | tf_op jit(solution)/shard_map/all_to_all | solution.py:295
  24.8 0.7 %shard_map.49.refs_0_ = f32[72,128]{1,0:T(8,128)S(1)} custom-call(f32[8,128]{1,0:T(8,128)S(1)} %get-tuple-element.15.refs_4_.refs_0_.info_ref, f32[8,8,256]{2,1,0:T(8,128)S(1)} %all_to_all.15.parts_ref, f32[64,128]{1,0:T(8,128)S(1)} %get-tuple-element.18.picked_ref, bf16[8,8,256,128]{3,2,1,0:T(8,128)(2,1)S(1)} %get-tuple-element.16.refs_5_.lik_ref.refs_4_.refs_3_), custom_call_target="tpu_custom_call" | custom-call | tf_op jit(solution)/shard_map/pallas_call | solution.py:235
  25.5 2.3 %collective-permute-start.8 = (f32[72,128]{1,0:T(8,128)S(1)}, f32[72,128]{1,0:T(8,128)S(1)}, u32[]{:S(2)}, u32[]{:S(2)}) collective-permute-start(f32[72,128]{1,0:T(8,128)S(1)} %shard_map.49.refs_0_), channel_id=1, source_target_pairs={{0,12},{1,13},{2,14},{3,15},{4,8},{5,9},{6,10},{7,11},{8,4},{9,5},... | collective-permute-start | bytes 110600 | tf_op jit(solution)/shard_map/ppermute | solution.py:28
  27.8 2.1 %collective-permute-start.6 = (f32[72,128]{1,0:T(8,128)S(1)}, f32[72,128]{1,0:T(8,128)S(1)}, u32[]{:S(2)}, u32[]{:S(2)}) collective-permute-start(f32[72,128]{1,0:T(8,128)S(1)} %shard_map.49.refs_0_), channel_id=1, source_target_pairs={{0,4},{1,5},{2,6},{3,7},{4,0},{5,1},{6,2},{7,3},{8,12},{9,13},{10,... | collective-permute-start | bytes 110600 | tf_op jit(solution)/shard_map/ppermute | solution.py:28
  30.0 1.8 %collective-permute-done.8.refs_3_ = f32[72,128]{1,0:T(8,128)S(1)} collective-permute-done((f32[72,128]{1,0:T(8,128)S(1)}, f32[72,128]{1,0:T(8,128)S(1)}, u32[]{:S(2)}, u32[]{:S(2)}) %collective-permute-start.8) | collective-permute-done | bytes 36896 | tf_op jit(solution)/shard_map/ppermute | solution.py:28
  31.8 0.9 %collective-permute-done.7.refs_2_ = f32[72,128]{1,0:T(8,128)S(1)} collective-permute-done((f32[72,128]{1,0:T(8,128)S(1)}, f32[72,128]{1,0:T(8,128)S(1)}, u32[]{:S(2)}, u32[]{:S(2)}) %collective-permute-start.7) | collective-permute-done | bytes 36896 | tf_op jit(solution)/shard_map/ppermute | solution.py:28
  32.7 0.3 shard_map.50
  33.1 0.5 collective-permute-start.10
  33.6 1.4 %collective-permute-start.11 = (f32[64,128]{1,0:T(8,128)S(1)}, f32[64,128]{1,0:T(8,128)S(1)}, u32[]{:S(2)}, u32[]{:S(2)}) collective-permute-start(f32[64,128]{1,0:T(8,128)S(1)} %get-tuple-element.22), channel_id=1, source_target_pairs={{0,3},{1,2},{2,1},{3,0},{4,7},{5,6},{6,5},{7,4},{8,11},{9,10},{10,... | collective-permute-start | bytes 98312 | tf_op jit(solution)/shard_map/ppermute | solution.py:28
  35.0 2.3 %collective-permute-done.10.refs_2_ = f32[64,128]{1,0:T(8,128)S(1)} collective-permute-done((f32[64,128]{1,0:T(8,128)S(1)}, f32[64,128]{1,0:T(8,128)S(1)}, u32[]{:S(2)}, u32[]{:S(2)}) %collective-permute-start.10) | collective-permute-done | bytes 32800 | tf_op jit(solution)/shard_map/ppermute | solution.py:28
  37.3 1.2 %shard_map.51 = (f32[8,8,256]{2,1,0:T(8,128)S(1)}, f32[64,128]{1,0:T(8,128)S(1)}) custom-call(f32[64,128]{1,0:T(8,128)S(1)} %get-tuple-element.19.refs_0_, f32[64,128]{1,0:T(8,128)S(1)} %collective-permute-done.9.refs_1_, f32[64,128]{1,0:T(8,128)S(1)} %collective-permute-done.10.refs_2_, f32[64,128]{1,0:T(8,128)S(1)} %collective-permute-done.11.refs_3_, ...), custom_call_target="tpu_custom_call" | custom-call | tf_op jit(solution)/shard_map/pallas_call | solution.py:235
  38.5 9.3 %all_to_all.16.refs_1_ = f32[8,8,256]{2,1,0:T(8,128)S(1)} all-to-all(f32[8,8,256]{2,1,0:T(8,128)S(1)} %get-tuple-element.23), channel_id=1, replica_groups={{8,10,12,14,0,2,4,6},{9,11,13,15,1,3,5,7},{24,26,28,30,16,18,20,22},{25..., dimensions={0} | all-to-all | bytes 131072 | tf_op jit(solution)/shard_map/all_to_all | solution.py:295
  47.7 0.9 %shard_map.52 = f32[16,12,128]{2,1,0:T(8,128)S(1)} custom-call(f32[8,128]{1,0:T(8,128)S(1)} %get-tuple-element.15.refs_4_.refs_0_.info_ref, f32[8,8,256]{2,1,0:T(8,128)S(1)} %all_to_all.16.refs_1_, f32[64,128]{1,0:T(8,128)S(1)} %get-tuple-element.24.refs_2_, bf16[8,8,256,128]{3,2,1,0:T(8,128)(2,1)S(1)} %get-tuple-element.16.refs_5_.lik_ref.refs_4_.refs_3_), custom_call_target="tpu_custom_call" | custom-call | tf_op jit(solution)/shard_map/pallas_call | solution.py:235
  48.7 9.4 %all_to_all.17 = f32[16,12,128]{2,1,0:T(8,128)S(1)} all-to-all(f32[16,12,128]{2,1,0:T(8,128)S(1)} %shard_map.52), channel_id=1, replica_groups={{9,8,11,10,13,12,15,14,1,0,3,2,5,4,7,6},{25,24,27,26,29,28,31,30,17,16,..., dimensions={0} | all-to-all | bytes 196608 | tf_op jit(solution)/shard_map/all_to_all | solution.py:332
  58.0 0.6 %multiply_bitcast_fusion = f32[1536]{0:T(1024)} fusion(f32[12,128]{1,0:T(8,128)S(1)} %reduce_sum.9), kind=kLoop, calls=%fused_computation | loop fusion | flops 1536 | bytes 12288 | tf_op jit(solution)/shard_map/mul | solution.py:333
  (17 shorter events, 0.2 us)
Async XLA Ops:
  0.0 9.8 %copy-start = (f32[1536]{0:T(1024)S(1)}, f32[1536]{0:T(1024)}, u32[]{:S(2)}) copy-start(f32[1536]{0:T(1024)} %param.7) | copy-start | bytes 18436
  0.0 8.0 %collective-permute-start.2 = (f32[12,128]{1,0:T(8,128)}, f32[12,128]{1,0:T(8,128)S(1)}, u32[]{:S(2)}, u32[]{:S(2)}) collective-permute-start(f32[12,128]{1,0:T(8,128)} %bitcast.3), channel_id=1, source_target_pairs={{0,12},{1,13},{2,14},{3,15},{4,8},{5,9},{6,10},{7,11},{8,4},{9,5},... | collective-permute-start | bytes 18440 | tf_op jit(solution)/shard_map/ppermute | solution.py:28
  5.1 4.8 %collective-permute-start.1 = (f32[12,128]{1,0:T(8,128)}, f32[12,128]{1,0:T(8,128)S(1)}, u32[]{:S(2)}, u32[]{:S(2)}) collective-permute-start(f32[12,128]{1,0:T(8,128)} %bitcast.4), channel_id=1, source_target_pairs={{0,8},{1,9},{2,10},{3,11},{4,12},{5,13},{6,14},{7,15},{8,0},{9,1},... | collective-permute-start | bytes 18440 | tf_op jit(solution)/shard_map/ppermute | solution.py:28
  5.1 4.8 %collective-permute-start = (f32[12,128]{1,0:T(8,128)}, f32[12,128]{1,0:T(8,128)S(1)}, u32[]{:S(2)}, u32[]{:S(2)}) collective-permute-start(f32[12,128]{1,0:T(8,128)} %bitcast.5), channel_id=1, source_target_pairs={{0,4},{1,5},{2,6},{3,7},{4,0},{5,1},{6,2},{7,3},{8,12},{9,13},{10,... | collective-permute-start | bytes 18440 | tf_op jit(solution)/shard_map/ppermute | solution.py:28
  9.8 3.7 %collective-permute-start.5 = (f32[64,128]{1,0:T(8,128)S(1)}, f32[64,128]{1,0:T(8,128)S(1)}, u32[]{:S(2)}, u32[]{:S(2)}) collective-permute-start(f32[64,128]{1,0:T(8,128)S(1)} %shard_map.47.refs_1_), channel_id=1, source_target_pairs={{0,3},{1,2},{2,1},{3,0},{4,7},{5,6},{6,5},{7,4},{8,11},{9,10},{10,... | collective-permute-start | bytes 98312 | tf_op jit(solution)/shard_map/ppermute | solution.py:28
  9.9 4.0 %collective-permute-start.4 = (f32[64,128]{1,0:T(8,128)S(1)}, f32[64,128]{1,0:T(8,128)S(1)}, u32[]{:S(2)}, u32[]{:S(2)}) collective-permute-start(f32[64,128]{1,0:T(8,128)S(1)} %shard_map.47.refs_1_), channel_id=1, source_target_pairs={{0,2},{1,3},{2,0},{3,1},{4,6},{5,7},{6,4},{7,5},{8,10},{9,11},{10,... | collective-permute-start | bytes 98312 | tf_op jit(solution)/shard_map/ppermute | solution.py:28
  11.5 2.4 %collective-permute-start.3 = (f32[64,128]{1,0:T(8,128)S(1)}, f32[64,128]{1,0:T(8,128)S(1)}, u32[]{:S(2)}, u32[]{:S(2)}) collective-permute-start(f32[64,128]{1,0:T(8,128)S(1)} %shard_map.47.refs_1_), channel_id=1, source_target_pairs={{0,1},{1,0},{2,3},{3,2},{4,5},{5,4},{6,7},{7,6},{8,9},{9,8},{10,11... | collective-permute-start | bytes 98312 | tf_op jit(solution)/shard_map/ppermute | solution.py:28
  25.5 6.3 %collective-permute-start.8 = (f32[72,128]{1,0:T(8,128)S(1)}, f32[72,128]{1,0:T(8,128)S(1)}, u32[]{:S(2)}, u32[]{:S(2)}) collective-permute-start(f32[72,128]{1,0:T(8,128)S(1)} %shard_map.49.refs_0_), channel_id=1, source_target_pairs={{0,12},{1,13},{2,14},{3,15},{4,8},{5,9},{6,10},{7,11},{8,4},{9,5},... | collective-permute-start | bytes 110600 | tf_op jit(solution)/shard_map/ppermute | solution.py:28
  27.8 4.9 %collective-permute-start.7 = (f32[72,128]{1,0:T(8,128)S(1)}, f32[72,128]{1,0:T(8,128)S(1)}, u32[]{:S(2)}, u32[]{:S(2)}) collective-permute-start(f32[72,128]{1,0:T(8,128)S(1)} %shard_map.49.refs_0_), channel_id=1, source_target_pairs={{0,8},{1,9},{2,10},{3,11},{4,12},{5,13},{6,14},{7,15},{8,0},{9,1},... | collective-permute-start | bytes 110600 | tf_op jit(solution)/shard_map/ppermute | solution.py:28
  27.8 4.9 %collective-permute-start.6 = (f32[72,128]{1,0:T(8,128)S(1)}, f32[72,128]{1,0:T(8,128)S(1)}, u32[]{:S(2)}, u32[]{:S(2)}) collective-permute-start(f32[72,128]{1,0:T(8,128)S(1)} %shard_map.49.refs_0_), channel_id=1, source_target_pairs={{0,4},{1,5},{2,6},{3,7},{4,0},{5,1},{6,2},{7,3},{8,12},{9,13},{10,... | collective-permute-start | bytes 110600 | tf_op jit(solution)/shard_map/ppermute | solution.py:28
  33.0 1.9 %collective-permute-start.9 = (f32[64,128]{1,0:T(8,128)S(1)}, f32[64,128]{1,0:T(8,128)S(1)}, u32[]{:S(2)}, u32[]{:S(2)}) collective-permute-start(f32[64,128]{1,0:T(8,128)S(1)} %get-tuple-element.20), channel_id=1, source_target_pairs={{0,1},{1,0},{2,3},{3,2},{4,5},{5,4},{6,7},{7,6},{8,9},{9,8},{10,11... | collective-permute-start | bytes 98312 | tf_op jit(solution)/shard_map/ppermute | solution.py:28
  33.1 4.2 %collective-permute-start.10 = (f32[64,128]{1,0:T(8,128)S(1)}, f32[64,128]{1,0:T(8,128)S(1)}, u32[]{:S(2)}, u32[]{:S(2)}) collective-permute-start(f32[64,128]{1,0:T(8,128)S(1)} %get-tuple-element.21), channel_id=1, source_target_pairs={{0,2},{1,3},{2,0},{3,1},{4,6},{5,7},{6,4},{7,5},{8,10},{9,11},{10,... | collective-permute-start | bytes 98312 | tf_op jit(solution)/shard_map/ppermute | solution.py:28
  33.6 3.7 %collective-permute-start.11 = (f32[64,128]{1,0:T(8,128)S(1)}, f32[64,128]{1,0:T(8,128)S(1)}, u32[]{:S(2)}, u32[]{:S(2)}) collective-permute-start(f32[64,128]{1,0:T(8,128)S(1)} %get-tuple-element.22), channel_id=1, source_target_pairs={{0,3},{1,2},{2,1},{3,0},{4,7},{5,6},{6,5},{7,4},{8,11},{9,10},{10,... | collective-permute-start | bytes 98312 | tf_op jit(solution)/shard_map/ppermute | solution.py:28

commit v8 on v7

--- a/solution.py
+++ b/solution.py
@@ -298,7 +298,7 @@
             0,
             0,
             tiled=True,
-            axis_index_groups=[middle_first(chips, chips // 2)],
+            axis_index_groups=[middle_first(chips, chips // 2 + 1)],
         )
         if step + 1 < ITERS:
             (contrib,) = call(
@@ -319,7 +319,7 @@
                 *wanted,
             )
             parts = [sums[0]] + [swap(sums[j], ALL, j) for j in range(1, near)]
-    order = middle_first(n, n // 2 + 1)
+    order = middle_first(n, n // 2 + 3)
     (counts,) = call(
         lambda *refs: last_column_kernel(order, *refs),
         [(n, own_blocks, cols)],

time: 58.9 us -> 57.4 us (0.975)
  blocking collectives: 28.1 us -> 25.5 us
  waiting for transfers between devices: 9.08 us -> 9.96 us
    all_to_all x2, blocking collectives: 18.7 us -> 17.2 us  [local(): lax.all_to_all(row_parts, 'genome', 0, 0, tiled=True, axis_index_groups=[...]
    all_to_all x1, blocking collectives: 9.36 us -> 8.33 us  [local(): lax.all_to_all(counts, ALL, 0, 0, tiled=True, axis_index_groups=[order])]
    ppermute x12, waiting for transfers between devices: 9.08 us -> 9.96 us  [swap(): return lax.ppermute(x, axes, [(i, i ^ k) for i in range(n)])]
  transfers between devices with their start and end apart: 12 -> 12, of which waited for: 6 -> 7; matrix products, arithmetic and copies ran while one was open for 0% -> 0% of each run, Pallas kernels for 4% -> 4%
where the time goes in v8:
time: 57.4 us; the launch traced here: 56.9 us
  blocking collectives  25.5 us (44%)
  starting transfers between devices  14 us (24%)
  waiting for transfers between devices  9.96 us (17%)
  Pallas kernels  6.76 us (12%)
  other arithmetic  0.62 us (1%)
    all_to_all x2, blocking collectives, local(): lax.all_to_all(row_parts, 'genome', 0, 0, tiled=True, axis_index_groups=[...  17.2 us
    ppermute x12, starting transfers between devices, swap(): return lax.ppermute(x, axes, [(i, i ^ k) for i in range(n)])  14 us
    ppermute x12, waiting for transfers between devices, swap(): return lax.ppermute(x, axes, [(i, i ^ k) for i in range(n)])  9.96 us
    all_to_all x1, blocking collectives, local(): lax.all_to_all(counts, ALL, 0, 0, tiled=True, axis_index_groups=[order])  8.33 us
    pallas_call x6, Pallas kernels, call(): pl.pallas_call(kernel, out_shape=[jax.ShapeDtypeStruct(shape, jnp.float32...  4.49 us
    pallas_call x1, Pallas kernels, prepare(): pl.pallas_call(lambda *refs: prepare_kernel(own_blocks, *refs), out_shape...  2.26 us
  transfers between devices with their start and end apart: 12, of which 7 were waited for; matrix products, arithmetic and copies ran while one was open for 0% of the time, Pallas kernels for 4%

profile of v8, /device:TPU:0, one launch (start us, length us, event | category | flops | bytes accessed | tf_op | source)
XLA Modules:
  0.0 56.9 jit_solution(3643609883316596981)
XLA Ops:
  0.0 5.0 %collective-permute-start.2 = (f32[12,128]{1,0:T(8,128)}, f32[12,128]{1,0:T(8,128)S(1)}, u32[]{:S(2)}, u32[]{:S(2)}) collective-permute-start(f32[12,128]{1,0:T(8,128)} %bitcast.3), channel_id=1, source_target_pairs={{0,12},{1,13},{2,14},{3,15},{4,8},{5,9},{6,10},{7,11},{8,4},{9,5},... | collective-permute-start | bytes 18440 | tf_op jit(solution)/shard_map/ppermute | solution.py:28
  5.1 0.6 %collective-permute-start = (f32[12,128]{1,0:T(8,128)}, f32[12,128]{1,0:T(8,128)S(1)}, u32[]{:S(2)}, u32[]{:S(2)}) collective-permute-start(f32[12,128]{1,0:T(8,128)} %bitcast.5), channel_id=1, source_target_pairs={{0,4},{1,5},{2,6},{3,7},{4,0},{5,1},{6,2},{7,3},{8,12},{9,13},{10,... | collective-permute-start | bytes 18440 | tf_op jit(solution)/shard_map/ppermute | solution.py:28
  5.7 2.3 %shard_map.46 = (bf16[8,8,256,128]{3,2,1,0:T(8,128)(2,1)S(1)}, f32[8,128]{1,0:T(8,128)S(1)}) custom-call(bf16[8,8,256,128]{3,2,1,0:T(8,128)(2,1)} %refs_0_.1, s32[8,8]{1,0:T(8,128)} %refs_1_.1, s32[8,8]{1,0:T(8,128)} %refs_2_.1), custom_call_target="tpu_custom_call" | custom-call | tf_op jit(solution)/shard_map/pallas_call | solution.py:247
  8.0 1.9 %collective-permute-done.1.refs_2_ = f32[12,128]{1,0:T(8,128)S(1)} collective-permute-done((f32[12,128]{1,0:T(8,128)}, f32[12,128]{1,0:T(8,128)S(1)}, u32[]{:S(2)}, u32[]{:S(2)}) %collective-permute-start.1) | collective-permute-done | bytes 6176 | tf_op jit(solution)/shard_map/ppermute | solution.py:28
  9.9 1.6 %collective-permute-start.4 = (f32[64,128]{1,0:T(8,128)S(1)}, f32[64,128]{1,0:T(8,128)S(1)}, u32[]{:S(2)}, u32[]{:S(2)}) collective-permute-start(f32[64,128]{1,0:T(8,128)S(1)} %shard_map.47.refs_1_), channel_id=1, source_target_pairs={{0,2},{1,3},{2,0},{3,1},{4,6},{5,7},{6,4},{7,5},{8,10},{9,11},{10,... | collective-permute-start | bytes 98312 | tf_op jit(solution)/shard_map/ppermute | solution.py:28
  11.5 0.3 collective-permute-start.3
  11.8 1.8 %collective-permute-done.5.refs_4_ = f32[64,128]{1,0:T(8,128)S(1)} collective-permute-done((f32[64,128]{1,0:T(8,128)S(1)}, f32[64,128]{1,0:T(8,128)S(1)}, u32[]{:S(2)}, u32[]{:S(2)}) %collective-permute-start.5) | collective-permute-done | bytes 32800 | tf_op jit(solution)/shard_map/ppermute | solution.py:28
  13.5 0.4 collective-permute-done.4.refs_3_
  13.9 1.4 %shard_map.48 = (f32[8,8,256]{2,1,0:T(8,128)S(1)}, f32[64,128]{1,0:T(8,128)S(1)}) custom-call(f32[8,128]{1,0:T(8,128)S(1)} %get-tuple-element.15.refs_4_.refs_0_.info_ref, f32[64,128]{1,0:T(8,128)S(1)} %shard_map.47.refs_1_, f32[64,128]{1,0:T(8,128)S(1)} %collective-permute-done.3.refs_2_, f32[64,128]{1,0:T(8,128)S(1)} %collective-permute-done.4.refs_3_, ...), custom_call_target="tpu_custom_call" | custom-call | tf_op jit(solution)/shard_map/pallas_call | solution.py:235
  15.3 8.8 %all_to_all.15.parts_ref = f32[8,8,256]{2,1,0:T(8,128)S(1)} all-to-all(f32[8,8,256]{2,1,0:T(8,128)S(1)} %get-tuple-element.17), channel_id=1, replica_groups={{10,8,14,12,2,0,6,4},{11,9,15,13,3,1,7,5},{26,24,30,28,18,16,22,20},{27..., dimensions={0} | all-to-all | bytes 131072 | tf_op jit(solution)/shard_map/all_to_all | solution.py:295
  24.1 0.7 %shard_map.49.refs_0_ = f32[72,128]{1,0:T(8,128)S(1)} custom-call(f32[8,128]{1,0:T(8,128)S(1)} %get-tuple-element.15.refs_4_.refs_0_.info_ref, f32[8,8,256]{2,1,0:T(8,128)S(1)} %all_to_all.15.parts_ref, f32[64,128]{1,0:T(8,128)S(1)} %get-tuple-element.18.picked_ref, bf16[8,8,256,128]{3,2,1,0:T(8,128)(2,1)S(1)} %get-tuple-element.16.refs_5_.lik_ref.refs_4_.refs_3_), custom_call_target="tpu_custom_call" | custom-call | tf_op jit(solution)/shard_map/pallas_call | solution.py:235
  24.8 2.3 %collective-permute-start.8 = (f32[72,128]{1,0:T(8,128)S(1)}, f32[72,128]{1,0:T(8,128)S(1)}, u32[]{:S(2)}, u32[]{:S(2)}) collective-permute-start(f32[72,128]{1,0:T(8,128)S(1)} %shard_map.49.refs_0_), channel_id=1, source_target_pairs={{0,12},{1,13},{2,14},{3,15},{4,8},{5,9},{6,10},{7,11},{8,4},{9,5},... | collective-permute-start | bytes 110600 | tf_op jit(solution)/shard_map/ppermute | solution.py:28
  27.2 2.1 %collective-permute-start.6 = (f32[72,128]{1,0:T(8,128)S(1)}, f32[72,128]{1,0:T(8,128)S(1)}, u32[]{:S(2)}, u32[]{:S(2)}) collective-permute-start(f32[72,128]{1,0:T(8,128)S(1)} %shard_map.49.refs_0_), channel_id=1, source_target_pairs={{0,4},{1,5},{2,6},{3,7},{4,0},{5,1},{6,2},{7,3},{8,12},{9,13},{10,... | collective-permute-start | bytes 110600 | tf_op jit(solution)/shard_map/ppermute | solution.py:28
  29.3 1.7 %collective-permute-done.8.refs_3_ = f32[72,128]{1,0:T(8,128)S(1)} collective-permute-done((f32[72,128]{1,0:T(8,128)S(1)}, f32[72,128]{1,0:T(8,128)S(1)}, u32[]{:S(2)}, u32[]{:S(2)}) %collective-permute-start.8) | collective-permute-done | bytes 36896 | tf_op jit(solution)/shard_map/ppermute | solution.py:28
  31.0 1.0 %collective-permute-done.7.refs_2_ = f32[72,128]{1,0:T(8,128)S(1)} collective-permute-done((f32[72,128]{1,0:T(8,128)S(1)}, f32[72,128]{1,0:T(8,128)S(1)}, u32[]{:S(2)}, u32[]{:S(2)}) %collective-permute-start.7) | collective-permute-done | bytes 36896 | tf_op jit(solution)/shard_map/ppermute | solution.py:28
  32.0 0.3 shard_map.50
  32.4 1.7 %collective-permute-start.10 = (f32[64,128]{1,0:T(8,128)S(1)}, f32[64,128]{1,0:T(8,128)S(1)}, u32[]{:S(2)}, u32[]{:S(2)}) collective-permute-start(f32[64,128]{1,0:T(8,128)S(1)} %get-tuple-element.21), channel_id=1, source_target_pairs={{0,2},{1,3},{2,0},{3,1},{4,6},{5,7},{6,4},{7,5},{8,10},{9,11},{10,... | collective-permute-start | bytes 98312 | tf_op jit(solution)/shard_map/ppermute | solution.py:28
  34.3 2.1 %collective-permute-done.10.refs_2_ = f32[64,128]{1,0:T(8,128)S(1)} collective-permute-done((f32[64,128]{1,0:T(8,128)S(1)}, f32[64,128]{1,0:T(8,128)S(1)}, u32[]{:S(2)}, u32[]{:S(2)}) %collective-permute-start.10) | collective-permute-done | bytes 32800 | tf_op jit(solution)/shard_map/ppermute | solution.py:28
  36.4 1.1 %collective-permute-done.11.refs_3_ = f32[64,128]{1,0:T(8,128)S(1)} collective-permute-done((f32[64,128]{1,0:T(8,128)S(1)}, f32[64,128]{1,0:T(8,128)S(1)}, u32[]{:S(2)}, u32[]{:S(2)}) %collective-permute-start.11) | collective-permute-done | bytes 32800 | tf_op jit(solution)/shard_map/ppermute | solution.py:28
  37.5 1.2 %shard_map.51 = (f32[8,8,256]{2,1,0:T(8,128)S(1)}, f32[64,128]{1,0:T(8,128)S(1)}) custom-call(f32[64,128]{1,0:T(8,128)S(1)} %get-tuple-element.19.refs_0_, f32[64,128]{1,0:T(8,128)S(1)} %collective-permute-done.9.refs_1_, f32[64,128]{1,0:T(8,128)S(1)} %collective-permute-done.10.refs_2_, f32[64,128]{1,0:T(8,128)S(1)} %collective-permute-done.11.refs_3_, ...), custom_call_target="tpu_custom_call" | custom-call | tf_op jit(solution)/shard_map/pallas_call | solution.py:235
  38.7 8.4 %all_to_all.16.refs_1_ = f32[8,8,256]{2,1,0:T(8,128)S(1)} all-to-all(f32[8,8,256]{2,1,0:T(8,128)S(1)} %get-tuple-element.23), channel_id=1, replica_groups={{10,8,14,12,2,0,6,4},{11,9,15,13,3,1,7,5},{26,24,30,28,18,16,22,20},{27..., dimensions={0} | all-to-all | bytes 131072 | tf_op jit(solution)/shard_map/all_to_all | solution.py:295
  47.1 0.9 %shard_map.52 = f32[16,12,128]{2,1,0:T(8,128)S(1)} custom-call(f32[8,128]{1,0:T(8,128)S(1)} %get-tuple-element.15.refs_4_.refs_0_.info_ref, f32[8,8,256]{2,1,0:T(8,128)S(1)} %all_to_all.16.refs_1_, f32[64,128]{1,0:T(8,128)S(1)} %get-tuple-element.24.refs_2_, bf16[8,8,256,128]{3,2,1,0:T(8,128)(2,1)S(1)} %get-tuple-element.16.refs_5_.lik_ref.refs_4_.refs_3_), custom_call_target="tpu_custom_call" | custom-call | tf_op jit(solution)/shard_map/pallas_call | solution.py:235
  48.0 8.3 %all_to_all.17 = f32[16,12,128]{2,1,0:T(8,128)S(1)} all-to-all(f32[16,12,128]{2,1,0:T(8,128)S(1)} %shard_map.52), channel_id=1, replica_groups={{11,10,9,8,15,14,13,12,3,2,1,0,7,6,5,4},{27,26,25,24,31,30,29,28,19,18,..., dimensions={0} | all-to-all | bytes 196608 | tf_op jit(solution)/shard_map/all_to_all | solution.py:332
  56.3 0.6 %multiply_bitcast_fusion = f32[1536]{0:T(1024)} fusion(f32[12,128]{1,0:T(8,128)S(1)} %reduce_sum.9), kind=kLoop, calls=%fused_computation | loop fusion | flops 1536 | bytes 12288 | tf_op jit(solution)/shard_map/mul | solution.py:333
  (17 shorter events, 0.4 us)
Async XLA Ops:
  0.0 9.8 %copy-start = (f32[1536]{0:T(1024)S(1)}, f32[1536]{0:T(1024)}, u32[]{:S(2)}) copy-start(f32[1536]{0:T(1024)} %param.7) | copy-start | bytes 18436
  0.0 8.0 %collective-permute-start.2 = (f32[12,128]{1,0:T(8,128)}, f32[12,128]{1,0:T(8,128)S(1)}, u32[]{:S(2)}, u32[]{:S(2)}) collective-permute-start(f32[12,128]{1,0:T(8,128)} %bitcast.3), channel_id=1, source_target_pairs={{0,12},{1,13},{2,14},{3,15},{4,8},{5,9},{6,10},{7,11},{8,4},{9,5},... | collective-permute-start | bytes 18440 | tf_op jit(solution)/shard_map/ppermute | solution.py:28
  5.1 4.8 %collective-permute-start.1 = (f32[12,128]{1,0:T(8,128)}, f32[12,128]{1,0:T(8,128)S(1)}, u32[]{:S(2)}, u32[]{:S(2)}) collective-permute-start(f32[12,128]{1,0:T(8,128)} %bitcast.4), channel_id=1, source_target_pairs={{0,8},{1,9},{2,10},{3,11},{4,12},{5,13},{6,14},{7,15},{8,0},{9,1},... | collective-permute-start | bytes 18440 | tf_op jit(solution)/shard_map/ppermute | solution.py:28
  5.1 4.8 %collective-permute-start = (f32[12,128]{1,0:T(8,128)}, f32[12,128]{1,0:T(8,128)S(1)}, u32[]{:S(2)}, u32[]{:S(2)}) collective-permute-start(f32[12,128]{1,0:T(8,128)} %bitcast.5), channel_id=1, source_target_pairs={{0,4},{1,5},{2,6},{3,7},{4,0},{5,1},{6,2},{7,3},{8,12},{9,13},{10,... | collective-permute-start | bytes 18440 | tf_op jit(solution)/shard_map/ppermute | solution.py:28
  9.8 3.7 %collective-permute-start.5 = (f32[64,128]{1,0:T(8,128)S(1)}, f32[64,128]{1,0:T(8,128)S(1)}, u32[]{:S(2)}, u32[]{:S(2)}) collective-permute-start(f32[64,128]{1,0:T(8,128)S(1)} %shard_map.47.refs_1_), channel_id=1, source_target_pairs={{0,3},{1,2},{2,1},{3,0},{4,7},{5,6},{6,5},{7,4},{8,11},{9,10},{10,... | collective-permute-start | bytes 98312 | tf_op jit(solution)/shard_map/ppermute | solution.py:28
  9.9 4.0 %collective-permute-start.4 = (f32[64,128]{1,0:T(8,128)S(1)}, f32[64,128]{1,0:T(8,128)S(1)}, u32[]{:S(2)}, u32[]{:S(2)}) collective-permute-start(f32[64,128]{1,0:T(8,128)S(1)} %shard_map.47.refs_1_), channel_id=1, source_target_pairs={{0,2},{1,3},{2,0},{3,1},{4,6},{5,7},{6,4},{7,5},{8,10},{9,11},{10,... | collective-permute-start | bytes 98312 | tf_op jit(solution)/shard_map/ppermute | solution.py:28
  11.5 2.4 %collective-permute-start.3 = (f32[64,128]{1,0:T(8,128)S(1)}, f32[64,128]{1,0:T(8,128)S(1)}, u32[]{:S(2)}, u32[]{:S(2)}) collective-permute-start(f32[64,128]{1,0:T(8,128)S(1)} %shard_map.47.refs_1_), channel_id=1, source_target_pairs={{0,1},{1,0},{2,3},{3,2},{4,5},{5,4},{6,7},{7,6},{8,9},{9,8},{10,11... | collective-permute-start | bytes 98312 | tf_op jit(solution)/shard_map/ppermute | solution.py:28
  24.8 6.2 %collective-permute-start.8 = (f32[72,128]{1,0:T(8,128)S(1)}, f32[72,128]{1,0:T(8,128)S(1)}, u32[]{:S(2)}, u32[]{:S(2)}) collective-permute-start(f32[72,128]{1,0:T(8,128)S(1)} %shard_map.49.refs_0_), channel_id=1, source_target_pairs={{0,12},{1,13},{2,14},{3,15},{4,8},{5,9},{6,10},{7,11},{8,4},{9,5},... | collective-permute-start | bytes 110600 | tf_op jit(solution)/shard_map/ppermute | solution.py:28
  27.2 4.9 %collective-permute-start.7 = (f32[72,128]{1,0:T(8,128)S(1)}, f32[72,128]{1,0:T(8,128)S(1)}, u32[]{:S(2)}, u32[]{:S(2)}) collective-permute-start(f32[72,128]{1,0:T(8,128)S(1)} %shard_map.49.refs_0_), channel_id=1, source_target_pairs={{0,8},{1,9},{2,10},{3,11},{4,12},{5,13},{6,14},{7,15},{8,0},{9,1},... | collective-permute-start | bytes 110600 | tf_op jit(solution)/shard_map/ppermute | solution.py:28
  27.2 4.9 %collective-permute-start.6 = (f32[72,128]{1,0:T(8,128)S(1)}, f32[72,128]{1,0:T(8,128)S(1)}, u32[]{:S(2)}, u32[]{:S(2)}) collective-permute-start(f32[72,128]{1,0:T(8,128)S(1)} %shard_map.49.refs_0_), channel_id=1, source_target_pairs={{0,4},{1,5},{2,6},{3,7},{4,0},{5,1},{6,2},{7,3},{8,12},{9,13},{10,... | collective-permute-start | bytes 110600 | tf_op jit(solution)/shard_map/ppermute | solution.py:28
  32.3 1.9 %collective-permute-start.9 = (f32[64,128]{1,0:T(8,128)S(1)}, f32[64,128]{1,0:T(8,128)S(1)}, u32[]{:S(2)}, u32[]{:S(2)}) collective-permute-start(f32[64,128]{1,0:T(8,128)S(1)} %get-tuple-element.20), channel_id=1, source_target_pairs={{0,1},{1,0},{2,3},{3,2},{4,5},{5,4},{6,7},{7,6},{8,9},{9,8},{10,11... | collective-permute-start | bytes 98312 | tf_op jit(solution)/shard_map/ppermute | solution.py:28
  32.4 4.0 %collective-permute-start.10 = (f32[64,128]{1,0:T(8,128)S(1)}, f32[64,128]{1,0:T(8,128)S(1)}, u32[]{:S(2)}, u32[]{:S(2)}) collective-permute-start(f32[64,128]{1,0:T(8,128)S(1)} %get-tuple-element.21), channel_id=1, source_target_pairs={{0,2},{1,3},{2,0},{3,1},{4,6},{5,7},{6,4},{7,5},{8,10},{9,11},{10,... | collective-permute-start | bytes 98312 | tf_op jit(solution)/shard_map/ppermute | solution.py:28
  34.1 3.3 %collective-permute-start.11 = (f32[64,128]{1,0:T(8,128)S(1)}, f32[64,128]{1,0:T(8,128)S(1)}, u32[]{:S(2)}, u32[]{:S(2)}) collective-permute-start(f32[64,128]{1,0:T(8,128)S(1)} %get-tuple-element.22), channel_id=1, source_target_pairs={{0,3},{1,2},{2,1},{3,0},{4,7},{5,6},{6,5},{7,4},{8,11},{9,10},{10,... | collective-permute-start | bytes 98312 | tf_op jit(solution)/shard_map/ppermute | solution.py:28

commit v9 on v8

v9 whole, which is shorter than its diff:
```python
import jax
import jax.numpy as jnp
from jax import lax
from jax.experimental import pallas as pl
from jax.experimental.pallas import tpu as pltpu
from jax.sharding import PartitionSpec as P

ITERS = 2
ALL = ("genome", "reads")
TERMS = 16
LANES = 128
VMEM = pl.BlockSpec(memory_space=pltpu.VMEM)
ANY = pl.BlockSpec(memory_space=pl.ANY)


def radices(n):
    out = []
    while n > 1:
        r = 4 if n % 4 == 0 else 2
        out.append(r)
        n //= r
    return out


def swap(x, axes, k):
    n = lax.axis_size(axes)
    return lax.ppermute(x, axes, [(i, i ^ k) for i in range(n)])


def middle_first(n, k):
    return [i ^ k for i in range(n)]


def gather_far(x, axes):
    parts = [x]
    stride = lax.axis_size(axes)
    for r in radices(stride)[:0:-1]:
        stride //= r
        sent = parts[0] if len(parts) == 1 else jnp.concatenate(parts, axis=0)
        parts = [sent] + [swap(sent, axes, j * stride) for j in range(1, r)]
    return parts


def far_order(n):
    order = [0]
    stride = n
    for r in radices(n)[:0:-1]:
        stride //= r
        order = [o ^ (j * stride) for j in range(r) for o in order]
    return order


def dot(a, b, dims=(((1,), (0,)), ((), ()))):
    return lax.dot_general(a, b, dims, preferred_element_type=jnp.float32)


def terms(x):
    hi = x.astype(jnp.bfloat16)
    rest = x - hi.astype(jnp.float32)
    mid = rest.astype(jnp.bfloat16)
    return hi, mid, (rest - mid.astype(jnp.float32)).astype(jnp.bfloat16)


def select_rows(hot, x):
    hi, mid, low = terms(x)
    hot = hot.astype(jnp.bfloat16)
    return dot(hot, hi) + dot(hot, mid) + dot(hot, low)


def split(row):
    x = jnp.broadcast_to(row, (TERMS, row.shape[1]))
    hi = x.astype(jnp.bfloat16).astype(jnp.float32)
    rest = x - hi
    mid = rest.astype(jnp.bfloat16).astype(jnp.float32)
    low = rest - mid
    at = lax.broadcasted_iota(jnp.int32, x.shape, 0)
    out = jnp.where(at == 0, hi, jnp.where(at == 1, mid, jnp.where(at == 2, low, 0.0)))
    return out.astype(jnp.bfloat16)


def down(row):
    return jnp.transpose(jnp.broadcast_to(row, (LANES, LANES)))


def hot_rows(values, count):
    column = down(values)
    blocks = []
    for start in range(0, count, LANES):
        width = min(LANES, count - start)
        lane = lax.broadcasted_iota(jnp.int32, (LANES, width), 1).astype(jnp.float32) + start
        blocks.append((column[:, :width] == lane).astype(jnp.float32))
    return blocks[0] if len(blocks) == 1 else jnp.concatenate(blocks, axis=1)


def prepare_kernel(
    first,
    weights_ref,
    ids_ref,
    valid_ref,
    lik_ref,
    out_ref,
    info_ref,
    held_ref,
    weights,
    ids,
    valid,
    wide,
    sems,
    held_sems,
):
    copies = [
        pltpu.make_async_copy(source, target, sems.at[i])
        for i, (source, target) in enumerate(
            [(ids_ref, ids), (valid_ref, valid), (weights_ref, weights)]
        )
    ]
    held = block_copies(lik_ref, held_ref, held_sems, 0)
    for copy in copies + held:
        copy.start()
    wide[...] = jnp.zeros_like(wide)
    for copy in copies:
        copy.wait()
    read_blocks, slots = ids.shape
    count, rows, cols = out_ref.shape
    own_blocks = weights.shape[0]
    lane = lax.broadcasted_iota(jnp.int32, (1, cols), 1)
    wide[:, :slots] = jnp.where(valid[...] > 0, ids[...], -1).astype(jnp.float32)
    flat = jnp.sum(
        pltpu.roll(wide[...], 0, 1, stride=slots, stride_axis=0), axis=0, keepdims=True
    )
    flat = jnp.where(lane < read_blocks * slots, flat, -1.0)
    for i in range(count):
        out_ref[i, :own_blocks, :] = weights[...]
        out_ref[i, own_blocks:, :] = jnp.broadcast_to(flat, (rows - own_blocks, cols))
    block = jnp.maximum(flat, 0.0)
    owner = ((block + 0.5) * (1.0 / own_blocks)).astype(jnp.int32)
    inside = block.astype(jnp.int32) - owner * own_blocks
    place = jnp.where(flat < 0, -1, (owner ^ first) * rows + inside).astype(jnp.float32)
    row = lax.broadcasted_iota(jnp.int32, info_ref.shape, 0)
    info_ref[...] = jnp.where(row == 0, flat, jnp.where(row == 1, place, 0.0))
    for copy in held:
        copy.wait()


def block_copies(lik_ref, held_ref, sems, start):
    return [
        pltpu.make_async_copy(lik_ref.at[start + b], held_ref.at[b], sems.at[b])
        for b in range(held_ref.shape[0])
    ]


def block_of(held_refs, b):
    first, second = held_refs
    return first.at[b] if b < first.shape[0] else second.at[b - first.shape[0]]


def row_sums(picked_ref, held_refs, out_ref, copies=()):
    slots = held_refs[0].shape[1]
    early = out_ref.shape[1] - len(copies)
    for b in range(out_ref.shape[1]):
        if copies and b >= early:
            copies[b - early].wait()
        lik_ref = block_of(held_refs, b)
        total = None
        for s in range(0, slots, 2):
            at = b * slots + s
            left = jnp.concatenate(
                [split(picked_ref[at : at + 1, :]), split(picked_ref[at + 1 : at + 2, :])], axis=1
            )
            right = jnp.concatenate([lik_ref[s], lik_ref[s + 1]], axis=1)
            part = dot(left, right, (((1,), (1,)), ((), ())))
            total = part if total is None else total + part
        row = jnp.sum(total, axis=0, keepdims=True)
        for i in range(out_ref.shape[0]):
            out_ref[i, b : b + 1, :] = row


def first_row_kernel(
    info_ref, table_ref, early_ref, lik_ref, out_ref, picked_ref, late_ref, sems
):
    copies = block_copies(lik_ref, late_ref, sems, early_ref.shape[0])
    for copy in copies:
        copy.start()
    count, rows, cols = table_ref.shape
    hot = hot_rows(info_ref[1:2, :], count * rows)
    table = table_ref[...].reshape(count * rows, cols)
    picked_ref[...] = select_rows(hot[: picked_ref.shape[0]], table)
    row_sums(picked_ref, (early_ref, late_ref), out_ref, copies)


def next_row_kernel(near, scale, *refs):
    parts, (early_ref, late_ref, out_ref, picked_ref) = refs[:near], refs[near:]
    total = parts[0][...]
    for part in parts[1:]:
        total = total + part[...]
    picked_ref[...] = total * scale
    row_sums(picked_ref, (early_ref, late_ref), out_ref)


def column_sums(parts_ref, picked_ref, held_refs, contrib_ref, inverse_ref):
    slots, cols = held_refs[0].shape[1], held_refs[0].shape[3]
    total = parts_ref[0]
    for i in range(1, parts_ref.shape[0]):
        total = total + parts_ref[i]
    inverse_ref[...] = 1.0 / total
    for b in range(inverse_ref.shape[0]):
        lik_ref = block_of(held_refs, b)
        left = split(inverse_ref[b : b + 1, :])
        for s in range(0, slots, 2):
            at = b * slots + s
            right = jnp.concatenate([lik_ref[s], lik_ref[s + 1]], axis=1)
            summed = jnp.sum(dot(left, right), axis=0, keepdims=True)
            contrib_ref[at : at + 1, :] = picked_ref[at : at + 1, :] * summed[:, :cols]
            contrib_ref[at + 1 : at + 2, :] = picked_ref[at + 1 : at + 2, :] * summed[:, cols:]


def column_kernel(parts_ref, picked_ref, early_ref, late_ref, out_ref, inverse_ref):
    column_sums(parts_ref, picked_ref, (early_ref, late_ref), out_ref, inverse_ref)


def last_column_kernel(
    order, info_ref, parts_ref, picked_ref, early_ref, late_ref, out_ref, inverse_ref, contrib_ref
):
    column_sums(parts_ref, picked_ref, (early_ref, late_ref), contrib_ref, inverse_ref)
    owners, own_blocks, cols = out_ref.shape
    all_slots = contrib_ref.shape[0]
    block = lax.broadcasted_iota(jnp.int32, (owners * own_blocks, all_slots), 0)
    hot = (block.astype(jnp.float32) == info_ref[0:1, :all_slots]).astype(jnp.float32)
    counts = select_rows(hot, contrib_ref[...])
    for i, owner in enumerate(order):
        out_ref[i] = counts[owner * own_blocks : (owner + 1) * own_blocks, :]


def wanted_kernel(first, own_blocks, table_ref, *refs):
    n = lax.axis_size(ALL)
    me = lax.axis_index("genome") * 2 + lax.axis_index("reads")
    near = radices(n)[0]
    given_refs, outs = refs[:-near], refs[-near:]
    all_slots = outs[0].shape[0]
    half = LANES // 2
    lane = lax.broadcasted_iota(jnp.int32, (1, LANES), 1)

    def ids_of(k):
        return table_ref[me ^ k ^ first, own_blocks : own_blocks + 1, :]

    ids = [ids_of(k) for k in far_order(n)]
    pairs = [
        jnp.where(lane < half, a, pltpu.roll(b, half, 1)) for a, b in zip(ids[::2], ids[1::2])
    ]
    given = terms(jnp.concatenate([ref[...] for ref in given_refs], axis=0))
    for j, out_ref in enumerate(outs):
        column = down(ids_of(j))[:all_slots]
        hot = jnp.concatenate([(column == pair).astype(jnp.float32) for pair in pairs], axis=1)
        hot = hot.astype(jnp.bfloat16)
        out_ref[...] = dot(hot, given[0]) + dot(hot, given[1]) + dot(hot, given[2])


PARAMS = pltpu.CompilerParams(vmem_limit_bytes=16 * 2**20)


def call(kernel, outs, scratch, *operands):
    return pl.pallas_call(
        kernel,
        out_shape=[jax.ShapeDtypeStruct(shape, jnp.float32) for shape in outs],
        in_specs=[VMEM] * len(operands),
        out_specs=[VMEM] * len(outs),
        scratch_shapes=[pltpu.VMEM(shape, jnp.float32) for shape in scratch],
        compiler_params=PARAMS,
    )(*operands)


def in_hbm(*arrays):
    return [pltpu.with_memory_space_constraint(x, pltpu.HBM) for x in arrays]


def prepare(shape, first, early, weights, block_ids, slot_valid, likelihood):
    return pl.pallas_call(
        lambda *refs: prepare_kernel(first, *refs),
        out_shape=[
            jax.ShapeDtypeStruct(shape, jnp.float32),
            jax.ShapeDtypeStruct((8, LANES), jnp.float32),
            pltpu.VMEM((early,) + likelihood.shape[1:], likelihood.dtype),
        ],
        in_specs=[ANY] * 4,
        out_specs=[VMEM] * 3,
        scratch_shapes=[
            pltpu.VMEM(weights.shape, jnp.float32),
            pltpu.VMEM(block_ids.shape, jnp.int32),
            pltpu.VMEM(block_ids.shape, jnp.int32),
            pltpu.VMEM((block_ids.shape[0], LANES), jnp.float32),
            pltpu.SemaphoreType.DMA((3,)),
            pltpu.SemaphoreType.DMA((early,)),
        ],
        compiler_params=PARAMS,
    )(*in_hbm(weights, block_ids, slot_valid, likelihood))


def first_rows(outs, info, table, held, likelihood):
    late = likelihood.shape[0] - held.shape[0]
    return pl.pallas_call(
        first_row_kernel,
        out_shape=[jax.ShapeDtypeStruct(shape, jnp.float32) for shape in outs]
        + [pltpu.VMEM((late,) + likelihood.shape[1:], likelihood.dtype)],
        in_specs=[VMEM] * 3 + [ANY],
        out_specs=[VMEM] * 3,
        scratch_shapes=[pltpu.SemaphoreType.DMA((late,))],
        compiler_params=PARAMS,
    )(info, table, held, *in_hbm(likelihood))


def local(likelihood, block_ids, slot_valid, start_weights):
    read_blocks, slots, reads, cols = likelihood.shape
    n = lax.axis_size(ALL)
    chips = lax.axis_size("genome")
    near = radices(n)[0]
    own_weights = start_weights.reshape(-1, cols)
    own_blocks = own_weights.shape[0]
    all_slots = read_blocks * slots
    total_reads = read_blocks * lax.axis_size("reads") * reads
    scale = n * own_blocks * cols / total_reads
    first_chip = chips // 2 + 1
    first = first_chip * 2 + 1
    order = middle_first(n, first)

    rows = -(-(own_blocks + 1) // 8) * 8
    early = read_blocks * 3 // 8
    sent, info, held = prepare(
        (n, rows, cols), first, early, own_weights, block_ids, slot_valid, likelihood
    )
    table = lax.all_to_all(sent, ALL, 0, 0, tiled=True, axis_index_groups=[order])

    outs = [(chips, read_blocks, reads), (all_slots, cols)]
    inverse = (read_blocks, reads)
    for step in range(ITERS):
        if step == 0:
            row_parts, picked, rest = first_rows(outs, info, table, held, likelihood)
            held = [held, rest]
        else:
            row_parts, picked = call(
                lambda *refs: next_row_kernel(near, scale, *refs), outs, [], *parts, *held
            )
        row_parts = lax.all_to_all(
            row_parts,
            "genome",
            0,
            0,
            tiled=True,
            axis_index_groups=[middle_first(chips, first_chip)],
        )
        if step + 1 < ITERS:
            (contrib,) = call(
                column_kernel, [(all_slots, cols)], [inverse], row_parts, picked, *held
            )
            sums = call(
                lambda *refs: wanted_kernel(first, own_blocks, *refs),
                [(all_slots, cols)] * near,
                [],
                table,
                *gather_far(contrib, ALL),
            )
            parts = [sums[0]] + [swap(sums[j], ALL, j) for j in range(1, near)]
    (counts,) = call(
        lambda *refs: last_column_kernel(order, *refs),
        [(n, own_blocks, cols)],
        [inverse, (all_slots, cols)],
        info,
        row_parts,
        picked,
        *held,
    )
    counts = lax.all_to_all(counts, ALL, 0, 0, tiled=True, axis_index_groups=[order])
    return (jnp.sum(counts, axis=0) * scale).reshape(-1)


def solution(mesh):
    placed = (
        P(("parts", "reads"), "genome", None, None),
        P(("parts", "reads"), "genome"),
        P(("parts", "reads"), "genome"),
        P(("parts", "genome", "reads")),
    )
    return jax.shard_map(
        local,
        mesh=mesh,
        in_specs=placed,
        out_specs=P(("parts", "genome", "reads")),
        check_vma=False,
    )
```

time: 57.4 us -> 58.6 us (1.021)
  blocking collectives: 25.5 us -> 37.2 us
  starting transfers between devices: 14 us -> 6.39 us
  waiting for transfers between devices: 9.96 us -> 5.9 us
  Pallas kernels: 6.76 us -> 7.93 us
    all_to_all x0 -> x1, blocking collectives: none -> 10.9 us  [local(): lax.all_to_all(sent, ALL, 0, 0, tiled=True, axis_index_groups=[order])]
    ppermute x12 -> x6, starting transfers between devices: 14 us -> 6.39 us  [swap(): return lax.ppermute(x, axes, [(i, i ^ k) for i in range(n)])]
    ppermute x12 -> x6, waiting for transfers between devices: 9.96 us -> 5.9 us  [swap(): return lax.ppermute(x, axes, [(i, i ^ k) for i in range(n)])]
    pallas_call x1 -> x2, Pallas kernels: 2.26 us -> 4.81 us  [the longest x1 3.36 us: first_rows(): pl.pallas_call(first_row_kernel, out_shape=[jax.ShapeDtypeStruct(shape, j...]
    pallas_call x6 -> x4, Pallas kernels: 4.49 us -> 3.12 us  [call(): pl.pallas_call(kernel, out_shape=[jax.ShapeDtypeStruct(shape, jnp.float32...]
    all_to_all x2, blocking collectives: 17.2 us -> 17.9 us  [local(): lax.all_to_all(row_parts, 'genome', 0, 0, tiled=True, axis_index_groups=[...]
  transfers between devices with their start and end apart: 12 -> 6, of which waited for: 7 -> 4; matrix products, arithmetic and copies ran while one was open for 0% -> 0% of each run, Pallas kernels for 4% -> 0%
where the time goes in v9:
time: 58.6 us; the launch traced here: 58.1 us
  blocking collectives  37.2 us (63%)
  Pallas kernels  7.93 us (14%)
  starting transfers between devices  6.39 us (11%)
  waiting for transfers between devices  5.9 us (10%)
  other arithmetic  0.62 us (1%)
    all_to_all x2, blocking collectives, local(): lax.all_to_all(row_parts, 'genome', 0, 0, tiled=True, axis_index_groups=[...  17.9 us
    all_to_all x1, blocking collectives, local(): lax.all_to_all(sent, ALL, 0, 0, tiled=True, axis_index_groups=[order])  10.9 us
    all_to_all x1, blocking collectives, local(): lax.all_to_all(counts, ALL, 0, 0, tiled=True, axis_index_groups=[order])  8.33 us
    ppermute x6, starting transfers between devices, swap(): return lax.ppermute(x, axes, [(i, i ^ k) for i in range(n)])  6.39 us
    ppermute x6, waiting for transfers between devices, swap(): return lax.ppermute(x, axes, [(i, i ^ k) for i in range(n)])  5.9 us
    pallas_call x1, Pallas kernels, first_rows(): pl.pallas_call(first_row_kernel, out_shape=[jax.ShapeDtypeStruct(shape, j...  3.36 us
    pallas_call x4, Pallas kernels, call(): pl.pallas_call(kernel, out_shape=[jax.ShapeDtypeStruct(shape, jnp.float32...  3.12 us
    pallas_call x1, Pallas kernels, prepare(): pl.pallas_call(lambda *refs: prepare_kernel(first, *refs), out_shape=[jax...  1.46 us
  transfers between devices with their start and end apart: 6, of which 4 were waited for; matrix products, arithmetic and copies ran while one was open for 0% of the time, Pallas kernels for 0%

profile of v9, /device:TPU:0, one launch (start us, length us, event | category | flops | bytes accessed | tf_op | source)
XLA Modules:
  0.0 58.1 jit_solution(14848131404339495561)
XLA Ops:
  0.0 1.5 %shard_map.46 = (f32[16,16,128]{2,1,0:T(8,128)S(1)}, f32[8,128]{1,0:T(8,128)S(1)}, bf16[3,8,256,128]{3,2,1,0:T(8,128)(2,1)S(1)}) custom-call(f32[12,128]{1,0:T(8,128)} %bitcast.3, s32[8,8]{1,0:T(8,128)} %refs_1_.1, s32[8,8]{1,0:T(8,128)} %refs_2_.1, bf16[8,8,256,128]{3,2,1,0:T(8,128)(2,1)} %lik_ref.1), custom_call_target="tpu_custom_call" | custom-call | tf_op jit(solution)/shard_map/pallas_call | solution.py:277
  1.5 10.9 %all_to_all.20.table_ref.refs_0_ = f32[16,16,128]{2,1,0:T(8,128)S(1)} all-to-all(f32[16,16,128]{2,1,0:T(8,128)S(1)} %get-tuple-element.18), channel_id=1, replica_groups={{11,10,9,8,15,14,13,12,3,2,1,0,7,6,5,4},{27,26,25,24,31,30,29,28,19,18,..., dimensions={0} | all-to-all | bytes 262144 | tf_op jit(solution)/shard_map/all_to_all | solution.py:330
  12.4 3.4 %shard_map.47 = (f32[8,8,256]{2,1,0:T(8,128)S(1)}, f32[64,128]{1,0:T(8,128)S(1)}, bf16[5,8,256,128]{3,2,1,0:T(8,128)(2,1)S(1)}) custom-call(f32[8,128]{1,0:T(8,128)S(1)} %get-tuple-element.17.info_ref.refs_0_, f32[16,16,128]{2,1,0:T(8,128)S(1)} %all_to_all.20.table_ref.refs_0_, bf16[3,8,256,128]{3,2,1,0:T(8,128)(2,1)S(1)} %get-tuple-element.19.early_ref.refs_4_.refs_3_, ...), custom_call_target="tpu_custom_call" | custom-call | tf_op jit(solution)/shard_map/pallas_call | solution.py:300
  15.7 9.6 %all_to_all.21.parts_ref = f32[8,8,256]{2,1,0:T(8,128)S(1)} all-to-all(f32[8,8,256]{2,1,0:T(8,128)S(1)} %get-tuple-element.20), channel_id=1, replica_groups={{10,8,14,12,2,0,6,4},{11,9,15,13,3,1,7,5},{26,24,30,28,18,16,22,20},{27..., dimensions={0} | all-to-all | bytes 131072 | tf_op jit(solution)/shard_map/all_to_all | solution.py:342
  25.3 0.7 %shard_map.48.refs_1_ = f32[64,128]{1,0:T(8,128)S(1)} custom-call(f32[8,8,256]{2,1,0:T(8,128)S(1)} %all_to_all.21.parts_ref, f32[64,128]{1,0:T(8,128)S(1)} %get-tuple-element.21.picked_ref, bf16[3,8,256,128]{3,2,1,0:T(8,128)(2,1)S(1)} %get-tuple-element.19.early_ref.refs_4_.refs_3_, bf16[5,8,256,128]{3,2,1,0:T(8,128)(2,1)S(1)} %get-tuple-element.22.late_ref.refs_5_.refs_4_), custom_call_target="tpu_custom_call" | custom-call | tf_op jit(solution)/shard_map/pallas_call | solution.py:262
  26.0 2.3 %collective-permute-start.2 = (f32[64,128]{1,0:T(8,128)S(1)}, f32[64,128]{1,0:T(8,128)S(1)}, u32[]{:S(2)}, u32[]{:S(2)}) collective-permute-start(f32[64,128]{1,0:T(8,128)S(1)} %shard_map.48.refs_1_), channel_id=1, source_target_pairs={{0,12},{1,13},{2,14},{3,15},{4,8},{5,9},{6,10},{7,11},{8,4},{9,5},... | collective-permute-start | bytes 98312 | tf_op jit(solution)/shard_map/ppermute | solution.py:27
  28.3 0.0 collective-permute-start.1
  28.3 2.1 %collective-permute-start = (f32[64,128]{1,0:T(8,128)S(1)}, f32[64,128]{1,0:T(8,128)S(1)}, u32[]{:S(2)}, u32[]{:S(2)}) collective-permute-start(f32[64,128]{1,0:T(8,128)S(1)} %shard_map.48.refs_1_), channel_id=1, source_target_pairs={{0,4},{1,5},{2,6},{3,7},{4,0},{5,1},{6,2},{7,3},{8,12},{9,13},{10,... | collective-permute-start | bytes 98312 | tf_op jit(solution)/shard_map/ppermute | solution.py:27
  30.4 1.4 %collective-permute-done.2.refs_4_ = f32[64,128]{1,0:T(8,128)S(1)} collective-permute-done((f32[64,128]{1,0:T(8,128)S(1)}, f32[64,128]{1,0:T(8,128)S(1)}, u32[]{:S(2)}, u32[]{:S(2)}) %collective-permute-start.2) | collective-permute-done | bytes 32800 | tf_op jit(solution)/shard_map/ppermute | solution.py:27
  31.8 1.3 %collective-permute-done.1.refs_3_ = f32[64,128]{1,0:T(8,128)S(1)} collective-permute-done((f32[64,128]{1,0:T(8,128)S(1)}, f32[64,128]{1,0:T(8,128)S(1)}, u32[]{:S(2)}, u32[]{:S(2)}) %collective-permute-start.1) | collective-permute-done | bytes 32800 | tf_op jit(solution)/shard_map/ppermute | solution.py:27
  33.1 0.0 collective-permute-done.refs_2_
  33.1 0.3 shard_map.49
  33.5 0.1 collective-permute-start.3
  33.5 1.7 %collective-permute-start.4 = (f32[64,128]{1,0:T(8,128)S(1)}, f32[64,128]{1,0:T(8,128)S(1)}, u32[]{:S(2)}, u32[]{:S(2)}) collective-permute-start(f32[64,128]{1,0:T(8,128)S(1)} %get-tuple-element.25), channel_id=1, source_target_pairs={{0,2},{1,3},{2,0},{3,1},{4,6},{5,7},{6,4},{7,5},{8,10},{9,11},{10,... | collective-permute-start | bytes 98312 | tf_op jit(solution)/shard_map/ppermute | solution.py:27
  35.3 0.1 collective-permute-start.5
  35.4 0.0 collective-permute-done.3.refs_1_
  35.4 2.1 %collective-permute-done.4.refs_2_ = f32[64,128]{1,0:T(8,128)S(1)} collective-permute-done((f32[64,128]{1,0:T(8,128)S(1)}, f32[64,128]{1,0:T(8,128)S(1)}, u32[]{:S(2)}, u32[]{:S(2)}) %collective-permute-start.4) | collective-permute-done | bytes 32800 | tf_op jit(solution)/shard_map/ppermute | solution.py:27
  37.5 1.1 %collective-permute-done.5.refs_3_ = f32[64,128]{1,0:T(8,128)S(1)} collective-permute-done((f32[64,128]{1,0:T(8,128)S(1)}, f32[64,128]{1,0:T(8,128)S(1)}, u32[]{:S(2)}, u32[]{:S(2)}) %collective-permute-start.5) | collective-permute-done | bytes 32800 | tf_op jit(solution)/shard_map/ppermute | solution.py:27
  38.6 1.2 %shard_map.50 = (f32[8,8,256]{2,1,0:T(8,128)S(1)}, f32[64,128]{1,0:T(8,128)S(1)}) custom-call(f32[64,128]{1,0:T(8,128)S(1)} %get-tuple-element.23.refs_0_, f32[64,128]{1,0:T(8,128)S(1)} %collective-permute-done.3.refs_1_, f32[64,128]{1,0:T(8,128)S(1)} %collective-permute-done.4.refs_2_, f32[64,128]{1,0:T(8,128)S(1)} %collective-permute-done.5.refs_3_, ...), custom_call_target="tpu_custom_call" | custom-call | tf_op jit(solution)/shard_map/pallas_call | solution.py:262
  39.8 8.4 %all_to_all.22.refs_1_ = f32[8,8,256]{2,1,0:T(8,128)S(1)} all-to-all(f32[8,8,256]{2,1,0:T(8,128)S(1)} %get-tuple-element.27), channel_id=1, replica_groups={{10,8,14,12,2,0,6,4},{11,9,15,13,3,1,7,5},{26,24,30,28,18,16,22,20},{27..., dimensions={0} | all-to-all | bytes 131072 | tf_op jit(solution)/shard_map/all_to_all | solution.py:342
  48.2 0.9 %shard_map.51 = f32[16,12,128]{2,1,0:T(8,128)S(1)} custom-call(f32[8,128]{1,0:T(8,128)S(1)} %get-tuple-element.17.info_ref.refs_0_, f32[8,8,256]{2,1,0:T(8,128)S(1)} %all_to_all.22.refs_1_, f32[64,128]{1,0:T(8,128)S(1)} %get-tuple-element.28.refs_2_, bf16[3,8,256,128]{3,2,1,0:T(8,128)(2,1)S(1)} %get-tuple-element.19.early_ref.refs_4_.refs_3_, ...), custom_call_target="tpu_custom_call" | custom-call | tf_op jit(solution)/shard_map/pallas_call | solution.py:262
  49.1 8.3 %all_to_all.23 = f32[16,12,128]{2,1,0:T(8,128)S(1)} all-to-all(f32[16,12,128]{2,1,0:T(8,128)S(1)} %shard_map.51), channel_id=1, replica_groups={{11,10,9,8,15,14,13,12,3,2,1,0,7,6,5,4},{27,26,25,24,31,30,29,28,19,18,..., dimensions={0} | all-to-all | bytes 196608 | tf_op jit(solution)/shard_map/all_to_all | solution.py:371
  57.5 0.6 %multiply_bitcast_fusion = f32[1536]{0:T(1024)} fusion(f32[12,128]{1,0:T(8,128)S(1)} %reduce_sum.9), kind=kLoop, calls=%fused_computation | loop fusion | flops 1536 | bytes 12288 | tf_op jit(solution)/shard_map/mul | solution.py:372
  (1 shorter events, 0.0 us)
Async XLA Ops:
  26.0 5.8 %collective-permute-start.2 = (f32[64,128]{1,0:T(8,128)S(1)}, f32[64,128]{1,0:T(8,128)S(1)}, u32[]{:S(2)}, u32[]{:S(2)}) collective-permute-start(f32[64,128]{1,0:T(8,128)S(1)} %shard_map.48.refs_1_), channel_id=1, source_target_pairs={{0,12},{1,13},{2,14},{3,15},{4,8},{5,9},{6,10},{7,11},{8,4},{9,5},... | collective-permute-start | bytes 98312 | tf_op jit(solution)/shard_map/ppermute | solution.py:27
  28.3 4.8 %collective-permute-start.1 = (f32[64,128]{1,0:T(8,128)S(1)}, f32[64,128]{1,0:T(8,128)S(1)}, u32[]{:S(2)}, u32[]{:S(2)}) collective-permute-start(f32[64,128]{1,0:T(8,128)S(1)} %shard_map.48.refs_1_), channel_id=1, source_target_pairs={{0,8},{1,9},{2,10},{3,11},{4,12},{5,13},{6,14},{7,15},{8,0},{9,1},... | collective-permute-start | bytes 98312 | tf_op jit(solution)/shard_map/ppermute | solution.py:27
  28.3 4.8 %collective-permute-start = (f32[64,128]{1,0:T(8,128)S(1)}, f32[64,128]{1,0:T(8,128)S(1)}, u32[]{:S(2)}, u32[]{:S(2)}) collective-permute-start(f32[64,128]{1,0:T(8,128)S(1)} %shard_map.48.refs_1_), channel_id=1, source_target_pairs={{0,4},{1,5},{2,6},{3,7},{4,0},{5,1},{6,2},{7,3},{8,12},{9,13},{10,... | collective-permute-start | bytes 98312 | tf_op jit(solution)/shard_map/ppermute | solution.py:27
  33.5 1.9 %collective-permute-start.3 = (f32[64,128]{1,0:T(8,128)S(1)}, f32[64,128]{1,0:T(8,128)S(1)}, u32[]{:S(2)}, u32[]{:S(2)}) collective-permute-start(f32[64,128]{1,0:T(8,128)S(1)} %get-tuple-element.24), channel_id=1, source_target_pairs={{0,1},{1,0},{2,3},{3,2},{4,5},{5,4},{6,7},{7,6},{8,9},{9,8},{10,11... | collective-permute-start | bytes 98312 | tf_op jit(solution)/shard_map/ppermute | solution.py:27
  33.5 4.0 %collective-permute-start.4 = (f32[64,128]{1,0:T(8,128)S(1)}, f32[64,128]{1,0:T(8,128)S(1)}, u32[]{:S(2)}, u32[]{:S(2)}) collective-permute-start(f32[64,128]{1,0:T(8,128)S(1)} %get-tuple-element.25), channel_id=1, source_target_pairs={{0,2},{1,3},{2,0},{3,1},{4,6},{5,7},{6,4},{7,5},{8,10},{9,11},{10,... | collective-permute-start | bytes 98312 | tf_op jit(solution)/shard_map/ppermute | solution.py:27
  35.3 3.3 %collective-permute-start.5 = (f32[64,128]{1,0:T(8,128)S(1)}, f32[64,128]{1,0:T(8,128)S(1)}, u32[]{:S(2)}, u32[]{:S(2)}) collective-permute-start(f32[64,128]{1,0:T(8,128)S(1)} %get-tuple-element.26), channel_id=1, source_target_pairs={{0,3},{1,2},{2,1},{3,0},{4,7},{5,6},{6,5},{7,4},{8,11},{9,10},{10,... | collective-permute-start | bytes 98312 | tf_op jit(solution)/shard_map/ppermute | solution.py:27

commit v10 on v8

--- a/solution.py
+++ b/solution.py
@@ -144,17 +144,24 @@
     return -(-(far * own_blocks + ID_ROWS) // 16) * 16
 
 
-def row_sums(picked_ref, lik_ref, out_ref):
+def flip_kernel(after_ref, lik_ref, out_ref):
     read_blocks, slots, reads, cols = lik_ref.shape
     for b in range(read_blocks):
+        for s in range(slots):
+            start = s % 2 * cols
+            out_ref[b, s // 2, start : start + cols, :] = jnp.transpose(lik_ref[b, s])
+
+
+def row_sums(picked_ref, flip_ref, out_ref):
+    read_blocks, pairs = flip_ref.shape[:2]
+    for b in range(read_blocks):
         total = None
-        for s in range(0, slots, 2):
-            at = b * slots + s
+        for s in range(pairs):
+            at = (b * pairs + s) * 2
             left = jnp.concatenate(
                 [split(picked_ref[at : at + 1, :]), split(picked_ref[at + 1 : at + 2, :])], axis=1
             )
-            right = jnp.concatenate([lik_ref[b, s], lik_ref[b, s + 1]], axis=1)
-            part = dot(left, right, (((1,), (1,)), ((), ())))
+            part = dot(left, flip_ref[b, s])
             total = part if total is None else total + part
         row = jnp.sum(total, axis=0, keepdims=True)
         for i in range(out_ref.shape[0]):
@@ -162,20 +169,20 @@
 
 
 def first_row_kernel(near, info_ref, *refs):
-    pieces, (lik_ref, out_ref, picked_ref) = refs[:near], refs[near:]
+    pieces, (flip_ref, out_ref, picked_ref) = refs[:near], refs[near:]
     table = jnp.concatenate([piece[...] for piece in pieces], axis=0)
     hot = hot_rows(info_ref[1:2, :], table.shape[0])
     picked_ref[...] = select_rows(hot[: picked_ref.shape[0]], table)
-    row_sums(picked_ref, lik_ref, out_ref)
+    row_sums(picked_ref, flip_ref, out_ref)
 
 
 def next_row_kernel(near, scale, *refs):
-    parts, (lik_ref, out_ref, picked_ref) = refs[:near], refs[near:]
+    parts, (flip_ref, out_ref, picked_ref) = refs[:near], refs[near:]
     total = parts[0][...]
     for part in parts[1:]:
         total = total + part[...]
     picked_ref[...] = total * scale
-    row_sums(picked_ref, lik_ref, out_ref)
+    row_sums(picked_ref, flip_ref, out_ref)
 
 
 def column_sums(parts_ref, picked_ref, lik_ref, contrib_ref, inverse_ref):
@@ -262,6 +269,17 @@
     )(*[pltpu.with_memory_space_constraint(x, pltpu.HBM) for x in (likelihood, block_ids, slot_valid)])
 
 
+def flip(after, likelihood):
+    read_blocks, slots, reads, cols = likelihood.shape
+    return pl.pallas_call(
+        flip_kernel,
+        out_shape=pltpu.VMEM((read_blocks, slots // 2, 2 * cols, reads), likelihood.dtype),
+        in_specs=[ANY, VMEM],
+        out_specs=VMEM,
+        compiler_params=pltpu.CompilerParams(vmem_limit_bytes=16 * 2**20),
+    )(after, likelihood)
+
+
 def local(likelihood, block_ids, slot_valid, start_weights):
     read_blocks, slots, reads, cols = likelihood.shape
     n = lax.axis_size(ALL)
@@ -277,6 +295,7 @@
     column = gather_far(own_weights, ALL)
     held, info = prepare(own_blocks, likelihood, block_ids, slot_valid)
     (sent,) = call(join_kernel, [(near_rows(far, own_blocks), cols)], [], *column, info)
+    flipped = flip(sent, held)
     pieces = [sent] + [swap(sent, ALL, j) for j in range(1, near)]
     at = far * own_blocks
     wanted = [info] + [piece[at : at + ID_ROWS] for piece in pieces[1:]]
@@ -286,11 +305,11 @@
     for step in range(ITERS):
         if step == 0:
             row_parts, picked = call(
-                lambda *refs: first_row_kernel(near, *refs), row_shapes, [], info, *pieces, held
+                lambda *refs: first_row_kernel(near, *refs), row_shapes, [], info, *pieces, flipped
             )
         else:
             row_parts, picked = call(
-                lambda *refs: next_row_kernel(near, scale, *refs), row_shapes, [], *parts, held
+                lambda *refs: next_row_kernel(near, scale, *refs), row_shapes, [], *parts, flipped
             )
         row_parts = lax.all_to_all(
             row_parts,

time: 57.4 us -> 56.3 us (0.981)
  waiting for transfers between devices: 9.96 us -> 8.83 us
    pallas_call x0 -> x1, Pallas kernels: none -> 1.13 us  [flip(): pl.pallas_call(flip_kernel, out_shape=pltpu.VMEM((read_blocks, slots // 2...]
    ppermute x12, waiting for transfers between devices: 9.96 us -> 8.83 us  [swap(): return lax.ppermute(x, axes, [(i, i ^ k) for i in range(n)])]
    pallas_call x6, Pallas kernels: 4.49 us -> 3.45 us  [call(): pl.pallas_call(kernel, out_shape=[jax.ShapeDtypeStruct(shape, jnp.float32...]
  transfers between devices with their start and end apart: 12 -> 12, of which waited for: 7 -> 7; matrix products, arithmetic and copies ran while one was open for 0% -> 0% of each run, Pallas kernels for 4% -> 6%
where the time goes in v10:
time: 56.3 us; the launch traced here: 55.9 us
  blocking collectives  25.5 us (45%)
  starting transfers between devices  14 us (25%)
  waiting for transfers between devices  8.83 us (16%)
  Pallas kernels  6.84 us (12%)
  other arithmetic  0.62 us (1%)
    all_to_all x2, blocking collectives, local(): lax.all_to_all(row_parts, 'genome', 0, 0, tiled=True, axis_index_groups=[...  17.2 us
    ppermute x12, starting transfers between devices, swap(): return lax.ppermute(x, axes, [(i, i ^ k) for i in range(n)])  14 us
    ppermute x12, waiting for transfers between devices, swap(): return lax.ppermute(x, axes, [(i, i ^ k) for i in range(n)])  8.83 us
    all_to_all x1, blocking collectives, local(): lax.all_to_all(counts, ALL, 0, 0, tiled=True, axis_index_groups=[order])  8.33 us
    pallas_call x6, Pallas kernels, call(): pl.pallas_call(kernel, out_shape=[jax.ShapeDtypeStruct(shape, jnp.float32...  3.45 us
    pallas_call x1, Pallas kernels, prepare(): pl.pallas_call(lambda *refs: prepare_kernel(own_blocks, *refs), out_shape...  2.26 us
    pallas_call x1, Pallas kernels, flip(): pl.pallas_call(flip_kernel, out_shape=pltpu.VMEM((read_blocks, slots // 2...  1.13 us
  transfers between devices with their start and end apart: 12, of which 7 were waited for; matrix products, arithmetic and copies ran while one was open for 0% of the time, Pallas kernels for 6%

profile of v10, /device:TPU:0, one launch (start us, length us, event | category | flops | bytes accessed | tf_op | source)
XLA Modules:
  0.0 55.9 jit_solution(9471746891615032895)
XLA Ops:
  0.0 5.0 %collective-permute-start.2 = (f32[12,128]{1,0:T(8,128)}, f32[12,128]{1,0:T(8,128)S(1)}, u32[]{:S(2)}, u32[]{:S(2)}) collective-permute-start(f32[12,128]{1,0:T(8,128)} %bitcast.3), channel_id=1, source_target_pairs={{0,12},{1,13},{2,14},{3,15},{4,8},{5,9},{6,10},{7,11},{8,4},{9,5},... | collective-permute-start | bytes 18440 | tf_op jit(solution)/shard_map/ppermute | solution.py:28
  5.1 0.6 %collective-permute-start = (f32[12,128]{1,0:T(8,128)}, f32[12,128]{1,0:T(8,128)S(1)}, u32[]{:S(2)}, u32[]{:S(2)}) collective-permute-start(f32[12,128]{1,0:T(8,128)} %bitcast.5), channel_id=1, source_target_pairs={{0,4},{1,5},{2,6},{3,7},{4,0},{5,1},{6,2},{7,3},{8,12},{9,13},{10,... | collective-permute-start | bytes 18440 | tf_op jit(solution)/shard_map/ppermute | solution.py:28
  5.7 2.3 %shard_map.46 = (bf16[8,8,256,128]{3,2,1,0:T(8,128)(2,1)S(1)}, f32[8,128]{1,0:T(8,128)S(1)}) custom-call(bf16[8,8,256,128]{3,2,1,0:T(8,128)(2,1)} %refs_0_.1, s32[8,8]{1,0:T(8,128)} %refs_1_.1, s32[8,8]{1,0:T(8,128)} %refs_2_.1), custom_call_target="tpu_custom_call" | custom-call | tf_op jit(solution)/shard_map/pallas_call | solution.py:254
  8.0 1.9 %collective-permute-done.1.refs_2_ = f32[12,128]{1,0:T(8,128)S(1)} collective-permute-done((f32[12,128]{1,0:T(8,128)}, f32[12,128]{1,0:T(8,128)S(1)}, u32[]{:S(2)}, u32[]{:S(2)}) %collective-permute-start.1) | collective-permute-done | bytes 6176 | tf_op jit(solution)/shard_map/ppermute | solution.py:28
  9.9 1.6 %collective-permute-start.4 = (f32[64,128]{1,0:T(8,128)S(1)}, f32[64,128]{1,0:T(8,128)S(1)}, u32[]{:S(2)}, u32[]{:S(2)}) collective-permute-start(f32[64,128]{1,0:T(8,128)S(1)} %shard_map.47.after_ref.refs_1_), channel_id=1, source_target_pairs={{0,2},{1,3},{2,0},{3,1},{4,6},{5,7},{6,4},{7,5},{8,10},{9,11},{10,... | collective-permute-start | bytes 98312 | tf_op jit(solution)/shard_map/ppermute | solution.py:28
  11.8 1.1 %shard_map.48.refs_5_.refs_4_ = bf16[8,4,256,256]{3,2,1,0:T(8,128)(2,1)S(1)} custom-call(f32[64,128]{1,0:T(8,128)S(1)} %shard_map.47.after_ref.refs_1_, bf16[8,8,256,128]{3,2,1,0:T(8,128)(2,1)S(1)} %get-tuple-element.16.lik_ref.refs_3_), custom_call_target="tpu_custom_call" | custom-call | tf_op jit(solution)/shard_map/pallas_call | solution.py:274
  12.9 0.6 %collective-permute-done.5.refs_4_ = f32[64,128]{1,0:T(8,128)S(1)} collective-permute-done((f32[64,128]{1,0:T(8,128)S(1)}, f32[64,128]{1,0:T(8,128)S(1)}, u32[]{:S(2)}, u32[]{:S(2)}) %collective-permute-start.5) | collective-permute-done | bytes 32800 | tf_op jit(solution)/shard_map/ppermute | solution.py:28
  13.5 0.4 collective-permute-done.4.refs_3_
  13.9 0.9 %shard_map.49 = (f32[8,8,256]{2,1,0:T(8,128)S(1)}, f32[64,128]{1,0:T(8,128)S(1)}) custom-call(f32[8,128]{1,0:T(8,128)S(1)} %get-tuple-element.15.refs_4_.refs_0_.info_ref, f32[64,128]{1,0:T(8,128)S(1)} %shard_map.47.after_ref.refs_1_, f32[64,128]{1,0:T(8,128)S(1)} %collective-permute-done.3.refs_2_, f32[64,128]{1,0:T(8,128)S(1)} %collective-permute-done.4.refs_3_, ...), custom_call_target="tpu_custom_call" | custom-call | tf_op jit(solution)/shard_map/pallas_call | solution.py:242
  14.8 8.8 %all_to_all.15.parts_ref = f32[8,8,256]{2,1,0:T(8,128)S(1)} all-to-all(f32[8,8,256]{2,1,0:T(8,128)S(1)} %get-tuple-element.17), channel_id=1, replica_groups={{10,8,14,12,2,0,6,4},{11,9,15,13,3,1,7,5},{26,24,30,28,18,16,22,20},{27..., dimensions={0} | all-to-all | bytes 131072 | tf_op jit(solution)/shard_map/all_to_all | solution.py:314
  23.6 0.7 %shard_map.50.refs_0_ = f32[72,128]{1,0:T(8,128)S(1)} custom-call(f32[8,128]{1,0:T(8,128)S(1)} %get-tuple-element.15.refs_4_.refs_0_.info_ref, f32[8,8,256]{2,1,0:T(8,128)S(1)} %all_to_all.15.parts_ref, f32[64,128]{1,0:T(8,128)S(1)} %get-tuple-element.18.picked_ref, bf16[8,8,256,128]{3,2,1,0:T(8,128)(2,1)S(1)} %get-tuple-element.16.lik_ref.refs_3_), custom_call_target="tpu_custom_call" | custom-call | tf_op jit(solution)/shard_map/pallas_call | solution.py:242
  24.3 2.3 %collective-permute-start.8 = (f32[72,128]{1,0:T(8,128)S(1)}, f32[72,128]{1,0:T(8,128)S(1)}, u32[]{:S(2)}, u32[]{:S(2)}) collective-permute-start(f32[72,128]{1,0:T(8,128)S(1)} %shard_map.50.refs_0_), channel_id=1, source_target_pairs={{0,12},{1,13},{2,14},{3,15},{4,8},{5,9},{6,10},{7,11},{8,4},{9,5},... | collective-permute-start | bytes 110600 | tf_op jit(solution)/shard_map/ppermute | solution.py:28
  26.7 2.1 %collective-permute-start.6 = (f32[72,128]{1,0:T(8,128)S(1)}, f32[72,128]{1,0:T(8,128)S(1)}, u32[]{:S(2)}, u32[]{:S(2)}) collective-permute-start(f32[72,128]{1,0:T(8,128)S(1)} %shard_map.50.refs_0_), channel_id=1, source_target_pairs={{0,4},{1,5},{2,6},{3,7},{4,0},{5,1},{6,2},{7,3},{8,12},{9,13},{10,... | collective-permute-start | bytes 110600 | tf_op jit(solution)/shard_map/ppermute | solution.py:28
  28.8 1.7 %collective-permute-done.8.refs_3_ = f32[72,128]{1,0:T(8,128)S(1)} collective-permute-done((f32[72,128]{1,0:T(8,128)S(1)}, f32[72,128]{1,0:T(8,128)S(1)}, u32[]{:S(2)}, u32[]{:S(2)}) %collective-permute-start.8) | collective-permute-done | bytes 36896 | tf_op jit(solution)/shard_map/ppermute | solution.py:28
  30.5 1.0 %collective-permute-done.7.refs_2_ = f32[72,128]{1,0:T(8,128)S(1)} collective-permute-done((f32[72,128]{1,0:T(8,128)S(1)}, f32[72,128]{1,0:T(8,128)S(1)}, u32[]{:S(2)}, u32[]{:S(2)}) %collective-permute-start.7) | collective-permute-done | bytes 36896 | tf_op jit(solution)/shard_map/ppermute | solution.py:28
  31.5 0.3 shard_map.51
  31.9 1.7 %collective-permute-start.10 = (f32[64,128]{1,0:T(8,128)S(1)}, f32[64,128]{1,0:T(8,128)S(1)}, u32[]{:S(2)}, u32[]{:S(2)}) collective-permute-start(f32[64,128]{1,0:T(8,128)S(1)} %get-tuple-element.21), channel_id=1, source_target_pairs={{0,2},{1,3},{2,0},{3,1},{4,6},{5,7},{6,4},{7,5},{8,10},{9,11},{10,... | collective-permute-start | bytes 98312 | tf_op jit(solution)/shard_map/ppermute | solution.py:28
  33.8 2.1 %collective-permute-done.10.refs_2_ = f32[64,128]{1,0:T(8,128)S(1)} collective-permute-done((f32[64,128]{1,0:T(8,128)S(1)}, f32[64,128]{1,0:T(8,128)S(1)}, u32[]{:S(2)}, u32[]{:S(2)}) %collective-permute-start.10) | collective-permute-done | bytes 32800 | tf_op jit(solution)/shard_map/ppermute | solution.py:28
  35.9 1.1 %collective-permute-done.11.refs_3_ = f32[64,128]{1,0:T(8,128)S(1)} collective-permute-done((f32[64,128]{1,0:T(8,128)S(1)}, f32[64,128]{1,0:T(8,128)S(1)}, u32[]{:S(2)}, u32[]{:S(2)}) %collective-permute-start.11) | collective-permute-done | bytes 32800 | tf_op jit(solution)/shard_map/ppermute | solution.py:28
  37.0 0.7 %shard_map.52 = (f32[8,8,256]{2,1,0:T(8,128)S(1)}, f32[64,128]{1,0:T(8,128)S(1)}) custom-call(f32[64,128]{1,0:T(8,128)S(1)} %get-tuple-element.19.refs_0_, f32[64,128]{1,0:T(8,128)S(1)} %collective-permute-done.9.refs_1_, f32[64,128]{1,0:T(8,128)S(1)} %collective-permute-done.10.refs_2_, f32[64,128]{1,0:T(8,128)S(1)} %collective-permute-done.11.refs_3_, ...), custom_call_target="tpu_custom_call" | custom-call | tf_op jit(solution)/shard_map/pallas_call | solution.py:242
  37.6 8.4 %all_to_all.16.refs_1_ = f32[8,8,256]{2,1,0:T(8,128)S(1)} all-to-all(f32[8,8,256]{2,1,0:T(8,128)S(1)} %get-tuple-element.23), channel_id=1, replica_groups={{10,8,14,12,2,0,6,4},{11,9,15,13,3,1,7,5},{26,24,30,28,18,16,22,20},{27..., dimensions={0} | all-to-all | bytes 131072 | tf_op jit(solution)/shard_map/all_to_all | solution.py:314
  46.0 0.9 %shard_map.53 = f32[16,12,128]{2,1,0:T(8,128)S(1)} custom-call(f32[8,128]{1,0:T(8,128)S(1)} %get-tuple-element.15.refs_4_.refs_0_.info_ref, f32[8,8,256]{2,1,0:T(8,128)S(1)} %all_to_all.16.refs_1_, f32[64,128]{1,0:T(8,128)S(1)} %get-tuple-element.24.refs_2_, bf16[8,8,256,128]{3,2,1,0:T(8,128)(2,1)S(1)} %get-tuple-element.16.lik_ref.refs_3_), custom_call_target="tpu_custom_call" | custom-call | tf_op jit(solution)/shard_map/pallas_call | solution.py:242
  46.9 8.3 %all_to_all.17 = f32[16,12,128]{2,1,0:T(8,128)S(1)} all-to-all(f32[16,12,128]{2,1,0:T(8,128)S(1)} %shard_map.53), channel_id=1, replica_groups={{11,10,9,8,15,14,13,12,3,2,1,0,7,6,5,4},{27,26,25,24,31,30,29,28,19,18,..., dimensions={0} | all-to-all | bytes 196608 | tf_op jit(solution)/shard_map/all_to_all | solution.py:351
  55.3 0.6 %multiply_bitcast_fusion = f32[1536]{0:T(1024)} fusion(f32[12,128]{1,0:T(8,128)S(1)} %reduce_sum.9), kind=kLoop, calls=%fused_computation | loop fusion | flops 1536 | bytes 12288 | tf_op jit(solution)/shard_map/mul | solution.py:352
  (18 shorter events, 0.6 us)
Async XLA Ops:
  0.0 9.8 %copy-start = (f32[1536]{0:T(1024)S(1)}, f32[1536]{0:T(1024)}, u32[]{:S(2)}) copy-start(f32[1536]{0:T(1024)} %param.7) | copy-start | bytes 18436
  0.0 8.0 %collective-permute-start.2 = (f32[12,128]{1,0:T(8,128)}, f32[12,128]{1,0:T(8,128)S(1)}, u32[]{:S(2)}, u32[]{:S(2)}) collective-permute-start(f32[12,128]{1,0:T(8,128)} %bitcast.3), channel_id=1, source_target_pairs={{0,12},{1,13},{2,14},{3,15},{4,8},{5,9},{6,10},{7,11},{8,4},{9,5},... | collective-permute-start | bytes 18440 | tf_op jit(solution)/shard_map/ppermute | solution.py:28
  5.1 4.8 %collective-permute-start.1 = (f32[12,128]{1,0:T(8,128)}, f32[12,128]{1,0:T(8,128)S(1)}, u32[]{:S(2)}, u32[]{:S(2)}) collective-permute-start(f32[12,128]{1,0:T(8,128)} %bitcast.4), channel_id=1, source_target_pairs={{0,8},{1,9},{2,10},{3,11},{4,12},{5,13},{6,14},{7,15},{8,0},{9,1},... | collective-permute-start | bytes 18440 | tf_op jit(solution)/shard_map/ppermute | solution.py:28
  5.1 4.8 %collective-permute-start = (f32[12,128]{1,0:T(8,128)}, f32[12,128]{1,0:T(8,128)S(1)}, u32[]{:S(2)}, u32[]{:S(2)}) collective-permute-start(f32[12,128]{1,0:T(8,128)} %bitcast.5), channel_id=1, source_target_pairs={{0,4},{1,5},{2,6},{3,7},{4,0},{5,1},{6,2},{7,3},{8,12},{9,13},{10,... | collective-permute-start | bytes 18440 | tf_op jit(solution)/shard_map/ppermute | solution.py:28
  9.8 3.7 %collective-permute-start.5 = (f32[64,128]{1,0:T(8,128)S(1)}, f32[64,128]{1,0:T(8,128)S(1)}, u32[]{:S(2)}, u32[]{:S(2)}) collective-permute-start(f32[64,128]{1,0:T(8,128)S(1)} %shard_map.47.after_ref.refs_1_), channel_id=1, source_target_pairs={{0,3},{1,2},{2,1},{3,0},{4,7},{5,6},{6,5},{7,4},{8,11},{9,10},{10,... | collective-permute-start | bytes 98312 | tf_op jit(solution)/shard_map/ppermute | solution.py:28
  9.9 4.0 %collective-permute-start.4 = (f32[64,128]{1,0:T(8,128)S(1)}, f32[64,128]{1,0:T(8,128)S(1)}, u32[]{:S(2)}, u32[]{:S(2)}) collective-permute-start(f32[64,128]{1,0:T(8,128)S(1)} %shard_map.47.after_ref.refs_1_), channel_id=1, source_target_pairs={{0,2},{1,3},{2,0},{3,1},{4,6},{5,7},{6,4},{7,5},{8,10},{9,11},{10,... | collective-permute-start | bytes 98312 | tf_op jit(solution)/shard_map/ppermute | solution.py:28
  11.5 2.4 %collective-permute-start.3 = (f32[64,128]{1,0:T(8,128)S(1)}, f32[64,128]{1,0:T(8,128)S(1)}, u32[]{:S(2)}, u32[]{:S(2)}) collective-permute-start(f32[64,128]{1,0:T(8,128)S(1)} %shard_map.47.after_ref.refs_1_), channel_id=1, source_target_pairs={{0,1},{1,0},{2,3},{3,2},{4,5},{5,4},{6,7},{7,6},{8,9},{9,8},{10,11... | collective-permute-start | bytes 98312 | tf_op jit(solution)/shard_map/ppermute | solution.py:28
  24.3 6.2 %collective-permute-start.8 = (f32[72,128]{1,0:T(8,128)S(1)}, f32[72,128]{1,0:T(8,128)S(1)}, u32[]{:S(2)}, u32[]{:S(2)}) collective-permute-start(f32[72,128]{1,0:T(8,128)S(1)} %shard_map.50.refs_0_), channel_id=1, source_target_pairs={{0,12},{1,13},{2,14},{3,15},{4,8},{5,9},{6,10},{7,11},{8,4},{9,5},... | collective-permute-start | bytes 110600 | tf_op jit(solution)/shard_map/ppermute | solution.py:28
  26.7 4.9 %collective-permute-start.7 = (f32[72,128]{1,0:T(8,128)S(1)}, f32[72,128]{1,0:T(8,128)S(1)}, u32[]{:S(2)}, u32[]{:S(2)}) collective-permute-start(f32[72,128]{1,0:T(8,128)S(1)} %shard_map.50.refs_0_), channel_id=1, source_target_pairs={{0,8},{1,9},{2,10},{3,11},{4,12},{5,13},{6,14},{7,15},{8,0},{9,1},... | collective-permute-start | bytes 110600 | tf_op jit(solution)/shard_map/ppermute | solution.py:28
  26.7 4.9 %collective-permute-start.6 = (f32[72,128]{1,0:T(8,128)S(1)}, f32[72,128]{1,0:T(8,128)S(1)}, u32[]{:S(2)}, u32[]{:S(2)}) collective-permute-start(f32[72,128]{1,0:T(8,128)S(1)} %shard_map.50.refs_0_), channel_id=1, source_target_pairs={{0,4},{1,5},{2,6},{3,7},{4,0},{5,1},{6,2},{7,3},{8,12},{9,13},{10,... | collective-permute-start | bytes 110600 | tf_op jit(solution)/shard_map/ppermute | solution.py:28
  31.8 1.9 %collective-permute-start.9 = (f32[64,128]{1,0:T(8,128)S(1)}, f32[64,128]{1,0:T(8,128)S(1)}, u32[]{:S(2)}, u32[]{:S(2)}) collective-permute-start(f32[64,128]{1,0:T(8,128)S(1)} %get-tuple-element.20), channel_id=1, source_target_pairs={{0,1},{1,0},{2,3},{3,2},{4,5},{5,4},{6,7},{7,6},{8,9},{9,8},{10,11... | collective-permute-start | bytes 98312 | tf_op jit(solution)/shard_map/ppermute | solution.py:28
  31.9 4.0 %collective-permute-start.10 = (f32[64,128]{1,0:T(8,128)S(1)}, f32[64,128]{1,0:T(8,128)S(1)}, u32[]{:S(2)}, u32[]{:S(2)}) collective-permute-start(f32[64,128]{1,0:T(8,128)S(1)} %get-tuple-element.21), channel_id=1, source_target_pairs={{0,2},{1,3},{2,0},{3,1},{4,6},{5,7},{6,4},{7,5},{8,10},{9,11},{10,... | collective-permute-start | bytes 98312 | tf_op jit(solution)/shard_map/ppermute | solution.py:28
  33.6 3.3 %collective-permute-start.11 = (f32[64,128]{1,0:T(8,128)S(1)}, f32[64,128]{1,0:T(8,128)S(1)}, u32[]{:S(2)}, u32[]{:S(2)}) collective-permute-start(f32[64,128]{1,0:T(8,128)S(1)} %get-tuple-element.22), channel_id=1, source_target_pairs={{0,3},{1,2},{2,1},{3,0},{4,7},{5,6},{6,5},{7,4},{8,11},{9,10},{10,... | collective-permute-start | bytes 98312 | tf_op jit(solution)/shard_map/ppermute | solution.py:28

commit v11 on v10

--- a/solution.py
+++ b/solution.py
@@ -49,6 +49,28 @@
         sent = parts[0] if len(parts) == 1 else jnp.concatenate(parts, axis=0)
         parts = [sent] + [swap(sent, axes, j * stride) for j in range(1, r)]
     return parts
+
+
+def gather_shared(x, axes):
+    n = lax.axis_size(axes)
+    radix = radices(n)[1:]
+    if radix[-1] != 4:
+        return gather_far(x, axes)
+    stride = n // 4
+    parts = [x]
+    step = radices(n)[0]
+    for r in radix[:-1]:
+        sent = parts[0] if len(parts) == 1 else jnp.concatenate(parts, axis=0)
+        parts = [sent] + [swap(sent, axes, j * step) for j in range(1, r)]
+        step *= r
+    x = parts[0] if len(parts) == 1 else jnp.concatenate(parts, axis=0)
+    other = lax.ppermute(x, axes, [(i, i ^ 1) for i in range(0, n, 2)])
+
+    def to(x, first, second):
+        pairs = [(i, i ^ (j * stride)) for i in range(n) if (j := (first, second)[i % 2])]
+        return lax.ppermute(x, axes, pairs)
+
+    return [x, to(x, 0, 1), to(x, 1, 2), to(x, 2, 3), to(other, 0, 3)]
 
 
 def dot(a, b, dims=(((1,), (0,)), ((), ()))):
@@ -227,6 +249,9 @@
         for at in range(0, ref.shape[0], rows):
             ids.append(ref[at + all_slots : at + all_slots + 1, :])
             values.append(ref[at : at + all_slots, :])
+    if len(ids) % 2:
+        ids.append(jnp.full_like(ids[0], -2.0))
+        values.append(jnp.zeros_like(values[0]))
     pairs = [
         jnp.where(lane < half, a, pltpu.roll(b, half, 1)) for a, b in zip(ids[::2], ids[1::2])
     ]
@@ -329,7 +354,7 @@
                 picked,
                 held,
             )
-            given = gather_far(contrib, ALL)
+            given = gather_shared(contrib, ALL)
             sums = call(
                 lambda *refs: wanted_kernel(near, all_slots, len(given), *refs),
                 [(all_slots, cols)] * near,

time: 56.3 us -> 61.6 us (1.094)
  starting transfers between devices: 14 us -> 19.4 us
    ppermute x0 -> x5, starting transfers between devices: none -> 5.52 us  [the longest x4 4.22 us: to(): return lax.ppermute(x, axes, pairs)]
    ppermute x12 -> x9, waiting for transfers between devices: 8.83 us -> 6.57 us  [swap(): return lax.ppermute(x, axes, [(i, i ^ k) for i in range(n)])]
    ppermute x0 -> x5, waiting for transfers between devices: none -> 1.96 us  [the longest x4 1.96 us: to(): return lax.ppermute(x, axes, pairs)]
    ppermute x12 -> x9, starting transfers between devices: 14 us -> 13.8 us  [swap(): return lax.ppermute(x, axes, [(i, i ^ k) for i in range(n)])]
  transfers between devices with their start and end apart: 12 -> 14, of which waited for: 7 -> 7; matrix products, arithmetic and copies ran while one was open for 0% -> 0% of each run, Pallas kernels for 6% -> 6%
where the time goes in v11:
time: 61.6 us; the launch traced here: 61.1 us
  blocking collectives  25.5 us (41%)
  starting transfers between devices  19.4 us (31%)
  waiting for transfers between devices  8.53 us (14%)
  Pallas kernels  6.93 us (11%)
  other arithmetic  0.62 us (1%)
    all_to_all x2, blocking collectives, local(): lax.all_to_all(row_parts, 'genome', 0, 0, tiled=True, axis_index_groups=[...  17.2 us
    ppermute x9, starting transfers between devices, swap(): return lax.ppermute(x, axes, [(i, i ^ k) for i in range(n)])  13.8 us
    all_to_all x1, blocking collectives, local(): lax.all_to_all(counts, ALL, 0, 0, tiled=True, axis_index_groups=[order])  8.33 us
    ppermute x9, waiting for transfers between devices, swap(): return lax.ppermute(x, axes, [(i, i ^ k) for i in range(n)])  6.57 us
    ppermute x4, starting transfers between devices, to(): return lax.ppermute(x, axes, pairs)  4.22 us
    pallas_call x6, Pallas kernels, call(): pl.pallas_call(kernel, out_shape=[jax.ShapeDtypeStruct(shape, jnp.float32...  3.54 us
    pallas_call x1, Pallas kernels, prepare(): pl.pallas_call(lambda *refs: prepare_kernel(own_blocks, *refs), out_shape...  2.26 us
    ppermute x4, waiting for transfers between devices, to(): return lax.ppermute(x, axes, pairs)  1.96 us
  transfers between devices with their start and end apart: 14, of which 7 were waited for; matrix products, arithmetic and copies ran while one was open for 0% of the time, Pallas kernels for 6%

profile of v11, /device:TPU:0, one launch (start us, length us, event | category | flops | bytes accessed | tf_op | source)
XLA Modules:
  0.0 61.1 jit_solution(9051118861777289646)
XLA Ops:
  0.0 5.0 %collective-permute-start.2 = (f32[12,128]{1,0:T(8,128)}, f32[12,128]{1,0:T(8,128)S(1)}, u32[]{:S(2)}, u32[]{:S(2)}) collective-permute-start(f32[12,128]{1,0:T(8,128)} %bitcast.3), channel_id=1, source_target_pairs={{0,12},{1,13},{2,14},{3,15},{4,8},{5,9},{6,10},{7,11},{8,4},{9,5},... | collective-permute-start | bytes 18440 | tf_op jit(solution)/shard_map/ppermute | solution.py:28
  5.1 0.6 %collective-permute-start = (f32[12,128]{1,0:T(8,128)}, f32[12,128]{1,0:T(8,128)S(1)}, u32[]{:S(2)}, u32[]{:S(2)}) collective-permute-start(f32[12,128]{1,0:T(8,128)} %bitcast.5), channel_id=1, source_target_pairs={{0,4},{1,5},{2,6},{3,7},{4,0},{5,1},{6,2},{7,3},{8,12},{9,13},{10,... | collective-permute-start | bytes 18440 | tf_op jit(solution)/shard_map/ppermute | solution.py:28
  5.7 2.3 %shard_map.46 = (bf16[8,8,256,128]{3,2,1,0:T(8,128)(2,1)S(1)}, f32[8,128]{1,0:T(8,128)S(1)}) custom-call(bf16[8,8,256,128]{3,2,1,0:T(8,128)(2,1)} %refs_0_.1, s32[8,8]{1,0:T(8,128)} %refs_1_.1, s32[8,8]{1,0:T(8,128)} %refs_2_.1), custom_call_target="tpu_custom_call" | custom-call | tf_op jit(solution)/shard_map/pallas_call | solution.py:279
  8.0 1.9 %collective-permute-done.1.refs_2_ = f32[12,128]{1,0:T(8,128)S(1)} collective-permute-done((f32[12,128]{1,0:T(8,128)}, f32[12,128]{1,0:T(8,128)S(1)}, u32[]{:S(2)}, u32[]{:S(2)}) %collective-permute-start.1) | collective-permute-done | bytes 6176 | tf_op jit(solution)/shard_map/ppermute | solution.py:28
  9.9 1.6 %collective-permute-start.4 = (f32[64,128]{1,0:T(8,128)S(1)}, f32[64,128]{1,0:T(8,128)S(1)}, u32[]{:S(2)}, u32[]{:S(2)}) collective-permute-start(f32[64,128]{1,0:T(8,128)S(1)} %shard_map.47.after_ref.refs_1_), channel_id=1, source_target_pairs={{0,2},{1,3},{2,0},{3,1},{4,6},{5,7},{6,4},{7,5},{8,10},{9,11},{10,... | collective-permute-start | bytes 98312 | tf_op jit(solution)/shard_map/ppermute | solution.py:28
  11.8 1.1 %shard_map.48.refs_5_.refs_4_ = bf16[8,4,256,256]{3,2,1,0:T(8,128)(2,1)S(1)} custom-call(f32[64,128]{1,0:T(8,128)S(1)} %shard_map.47.after_ref.refs_1_, bf16[8,8,256,128]{3,2,1,0:T(8,128)(2,1)S(1)} %get-tuple-element.16.lik_ref.refs_3_), custom_call_target="tpu_custom_call" | custom-call | tf_op jit(solution)/shard_map/pallas_call | solution.py:299
  13.9 0.9 %shard_map.49 = (f32[8,8,256]{2,1,0:T(8,128)S(1)}, f32[64,128]{1,0:T(8,128)S(1)}) custom-call(f32[8,128]{1,0:T(8,128)S(1)} %get-tuple-element.15.refs_4_.refs_0_.info_ref.refs_5_, f32[64,128]{1,0:T(8,128)S(1)} %shard_map.47.after_ref.refs_1_, f32[64,128]{1,0:T(8,128)S(1)} %collective-permute-done.3.refs_2_, f32[64,128]{1,0:T(8,128)S(1)} %collective-permute-done.4.refs_3_, ...), custom_call_target="tpu_custom_call" | custom-call | tf_op jit(solution)/shard_map/pallas_call | solution.py:267
  14.8 8.8 %all_to_all.15.parts_ref = f32[8,8,256]{2,1,0:T(8,128)S(1)} all-to-all(f32[8,8,256]{2,1,0:T(8,128)S(1)} %get-tuple-element.17), channel_id=1, replica_groups={{10,8,14,12,2,0,6,4},{11,9,15,13,3,1,7,5},{26,24,30,28,18,16,22,20},{27..., dimensions={0} | all-to-all | bytes 131072 | tf_op jit(solution)/shard_map/all_to_all | solution.py:339
  23.6 0.7 %shard_map.50.refs_0_ = f32[72,128]{1,0:T(8,128)S(1)} custom-call(f32[8,128]{1,0:T(8,128)S(1)} %get-tuple-element.15.refs_4_.refs_0_.info_ref.refs_5_, f32[8,8,256]{2,1,0:T(8,128)S(1)} %all_to_all.15.parts_ref, f32[64,128]{1,0:T(8,128)S(1)} %get-tuple-element.18.picked_ref, bf16[8,8,256,128]{3,2,1,0:T(8,128)(2,1)S(1)} %get-tuple-element.16.lik_ref.refs_3_), custom_call_target="tpu_custom_call" | custom-call | tf_op jit(solution)/shard_map/pallas_call | solution.py:267
  24.3 1.3 %collective-permute-start.9 = (f32[72,128]{1,0:T(8,128)S(1)}, f32[72,128]{1,0:T(8,128)S(1)}, u32[]{:S(2)}, u32[]{:S(2)}) collective-permute-start(f32[72,128]{1,0:T(8,128)S(1)} %shard_map.50.refs_0_), channel_id=1, source_target_pairs={{0,1},{2,3},{4,5},{6,7},{8,9},{10,11},{12,13},{14,15},{16,17},{18,... | collective-permute-start | bytes 110600 | tf_op jit(solution)/shard_map/ppermute | solution.py:67
  25.6 1.8 %collective-permute-start.8 = (f32[72,128]{1,0:T(8,128)S(1)}, f32[72,128]{1,0:T(8,128)S(1)}, u32[]{:S(2)}, u32[]{:S(2)}) collective-permute-start(f32[72,128]{1,0:T(8,128)S(1)} %shard_map.50.refs_0_), channel_id=1, source_target_pairs={{0,8},{1,13},{2,10},{3,15},{4,12},{5,9},{6,14},{7,11},{8,0},{9,5},... | collective-permute-start | bytes 110600 | tf_op jit(solution)/shard_map/ppermute | solution.py:71
  27.4 1.1 %collective-permute-start.7 = (f32[72,128]{1,0:T(8,128)S(1)}, f32[72,128]{1,0:T(8,128)S(1)}, u32[]{:S(2)}, u32[]{:S(2)}) collective-permute-start(f32[72,128]{1,0:T(8,128)S(1)} %shard_map.50.refs_0_), channel_id=1, source_target_pairs={{0,4},{1,9},{2,6},{3,11},{4,0},{5,13},{6,2},{7,15},{8,12},{9,1},{1... | collective-permute-start | bytes 110600 | tf_op jit(solution)/shard_map/ppermute | solution.py:71
  28.5 0.7 %collective-permute-start.6 = (f32[72,128]{1,0:T(8,128)S(1)}, f32[72,128]{1,0:T(8,128)S(1)}, u32[]{:S(2)}, u32[]{:S(2)}) collective-permute-start(f32[72,128]{1,0:T(8,128)S(1)} %shard_map.50.refs_0_), channel_id=1, source_target_pairs={{1,5},{3,7},{5,1},{7,3},{9,13},{11,15},{13,9},{15,11},{17,21},{19,... | collective-permute-start | bytes 110600 | tf_op jit(solution)/shard_map/ppermute | solution.py:71
  29.2 0.7 %collective-permute-start.10 = (f32[72,128]{1,0:T(8,128)S(1)}, f32[72,128]{1,0:T(8,128)S(1)}, u32[]{:S(2)}, u32[]{:S(2)}) collective-permute-start(f32[72,128]{1,0:T(8,128)S(1)} %collective-permute-done.9), channel_id=1, source_target_pairs={{1,13},{3,15},{5,9},{7,11},{9,5},{11,7},{13,1},{15,3},{17,29},{19,... | collective-permute-start | bytes 110600 | tf_op jit(solution)/shard_map/ppermute | solution.py:71
  29.9 1.2 %collective-permute-done.8.refs_3_ = f32[72,128]{1,0:T(8,128)S(1)} collective-permute-done((f32[72,128]{1,0:T(8,128)S(1)}, f32[72,128]{1,0:T(8,128)S(1)}, u32[]{:S(2)}, u32[]{:S(2)}) %collective-permute-start.8) | collective-permute-done | bytes 36896 | tf_op jit(solution)/shard_map/ppermute | solution.py:71
  31.1 0.8 %collective-permute-done.7.refs_2_ = f32[72,128]{1,0:T(8,128)S(1)} collective-permute-done((f32[72,128]{1,0:T(8,128)S(1)}, f32[72,128]{1,0:T(8,128)S(1)}, u32[]{:S(2)}, u32[]{:S(2)}) %collective-permute-start.7) | collective-permute-done | bytes 36896 | tf_op jit(solution)/shard_map/ppermute | solution.py:71
  32.3 4.6 %collective-permute-start.11 = (f32[64,128]{1,0:T(8,128)S(1)}, f32[64,128]{1,0:T(8,128)S(1)}, u32[]{:S(2)}, u32[]{:S(2)}) collective-permute-start(f32[64,128]{1,0:T(8,128)S(1)} %get-tuple-element.20), channel_id=1, source_target_pairs={{0,1},{1,0},{2,3},{3,2},{4,5},{5,4},{6,7},{7,6},{8,9},{9,8},{10,11... | collective-permute-start | bytes 98312 | tf_op jit(solution)/shard_map/ppermute | solution.py:28
  36.8 1.7 %collective-permute-start.12 = (f32[64,128]{1,0:T(8,128)S(1)}, f32[64,128]{1,0:T(8,128)S(1)}, u32[]{:S(2)}, u32[]{:S(2)}) collective-permute-start(f32[64,128]{1,0:T(8,128)S(1)} %get-tuple-element.21), channel_id=1, source_target_pairs={{0,2},{1,3},{2,0},{3,1},{4,6},{5,7},{6,4},{7,5},{8,10},{9,11},{10,... | collective-permute-start | bytes 98312 | tf_op jit(solution)/shard_map/ppermute | solution.py:28
  38.5 2.2 %collective-permute-done.12.refs_2_ = f32[64,128]{1,0:T(8,128)S(1)} collective-permute-done((f32[64,128]{1,0:T(8,128)S(1)}, f32[64,128]{1,0:T(8,128)S(1)}, u32[]{:S(2)}, u32[]{:S(2)}) %collective-permute-start.12) | collective-permute-done | bytes 32800 | tf_op jit(solution)/shard_map/ppermute | solution.py:28
  40.7 1.4 %collective-permute-done.13.refs_3_ = f32[64,128]{1,0:T(8,128)S(1)} collective-permute-done((f32[64,128]{1,0:T(8,128)S(1)}, f32[64,128]{1,0:T(8,128)S(1)}, u32[]{:S(2)}, u32[]{:S(2)}) %collective-permute-start.13) | collective-permute-done | bytes 32800 | tf_op jit(solution)/shard_map/ppermute | solution.py:28
  42.2 0.7 %shard_map.52 = (f32[8,8,256]{2,1,0:T(8,128)S(1)}, f32[64,128]{1,0:T(8,128)S(1)}) custom-call(f32[64,128]{1,0:T(8,128)S(1)} %get-tuple-element.19.refs_0_, f32[64,128]{1,0:T(8,128)S(1)} %collective-permute-done.11.refs_1_, f32[64,128]{1,0:T(8,128)S(1)} %collective-permute-done.12.refs_2_, f32[64,128]{1,0:T(8,128)S(1)} %collective-permute-done.13.refs_3_, ...), custom_call_target="tpu_custom_call" | custom-call | tf_op jit(solution)/shard_map/pallas_call | solution.py:267
  42.9 8.4 %all_to_all.16.refs_1_ = f32[8,8,256]{2,1,0:T(8,128)S(1)} all-to-all(f32[8,8,256]{2,1,0:T(8,128)S(1)} %get-tuple-element.23), channel_id=1, replica_groups={{10,8,14,12,2,0,6,4},{11,9,15,13,3,1,7,5},{26,24,30,28,18,16,22,20},{27..., dimensions={0} | all-to-all | bytes 131072 | tf_op jit(solution)/shard_map/all_to_all | solution.py:339
  51.2 0.9 %shard_map.53 = f32[16,12,128]{2,1,0:T(8,128)S(1)} custom-call(f32[8,128]{1,0:T(8,128)S(1)} %get-tuple-element.15.refs_4_.refs_0_.info_ref.refs_5_, f32[8,8,256]{2,1,0:T(8,128)S(1)} %all_to_all.16.refs_1_, f32[64,128]{1,0:T(8,128)S(1)} %get-tuple-element.24.refs_2_, bf16[8,8,256,128]{3,2,1,0:T(8,128)(2,1)S(1)} %get-tuple-element.16.lik_ref.refs_3_), custom_call_target="tpu_custom_call" | custom-call | tf_op jit(solution)/shard_map/pallas_call | solution.py:267
  52.1 8.3 %all_to_all.17 = f32[16,12,128]{2,1,0:T(8,128)S(1)} all-to-all(f32[16,12,128]{2,1,0:T(8,128)S(1)} %shard_map.53), channel_id=1, replica_groups={{11,10,9,8,15,14,13,12,3,2,1,0,7,6,5,4},{27,26,25,24,31,30,29,28,19,18,..., dimensions={0} | all-to-all | bytes 196608 | tf_op jit(solution)/shard_map/all_to_all | solution.py:376
  (22 shorter events, 2.4 us)
Async XLA Ops:
  0.0 9.8 %copy-start = (f32[1536]{0:T(1024)S(1)}, f32[1536]{0:T(1024)}, u32[]{:S(2)}) copy-start(f32[1536]{0:T(1024)} %param.7) | copy-start | bytes 18436
  0.0 8.0 %collective-permute-start.2 = (f32[12,128]{1,0:T(8,128)}, f32[12,128]{1,0:T(8,128)S(1)}, u32[]{:S(2)}, u32[]{:S(2)}) collective-permute-start(f32[12,128]{1,0:T(8,128)} %bitcast.3), channel_id=1, source_target_pairs={{0,12},{1,13},{2,14},{3,15},{4,8},{5,9},{6,10},{7,11},{8,4},{9,5},... | collective-permute-start | bytes 18440 | tf_op jit(solution)/shard_map/ppermute | solution.py:28
  5.1 4.8 %collective-permute-start.1 = (f32[12,128]{1,0:T(8,128)}, f32[12,128]{1,0:T(8,128)S(1)}, u32[]{:S(2)}, u32[]{:S(2)}) collective-permute-start(f32[12,128]{1,0:T(8,128)} %bitcast.4), channel_id=1, source_target_pairs={{0,8},{1,9},{2,10},{3,11},{4,12},{5,13},{6,14},{7,15},{8,0},{9,1},... | collective-permute-start | bytes 18440 | tf_op jit(solution)/shard_map/ppermute | solution.py:28
  5.1 4.8 %collective-permute-start = (f32[12,128]{1,0:T(8,128)}, f32[12,128]{1,0:T(8,128)S(1)}, u32[]{:S(2)}, u32[]{:S(2)}) collective-permute-start(f32[12,128]{1,0:T(8,128)} %bitcast.5), channel_id=1, source_target_pairs={{0,4},{1,5},{2,6},{3,7},{4,0},{5,1},{6,2},{7,3},{8,12},{9,13},{10,... | collective-permute-start | bytes 18440 | tf_op jit(solution)/shard_map/ppermute | solution.py:28
  9.8 3.7 %collective-permute-start.5 = (f32[64,128]{1,0:T(8,128)S(1)}, f32[64,128]{1,0:T(8,128)S(1)}, u32[]{:S(2)}, u32[]{:S(2)}) collective-permute-start(f32[64,128]{1,0:T(8,128)S(1)} %shard_map.47.after_ref.refs_1_), channel_id=1, source_target_pairs={{0,3},{1,2},{2,1},{3,0},{4,7},{5,6},{6,5},{7,4},{8,11},{9,10},{10,... | collective-permute-start | bytes 98312 | tf_op jit(solution)/shard_map/ppermute | solution.py:28
  9.9 4.0 %collective-permute-start.4 = (f32[64,128]{1,0:T(8,128)S(1)}, f32[64,128]{1,0:T(8,128)S(1)}, u32[]{:S(2)}, u32[]{:S(2)}) collective-permute-start(f32[64,128]{1,0:T(8,128)S(1)} %shard_map.47.after_ref.refs_1_), channel_id=1, source_target_pairs={{0,2},{1,3},{2,0},{3,1},{4,6},{5,7},{6,4},{7,5},{8,10},{9,11},{10,... | collective-permute-start | bytes 98312 | tf_op jit(solution)/shard_map/ppermute | solution.py:28
  11.5 2.4 %collective-permute-start.3 = (f32[64,128]{1,0:T(8,128)S(1)}, f32[64,128]{1,0:T(8,128)S(1)}, u32[]{:S(2)}, u32[]{:S(2)}) collective-permute-start(f32[64,128]{1,0:T(8,128)S(1)} %shard_map.47.after_ref.refs_1_), channel_id=1, source_target_pairs={{0,1},{1,0},{2,3},{3,2},{4,5},{5,4},{6,7},{7,6},{8,9},{9,8},{10,11... | collective-permute-start | bytes 98312 | tf_op jit(solution)/shard_map/ppermute | solution.py:28
  24.3 4.9 %collective-permute-start.9 = (f32[72,128]{1,0:T(8,128)S(1)}, f32[72,128]{1,0:T(8,128)S(1)}, u32[]{:S(2)}, u32[]{:S(2)}) collective-permute-start(f32[72,128]{1,0:T(8,128)S(1)} %shard_map.50.refs_0_), channel_id=1, source_target_pairs={{0,1},{2,3},{4,5},{6,7},{8,9},{10,11},{12,13},{14,15},{16,17},{18,... | collective-permute-start | bytes 110600 | tf_op jit(solution)/shard_map/ppermute | solution.py:67
  25.6 5.5 %collective-permute-start.8 = (f32[72,128]{1,0:T(8,128)S(1)}, f32[72,128]{1,0:T(8,128)S(1)}, u32[]{:S(2)}, u32[]{:S(2)}) collective-permute-start(f32[72,128]{1,0:T(8,128)S(1)} %shard_map.50.refs_0_), channel_id=1, source_target_pairs={{0,8},{1,13},{2,10},{3,15},{4,12},{5,9},{6,14},{7,11},{8,0},{9,5},... | collective-permute-start | bytes 110600 | tf_op jit(solution)/shard_map/ppermute | solution.py:71
  27.4 4.4 %collective-permute-start.7 = (f32[72,128]{1,0:T(8,128)S(1)}, f32[72,128]{1,0:T(8,128)S(1)}, u32[]{:S(2)}, u32[]{:S(2)}) collective-permute-start(f32[72,128]{1,0:T(8,128)S(1)} %shard_map.50.refs_0_), channel_id=1, source_target_pairs={{0,4},{1,9},{2,6},{3,11},{4,0},{5,13},{6,2},{7,15},{8,12},{9,1},{1... | collective-permute-start | bytes 110600 | tf_op jit(solution)/shard_map/ppermute | solution.py:71
  28.5 3.3 %collective-permute-start.6 = (f32[72,128]{1,0:T(8,128)S(1)}, f32[72,128]{1,0:T(8,128)S(1)}, u32[]{:S(2)}, u32[]{:S(2)}) collective-permute-start(f32[72,128]{1,0:T(8,128)S(1)} %shard_map.50.refs_0_), channel_id=1, source_target_pairs={{1,5},{3,7},{5,1},{7,3},{9,13},{11,15},{13,9},{15,11},{17,21},{19,... | collective-permute-start | bytes 110600 | tf_op jit(solution)/shard_map/ppermute | solution.py:71
  29.2 2.7 %collective-permute-start.10 = (f32[72,128]{1,0:T(8,128)S(1)}, f32[72,128]{1,0:T(8,128)S(1)}, u32[]{:S(2)}, u32[]{:S(2)}) collective-permute-start(f32[72,128]{1,0:T(8,128)S(1)} %collective-permute-done.9), channel_id=1, source_target_pairs={{1,13},{3,15},{5,9},{7,11},{9,5},{11,7},{13,1},{15,3},{17,29},{19,... | collective-permute-start | bytes 110600 | tf_op jit(solution)/shard_map/ppermute | solution.py:71
  32.3 6.2 %collective-permute-start.11 = (f32[64,128]{1,0:T(8,128)S(1)}, f32[64,128]{1,0:T(8,128)S(1)}, u32[]{:S(2)}, u32[]{:S(2)}) collective-permute-start(f32[64,128]{1,0:T(8,128)S(1)} %get-tuple-element.20), channel_id=1, source_target_pairs={{0,1},{1,0},{2,3},{3,2},{4,5},{5,4},{6,7},{7,6},{8,9},{9,8},{10,11... | collective-permute-start | bytes 98312 | tf_op jit(solution)/shard_map/ppermute | solution.py:28
  36.8 3.9 %collective-permute-start.12 = (f32[64,128]{1,0:T(8,128)S(1)}, f32[64,128]{1,0:T(8,128)S(1)}, u32[]{:S(2)}, u32[]{:S(2)}) collective-permute-start(f32[64,128]{1,0:T(8,128)S(1)} %get-tuple-element.21), channel_id=1, source_target_pairs={{0,2},{1,3},{2,0},{3,1},{4,6},{5,7},{6,4},{7,5},{8,10},{9,11},{10,... | collective-permute-start | bytes 98312 | tf_op jit(solution)/shard_map/ppermute | solution.py:28
  38.5 3.7 %collective-permute-start.13 = (f32[64,128]{1,0:T(8,128)S(1)}, f32[64,128]{1,0:T(8,128)S(1)}, u32[]{:S(2)}, u32[]{:S(2)}) collective-permute-start(f32[64,128]{1,0:T(8,128)S(1)} %get-tuple-element.22), channel_id=1, source_target_pairs={{0,3},{1,2},{2,1},{3,0},{4,7},{5,6},{6,5},{7,4},{8,11},{9,10},{10,... | collective-permute-start | bytes 98312 | tf_op jit(solution)/shard_map/ppermute | solution.py:28

commit v12 on v10

--- a/solution.py
+++ b/solution.py
@@ -47,7 +47,7 @@
     for r in radices(stride)[:0:-1]:
         stride //= r
         sent = parts[0] if len(parts) == 1 else jnp.concatenate(parts, axis=0)
-        parts = [sent] + [swap(sent, axes, j * stride) for j in range(1, r)]
+        parts = [sent] + [swap(sent, axes, j * stride + 1) for j in range(1, r)]
     return parts
 
 
@@ -121,6 +121,10 @@
     owner = ((flat + 0.5) * (1.0 / own_blocks)).astype(jnp.int32)
     inside = flat.astype(jnp.int32) - owner * own_blocks
     away = owner ^ me
+    rest = away // near
+    for r in radices(n)[1:]:
+        away = away ^ jnp.where(rest % r > 0, 1, 0)
+        rest = rest // r
     place = position(away, n)
     place = (place // far) * near_rows(far, own_blocks) + (place % far) * own_blocks + inside
     place = jnp.where(flat < 0, -1, place).astype(jnp.float32)

time: 56.3 us -> 56.2 us (level)
  waiting for transfers between devices: 8.83 us -> 9.95 us
  starting transfers between devices: 14 us -> 13.2 us
    ppermute x12, waiting for transfers between devices: 8.83 us -> 9.95 us  [swap(): return lax.ppermute(x, axes, [(i, i ^ k) for i in range(n)])]
    ppermute x12, starting transfers between devices: 14 us -> 13.2 us  [swap(): return lax.ppermute(x, axes, [(i, i ^ k) for i in range(n)])]
  transfers between devices with their start and end apart: 12 -> 12, of which waited for: 7 -> 6; matrix products, arithmetic and copies ran while one was open for 0% -> 0% of each run, Pallas kernels for 6% -> 6%
where the time goes in v12:
time: 56.2 us; the launch traced here: 55.8 us
  blocking collectives  25.1 us (45%)
  starting transfers between devices  13.2 us (23%)
  waiting for transfers between devices  9.95 us (18%)
  Pallas kernels  6.85 us (12%)
  other arithmetic  0.62 us (1%)
    all_to_all x2, blocking collectives, local(): lax.all_to_all(row_parts, 'genome', 0, 0, tiled=True, axis_index_groups=[...  16.7 us
    ppermute x12, starting transfers between devices, swap(): return lax.ppermute(x, axes, [(i, i ^ k) for i in range(n)])  13.2 us
    ppermute x12, waiting for transfers between devices, swap(): return lax.ppermute(x, axes, [(i, i ^ k) for i in range(n)])  9.95 us
    all_to_all x1, blocking collectives, local(): lax.all_to_all(counts, ALL, 0, 0, tiled=True, axis_index_groups=[order])  8.33 us
    pallas_call x6, Pallas kernels, call(): pl.pallas_call(kernel, out_shape=[jax.ShapeDtypeStruct(shape, jnp.float32...  3.46 us
    pallas_call x1, Pallas kernels, prepare(): pl.pallas_call(lambda *refs: prepare_kernel(own_blocks, *refs), out_shape...  2.26 us
    pallas_call x1, Pallas kernels, flip(): pl.pallas_call(flip_kernel, out_shape=pltpu.VMEM((read_blocks, slots // 2...  1.13 us
  transfers between devices with their start and end apart: 12, of which 6 were waited for; matrix products, arithmetic and copies ran while one was open for 0% of the time, Pallas kernels for 6%

profile of v12, /device:TPU:0, one launch (start us, length us, event | category | flops | bytes accessed | tf_op | source)
XLA Modules:
  0.0 55.8 jit_solution(5666019585751161230)
XLA Ops:
  0.0 4.5 %collective-permute-start.2 = (f32[12,128]{1,0:T(8,128)}, f32[12,128]{1,0:T(8,128)S(1)}, u32[]{:S(2)}, u32[]{:S(2)}) collective-permute-start(f32[12,128]{1,0:T(8,128)} %bitcast.3), channel_id=1, source_target_pairs={{0,13},{1,12},{2,15},{3,14},{4,9},{5,8},{6,11},{7,10},{8,5},{9,4},... | collective-permute-start | bytes 18440 | tf_op jit(solution)/shard_map/ppermute | solution.py:28
  4.5 0.9 %collective-permute-start = (f32[12,128]{1,0:T(8,128)}, f32[12,128]{1,0:T(8,128)S(1)}, u32[]{:S(2)}, u32[]{:S(2)}) collective-permute-start(f32[12,128]{1,0:T(8,128)} %bitcast.5), channel_id=1, source_target_pairs={{0,5},{1,4},{2,7},{3,6},{4,1},{5,0},{6,3},{7,2},{8,13},{9,12},{10,... | collective-permute-start | bytes 18440 | tf_op jit(solution)/shard_map/ppermute | solution.py:28
  5.4 2.3 %shard_map.46 = (bf16[8,8,256,128]{3,2,1,0:T(8,128)(2,1)S(1)}, f32[8,128]{1,0:T(8,128)S(1)}) custom-call(bf16[8,8,256,128]{3,2,1,0:T(8,128)(2,1)} %refs_0_.1, s32[8,8]{1,0:T(8,128)} %refs_1_.1, s32[8,8]{1,0:T(8,128)} %refs_2_.1), custom_call_target="tpu_custom_call" | custom-call | tf_op jit(solution)/shard_map/pallas_call | solution.py:258
  7.7 1.0 %collective-permute-done.1.refs_2_ = f32[12,128]{1,0:T(8,128)S(1)} collective-permute-done((f32[12,128]{1,0:T(8,128)}, f32[12,128]{1,0:T(8,128)S(1)}, u32[]{:S(2)}, u32[]{:S(2)}) %collective-permute-start.1) | collective-permute-done | bytes 6176 | tf_op jit(solution)/shard_map/ppermute | solution.py:28
  8.7 1.8 %collective-permute-start.5 = (f32[64,128]{1,0:T(8,128)S(1)}, f32[64,128]{1,0:T(8,128)S(1)}, u32[]{:S(2)}, u32[]{:S(2)}) collective-permute-start(f32[64,128]{1,0:T(8,128)S(1)} %shard_map.47.after_ref.refs_1_), channel_id=1, source_target_pairs={{0,3},{1,2},{2,1},{3,0},{4,7},{5,6},{6,5},{7,4},{8,11},{9,10},{10,... | collective-permute-start | bytes 98312 | tf_op jit(solution)/shard_map/ppermute | solution.py:28
  10.6 0.5 collective-permute-start.4
  11.1 1.1 %shard_map.48.refs_5_.refs_4_ = bf16[8,4,256,256]{3,2,1,0:T(8,128)(2,1)S(1)} custom-call(f32[64,128]{1,0:T(8,128)S(1)} %shard_map.47.after_ref.refs_1_, bf16[8,8,256,128]{3,2,1,0:T(8,128)(2,1)S(1)} %get-tuple-element.16.lik_ref.refs_3_), custom_call_target="tpu_custom_call" | custom-call | tf_op jit(solution)/shard_map/pallas_call | solution.py:278
  12.2 2.3 %collective-permute-done.4.refs_3_ = f32[64,128]{1,0:T(8,128)S(1)} collective-permute-done((f32[64,128]{1,0:T(8,128)S(1)}, f32[64,128]{1,0:T(8,128)S(1)}, u32[]{:S(2)}, u32[]{:S(2)}) %collective-permute-start.4) | collective-permute-done | bytes 32800 | tf_op jit(solution)/shard_map/ppermute | solution.py:28
  14.5 0.9 %shard_map.49 = (f32[8,8,256]{2,1,0:T(8,128)S(1)}, f32[64,128]{1,0:T(8,128)S(1)}) custom-call(f32[8,128]{1,0:T(8,128)S(1)} %get-tuple-element.15.refs_4_.refs_0_.info_ref, f32[64,128]{1,0:T(8,128)S(1)} %shard_map.47.after_ref.refs_1_, f32[64,128]{1,0:T(8,128)S(1)} %collective-permute-done.3.refs_2_, f32[64,128]{1,0:T(8,128)S(1)} %collective-permute-done.4.refs_3_, ...), custom_call_target="tpu_custom_call" | custom-call | tf_op jit(solution)/shard_map/pallas_call | solution.py:246
  15.4 8.4 %all_to_all.15.parts_ref = f32[8,8,256]{2,1,0:T(8,128)S(1)} all-to-all(f32[8,8,256]{2,1,0:T(8,128)S(1)} %get-tuple-element.17), channel_id=1, replica_groups={{10,8,14,12,2,0,6,4},{11,9,15,13,3,1,7,5},{26,24,30,28,18,16,22,20},{27..., dimensions={0} | all-to-all | bytes 131072 | tf_op jit(solution)/shard_map/all_to_all | solution.py:318
  23.7 0.7 %shard_map.50.refs_0_ = f32[72,128]{1,0:T(8,128)S(1)} custom-call(f32[8,128]{1,0:T(8,128)S(1)} %get-tuple-element.15.refs_4_.refs_0_.info_ref, f32[8,8,256]{2,1,0:T(8,128)S(1)} %all_to_all.15.parts_ref, f32[64,128]{1,0:T(8,128)S(1)} %get-tuple-element.18.picked_ref, bf16[8,8,256,128]{3,2,1,0:T(8,128)(2,1)S(1)} %get-tuple-element.16.lik_ref.refs_3_), custom_call_target="tpu_custom_call" | custom-call | tf_op jit(solution)/shard_map/pallas_call | solution.py:246
  24.5 2.0 %collective-permute-start.7 = (f32[72,128]{1,0:T(8,128)S(1)}, f32[72,128]{1,0:T(8,128)S(1)}, u32[]{:S(2)}, u32[]{:S(2)}) collective-permute-start(f32[72,128]{1,0:T(8,128)S(1)} %shard_map.50.refs_0_), channel_id=1, source_target_pairs={{0,9},{1,8},{2,11},{3,10},{4,13},{5,12},{6,15},{7,14},{8,1},{9,0},... | collective-permute-start | bytes 110600 | tf_op jit(solution)/shard_map/ppermute | solution.py:28
  26.5 0.6 %collective-permute-start.6 = (f32[72,128]{1,0:T(8,128)S(1)}, f32[72,128]{1,0:T(8,128)S(1)}, u32[]{:S(2)}, u32[]{:S(2)}) collective-permute-start(f32[72,128]{1,0:T(8,128)S(1)} %shard_map.50.refs_0_), channel_id=1, source_target_pairs={{0,5},{1,4},{2,7},{3,6},{4,1},{5,0},{6,3},{7,2},{8,13},{9,12},{10,... | collective-permute-start | bytes 110600 | tf_op jit(solution)/shard_map/ppermute | solution.py:28
  27.1 2.6 %collective-permute-done.8.refs_3_ = f32[72,128]{1,0:T(8,128)S(1)} collective-permute-done((f32[72,128]{1,0:T(8,128)S(1)}, f32[72,128]{1,0:T(8,128)S(1)}, u32[]{:S(2)}, u32[]{:S(2)}) %collective-permute-start.8) | collective-permute-done | bytes 36896 | tf_op jit(solution)/shard_map/ppermute | solution.py:28
  29.7 0.4 collective-permute-done.6.refs_1_
  30.4 1.1 %collective-permute-start.9 = (f32[64,128]{1,0:T(8,128)S(1)}, f32[64,128]{1,0:T(8,128)S(1)}, u32[]{:S(2)}, u32[]{:S(2)}) collective-permute-start(f32[64,128]{1,0:T(8,128)S(1)} %get-tuple-element.20), channel_id=1, source_target_pairs={{0,1},{1,0},{2,3},{3,2},{4,5},{5,4},{6,7},{7,6},{8,9},{9,8},{10,11... | collective-permute-start | bytes 98312 | tf_op jit(solution)/shard_map/ppermute | solution.py:28
  31.5 1.6 %collective-permute-start.10 = (f32[64,128]{1,0:T(8,128)S(1)}, f32[64,128]{1,0:T(8,128)S(1)}, u32[]{:S(2)}, u32[]{:S(2)}) collective-permute-start(f32[64,128]{1,0:T(8,128)S(1)} %get-tuple-element.21), channel_id=1, source_target_pairs={{0,2},{1,3},{2,0},{3,1},{4,6},{5,7},{6,4},{7,5},{8,10},{9,11},{10,... | collective-permute-start | bytes 98312 | tf_op jit(solution)/shard_map/ppermute | solution.py:28
  33.2 2.3 %collective-permute-done.10.refs_2_ = f32[64,128]{1,0:T(8,128)S(1)} collective-permute-done((f32[64,128]{1,0:T(8,128)S(1)}, f32[64,128]{1,0:T(8,128)S(1)}, u32[]{:S(2)}, u32[]{:S(2)}) %collective-permute-start.10) | collective-permute-done | bytes 32800 | tf_op jit(solution)/shard_map/ppermute | solution.py:28
  35.4 1.4 %collective-permute-done.11.refs_3_ = f32[64,128]{1,0:T(8,128)S(1)} collective-permute-done((f32[64,128]{1,0:T(8,128)S(1)}, f32[64,128]{1,0:T(8,128)S(1)}, u32[]{:S(2)}, u32[]{:S(2)}) %collective-permute-start.11) | collective-permute-done | bytes 32800 | tf_op jit(solution)/shard_map/ppermute | solution.py:28
  36.8 0.7 %shard_map.52 = (f32[8,8,256]{2,1,0:T(8,128)S(1)}, f32[64,128]{1,0:T(8,128)S(1)}) custom-call(f32[64,128]{1,0:T(8,128)S(1)} %get-tuple-element.19.refs_0_, f32[64,128]{1,0:T(8,128)S(1)} %collective-permute-done.9.refs_1_, f32[64,128]{1,0:T(8,128)S(1)} %collective-permute-done.10.refs_2_, f32[64,128]{1,0:T(8,128)S(1)} %collective-permute-done.11.refs_3_, ...), custom_call_target="tpu_custom_call" | custom-call | tf_op jit(solution)/shard_map/pallas_call | solution.py:246
  37.5 8.4 %all_to_all.16.refs_1_ = f32[8,8,256]{2,1,0:T(8,128)S(1)} all-to-all(f32[8,8,256]{2,1,0:T(8,128)S(1)} %get-tuple-element.23), channel_id=1, replica_groups={{10,8,14,12,2,0,6,4},{11,9,15,13,3,1,7,5},{26,24,30,28,18,16,22,20},{27..., dimensions={0} | all-to-all | bytes 131072 | tf_op jit(solution)/shard_map/all_to_all | solution.py:318
  45.9 0.9 %shard_map.53 = f32[16,12,128]{2,1,0:T(8,128)S(1)} custom-call(f32[8,128]{1,0:T(8,128)S(1)} %get-tuple-element.15.refs_4_.refs_0_.info_ref, f32[8,8,256]{2,1,0:T(8,128)S(1)} %all_to_all.16.refs_1_, f32[64,128]{1,0:T(8,128)S(1)} %get-tuple-element.24.refs_2_, bf16[8,8,256,128]{3,2,1,0:T(8,128)(2,1)S(1)} %get-tuple-element.16.lik_ref.refs_3_), custom_call_target="tpu_custom_call" | custom-call | tf_op jit(solution)/shard_map/pallas_call | solution.py:246
  46.8 8.3 %all_to_all.17 = f32[16,12,128]{2,1,0:T(8,128)S(1)} all-to-all(f32[16,12,128]{2,1,0:T(8,128)S(1)} %shard_map.53), channel_id=1, replica_groups={{11,10,9,8,15,14,13,12,3,2,1,0,7,6,5,4},{27,26,25,24,31,30,29,28,19,18,..., dimensions={0} | all-to-all | bytes 196608 | tf_op jit(solution)/shard_map/all_to_all | solution.py:355
  55.2 0.6 %multiply_bitcast_fusion = f32[1536]{0:T(1024)} fusion(f32[12,128]{1,0:T(8,128)S(1)} %reduce_sum.9), kind=kLoop, calls=%fused_computation | loop fusion | flops 1536 | bytes 12288 | tf_op jit(solution)/shard_map/mul | solution.py:356
  (18 shorter events, 0.5 us)
Async XLA Ops:
  0.0 8.7 %copy-start = (f32[1536]{0:T(1024)S(1)}, f32[1536]{0:T(1024)}, u32[]{:S(2)}) copy-start(f32[1536]{0:T(1024)} %param.7) | copy-start | bytes 18436
  0.0 7.7 %collective-permute-start.2 = (f32[12,128]{1,0:T(8,128)}, f32[12,128]{1,0:T(8,128)S(1)}, u32[]{:S(2)}, u32[]{:S(2)}) collective-permute-start(f32[12,128]{1,0:T(8,128)} %bitcast.3), channel_id=1, source_target_pairs={{0,13},{1,12},{2,15},{3,14},{4,9},{5,8},{6,11},{7,10},{8,5},{9,4},... | collective-permute-start | bytes 18440 | tf_op jit(solution)/shard_map/ppermute | solution.py:28
  4.5 4.2 %collective-permute-start.1 = (f32[12,128]{1,0:T(8,128)}, f32[12,128]{1,0:T(8,128)S(1)}, u32[]{:S(2)}, u32[]{:S(2)}) collective-permute-start(f32[12,128]{1,0:T(8,128)} %bitcast.4), channel_id=1, source_target_pairs={{0,9},{1,8},{2,11},{3,10},{4,13},{5,12},{6,15},{7,14},{8,1},{9,0},... | collective-permute-start | bytes 18440 | tf_op jit(solution)/shard_map/ppermute | solution.py:28
  4.5 4.2 %collective-permute-start = (f32[12,128]{1,0:T(8,128)}, f32[12,128]{1,0:T(8,128)S(1)}, u32[]{:S(2)}, u32[]{:S(2)}) collective-permute-start(f32[12,128]{1,0:T(8,128)} %bitcast.5), channel_id=1, source_target_pairs={{0,5},{1,4},{2,7},{3,6},{4,1},{5,0},{6,3},{7,2},{8,13},{9,12},{10,... | collective-permute-start | bytes 18440 | tf_op jit(solution)/shard_map/ppermute | solution.py:28
  8.7 3.5 %collective-permute-start.5 = (f32[64,128]{1,0:T(8,128)S(1)}, f32[64,128]{1,0:T(8,128)S(1)}, u32[]{:S(2)}, u32[]{:S(2)}) collective-permute-start(f32[64,128]{1,0:T(8,128)S(1)} %shard_map.47.after_ref.refs_1_), channel_id=1, source_target_pairs={{0,3},{1,2},{2,1},{3,0},{4,7},{5,6},{6,5},{7,4},{8,11},{9,10},{10,... | collective-permute-start | bytes 98312 | tf_op jit(solution)/shard_map/ppermute | solution.py:28
  10.6 3.9 %collective-permute-start.4 = (f32[64,128]{1,0:T(8,128)S(1)}, f32[64,128]{1,0:T(8,128)S(1)}, u32[]{:S(2)}, u32[]{:S(2)}) collective-permute-start(f32[64,128]{1,0:T(8,128)S(1)} %shard_map.47.after_ref.refs_1_), channel_id=1, source_target_pairs={{0,2},{1,3},{2,0},{3,1},{4,6},{5,7},{6,4},{7,5},{8,10},{9,11},{10,... | collective-permute-start | bytes 98312 | tf_op jit(solution)/shard_map/ppermute | solution.py:28
  11.1 3.4 %collective-permute-start.3 = (f32[64,128]{1,0:T(8,128)S(1)}, f32[64,128]{1,0:T(8,128)S(1)}, u32[]{:S(2)}, u32[]{:S(2)}) collective-permute-start(f32[64,128]{1,0:T(8,128)S(1)} %shard_map.47.after_ref.refs_1_), channel_id=1, source_target_pairs={{0,1},{1,0},{2,3},{3,2},{4,5},{5,4},{6,7},{7,6},{8,9},{9,8},{10,11... | collective-permute-start | bytes 98312 | tf_op jit(solution)/shard_map/ppermute | solution.py:28
  24.4 5.3 %collective-permute-start.8 = (f32[72,128]{1,0:T(8,128)S(1)}, f32[72,128]{1,0:T(8,128)S(1)}, u32[]{:S(2)}, u32[]{:S(2)}) collective-permute-start(f32[72,128]{1,0:T(8,128)S(1)} %shard_map.50.refs_0_), channel_id=1, source_target_pairs={{0,13},{1,12},{2,15},{3,14},{4,9},{5,8},{6,11},{7,10},{8,5},{9,4},... | collective-permute-start | bytes 110600 | tf_op jit(solution)/shard_map/ppermute | solution.py:28
  24.5 5.2 %collective-permute-start.7 = (f32[72,128]{1,0:T(8,128)S(1)}, f32[72,128]{1,0:T(8,128)S(1)}, u32[]{:S(2)}, u32[]{:S(2)}) collective-permute-start(f32[72,128]{1,0:T(8,128)S(1)} %shard_map.50.refs_0_), channel_id=1, source_target_pairs={{0,9},{1,8},{2,11},{3,10},{4,13},{5,12},{6,15},{7,14},{8,1},{9,0},... | collective-permute-start | bytes 110600 | tf_op jit(solution)/shard_map/ppermute | solution.py:28
  26.5 3.6 %collective-permute-start.6 = (f32[72,128]{1,0:T(8,128)S(1)}, f32[72,128]{1,0:T(8,128)S(1)}, u32[]{:S(2)}, u32[]{:S(2)}) collective-permute-start(f32[72,128]{1,0:T(8,128)S(1)} %shard_map.50.refs_0_), channel_id=1, source_target_pairs={{0,5},{1,4},{2,7},{3,6},{4,1},{5,0},{6,3},{7,2},{8,13},{9,12},{10,... | collective-permute-start | bytes 110600 | tf_op jit(solution)/shard_map/ppermute | solution.py:28
  30.4 2.8 %collective-permute-start.9 = (f32[64,128]{1,0:T(8,128)S(1)}, f32[64,128]{1,0:T(8,128)S(1)}, u32[]{:S(2)}, u32[]{:S(2)}) collective-permute-start(f32[64,128]{1,0:T(8,128)S(1)} %get-tuple-element.20), channel_id=1, source_target_pairs={{0,1},{1,0},{2,3},{3,2},{4,5},{5,4},{6,7},{7,6},{8,9},{9,8},{10,11... | collective-permute-start | bytes 98312 | tf_op jit(solution)/shard_map/ppermute | solution.py:28
  31.5 3.9 %collective-permute-start.10 = (f32[64,128]{1,0:T(8,128)S(1)}, f32[64,128]{1,0:T(8,128)S(1)}, u32[]{:S(2)}, u32[]{:S(2)}) collective-permute-start(f32[64,128]{1,0:T(8,128)S(1)} %get-tuple-element.21), channel_id=1, source_target_pairs={{0,2},{1,3},{2,0},{3,1},{4,6},{5,7},{6,4},{7,5},{8,10},{9,11},{10,... | collective-permute-start | bytes 98312 | tf_op jit(solution)/shard_map/ppermute | solution.py:28
  33.2 3.7 %collective-permute-start.11 = (f32[64,128]{1,0:T(8,128)S(1)}, f32[64,128]{1,0:T(8,128)S(1)}, u32[]{:S(2)}, u32[]{:S(2)}) collective-permute-start(f32[64,128]{1,0:T(8,128)S(1)} %get-tuple-element.22), channel_id=1, source_target_pairs={{0,3},{1,2},{2,1},{3,0},{4,7},{5,6},{6,5},{7,4},{8,11},{9,10},{10,... | collective-permute-start | bytes 98312 | tf_op jit(solution)/shard_map/ppermute | solution.py:28

commit v13 on v12

--- a/solution.py
+++ b/solution.py
@@ -93,16 +93,25 @@
     return blocks[0] if len(blocks) == 1 else jnp.concatenate(blocks, axis=1)
 
 
-def prepare_kernel(own_blocks, lik_ref, ids_ref, valid_ref, held_ref, info_ref, ids, valid, wide, sems):
+def prepare_kernel(
+    own_blocks,
+    lik_ref,
+    ids_ref,
+    valid_ref,
+    held_ref,
+    info_ref,
+    ids,
+    valid,
+    wide,
+    sems,
+    held_sems,
+):
     read_blocks, slots = ids.shape
     copies = [
         pltpu.make_async_copy(ids_ref, ids, sems.at[0]),
         pltpu.make_async_copy(valid_ref, valid, sems.at[1]),
     ]
-    held = [
-        pltpu.make_async_copy(lik_ref.at[b], held_ref.at[b], sems.at[2 + b])
-        for b in range(held_ref.shape[0])
-    ]
+    held = block_copies(lik_ref, held_ref, held_sems, 0)
     for copy in copies + held:
         copy.start()
     for copy in copies:
@@ -148,12 +157,32 @@
     return -(-(far * own_blocks + ID_ROWS) // 16) * 16
 
 
-def flip_kernel(after_ref, lik_ref, out_ref):
-    read_blocks, slots, reads, cols = lik_ref.shape
-    for b in range(read_blocks):
+def flip_kernel(after_ref, early_ref, lik_ref, late_ref, out_ref, sems):
+    early = early_ref.shape[0]
+    copies = block_copies(lik_ref, late_ref, sems, early)
+    for copy in copies:
+        copy.start()
+    for b in range(out_ref.shape[0]):
+        if b >= early:
+            copies[b - early].wait()
+        held_ref = block_of((early_ref, late_ref), b)
+        slots, reads, cols = held_ref.shape
         for s in range(slots):
             start = s % 2 * cols
-            out_ref[b, s // 2, start : start + cols, :] = jnp.transpose(lik_ref[b, s])
+            out_ref[b, s // 2, start : start + cols, :] = jnp.transpose(held_ref[s])
+
+
+def block_copies(lik_ref, held_ref, sems, start):
+    return [
+        pltpu.make_async_copy(lik_ref.at[start + b], held_ref.at[b], sems.at[b])
+        for b in range(held_ref.shape[0])
+    ]
+
+
+def block_of(held_refs, b):
+    early_ref, late_ref = held_refs
+    early = early_ref.shape[0]
+    return early_ref.at[b] if b < early else late_ref.at[b - early]
 
 
 def row_sums(picked_ref, flip_ref, out_ref):
@@ -189,29 +218,32 @@
     row_sums(picked_ref, flip_ref, out_ref)
 
 
-def column_sums(parts_ref, picked_ref, lik_ref, contrib_ref, inverse_ref):
-    read_blocks, slots, reads, cols = lik_ref.shape
+def column_sums(parts_ref, picked_ref, held_refs, contrib_ref, inverse_ref):
+    slots, reads, cols = held_refs[0].shape[1:]
     total = parts_ref[0]
     for i in range(1, parts_ref.shape[0]):
         total = total + parts_ref[i]
     inverse_ref[...] = 1.0 / total
-    for b in range(read_blocks):
+    for b in range(inverse_ref.shape[0]):
+        held_ref = block_of(held_refs, b)
         left = split(inverse_ref[b : b + 1, :])
         for s in range(0, slots, 2):
             at = b * slots + s
-            right = jnp.concatenate([lik_ref[b, s], lik_ref[b, s + 1]], axis=1)
+            right = jnp.concatenate([held_ref[s], held_ref[s + 1]], axis=1)
             summed = jnp.sum(dot(left, right), axis=0, keepdims=True)
             contrib_ref[at : at + 1, :] = picked_ref[at : at + 1, :] * summed[:, :cols]
             contrib_ref[at + 1 : at + 2, :] = picked_ref[at + 1 : at + 2, :] * summed[:, cols:]
 
 
-def column_kernel(info_ref, parts_ref, picked_ref, lik_ref, out_ref, inverse_ref):
-    column_sums(parts_ref, picked_ref, lik_ref, out_ref, inverse_ref)
+def column_kernel(info_ref, parts_ref, picked_ref, early_ref, late_ref, out_ref, inverse_ref):
+    column_sums(parts_ref, picked_ref, (early_ref, late_ref), out_ref, inverse_ref)
     out_ref[picked_ref.shape[0] :, :] = info_ref[...]
 
 
-def last_column_kernel(order, info_ref, parts_ref, picked_ref, lik_ref, out_ref, inverse_ref, contrib_ref):
-    column_sums(parts_ref, picked_ref, lik_ref, contrib_ref, inverse_ref)
+def last_column_kernel(
+    order, info_ref, parts_ref, picked_ref, early_ref, late_ref, out_ref, inverse_ref, contrib_ref
+):
+    column_sums(parts_ref, picked_ref, (early_ref, late_ref), contrib_ref, inverse_ref)
     owners, own_blocks, cols = out_ref.shape
     all_slots = contrib_ref.shape[0]
     block = lax.broadcasted_iota(jnp.int32, (owners * own_blocks, all_slots), 0)
@@ -249,16 +281,23 @@
         in_specs=[VMEM] * len(operands),
         out_specs=[VMEM] * len(outs),
         scratch_shapes=[pltpu.VMEM(shape, jnp.float32) for shape in scratch],
-        compiler_params=pltpu.CompilerParams(vmem_limit_bytes=16 * 2**20),
+        compiler_params=PARAMS,
     )(*operands)
 
 
-def prepare(own_blocks, likelihood, block_ids, slot_valid):
+PARAMS = pltpu.CompilerParams(vmem_limit_bytes=16 * 2**20)
+
+
+def in_hbm(*arrays):
+    return [pltpu.with_memory_space_constraint(x, pltpu.HBM) for x in arrays]
+
+
+def prepare(own_blocks, early, likelihood, block_ids, slot_valid):
     read_blocks, slots = block_ids.shape
     return pl.pallas_call(
         lambda *refs: prepare_kernel(own_blocks, *refs),
         out_shape=[
-            pltpu.VMEM(likelihood.shape, likelihood.dtype),
+            pltpu.VMEM((early,) + likelihood.shape[1:], likelihood.dtype),
             jax.ShapeDtypeStruct((ID_ROWS, LANES), jnp.float32),
         ],
         in_specs=[ANY] * 3,
@@ -267,21 +306,27 @@
             pltpu.VMEM((read_blocks, slots), jnp.int32),
             pltpu.VMEM((read_blocks, slots), jnp.int32),
             pltpu.VMEM((read_blocks, LANES), jnp.float32),
-            pltpu.SemaphoreType.DMA((2 + read_blocks,)),
+            pltpu.SemaphoreType.DMA((2,)),
+            pltpu.SemaphoreType.DMA((early,)),
         ],
-        compiler_params=pltpu.CompilerParams(vmem_limit_bytes=16 * 2**20),
-    )(*[pltpu.with_memory_space_constraint(x, pltpu.HBM) for x in (likelihood, block_ids, slot_valid)])
-
-
-def flip(after, likelihood):
+        compiler_params=PARAMS,
+    )(*in_hbm(likelihood, block_ids, slot_valid))
+
+
+def flip(after, held, likelihood):
     read_blocks, slots, reads, cols = likelihood.shape
+    late = read_blocks - held.shape[0]
     return pl.pallas_call(
         flip_kernel,
-        out_shape=pltpu.VMEM((read_blocks, slots // 2, 2 * cols, reads), likelihood.dtype),
-        in_specs=[ANY, VMEM],
-        out_specs=VMEM,
-        compiler_params=pltpu.CompilerParams(vmem_limit_bytes=16 * 2**20),
-    )(after, likelihood)
+        out_shape=[
+            pltpu.VMEM((late,) + likelihood.shape[1:], likelihood.dtype),
+            pltpu.VMEM((read_blocks, slots // 2, 2 * cols, reads), likelihood.dtype),
+        ],
+        in_specs=[ANY, VMEM, ANY],
+        out_specs=[VMEM] * 2,
+        scratch_shapes=[pltpu.SemaphoreType.DMA((late,))],
+        compiler_params=PARAMS,
+    )(after, held, *in_hbm(likelihood))
 
 
 def local(likelihood, block_ids, slot_valid, start_weights):
@@ -297,9 +342,9 @@
     scale = n * own_blocks * cols / total_reads
 
     column = gather_far(own_weights, ALL)
-    held, info = prepare(own_blocks, likelihood, block_ids, slot_valid)
+    held, info = prepare(own_blocks, read_blocks // 2, likelihood, block_ids, slot_valid)
     (sent,) = call(join_kernel, [(near_rows(far, own_blocks), cols)], [], *column, info)
-    flipped = flip(sent, held)
+    rest, flipped = flip(sent, held, likelihood)
     pieces = [sent] + [swap(sent, ALL, j) for j in range(1, near)]
     at = far * own_blocks
     wanted = [info] + [piece[at : at + ID_ROWS] for piece in pieces[1:]]
@@ -332,6 +377,7 @@
                 row_parts,
                 picked,
                 held,
+                rest,
             )
             given = gather_far(contrib, ALL)
             sums = call(
@@ -351,6 +397,7 @@
         row_parts,
         picked,
         held,
+        rest,
     )
     counts = lax.all_to_all(counts, ALL, 0, 0, tiled=True, axis_index_groups=[order])
     return (jnp.sum(counts, axis=0) * scale).reshape(-1)

time: 56.2 us -> 56.3 us (level)
    pallas_call x1, Pallas kernels: 1.13 us -> 1.84 us  [flip(): pl.pallas_call(flip_kernel, out_shape=[pltpu.VMEM((late,) + likelihood.sh...]
    pallas_call x1, Pallas kernels: 2.26 us -> 1.6 us  [prepare(): pl.pallas_call(lambda *refs: prepare_kernel(own_blocks, *refs), out_shape...]
where the time goes in v13:
time: 56.3 us; the launch traced here: 55.8 us
  blocking collectives  25.1 us (45%)
  starting transfers between devices  13.2 us (23%)
  waiting for transfers between devices  9.91 us (18%)
  Pallas kernels  6.9 us (12%)
  other arithmetic  0.62 us (1%)
    all_to_all x2, blocking collectives, local(): lax.all_to_all(row_parts, 'genome', 0, 0, tiled=True, axis_index_groups=[...  16.7 us
    ppermute x12, starting transfers between devices, swap(): return lax.ppermute(x, axes, [(i, i ^ k) for i in range(n)])  13.2 us
    ppermute x12, waiting for transfers between devices, swap(): return lax.ppermute(x, axes, [(i, i ^ k) for i in range(n)])  9.91 us
    all_to_all x1, blocking collectives, local(): lax.all_to_all(counts, ALL, 0, 0, tiled=True, axis_index_groups=[order])  8.33 us
    pallas_call x6, Pallas kernels, call(): pl.pallas_call(kernel, out_shape=[jax.ShapeDtypeStruct(shape, jnp.float32...  3.47 us
    pallas_call x1, Pallas kernels, flip(): pl.pallas_call(flip_kernel, out_shape=[pltpu.VMEM((late,) + likelihood.sh...  1.84 us
    pallas_call x1, Pallas kernels, prepare(): pl.pallas_call(lambda *refs: prepare_kernel(own_blocks, *refs), out_shape...  1.6 us
  transfers between devices with their start and end apart: 12, of which 6 were waited for; matrix products, arithmetic and copies ran while one was open for 0% of the time, Pallas kernels for 6%

profile of v13, /device:TPU:0, one launch (start us, length us, event | category | flops | bytes accessed | tf_op | source)
XLA Modules:
  0.0 55.8 jit_solution(13923495307101741357)
XLA Ops:
  0.0 4.5 %collective-permute-start.2 = (f32[12,128]{1,0:T(8,128)}, f32[12,128]{1,0:T(8,128)S(1)}, u32[]{:S(2)}, u32[]{:S(2)}) collective-permute-start(f32[12,128]{1,0:T(8,128)} %bitcast.3), channel_id=1, source_target_pairs={{0,13},{1,12},{2,15},{3,14},{4,9},{5,8},{6,11},{7,10},{8,5},{9,4},... | collective-permute-start | bytes 18440 | tf_op jit(solution)/shard_map/ppermute | solution.py:28
  4.5 0.9 %collective-permute-start = (f32[12,128]{1,0:T(8,128)}, f32[12,128]{1,0:T(8,128)S(1)}, u32[]{:S(2)}, u32[]{:S(2)}) collective-permute-start(f32[12,128]{1,0:T(8,128)} %bitcast.5), channel_id=1, source_target_pairs={{0,5},{1,4},{2,7},{3,6},{4,1},{5,0},{6,3},{7,2},{8,13},{9,12},{10,... | collective-permute-start | bytes 18440 | tf_op jit(solution)/shard_map/ppermute | solution.py:28
  5.4 1.6 %shard_map.46 = (bf16[4,8,256,128]{3,2,1,0:T(8,128)(2,1)S(1)}, f32[8,128]{1,0:T(8,128)S(1)}) custom-call(bf16[8,8,256,128]{3,2,1,0:T(8,128)(2,1)} %lik_ref.1, s32[8,8]{1,0:T(8,128)} %refs_1_.1, s32[8,8]{1,0:T(8,128)} %refs_2_.1), custom_call_target="tpu_custom_call" | custom-call | tf_op jit(solution)/shard_map/pallas_call | solution.py:297
  7.0 1.7 %collective-permute-done.1.refs_2_ = f32[12,128]{1,0:T(8,128)S(1)} collective-permute-done((f32[12,128]{1,0:T(8,128)}, f32[12,128]{1,0:T(8,128)S(1)}, u32[]{:S(2)}, u32[]{:S(2)}) %collective-permute-start.1) | collective-permute-done | bytes 6176 | tf_op jit(solution)/shard_map/ppermute | solution.py:28
  8.7 1.8 %collective-permute-start.5 = (f32[64,128]{1,0:T(8,128)S(1)}, f32[64,128]{1,0:T(8,128)S(1)}, u32[]{:S(2)}, u32[]{:S(2)}) collective-permute-start(f32[64,128]{1,0:T(8,128)S(1)} %shard_map.47.after_ref.refs_1_), channel_id=1, source_target_pairs={{0,3},{1,2},{2,1},{3,0},{4,7},{5,6},{6,5},{7,4},{8,11},{9,10},{10,... | collective-permute-start | bytes 98312 | tf_op jit(solution)/shard_map/ppermute | solution.py:28
  10.6 0.5 collective-permute-start.4
  11.1 1.8 %shard_map.48 = (bf16[4,8,256,128]{3,2,1,0:T(8,128)(2,1)S(1)}, bf16[8,4,256,256]{3,2,1,0:T(8,128)(2,1)S(1)}) custom-call(f32[64,128]{1,0:T(8,128)S(1)} %shard_map.47.after_ref.refs_1_, bf16[4,8,256,128]{3,2,1,0:T(8,128)(2,1)S(1)} %get-tuple-element.18.early_ref.refs_3_, bf16[8,8,256,128]{3,2,1,0:T(8,128)(2,1)} %lik_ref.1), custom_call_target="tpu_custom_call" | custom-call | tf_op jit(solution)/shard_map/pallas_call | solution.py:319
  12.9 1.5 %collective-permute-done.4.refs_3_ = f32[64,128]{1,0:T(8,128)S(1)} collective-permute-done((f32[64,128]{1,0:T(8,128)S(1)}, f32[64,128]{1,0:T(8,128)S(1)}, u32[]{:S(2)}, u32[]{:S(2)}) %collective-permute-start.4) | collective-permute-done | bytes 32800 | tf_op jit(solution)/shard_map/ppermute | solution.py:28
  14.5 0.9 %shard_map.49 = (f32[8,8,256]{2,1,0:T(8,128)S(1)}, f32[64,128]{1,0:T(8,128)S(1)}) custom-call(f32[8,128]{1,0:T(8,128)S(1)} %get-tuple-element.17.refs_4_.refs_0_.info_ref, f32[64,128]{1,0:T(8,128)S(1)} %shard_map.47.after_ref.refs_1_, f32[64,128]{1,0:T(8,128)S(1)} %collective-permute-done.3.refs_2_, f32[64,128]{1,0:T(8,128)S(1)} %collective-permute-done.4.refs_3_, ...), custom_call_target="tpu_custom_call" | custom-call | tf_op jit(solution)/shard_map/pallas_call | solution.py:278
  15.4 8.4 %all_to_all.15.parts_ref = f32[8,8,256]{2,1,0:T(8,128)S(1)} all-to-all(f32[8,8,256]{2,1,0:T(8,128)S(1)} %get-tuple-element.20), channel_id=1, replica_groups={{10,8,14,12,2,0,6,4},{11,9,15,13,3,1,7,5},{26,24,30,28,18,16,22,20},{27..., dimensions={0} | all-to-all | bytes 131072 | tf_op jit(solution)/shard_map/all_to_all | solution.py:363
  23.7 0.7 %shard_map.50.refs_0_ = f32[72,128]{1,0:T(8,128)S(1)} custom-call(f32[8,128]{1,0:T(8,128)S(1)} %get-tuple-element.17.refs_4_.refs_0_.info_ref, f32[8,8,256]{2,1,0:T(8,128)S(1)} %all_to_all.15.parts_ref, f32[64,128]{1,0:T(8,128)S(1)} %get-tuple-element.21.picked_ref, bf16[4,8,256,128]{3,2,1,0:T(8,128)(2,1)S(1)} %get-tuple-element.18.early_ref.refs_3_, ...), custom_call_target="tpu_custom_call" | custom-call | tf_op jit(solution)/shard_map/pallas_call | solution.py:278
  24.5 2.0 %collective-permute-start.7 = (f32[72,128]{1,0:T(8,128)S(1)}, f32[72,128]{1,0:T(8,128)S(1)}, u32[]{:S(2)}, u32[]{:S(2)}) collective-permute-start(f32[72,128]{1,0:T(8,128)S(1)} %shard_map.50.refs_0_), channel_id=1, source_target_pairs={{0,9},{1,8},{2,11},{3,10},{4,13},{5,12},{6,15},{7,14},{8,1},{9,0},... | collective-permute-start | bytes 110600 | tf_op jit(solution)/shard_map/ppermute | solution.py:28
  26.5 0.6 %collective-permute-start.6 = (f32[72,128]{1,0:T(8,128)S(1)}, f32[72,128]{1,0:T(8,128)S(1)}, u32[]{:S(2)}, u32[]{:S(2)}) collective-permute-start(f32[72,128]{1,0:T(8,128)S(1)} %shard_map.50.refs_0_), channel_id=1, source_target_pairs={{0,5},{1,4},{2,7},{3,6},{4,1},{5,0},{6,3},{7,2},{8,13},{9,12},{10,... | collective-permute-start | bytes 110600 | tf_op jit(solution)/shard_map/ppermute | solution.py:28
  27.1 2.6 %collective-permute-done.8.refs_3_ = f32[72,128]{1,0:T(8,128)S(1)} collective-permute-done((f32[72,128]{1,0:T(8,128)S(1)}, f32[72,128]{1,0:T(8,128)S(1)}, u32[]{:S(2)}, u32[]{:S(2)}) %collective-permute-start.8) | collective-permute-done | bytes 36896 | tf_op jit(solution)/shard_map/ppermute | solution.py:28
  29.7 0.4 collective-permute-done.6.refs_1_
  30.4 1.1 %collective-permute-start.9 = (f32[64,128]{1,0:T(8,128)S(1)}, f32[64,128]{1,0:T(8,128)S(1)}, u32[]{:S(2)}, u32[]{:S(2)}) collective-permute-start(f32[64,128]{1,0:T(8,128)S(1)} %get-tuple-element.24), channel_id=1, source_target_pairs={{0,1},{1,0},{2,3},{3,2},{4,5},{5,4},{6,7},{7,6},{8,9},{9,8},{10,11... | collective-permute-start | bytes 98312 | tf_op jit(solution)/shard_map/ppermute | solution.py:28
  31.5 1.6 %collective-permute-start.10 = (f32[64,128]{1,0:T(8,128)S(1)}, f32[64,128]{1,0:T(8,128)S(1)}, u32[]{:S(2)}, u32[]{:S(2)}) collective-permute-start(f32[64,128]{1,0:T(8,128)S(1)} %get-tuple-element.25), channel_id=1, source_target_pairs={{0,2},{1,3},{2,0},{3,1},{4,6},{5,7},{6,4},{7,5},{8,10},{9,11},{10,... | collective-permute-start | bytes 98312 | tf_op jit(solution)/shard_map/ppermute | solution.py:28
  33.2 2.3 %collective-permute-done.10.refs_2_ = f32[64,128]{1,0:T(8,128)S(1)} collective-permute-done((f32[64,128]{1,0:T(8,128)S(1)}, f32[64,128]{1,0:T(8,128)S(1)}, u32[]{:S(2)}, u32[]{:S(2)}) %collective-permute-start.10) | collective-permute-done | bytes 32800 | tf_op jit(solution)/shard_map/ppermute | solution.py:28
  35.5 1.4 %collective-permute-done.11.refs_3_ = f32[64,128]{1,0:T(8,128)S(1)} collective-permute-done((f32[64,128]{1,0:T(8,128)S(1)}, f32[64,128]{1,0:T(8,128)S(1)}, u32[]{:S(2)}, u32[]{:S(2)}) %collective-permute-start.11) | collective-permute-done | bytes 32800 | tf_op jit(solution)/shard_map/ppermute | solution.py:28
  36.8 0.7 %shard_map.52 = (f32[8,8,256]{2,1,0:T(8,128)S(1)}, f32[64,128]{1,0:T(8,128)S(1)}) custom-call(f32[64,128]{1,0:T(8,128)S(1)} %get-tuple-element.23.refs_0_, f32[64,128]{1,0:T(8,128)S(1)} %collective-permute-done.9.refs_1_, f32[64,128]{1,0:T(8,128)S(1)} %collective-permute-done.10.refs_2_, f32[64,128]{1,0:T(8,128)S(1)} %collective-permute-done.11.refs_3_, ...), custom_call_target="tpu_custom_call" | custom-call | tf_op jit(solution)/shard_map/pallas_call | solution.py:278
  37.5 8.4 %all_to_all.16.refs_1_ = f32[8,8,256]{2,1,0:T(8,128)S(1)} all-to-all(f32[8,8,256]{2,1,0:T(8,128)S(1)} %get-tuple-element.27), channel_id=1, replica_groups={{10,8,14,12,2,0,6,4},{11,9,15,13,3,1,7,5},{26,24,30,28,18,16,22,20},{27..., dimensions={0} | all-to-all | bytes 131072 | tf_op jit(solution)/shard_map/all_to_all | solution.py:363
  45.9 0.9 %shard_map.53 = f32[16,12,128]{2,1,0:T(8,128)S(1)} custom-call(f32[8,128]{1,0:T(8,128)S(1)} %get-tuple-element.17.refs_4_.refs_0_.info_ref, f32[8,8,256]{2,1,0:T(8,128)S(1)} %all_to_all.16.refs_1_, f32[64,128]{1,0:T(8,128)S(1)} %get-tuple-element.28.refs_2_, bf16[4,8,256,128]{3,2,1,0:T(8,128)(2,1)S(1)} %get-tuple-element.18.early_ref.refs_3_, ...), custom_call_target="tpu_custom_call" | custom-call | tf_op jit(solution)/shard_map/pallas_call | solution.py:278
  46.8 8.3 %all_to_all.17 = f32[16,12,128]{2,1,0:T(8,128)S(1)} all-to-all(f32[16,12,128]{2,1,0:T(8,128)S(1)} %shard_map.53), channel_id=1, replica_groups={{11,10,9,8,15,14,13,12,3,2,1,0,7,6,5,4},{27,26,25,24,31,30,29,28,19,18,..., dimensions={0} | all-to-all | bytes 196608 | tf_op jit(solution)/shard_map/all_to_all | solution.py:402
  55.2 0.6 %multiply_bitcast_fusion = f32[1536]{0:T(1024)} fusion(f32[12,128]{1,0:T(8,128)S(1)} %reduce_sum.9), kind=kLoop, calls=%fused_computation | loop fusion | flops 1536 | bytes 12288 | tf_op jit(solution)/shard_map/mul | solution.py:403
  (18 shorter events, 0.5 us)
Async XLA Ops:
  0.0 8.7 %copy-start = (f32[1536]{0:T(1024)S(1)}, f32[1536]{0:T(1024)}, u32[]{:S(2)}) copy-start(f32[1536]{0:T(1024)} %param.7) | copy-start | bytes 18436
  0.0 7.0 %collective-permute-start.2 = (f32[12,128]{1,0:T(8,128)}, f32[12,128]{1,0:T(8,128)S(1)}, u32[]{:S(2)}, u32[]{:S(2)}) collective-permute-start(f32[12,128]{1,0:T(8,128)} %bitcast.3), channel_id=1, source_target_pairs={{0,13},{1,12},{2,15},{3,14},{4,9},{5,8},{6,11},{7,10},{8,5},{9,4},... | collective-permute-start | bytes 18440 | tf_op jit(solution)/shard_map/ppermute | solution.py:28
  4.5 4.2 %collective-permute-start.1 = (f32[12,128]{1,0:T(8,128)}, f32[12,128]{1,0:T(8,128)S(1)}, u32[]{:S(2)}, u32[]{:S(2)}) collective-permute-start(f32[12,128]{1,0:T(8,128)} %bitcast.4), channel_id=1, source_target_pairs={{0,9},{1,8},{2,11},{3,10},{4,13},{5,12},{6,15},{7,14},{8,1},{9,0},... | collective-permute-start | bytes 18440 | tf_op jit(solution)/shard_map/ppermute | solution.py:28
  4.5 4.2 %collective-permute-start = (f32[12,128]{1,0:T(8,128)}, f32[12,128]{1,0:T(8,128)S(1)}, u32[]{:S(2)}, u32[]{:S(2)}) collective-permute-start(f32[12,128]{1,0:T(8,128)} %bitcast.5), channel_id=1, source_target_pairs={{0,5},{1,4},{2,7},{3,6},{4,1},{5,0},{6,3},{7,2},{8,13},{9,12},{10,... | collective-permute-start | bytes 18440 | tf_op jit(solution)/shard_map/ppermute | solution.py:28
  8.7 4.2 %collective-permute-start.5 = (f32[64,128]{1,0:T(8,128)S(1)}, f32[64,128]{1,0:T(8,128)S(1)}, u32[]{:S(2)}, u32[]{:S(2)}) collective-permute-start(f32[64,128]{1,0:T(8,128)S(1)} %shard_map.47.after_ref.refs_1_), channel_id=1, source_target_pairs={{0,3},{1,2},{2,1},{3,0},{4,7},{5,6},{6,5},{7,4},{8,11},{9,10},{10,... | collective-permute-start | bytes 98312 | tf_op jit(solution)/shard_map/ppermute | solution.py:28
  10.6 3.9 %collective-permute-start.4 = (f32[64,128]{1,0:T(8,128)S(1)}, f32[64,128]{1,0:T(8,128)S(1)}, u32[]{:S(2)}, u32[]{:S(2)}) collective-permute-start(f32[64,128]{1,0:T(8,128)S(1)} %shard_map.47.after_ref.refs_1_), channel_id=1, source_target_pairs={{0,2},{1,3},{2,0},{3,1},{4,6},{5,7},{6,4},{7,5},{8,10},{9,11},{10,... | collective-permute-start | bytes 98312 | tf_op jit(solution)/shard_map/ppermute | solution.py:28
  11.1 3.4 %collective-permute-start.3 = (f32[64,128]{1,0:T(8,128)S(1)}, f32[64,128]{1,0:T(8,128)S(1)}, u32[]{:S(2)}, u32[]{:S(2)}) collective-permute-start(f32[64,128]{1,0:T(8,128)S(1)} %shard_map.47.after_ref.refs_1_), channel_id=1, source_target_pairs={{0,1},{1,0},{2,3},{3,2},{4,5},{5,4},{6,7},{7,6},{8,9},{9,8},{10,11... | collective-permute-start | bytes 98312 | tf_op jit(solution)/shard_map/ppermute | solution.py:28
  24.4 5.3 %collective-permute-start.8 = (f32[72,128]{1,0:T(8,128)S(1)}, f32[72,128]{1,0:T(8,128)S(1)}, u32[]{:S(2)}, u32[]{:S(2)}) collective-permute-start(f32[72,128]{1,0:T(8,128)S(1)} %shard_map.50.refs_0_), channel_id=1, source_target_pairs={{0,13},{1,12},{2,15},{3,14},{4,9},{5,8},{6,11},{7,10},{8,5},{9,4},... | collective-permute-start | bytes 110600 | tf_op jit(solution)/shard_map/ppermute | solution.py:28
  24.5 5.2 %collective-permute-start.7 = (f32[72,128]{1,0:T(8,128)S(1)}, f32[72,128]{1,0:T(8,128)S(1)}, u32[]{:S(2)}, u32[]{:S(2)}) collective-permute-start(f32[72,128]{1,0:T(8,128)S(1)} %shard_map.50.refs_0_), channel_id=1, source_target_pairs={{0,9},{1,8},{2,11},{3,10},{4,13},{5,12},{6,15},{7,14},{8,1},{9,0},... | collective-permute-start | bytes 110600 | tf_op jit(solution)/shard_map/ppermute | solution.py:28
  26.5 3.6 %collective-permute-start.6 = (f32[72,128]{1,0:T(8,128)S(1)}, f32[72,128]{1,0:T(8,128)S(1)}, u32[]{:S(2)}, u32[]{:S(2)}) collective-permute-start(f32[72,128]{1,0:T(8,128)S(1)} %shard_map.50.refs_0_), channel_id=1, source_target_pairs={{0,5},{1,4},{2,7},{3,6},{4,1},{5,0},{6,3},{7,2},{8,13},{9,12},{10,... | collective-permute-start | bytes 110600 | tf_op jit(solution)/shard_map/ppermute | solution.py:28
  30.4 2.8 %collective-permute-start.9 = (f32[64,128]{1,0:T(8,128)S(1)}, f32[64,128]{1,0:T(8,128)S(1)}, u32[]{:S(2)}, u32[]{:S(2)}) collective-permute-start(f32[64,128]{1,0:T(8,128)S(1)} %get-tuple-element.24), channel_id=1, source_target_pairs={{0,1},{1,0},{2,3},{3,2},{4,5},{5,4},{6,7},{7,6},{8,9},{9,8},{10,11... | collective-permute-start | bytes 98312 | tf_op jit(solution)/shard_map/ppermute | solution.py:28
  31.5 3.9 %collective-permute-start.10 = (f32[64,128]{1,0:T(8,128)S(1)}, f32[64,128]{1,0:T(8,128)S(1)}, u32[]{:S(2)}, u32[]{:S(2)}) collective-permute-start(f32[64,128]{1,0:T(8,128)S(1)} %get-tuple-element.25), channel_id=1, source_target_pairs={{0,2},{1,3},{2,0},{3,1},{4,6},{5,7},{6,4},{7,5},{8,10},{9,11},{10,... | collective-permute-start | bytes 98312 | tf_op jit(solution)/shard_map/ppermute | solution.py:28
  33.2 3.7 %collective-permute-start.11 = (f32[64,128]{1,0:T(8,128)S(1)}, f32[64,128]{1,0:T(8,128)S(1)}, u32[]{:S(2)}, u32[]{:S(2)}) collective-permute-start(f32[64,128]{1,0:T(8,128)S(1)} %get-tuple-element.26), channel_id=1, source_target_pairs={{0,3},{1,2},{2,1},{3,0},{4,7},{5,6},{6,5},{7,4},{8,11},{9,10},{10,... | collective-permute-start | bytes 98312 | tf_op jit(solution)/shard_map/ppermute | solution.py:28

commit v14 on v13

--- a/solution.py
+++ b/solution.py
@@ -366,7 +366,7 @@
             0,
             0,
             tiled=True,
-            axis_index_groups=[middle_first(chips, chips // 2 + 1)],
+            axis_index_groups=[middle_first(chips, chips // 2 + step)],
         )
         if step + 1 < ITERS:
             (contrib,) = call(

time: 56.3 us -> 55.6 us (0.988)
  waiting for transfers between devices: 9.91 us -> 8.79 us
    ppermute x12, waiting for transfers between devices: 9.91 us -> 8.79 us  [swap(): return lax.ppermute(x, axes, [(i, i ^ k) for i in range(n)])]
  transfers between devices with their start and end apart: 12 -> 12, of which waited for: 6 -> 5; matrix products, arithmetic and copies ran while one was open for 0% -> 0% of each run, Pallas kernels for 6% -> 6%
where the time goes in v14:
time: 55.6 us; the launch traced here: 55.1 us
  blocking collectives  25.6 us (46%)
  starting transfers between devices  13.1 us (24%)
  waiting for transfers between devices  8.79 us (16%)
  Pallas kernels  6.89 us (12%)
  other arithmetic  0.62 us (1%)
    all_to_all x2, blocking collectives, local(): lax.all_to_all(row_parts, 'genome', 0, 0, tiled=True, axis_index_groups=[...  17.2 us
    ppermute x12, starting transfers between devices, swap(): return lax.ppermute(x, axes, [(i, i ^ k) for i in range(n)])  13.1 us
    ppermute x12, waiting for transfers between devices, swap(): return lax.ppermute(x, axes, [(i, i ^ k) for i in range(n)])  8.79 us
    all_to_all x1, blocking collectives, local(): lax.all_to_all(counts, ALL, 0, 0, tiled=True, axis_index_groups=[order])  8.33 us
    pallas_call x6, Pallas kernels, call(): pl.pallas_call(kernel, out_shape=[jax.ShapeDtypeStruct(shape, jnp.float32...  3.46 us
    pallas_call x1, Pallas kernels, flip(): pl.pallas_call(flip_kernel, out_shape=[pltpu.VMEM((late,) + likelihood.sh...  1.84 us
    pallas_call x1, Pallas kernels, prepare(): pl.pallas_call(lambda *refs: prepare_kernel(own_blocks, *refs), out_shape...  1.6 us
  transfers between devices with their start and end apart: 12, of which 5 were waited for; matrix products, arithmetic and copies ran while one was open for 0% of the time, Pallas kernels for 6%

profile of v14, /device:TPU:0, one launch (start us, length us, event | category | flops | bytes accessed | tf_op | source)
XLA Modules:
  0.0 55.1 jit_solution(5395965247652822448)
XLA Ops:
  0.0 4.5 %collective-permute-start.2 = (f32[12,128]{1,0:T(8,128)}, f32[12,128]{1,0:T(8,128)S(1)}, u32[]{:S(2)}, u32[]{:S(2)}) collective-permute-start(f32[12,128]{1,0:T(8,128)} %bitcast.3), channel_id=1, source_target_pairs={{0,13},{1,12},{2,15},{3,14},{4,9},{5,8},{6,11},{7,10},{8,5},{9,4},... | collective-permute-start | bytes 18440 | tf_op jit(solution)/shard_map/ppermute | solution.py:28
  4.5 0.9 %collective-permute-start = (f32[12,128]{1,0:T(8,128)}, f32[12,128]{1,0:T(8,128)S(1)}, u32[]{:S(2)}, u32[]{:S(2)}) collective-permute-start(f32[12,128]{1,0:T(8,128)} %bitcast.5), channel_id=1, source_target_pairs={{0,5},{1,4},{2,7},{3,6},{4,1},{5,0},{6,3},{7,2},{8,13},{9,12},{10,... | collective-permute-start | bytes 18440 | tf_op jit(solution)/shard_map/ppermute | solution.py:28
  5.4 1.6 %shard_map.46 = (bf16[4,8,256,128]{3,2,1,0:T(8,128)(2,1)S(1)}, f32[8,128]{1,0:T(8,128)S(1)}) custom-call(bf16[8,8,256,128]{3,2,1,0:T(8,128)(2,1)} %lik_ref.1, s32[8,8]{1,0:T(8,128)} %refs_1_.1, s32[8,8]{1,0:T(8,128)} %refs_2_.1), custom_call_target="tpu_custom_call" | custom-call | tf_op jit(solution)/shard_map/pallas_call | solution.py:297
  7.0 1.7 %collective-permute-done.1.refs_2_ = f32[12,128]{1,0:T(8,128)S(1)} collective-permute-done((f32[12,128]{1,0:T(8,128)}, f32[12,128]{1,0:T(8,128)S(1)}, u32[]{:S(2)}, u32[]{:S(2)}) %collective-permute-start.1) | collective-permute-done | bytes 6176 | tf_op jit(solution)/shard_map/ppermute | solution.py:28
  8.7 1.8 %collective-permute-start.5 = (f32[64,128]{1,0:T(8,128)S(1)}, f32[64,128]{1,0:T(8,128)S(1)}, u32[]{:S(2)}, u32[]{:S(2)}) collective-permute-start(f32[64,128]{1,0:T(8,128)S(1)} %shard_map.47.after_ref.refs_1_), channel_id=1, source_target_pairs={{0,3},{1,2},{2,1},{3,0},{4,7},{5,6},{6,5},{7,4},{8,11},{9,10},{10,... | collective-permute-start | bytes 98312 | tf_op jit(solution)/shard_map/ppermute | solution.py:28
  10.6 0.5 collective-permute-start.4
  11.1 1.8 %shard_map.48 = (bf16[4,8,256,128]{3,2,1,0:T(8,128)(2,1)S(1)}, bf16[8,4,256,256]{3,2,1,0:T(8,128)(2,1)S(1)}) custom-call(f32[64,128]{1,0:T(8,128)S(1)} %shard_map.47.after_ref.refs_1_, bf16[4,8,256,128]{3,2,1,0:T(8,128)(2,1)S(1)} %get-tuple-element.18.early_ref.refs_3_, bf16[8,8,256,128]{3,2,1,0:T(8,128)(2,1)} %lik_ref.1), custom_call_target="tpu_custom_call" | custom-call | tf_op jit(solution)/shard_map/pallas_call | solution.py:319
  12.9 1.5 %collective-permute-done.4.refs_3_ = f32[64,128]{1,0:T(8,128)S(1)} collective-permute-done((f32[64,128]{1,0:T(8,128)S(1)}, f32[64,128]{1,0:T(8,128)S(1)}, u32[]{:S(2)}, u32[]{:S(2)}) %collective-permute-start.4) | collective-permute-done | bytes 32800 | tf_op jit(solution)/shard_map/ppermute | solution.py:28
  14.5 0.9 %shard_map.49 = (f32[8,8,256]{2,1,0:T(8,128)S(1)}, f32[64,128]{1,0:T(8,128)S(1)}) custom-call(f32[8,128]{1,0:T(8,128)S(1)} %get-tuple-element.17.refs_4_.refs_0_.info_ref, f32[64,128]{1,0:T(8,128)S(1)} %shard_map.47.after_ref.refs_1_, f32[64,128]{1,0:T(8,128)S(1)} %collective-permute-done.3.refs_2_, f32[64,128]{1,0:T(8,128)S(1)} %collective-permute-done.4.refs_3_, ...), custom_call_target="tpu_custom_call" | custom-call | tf_op jit(solution)/shard_map/pallas_call | solution.py:278
  15.4 8.7 %all_to_all.15.parts_ref = f32[8,8,256]{2,1,0:T(8,128)S(1)} all-to-all(f32[8,8,256]{2,1,0:T(8,128)S(1)} %get-tuple-element.20), channel_id=1, replica_groups={{8,10,12,14,0,2,4,6},{9,11,13,15,1,3,5,7},{24,26,28,30,16,18,20,22},{25..., dimensions={0} | all-to-all | bytes 131072 | tf_op jit(solution)/shard_map/all_to_all | solution.py:363
  24.1 0.7 %shard_map.50.refs_0_ = f32[72,128]{1,0:T(8,128)S(1)} custom-call(f32[8,128]{1,0:T(8,128)S(1)} %get-tuple-element.17.refs_4_.refs_0_.info_ref, f32[8,8,256]{2,1,0:T(8,128)S(1)} %all_to_all.15.parts_ref, f32[64,128]{1,0:T(8,128)S(1)} %get-tuple-element.21.picked_ref, bf16[4,8,256,128]{3,2,1,0:T(8,128)(2,1)S(1)} %get-tuple-element.18.early_ref.refs_3_, ...), custom_call_target="tpu_custom_call" | custom-call | tf_op jit(solution)/shard_map/pallas_call | solution.py:278
  25.0 1.5 %collective-permute-start.7 = (f32[72,128]{1,0:T(8,128)S(1)}, f32[72,128]{1,0:T(8,128)S(1)}, u32[]{:S(2)}, u32[]{:S(2)}) collective-permute-start(f32[72,128]{1,0:T(8,128)S(1)} %shard_map.50.refs_0_), channel_id=1, source_target_pairs={{0,9},{1,8},{2,11},{3,10},{4,13},{5,12},{6,15},{7,14},{8,1},{9,0},... | collective-permute-start | bytes 110600 | tf_op jit(solution)/shard_map/ppermute | solution.py:28
  26.6 0.9 %collective-permute-start.6 = (f32[72,128]{1,0:T(8,128)S(1)}, f32[72,128]{1,0:T(8,128)S(1)}, u32[]{:S(2)}, u32[]{:S(2)}) collective-permute-start(f32[72,128]{1,0:T(8,128)S(1)} %shard_map.50.refs_0_), channel_id=1, source_target_pairs={{0,5},{1,4},{2,7},{3,6},{4,1},{5,0},{6,3},{7,2},{8,13},{9,12},{10,... | collective-permute-start | bytes 110600 | tf_op jit(solution)/shard_map/ppermute | solution.py:28
  27.5 2.6 %collective-permute-done.8.refs_3_ = f32[72,128]{1,0:T(8,128)S(1)} collective-permute-done((f32[72,128]{1,0:T(8,128)S(1)}, f32[72,128]{1,0:T(8,128)S(1)}, u32[]{:S(2)}, u32[]{:S(2)}) %collective-permute-start.8) | collective-permute-done | bytes 36896 | tf_op jit(solution)/shard_map/ppermute | solution.py:28
  30.4 0.3 shard_map.51
  30.7 1.2 %collective-permute-start.9 = (f32[64,128]{1,0:T(8,128)S(1)}, f32[64,128]{1,0:T(8,128)S(1)}, u32[]{:S(2)}, u32[]{:S(2)}) collective-permute-start(f32[64,128]{1,0:T(8,128)S(1)} %get-tuple-element.24), channel_id=1, source_target_pairs={{0,1},{1,0},{2,3},{3,2},{4,5},{5,4},{6,7},{7,6},{8,9},{9,8},{10,11... | collective-permute-start | bytes 98312 | tf_op jit(solution)/shard_map/ppermute | solution.py:28
  31.9 0.4 collective-permute-start.10
  32.3 1.0 %collective-permute-start.11 = (f32[64,128]{1,0:T(8,128)S(1)}, f32[64,128]{1,0:T(8,128)S(1)}, u32[]{:S(2)}, u32[]{:S(2)}) collective-permute-start(f32[64,128]{1,0:T(8,128)S(1)} %get-tuple-element.26), channel_id=1, source_target_pairs={{0,3},{1,2},{2,1},{3,0},{4,7},{5,6},{6,5},{7,4},{8,11},{9,10},{10,... | collective-permute-start | bytes 98312 | tf_op jit(solution)/shard_map/ppermute | solution.py:28
  33.3 2.6 %collective-permute-done.10.refs_2_ = f32[64,128]{1,0:T(8,128)S(1)} collective-permute-done((f32[64,128]{1,0:T(8,128)S(1)}, f32[64,128]{1,0:T(8,128)S(1)}, u32[]{:S(2)}, u32[]{:S(2)}) %collective-permute-start.10) | collective-permute-done | bytes 32800 | tf_op jit(solution)/shard_map/ppermute | solution.py:28
  36.0 0.7 %shard_map.52 = (f32[8,8,256]{2,1,0:T(8,128)S(1)}, f32[64,128]{1,0:T(8,128)S(1)}) custom-call(f32[64,128]{1,0:T(8,128)S(1)} %get-tuple-element.23.refs_0_, f32[64,128]{1,0:T(8,128)S(1)} %collective-permute-done.9.refs_1_, f32[64,128]{1,0:T(8,128)S(1)} %collective-permute-done.10.refs_2_, f32[64,128]{1,0:T(8,128)S(1)} %collective-permute-done.11.refs_3_, ...), custom_call_target="tpu_custom_call" | custom-call | tf_op jit(solution)/shard_map/pallas_call | solution.py:278
  36.7 8.5 %all_to_all.16.refs_1_ = f32[8,8,256]{2,1,0:T(8,128)S(1)} all-to-all(f32[8,8,256]{2,1,0:T(8,128)S(1)} %get-tuple-element.27), channel_id=1, replica_groups={{10,8,14,12,2,0,6,4},{11,9,15,13,3,1,7,5},{26,24,30,28,18,16,22,20},{27..., dimensions={0} | all-to-all | bytes 131072 | tf_op jit(solution)/shard_map/all_to_all | solution.py:363
  45.2 0.9 %shard_map.53 = f32[16,12,128]{2,1,0:T(8,128)S(1)} custom-call(f32[8,128]{1,0:T(8,128)S(1)} %get-tuple-element.17.refs_4_.refs_0_.info_ref, f32[8,8,256]{2,1,0:T(8,128)S(1)} %all_to_all.16.refs_1_, f32[64,128]{1,0:T(8,128)S(1)} %get-tuple-element.28.refs_2_, bf16[4,8,256,128]{3,2,1,0:T(8,128)(2,1)S(1)} %get-tuple-element.18.early_ref.refs_3_, ...), custom_call_target="tpu_custom_call" | custom-call | tf_op jit(solution)/shard_map/pallas_call | solution.py:278
  46.1 8.3 %all_to_all.17 = f32[16,12,128]{2,1,0:T(8,128)S(1)} all-to-all(f32[16,12,128]{2,1,0:T(8,128)S(1)} %shard_map.53), channel_id=1, replica_groups={{11,10,9,8,15,14,13,12,3,2,1,0,7,6,5,4},{27,26,25,24,31,30,29,28,19,18,..., dimensions={0} | all-to-all | bytes 196608 | tf_op jit(solution)/shard_map/all_to_all | solution.py:402
  54.5 0.6 %multiply_bitcast_fusion = f32[1536]{0:T(1024)} fusion(f32[12,128]{1,0:T(8,128)S(1)} %reduce_sum.9), kind=kLoop, calls=%fused_computation | loop fusion | flops 1536 | bytes 12288 | tf_op jit(solution)/shard_map/mul | solution.py:403
  (18 shorter events, 0.6 us)
Async XLA Ops:
  0.0 8.7 %copy-start = (f32[1536]{0:T(1024)S(1)}, f32[1536]{0:T(1024)}, u32[]{:S(2)}) copy-start(f32[1536]{0:T(1024)} %param.7) | copy-start | bytes 18436
  0.0 7.0 %collective-permute-start.2 = (f32[12,128]{1,0:T(8,128)}, f32[12,128]{1,0:T(8,128)S(1)}, u32[]{:S(2)}, u32[]{:S(2)}) collective-permute-start(f32[12,128]{1,0:T(8,128)} %bitcast.3), channel_id=1, source_target_pairs={{0,13},{1,12},{2,15},{3,14},{4,9},{5,8},{6,11},{7,10},{8,5},{9,4},... | collective-permute-start | bytes 18440 | tf_op jit(solution)/shard_map/ppermute | solution.py:28
  4.5 4.2 %collective-permute-start.1 = (f32[12,128]{1,0:T(8,128)}, f32[12,128]{1,0:T(8,128)S(1)}, u32[]{:S(2)}, u32[]{:S(2)}) collective-permute-start(f32[12,128]{1,0:T(8,128)} %bitcast.4), channel_id=1, source_target_pairs={{0,9},{1,8},{2,11},{3,10},{4,13},{5,12},{6,15},{7,14},{8,1},{9,0},... | collective-permute-start | bytes 18440 | tf_op jit(solution)/shard_map/ppermute | solution.py:28
  4.5 4.2 %collective-permute-start = (f32[12,128]{1,0:T(8,128)}, f32[12,128]{1,0:T(8,128)S(1)}, u32[]{:S(2)}, u32[]{:S(2)}) collective-permute-start(f32[12,128]{1,0:T(8,128)} %bitcast.5), channel_id=1, source_target_pairs={{0,5},{1,4},{2,7},{3,6},{4,1},{5,0},{6,3},{7,2},{8,13},{9,12},{10,... | collective-permute-start | bytes 18440 | tf_op jit(solution)/shard_map/ppermute | solution.py:28
  8.7 4.2 %collective-permute-start.5 = (f32[64,128]{1,0:T(8,128)S(1)}, f32[64,128]{1,0:T(8,128)S(1)}, u32[]{:S(2)}, u32[]{:S(2)}) collective-permute-start(f32[64,128]{1,0:T(8,128)S(1)} %shard_map.47.after_ref.refs_1_), channel_id=1, source_target_pairs={{0,3},{1,2},{2,1},{3,0},{4,7},{5,6},{6,5},{7,4},{8,11},{9,10},{10,... | collective-permute-start | bytes 98312 | tf_op jit(solution)/shard_map/ppermute | solution.py:28
  10.6 3.9 %collective-permute-start.4 = (f32[64,128]{1,0:T(8,128)S(1)}, f32[64,128]{1,0:T(8,128)S(1)}, u32[]{:S(2)}, u32[]{:S(2)}) collective-permute-start(f32[64,128]{1,0:T(8,128)S(1)} %shard_map.47.after_ref.refs_1_), channel_id=1, source_target_pairs={{0,2},{1,3},{2,0},{3,1},{4,6},{5,7},{6,4},{7,5},{8,10},{9,11},{10,... | collective-permute-start | bytes 98312 | tf_op jit(solution)/shard_map/ppermute | solution.py:28
  11.1 3.4 %collective-permute-start.3 = (f32[64,128]{1,0:T(8,128)S(1)}, f32[64,128]{1,0:T(8,128)S(1)}, u32[]{:S(2)}, u32[]{:S(2)}) collective-permute-start(f32[64,128]{1,0:T(8,128)S(1)} %shard_map.47.after_ref.refs_1_), channel_id=1, source_target_pairs={{0,1},{1,0},{2,3},{3,2},{4,5},{5,4},{6,7},{7,6},{8,9},{9,8},{10,11... | collective-permute-start | bytes 98312 | tf_op jit(solution)/shard_map/ppermute | solution.py:28
  24.8 5.4 %collective-permute-start.8 = (f32[72,128]{1,0:T(8,128)S(1)}, f32[72,128]{1,0:T(8,128)S(1)}, u32[]{:S(2)}, u32[]{:S(2)}) collective-permute-start(f32[72,128]{1,0:T(8,128)S(1)} %shard_map.50.refs_0_), channel_id=1, source_target_pairs={{0,13},{1,12},{2,15},{3,14},{4,9},{5,8},{6,11},{7,10},{8,5},{9,4},... | collective-permute-start | bytes 110600 | tf_op jit(solution)/shard_map/ppermute | solution.py:28
  25.0 5.1 %collective-permute-start.7 = (f32[72,128]{1,0:T(8,128)S(1)}, f32[72,128]{1,0:T(8,128)S(1)}, u32[]{:S(2)}, u32[]{:S(2)}) collective-permute-start(f32[72,128]{1,0:T(8,128)S(1)} %shard_map.50.refs_0_), channel_id=1, source_target_pairs={{0,9},{1,8},{2,11},{3,10},{4,13},{5,12},{6,15},{7,14},{8,1},{9,0},... | collective-permute-start | bytes 110600 | tf_op jit(solution)/shard_map/ppermute | solution.py:28
  26.6 3.8 %collective-permute-start.6 = (f32[72,128]{1,0:T(8,128)S(1)}, f32[72,128]{1,0:T(8,128)S(1)}, u32[]{:S(2)}, u32[]{:S(2)}) collective-permute-start(f32[72,128]{1,0:T(8,128)S(1)} %shard_map.50.refs_0_), channel_id=1, source_target_pairs={{0,5},{1,4},{2,7},{3,6},{4,1},{5,0},{6,3},{7,2},{8,13},{9,12},{10,... | collective-permute-start | bytes 110600 | tf_op jit(solution)/shard_map/ppermute | solution.py:28
  30.7 2.7 %collective-permute-start.9 = (f32[64,128]{1,0:T(8,128)S(1)}, f32[64,128]{1,0:T(8,128)S(1)}, u32[]{:S(2)}, u32[]{:S(2)}) collective-permute-start(f32[64,128]{1,0:T(8,128)S(1)} %get-tuple-element.24), channel_id=1, source_target_pairs={{0,1},{1,0},{2,3},{3,2},{4,5},{5,4},{6,7},{7,6},{8,9},{9,8},{10,11... | collective-permute-start | bytes 98312 | tf_op jit(solution)/shard_map/ppermute | solution.py:28
  31.9 4.1 %collective-permute-start.10 = (f32[64,128]{1,0:T(8,128)S(1)}, f32[64,128]{1,0:T(8,128)S(1)}, u32[]{:S(2)}, u32[]{:S(2)}) collective-permute-start(f32[64,128]{1,0:T(8,128)S(1)} %get-tuple-element.25), channel_id=1, source_target_pairs={{0,2},{1,3},{2,0},{3,1},{4,6},{5,7},{6,4},{7,5},{8,10},{9,11},{10,... | collective-permute-start | bytes 98312 | tf_op jit(solution)/shard_map/ppermute | solution.py:28
  32.3 3.7 %collective-permute-start.11 = (f32[64,128]{1,0:T(8,128)S(1)}, f32[64,128]{1,0:T(8,128)S(1)}, u32[]{:S(2)}, u32[]{:S(2)}) collective-permute-start(f32[64,128]{1,0:T(8,128)S(1)} %get-tuple-element.26), channel_id=1, source_target_pairs={{0,3},{1,2},{2,1},{3,0},{4,7},{5,6},{6,5},{7,4},{8,11},{9,10},{10,... | collective-permute-start | bytes 98312 | tf_op jit(solution)/shard_map/ppermute | solution.py:28

commit v15 on v14

--- a/solution.py
+++ b/solution.py
@@ -9,6 +9,7 @@
 ALL = ("genome", "reads")
 TERMS = 16
 ID_ROWS = 8
+CROSSED = (1,)
 LANES = 128
 VMEM = pl.BlockSpec(memory_space=pltpu.VMEM)
 ANY = pl.BlockSpec(memory_space=pl.ANY)
@@ -41,13 +42,13 @@
     return place
 
 
-def gather_far(x, axes):
+def gather_far(x, axes, crossed):
     parts = [x]
     stride = lax.axis_size(axes)
     for r in radices(stride)[:0:-1]:
         stride //= r
         sent = parts[0] if len(parts) == 1 else jnp.concatenate(parts, axis=0)
-        parts = [sent] + [swap(sent, axes, j * stride + 1) for j in range(1, r)]
+        parts = [sent] + [swap(sent, axes, j * stride + (j in crossed)) for j in range(1, r)]
     return parts
 
 
@@ -132,7 +133,8 @@
     away = owner ^ me
     rest = away // near
     for r in radices(n)[1:]:
-        away = away ^ jnp.where(rest % r > 0, 1, 0)
+        for j in CROSSED:
+            away = away ^ jnp.where(rest % r == j, 1, 0)
         rest = rest // r
     place = position(away, n)
     place = (place // far) * near_rows(far, own_blocks) + (place % far) * own_blocks + inside
@@ -341,7 +343,7 @@
     total_reads = read_blocks * lax.axis_size("reads") * reads
     scale = n * own_blocks * cols / total_reads
 
-    column = gather_far(own_weights, ALL)
+    column = gather_far(own_weights, ALL, CROSSED)
     held, info = prepare(own_blocks, read_blocks // 2, likelihood, block_ids, slot_valid)
     (sent,) = call(join_kernel, [(near_rows(far, own_blocks), cols)], [], *column, info)
     rest, flipped = flip(sent, held, likelihood)
@@ -379,7 +381,7 @@
                 held,
                 rest,
             )
-            given = gather_far(contrib, ALL)
+            given = gather_far(contrib, ALL, (1, 2, 3))
             sums = call(
                 lambda *refs: wanted_kernel(near, all_slots, len(given), *refs),
                 [(all_slots, cols)] * near,
@@ -387,7 +389,7 @@
                 *given,
                 *wanted,
             )
-            parts = [sums[0]] + [swap(sums[j], ALL, j) for j in range(1, near)]
+            parts = [sums[0]] + [swap(sums[j], ALL, j) for j in range(near - 1, 0, -1)]
     order = middle_first(n, n // 2 + 3)
     (counts,) = call(
         lambda *refs: last_column_kernel(order, *refs),

time: 55.6 us -> 55.6 us (level)
  blocking collectives: 25.6 us -> 26.4 us
  starting transfers between devices: 13.1 us -> 12.5 us
    all_to_all x2, blocking collectives: 17.2 us -> 18 us  [local(): lax.all_to_all(row_parts, 'genome', 0, 0, tiled=True, axis_index_groups=[...]
    ppermute x12, starting transfers between devices: 13.1 us -> 12.5 us  [swap(): return lax.ppermute(x, axes, [(i, i ^ k) for i in range(n)])]
  transfers between devices with their start and end apart: 12 -> 12, of which waited for: 5 -> 7; matrix products, arithmetic and copies ran while one was open for 0% -> 0% of each run, Pallas kernels for 6% -> 6%
where the time goes in v15:
time: 55.6 us; the launch traced here: 55.1 us
  blocking collectives  26.4 us (47%)
  starting transfers between devices  12.5 us (22%)
  waiting for transfers between devices  8.63 us (16%)
  Pallas kernels  6.9 us (12%)
  other arithmetic  0.62 us (1%)
    all_to_all x2, blocking collectives, local(): lax.all_to_all(row_parts, 'genome', 0, 0, tiled=True, axis_index_groups=[...  18 us
    ppermute x12, starting transfers between devices, swap(): return lax.ppermute(x, axes, [(i, i ^ k) for i in range(n)])  12.5 us
    ppermute x12, waiting for transfers between devices, swap(): return lax.ppermute(x, axes, [(i, i ^ k) for i in range(n)])  8.63 us
    all_to_all x1, blocking collectives, local(): lax.all_to_all(counts, ALL, 0, 0, tiled=True, axis_index_groups=[order])  8.33 us
    pallas_call x6, Pallas kernels, call(): pl.pallas_call(kernel, out_shape=[jax.ShapeDtypeStruct(shape, jnp.float32...  3.46 us
    pallas_call x1, Pallas kernels, flip(): pl.pallas_call(flip_kernel, out_shape=[pltpu.VMEM((late,) + likelihood.sh...  1.84 us
    pallas_call x1, Pallas kernels, prepare(): pl.pallas_call(lambda *refs: prepare_kernel(own_blocks, *refs), out_shape...  1.6 us
  transfers between devices with their start and end apart: 12, of which 7 were waited for; matrix products, arithmetic and copies ran while one was open for 0% of the time, Pallas kernels for 6%

profile of v15, /device:TPU:0, one launch (start us, length us, event | category | flops | bytes accessed | tf_op | source)
XLA Modules:
  0.0 55.1 jit_solution(20647712573026910)
XLA Ops:
  0.0 5.0 %collective-permute-start.2 = (f32[12,128]{1,0:T(8,128)}, f32[12,128]{1,0:T(8,128)S(1)}, u32[]{:S(2)}, u32[]{:S(2)}) collective-permute-start(f32[12,128]{1,0:T(8,128)} %bitcast.3), channel_id=1, source_target_pairs={{0,12},{1,13},{2,14},{3,15},{4,8},{5,9},{6,10},{7,11},{8,4},{9,5},... | collective-permute-start | bytes 18440 | tf_op jit(solution)/shard_map/ppermute | solution.py:29
  5.1 1.6 %shard_map.46 = (bf16[4,8,256,128]{3,2,1,0:T(8,128)(2,1)S(1)}, f32[8,128]{1,0:T(8,128)S(1)}) custom-call(bf16[8,8,256,128]{3,2,1,0:T(8,128)(2,1)} %lik_ref.1, s32[8,8]{1,0:T(8,128)} %refs_1_.1, s32[8,8]{1,0:T(8,128)} %refs_2_.1), custom_call_target="tpu_custom_call" | custom-call | tf_op jit(solution)/shard_map/pallas_call | solution.py:299
  6.7 0.3 collective-permute-done.2.refs_3_
  7.0 2.9 %collective-permute-done.1.refs_2_ = f32[12,128]{1,0:T(8,128)S(1)} collective-permute-done((f32[12,128]{1,0:T(8,128)}, f32[12,128]{1,0:T(8,128)S(1)}, u32[]{:S(2)}, u32[]{:S(2)}) %collective-permute-start.1) | collective-permute-done | bytes 6176 | tf_op jit(solution)/shard_map/ppermute | solution.py:29
  9.9 1.6 %collective-permute-start.4 = (f32[64,128]{1,0:T(8,128)S(1)}, f32[64,128]{1,0:T(8,128)S(1)}, u32[]{:S(2)}, u32[]{:S(2)}) collective-permute-start(f32[64,128]{1,0:T(8,128)S(1)} %shard_map.47.after_ref.refs_1_), channel_id=1, source_target_pairs={{0,2},{1,3},{2,0},{3,1},{4,6},{5,7},{6,4},{7,5},{8,10},{9,11},{10,... | collective-permute-start | bytes 98312 | tf_op jit(solution)/shard_map/ppermute | solution.py:29
  11.8 1.8 %shard_map.48 = (bf16[4,8,256,128]{3,2,1,0:T(8,128)(2,1)S(1)}, bf16[8,4,256,256]{3,2,1,0:T(8,128)(2,1)S(1)}) custom-call(f32[64,128]{1,0:T(8,128)S(1)} %shard_map.47.after_ref.refs_1_, bf16[4,8,256,128]{3,2,1,0:T(8,128)(2,1)S(1)} %get-tuple-element.18.early_ref.refs_3_, bf16[8,8,256,128]{3,2,1,0:T(8,128)(2,1)} %lik_ref.1), custom_call_target="tpu_custom_call" | custom-call | tf_op jit(solution)/shard_map/pallas_call | solution.py:321
  13.6 0.3 collective-permute-done.4.refs_3_
  13.9 0.9 %shard_map.49 = (f32[8,8,256]{2,1,0:T(8,128)S(1)}, f32[64,128]{1,0:T(8,128)S(1)}) custom-call(f32[8,128]{1,0:T(8,128)S(1)} %get-tuple-element.17.refs_4_.refs_0_.info_ref, f32[64,128]{1,0:T(8,128)S(1)} %shard_map.47.after_ref.refs_1_, f32[64,128]{1,0:T(8,128)S(1)} %collective-permute-done.3.refs_2_, f32[64,128]{1,0:T(8,128)S(1)} %collective-permute-done.4.refs_3_, ...), custom_call_target="tpu_custom_call" | custom-call | tf_op jit(solution)/shard_map/pallas_call | solution.py:280
  14.8 9.5 %all_to_all.15.parts_ref = f32[8,8,256]{2,1,0:T(8,128)S(1)} all-to-all(f32[8,8,256]{2,1,0:T(8,128)S(1)} %get-tuple-element.20), channel_id=1, replica_groups={{8,10,12,14,0,2,4,6},{9,11,13,15,1,3,5,7},{24,26,28,30,16,18,20,22},{25..., dimensions={0} | all-to-all | bytes 131072 | tf_op jit(solution)/shard_map/all_to_all | solution.py:365
  24.3 0.7 %shard_map.50.refs_0_ = f32[72,128]{1,0:T(8,128)S(1)} custom-call(f32[8,128]{1,0:T(8,128)S(1)} %get-tuple-element.17.refs_4_.refs_0_.info_ref, f32[8,8,256]{2,1,0:T(8,128)S(1)} %all_to_all.15.parts_ref, f32[64,128]{1,0:T(8,128)S(1)} %get-tuple-element.21.picked_ref, bf16[4,8,256,128]{3,2,1,0:T(8,128)(2,1)S(1)} %get-tuple-element.18.early_ref.refs_3_, ...), custom_call_target="tpu_custom_call" | custom-call | tf_op jit(solution)/shard_map/pallas_call | solution.py:280
  25.0 0.4 collective-permute-start.8
  25.4 1.4 %collective-permute-start.7 = (f32[72,128]{1,0:T(8,128)S(1)}, f32[72,128]{1,0:T(8,128)S(1)}, u32[]{:S(2)}, u32[]{:S(2)}) collective-permute-start(f32[72,128]{1,0:T(8,128)S(1)} %shard_map.50.refs_0_), channel_id=1, source_target_pairs={{0,9},{1,8},{2,11},{3,10},{4,13},{5,12},{6,15},{7,14},{8,1},{9,0},... | collective-permute-start | bytes 110600 | tf_op jit(solution)/shard_map/ppermute | solution.py:29
  26.8 0.9 %collective-permute-start.6 = (f32[72,128]{1,0:T(8,128)S(1)}, f32[72,128]{1,0:T(8,128)S(1)}, u32[]{:S(2)}, u32[]{:S(2)}) collective-permute-start(f32[72,128]{1,0:T(8,128)S(1)} %shard_map.50.refs_0_), channel_id=1, source_target_pairs={{0,5},{1,4},{2,7},{3,6},{4,1},{5,0},{6,3},{7,2},{8,13},{9,12},{10,... | collective-permute-start | bytes 110600 | tf_op jit(solution)/shard_map/ppermute | solution.py:29
  27.7 2.6 %collective-permute-done.8.refs_3_ = f32[72,128]{1,0:T(8,128)S(1)} collective-permute-done((f32[72,128]{1,0:T(8,128)S(1)}, f32[72,128]{1,0:T(8,128)S(1)}, u32[]{:S(2)}, u32[]{:S(2)}) %collective-permute-start.8) | collective-permute-done | bytes 36896 | tf_op jit(solution)/shard_map/ppermute | solution.py:29
  30.6 0.3 shard_map.51
  30.9 1.2 %collective-permute-start.9 = (f32[64,128]{1,0:T(8,128)S(1)}, f32[64,128]{1,0:T(8,128)S(1)}, u32[]{:S(2)}, u32[]{:S(2)}) collective-permute-start(f32[64,128]{1,0:T(8,128)S(1)} %get-tuple-element.24), channel_id=1, source_target_pairs={{0,3},{1,2},{2,1},{3,0},{4,7},{5,6},{6,5},{7,4},{8,11},{9,10},{10,... | collective-permute-start | bytes 98312 | tf_op jit(solution)/shard_map/ppermute | solution.py:29
  32.1 1.6 %collective-permute-start.10 = (f32[64,128]{1,0:T(8,128)S(1)}, f32[64,128]{1,0:T(8,128)S(1)}, u32[]{:S(2)}, u32[]{:S(2)}) collective-permute-start(f32[64,128]{1,0:T(8,128)S(1)} %get-tuple-element.25), channel_id=1, source_target_pairs={{0,2},{1,3},{2,0},{3,1},{4,6},{5,7},{6,4},{7,5},{8,10},{9,11},{10,... | collective-permute-start | bytes 98312 | tf_op jit(solution)/shard_map/ppermute | solution.py:29
  33.8 0.6 %collective-permute-done.9.refs_1_ = f32[64,128]{1,0:T(8,128)S(1)} collective-permute-done((f32[64,128]{1,0:T(8,128)S(1)}, f32[64,128]{1,0:T(8,128)S(1)}, u32[]{:S(2)}, u32[]{:S(2)}) %collective-permute-start.9) | collective-permute-done | bytes 32800 | tf_op jit(solution)/shard_map/ppermute | solution.py:29
  34.3 1.7 %collective-permute-done.10.refs_2_ = f32[64,128]{1,0:T(8,128)S(1)} collective-permute-done((f32[64,128]{1,0:T(8,128)S(1)}, f32[64,128]{1,0:T(8,128)S(1)}, u32[]{:S(2)}, u32[]{:S(2)}) %collective-permute-start.10) | collective-permute-done | bytes 32800 | tf_op jit(solution)/shard_map/ppermute | solution.py:29
  36.0 0.7 %shard_map.52 = (f32[8,8,256]{2,1,0:T(8,128)S(1)}, f32[64,128]{1,0:T(8,128)S(1)}) custom-call(f32[64,128]{1,0:T(8,128)S(1)} %get-tuple-element.23.refs_0_, f32[64,128]{1,0:T(8,128)S(1)} %collective-permute-done.9.refs_1_, f32[64,128]{1,0:T(8,128)S(1)} %collective-permute-done.10.refs_2_, f32[64,128]{1,0:T(8,128)S(1)} %collective-permute-done.11.refs_3_, ...), custom_call_target="tpu_custom_call" | custom-call | tf_op jit(solution)/shard_map/pallas_call | solution.py:280
  36.7 8.5 %all_to_all.16.refs_1_ = f32[8,8,256]{2,1,0:T(8,128)S(1)} all-to-all(f32[8,8,256]{2,1,0:T(8,128)S(1)} %get-tuple-element.27), channel_id=1, replica_groups={{10,8,14,12,2,0,6,4},{11,9,15,13,3,1,7,5},{26,24,30,28,18,16,22,20},{27..., dimensions={0} | all-to-all | bytes 131072 | tf_op jit(solution)/shard_map/all_to_all | solution.py:365
  45.3 0.9 %shard_map.53 = f32[16,12,128]{2,1,0:T(8,128)S(1)} custom-call(f32[8,128]{1,0:T(8,128)S(1)} %get-tuple-element.17.refs_4_.refs_0_.info_ref, f32[8,8,256]{2,1,0:T(8,128)S(1)} %all_to_all.16.refs_1_, f32[64,128]{1,0:T(8,128)S(1)} %get-tuple-element.28.refs_2_, bf16[4,8,256,128]{3,2,1,0:T(8,128)(2,1)S(1)} %get-tuple-element.18.early_ref.refs_3_, ...), custom_call_target="tpu_custom_call" | custom-call | tf_op jit(solution)/shard_map/pallas_call | solution.py:280
  46.2 8.3 %all_to_all.17 = f32[16,12,128]{2,1,0:T(8,128)S(1)} all-to-all(f32[16,12,128]{2,1,0:T(8,128)S(1)} %shard_map.53), channel_id=1, replica_groups={{11,10,9,8,15,14,13,12,3,2,1,0,7,6,5,4},{27,26,25,24,31,30,29,28,19,18,..., dimensions={0} | all-to-all | bytes 196608 | tf_op jit(solution)/shard_map/all_to_all | solution.py:404
  54.5 0.6 %multiply_bitcast_fusion = f32[1536]{0:T(1024)} fusion(f32[12,128]{1,0:T(8,128)S(1)} %reduce_sum.9), kind=kLoop, calls=%fused_computation | loop fusion | flops 1536 | bytes 12288 | tf_op jit(solution)/shard_map/mul | solution.py:405
  (18 shorter events, 0.6 us)
Async XLA Ops:
  0.0 9.8 %copy-start = (f32[1536]{0:T(1024)S(1)}, f32[1536]{0:T(1024)}, u32[]{:S(2)}) copy-start(f32[1536]{0:T(1024)} %param.7) | copy-start | bytes 18436
  0.0 7.0 %collective-permute-start.2 = (f32[12,128]{1,0:T(8,128)}, f32[12,128]{1,0:T(8,128)S(1)}, u32[]{:S(2)}, u32[]{:S(2)}) collective-permute-start(f32[12,128]{1,0:T(8,128)} %bitcast.3), channel_id=1, source_target_pairs={{0,12},{1,13},{2,14},{3,15},{4,8},{5,9},{6,10},{7,11},{8,4},{9,5},... | collective-permute-start | bytes 18440 | tf_op jit(solution)/shard_map/ppermute | solution.py:29
  5.1 4.8 %collective-permute-start.1 = (f32[12,128]{1,0:T(8,128)}, f32[12,128]{1,0:T(8,128)S(1)}, u32[]{:S(2)}, u32[]{:S(2)}) collective-permute-start(f32[12,128]{1,0:T(8,128)} %bitcast.4), channel_id=1, source_target_pairs={{0,8},{1,9},{2,10},{3,11},{4,12},{5,13},{6,14},{7,15},{8,0},{9,1},... | collective-permute-start | bytes 18440 | tf_op jit(solution)/shard_map/ppermute | solution.py:29
  5.1 4.8 %collective-permute-start = (f32[12,128]{1,0:T(8,128)}, f32[12,128]{1,0:T(8,128)S(1)}, u32[]{:S(2)}, u32[]{:S(2)}) collective-permute-start(f32[12,128]{1,0:T(8,128)} %bitcast.5), channel_id=1, source_target_pairs={{0,5},{1,4},{2,7},{3,6},{4,1},{5,0},{6,3},{7,2},{8,13},{9,12},{10,... | collective-permute-start | bytes 18440 | tf_op jit(solution)/shard_map/ppermute | solution.py:29
  9.8 3.8 %collective-permute-start.5 = (f32[64,128]{1,0:T(8,128)S(1)}, f32[64,128]{1,0:T(8,128)S(1)}, u32[]{:S(2)}, u32[]{:S(2)}) collective-permute-start(f32[64,128]{1,0:T(8,128)S(1)} %shard_map.47.after_ref.refs_1_), channel_id=1, source_target_pairs={{0,3},{1,2},{2,1},{3,0},{4,7},{5,6},{6,5},{7,4},{8,11},{9,10},{10,... | collective-permute-start | bytes 98312 | tf_op jit(solution)/shard_map/ppermute | solution.py:29
  9.9 4.0 %collective-permute-start.4 = (f32[64,128]{1,0:T(8,128)S(1)}, f32[64,128]{1,0:T(8,128)S(1)}, u32[]{:S(2)}, u32[]{:S(2)}) collective-permute-start(f32[64,128]{1,0:T(8,128)S(1)} %shard_map.47.after_ref.refs_1_), channel_id=1, source_target_pairs={{0,2},{1,3},{2,0},{3,1},{4,6},{5,7},{6,4},{7,5},{8,10},{9,11},{10,... | collective-permute-start | bytes 98312 | tf_op jit(solution)/shard_map/ppermute | solution.py:29
  11.5 2.4 %collective-permute-start.3 = (f32[64,128]{1,0:T(8,128)S(1)}, f32[64,128]{1,0:T(8,128)S(1)}, u32[]{:S(2)}, u32[]{:S(2)}) collective-permute-start(f32[64,128]{1,0:T(8,128)S(1)} %shard_map.47.after_ref.refs_1_), channel_id=1, source_target_pairs={{0,1},{1,0},{2,3},{3,2},{4,5},{5,4},{6,7},{7,6},{8,9},{9,8},{10,11... | collective-permute-start | bytes 98312 | tf_op jit(solution)/shard_map/ppermute | solution.py:29
  25.0 5.4 %collective-permute-start.8 = (f32[72,128]{1,0:T(8,128)S(1)}, f32[72,128]{1,0:T(8,128)S(1)}, u32[]{:S(2)}, u32[]{:S(2)}) collective-permute-start(f32[72,128]{1,0:T(8,128)S(1)} %shard_map.50.refs_0_), channel_id=1, source_target_pairs={{0,13},{1,12},{2,15},{3,14},{4,9},{5,8},{6,11},{7,10},{8,5},{9,4},... | collective-permute-start | bytes 110600 | tf_op jit(solution)/shard_map/ppermute | solution.py:29
  25.4 5.0 %collective-permute-start.7 = (f32[72,128]{1,0:T(8,128)S(1)}, f32[72,128]{1,0:T(8,128)S(1)}, u32[]{:S(2)}, u32[]{:S(2)}) collective-permute-start(f32[72,128]{1,0:T(8,128)S(1)} %shard_map.50.refs_0_), channel_id=1, source_target_pairs={{0,9},{1,8},{2,11},{3,10},{4,13},{5,12},{6,15},{7,14},{8,1},{9,0},... | collective-permute-start | bytes 110600 | tf_op jit(solution)/shard_map/ppermute | solution.py:29
  26.8 3.8 %collective-permute-start.6 = (f32[72,128]{1,0:T(8,128)S(1)}, f32[72,128]{1,0:T(8,128)S(1)}, u32[]{:S(2)}, u32[]{:S(2)}) collective-permute-start(f32[72,128]{1,0:T(8,128)S(1)} %shard_map.50.refs_0_), channel_id=1, source_target_pairs={{0,5},{1,4},{2,7},{3,6},{4,1},{5,0},{6,3},{7,2},{8,13},{9,12},{10,... | collective-permute-start | bytes 110600 | tf_op jit(solution)/shard_map/ppermute | solution.py:29
  30.9 3.4 %collective-permute-start.9 = (f32[64,128]{1,0:T(8,128)S(1)}, f32[64,128]{1,0:T(8,128)S(1)}, u32[]{:S(2)}, u32[]{:S(2)}) collective-permute-start(f32[64,128]{1,0:T(8,128)S(1)} %get-tuple-element.24), channel_id=1, source_target_pairs={{0,3},{1,2},{2,1},{3,0},{4,7},{5,6},{6,5},{7,4},{8,11},{9,10},{10,... | collective-permute-start | bytes 98312 | tf_op jit(solution)/shard_map/ppermute | solution.py:29
  32.1 3.9 %collective-permute-start.10 = (f32[64,128]{1,0:T(8,128)S(1)}, f32[64,128]{1,0:T(8,128)S(1)}, u32[]{:S(2)}, u32[]{:S(2)}) collective-permute-start(f32[64,128]{1,0:T(8,128)S(1)} %get-tuple-element.25), channel_id=1, source_target_pairs={{0,2},{1,3},{2,0},{3,1},{4,6},{5,7},{6,4},{7,5},{8,10},{9,11},{10,... | collective-permute-start | bytes 98312 | tf_op jit(solution)/shard_map/ppermute | solution.py:29
  33.8 2.3 %collective-permute-start.11 = (f32[64,128]{1,0:T(8,128)S(1)}, f32[64,128]{1,0:T(8,128)S(1)}, u32[]{:S(2)}, u32[]{:S(2)}) collective-permute-start(f32[64,128]{1,0:T(8,128)S(1)} %get-tuple-element.26), channel_id=1, source_target_pairs={{0,1},{1,0},{2,3},{3,2},{4,5},{5,4},{6,7},{7,6},{8,9},{9,8},{10,11... | collective-permute-start | bytes 98312 | tf_op jit(solution)/shard_map/ppermute | solution.py:29

commit v16 on v15

--- a/solution.py
+++ b/solution.py
@@ -381,7 +381,7 @@
                 held,
                 rest,
             )
-            given = gather_far(contrib, ALL, (1, 2, 3))
+            given = gather_far(contrib, ALL, (3,))
             sums = call(
                 lambda *refs: wanted_kernel(near, all_slots, len(given), *refs),
                 [(all_slots, cols)] * near,
@@ -389,7 +389,7 @@
                 *given,
                 *wanted,
             )
-            parts = [sums[0]] + [swap(sums[j], ALL, j) for j in range(near - 1, 0, -1)]
+            parts = [sums[0]] + [swap(sums[j], ALL, j) for j in list(range(2, near)) + [1]]
     order = middle_first(n, n // 2 + 3)
     (counts,) = call(
         lambda *refs: last_column_kernel(order, *refs),

time: 55.6 us -> 55.7 us (level)
  waiting for transfers between devices: 8.63 us -> 9.2 us
    ppermute x12, waiting for transfers between devices: 8.63 us -> 9.2 us  [swap(): return lax.ppermute(x, axes, [(i, i ^ k) for i in range(n)])]
where the time goes in v16:
time: 55.7 us; the launch traced here: 55.2 us
  blocking collectives  26.2 us (47%)
  starting transfers between devices  12.2 us (22%)
  waiting for transfers between devices  9.2 us (17%)
  Pallas kernels  6.91 us (12%)
  other arithmetic  0.62 us (1%)
    all_to_all x2, blocking collectives, local(): lax.all_to_all(row_parts, 'genome', 0, 0, tiled=True, axis_index_groups=[...  17.9 us
    ppermute x12, starting transfers between devices, swap(): return lax.ppermute(x, axes, [(i, i ^ k) for i in range(n)])  12.2 us
    ppermute x12, waiting for transfers between devices, swap(): return lax.ppermute(x, axes, [(i, i ^ k) for i in range(n)])  9.2 us
    all_to_all x1, blocking collectives, local(): lax.all_to_all(counts, ALL, 0, 0, tiled=True, axis_index_groups=[order])  8.33 us
    pallas_call x6, Pallas kernels, call(): pl.pallas_call(kernel, out_shape=[jax.ShapeDtypeStruct(shape, jnp.float32...  3.47 us
    pallas_call x1, Pallas kernels, flip(): pl.pallas_call(flip_kernel, out_shape=[pltpu.VMEM((late,) + likelihood.sh...  1.84 us
    pallas_call x1, Pallas kernels, prepare(): pl.pallas_call(lambda *refs: prepare_kernel(own_blocks, *refs), out_shape...  1.6 us
  transfers between devices with their start and end apart: 12, of which 7 were waited for; matrix products, arithmetic and copies ran while one was open for 0% of the time, Pallas kernels for 6%

profile of v16, /device:TPU:0, one launch (start us, length us, event | category | flops | bytes accessed | tf_op | source)
XLA Modules:
  0.0 55.2 jit_solution(11269723346074848588)
XLA Ops:
  0.0 5.0 %collective-permute-start.2 = (f32[12,128]{1,0:T(8,128)}, f32[12,128]{1,0:T(8,128)S(1)}, u32[]{:S(2)}, u32[]{:S(2)}) collective-permute-start(f32[12,128]{1,0:T(8,128)} %bitcast.3), channel_id=1, source_target_pairs={{0,12},{1,13},{2,14},{3,15},{4,8},{5,9},{6,10},{7,11},{8,4},{9,5},... | collective-permute-start | bytes 18440 | tf_op jit(solution)/shard_map/ppermute | solution.py:29
  5.1 1.6 %shard_map.46 = (bf16[4,8,256,128]{3,2,1,0:T(8,128)(2,1)S(1)}, f32[8,128]{1,0:T(8,128)S(1)}) custom-call(bf16[8,8,256,128]{3,2,1,0:T(8,128)(2,1)} %lik_ref.1, s32[8,8]{1,0:T(8,128)} %refs_1_.1, s32[8,8]{1,0:T(8,128)} %refs_2_.1), custom_call_target="tpu_custom_call" | custom-call | tf_op jit(solution)/shard_map/pallas_call | solution.py:299
  7.0 2.9 %collective-permute-done.1.refs_2_ = f32[12,128]{1,0:T(8,128)S(1)} collective-permute-done((f32[12,128]{1,0:T(8,128)}, f32[12,128]{1,0:T(8,128)S(1)}, u32[]{:S(2)}, u32[]{:S(2)}) %collective-permute-start.1) | collective-permute-done | bytes 6176 | tf_op jit(solution)/shard_map/ppermute | solution.py:29
  9.9 1.6 %collective-permute-start.4 = (f32[64,128]{1,0:T(8,128)S(1)}, f32[64,128]{1,0:T(8,128)S(1)}, u32[]{:S(2)}, u32[]{:S(2)}) collective-permute-start(f32[64,128]{1,0:T(8,128)S(1)} %shard_map.47.after_ref.refs_1_), channel_id=1, source_target_pairs={{0,2},{1,3},{2,0},{3,1},{4,6},{5,7},{6,4},{7,5},{8,10},{9,11},{10,... | collective-permute-start | bytes 98312 | tf_op jit(solution)/shard_map/ppermute | solution.py:29
  11.8 1.8 %shard_map.48 = (bf16[4,8,256,128]{3,2,1,0:T(8,128)(2,1)S(1)}, bf16[8,4,256,256]{3,2,1,0:T(8,128)(2,1)S(1)}) custom-call(f32[64,128]{1,0:T(8,128)S(1)} %shard_map.47.after_ref.refs_1_, bf16[4,8,256,128]{3,2,1,0:T(8,128)(2,1)S(1)} %get-tuple-element.18.early_ref.refs_3_, bf16[8,8,256,128]{3,2,1,0:T(8,128)(2,1)} %lik_ref.1), custom_call_target="tpu_custom_call" | custom-call | tf_op jit(solution)/shard_map/pallas_call | solution.py:321
  13.6 0.3 collective-permute-done.4.refs_3_
  13.9 0.9 %shard_map.49 = (f32[8,8,256]{2,1,0:T(8,128)S(1)}, f32[64,128]{1,0:T(8,128)S(1)}) custom-call(f32[8,128]{1,0:T(8,128)S(1)} %get-tuple-element.17.refs_4_.refs_0_.info_ref, f32[64,128]{1,0:T(8,128)S(1)} %shard_map.47.after_ref.refs_1_, f32[64,128]{1,0:T(8,128)S(1)} %collective-permute-done.3.refs_2_, f32[64,128]{1,0:T(8,128)S(1)} %collective-permute-done.4.refs_3_, ...), custom_call_target="tpu_custom_call" | custom-call | tf_op jit(solution)/shard_map/pallas_call | solution.py:280
  14.8 9.5 %all_to_all.15.parts_ref = f32[8,8,256]{2,1,0:T(8,128)S(1)} all-to-all(f32[8,8,256]{2,1,0:T(8,128)S(1)} %get-tuple-element.20), channel_id=1, replica_groups={{8,10,12,14,0,2,4,6},{9,11,13,15,1,3,5,7},{24,26,28,30,16,18,20,22},{25..., dimensions={0} | all-to-all | bytes 131072 | tf_op jit(solution)/shard_map/all_to_all | solution.py:365
  24.3 0.7 %shard_map.50.refs_0_ = f32[72,128]{1,0:T(8,128)S(1)} custom-call(f32[8,128]{1,0:T(8,128)S(1)} %get-tuple-element.17.refs_4_.refs_0_.info_ref, f32[8,8,256]{2,1,0:T(8,128)S(1)} %all_to_all.15.parts_ref, f32[64,128]{1,0:T(8,128)S(1)} %get-tuple-element.21.picked_ref, bf16[4,8,256,128]{3,2,1,0:T(8,128)(2,1)S(1)} %get-tuple-element.18.early_ref.refs_3_, ...), custom_call_target="tpu_custom_call" | custom-call | tf_op jit(solution)/shard_map/pallas_call | solution.py:280
  25.0 0.4 collective-permute-start.8
  25.4 0.9 %collective-permute-start.7 = (f32[72,128]{1,0:T(8,128)S(1)}, f32[72,128]{1,0:T(8,128)S(1)}, u32[]{:S(2)}, u32[]{:S(2)}) collective-permute-start(f32[72,128]{1,0:T(8,128)S(1)} %shard_map.50.refs_0_), channel_id=1, source_target_pairs={{0,8},{1,9},{2,10},{3,11},{4,12},{5,13},{6,14},{7,15},{8,0},{9,1},... | collective-permute-start | bytes 110600 | tf_op jit(solution)/shard_map/ppermute | solution.py:29
  26.3 1.7 %collective-permute-start.6 = (f32[72,128]{1,0:T(8,128)S(1)}, f32[72,128]{1,0:T(8,128)S(1)}, u32[]{:S(2)}, u32[]{:S(2)}) collective-permute-start(f32[72,128]{1,0:T(8,128)S(1)} %shard_map.50.refs_0_), channel_id=1, source_target_pairs={{0,4},{1,5},{2,6},{3,7},{4,0},{5,1},{6,2},{7,3},{8,12},{9,13},{10,... | collective-permute-start | bytes 110600 | tf_op jit(solution)/shard_map/ppermute | solution.py:29
  28.0 2.5 %collective-permute-done.8.refs_3_ = f32[72,128]{1,0:T(8,128)S(1)} collective-permute-done((f32[72,128]{1,0:T(8,128)S(1)}, f32[72,128]{1,0:T(8,128)S(1)}, u32[]{:S(2)}, u32[]{:S(2)}) %collective-permute-start.8) | collective-permute-done | bytes 36896 | tf_op jit(solution)/shard_map/ppermute | solution.py:29
  30.5 1.0 %collective-permute-done.7.refs_2_ = f32[72,128]{1,0:T(8,128)S(1)} collective-permute-done((f32[72,128]{1,0:T(8,128)S(1)}, f32[72,128]{1,0:T(8,128)S(1)}, u32[]{:S(2)}, u32[]{:S(2)}) %collective-permute-start.7) | collective-permute-done | bytes 36896 | tf_op jit(solution)/shard_map/ppermute | solution.py:29
  31.5 0.3 shard_map.51
  31.8 0.7 %collective-permute-start.9 = (f32[64,128]{1,0:T(8,128)S(1)}, f32[64,128]{1,0:T(8,128)S(1)}, u32[]{:S(2)}, u32[]{:S(2)}) collective-permute-start(f32[64,128]{1,0:T(8,128)S(1)} %get-tuple-element.24), channel_id=1, source_target_pairs={{0,2},{1,3},{2,0},{3,1},{4,6},{5,7},{6,4},{7,5},{8,10},{9,11},{10,... | collective-permute-start | bytes 98312 | tf_op jit(solution)/shard_map/ppermute | solution.py:29
  32.6 0.8 %collective-permute-start.10 = (f32[64,128]{1,0:T(8,128)S(1)}, f32[64,128]{1,0:T(8,128)S(1)}, u32[]{:S(2)}, u32[]{:S(2)}) collective-permute-start(f32[64,128]{1,0:T(8,128)S(1)} %get-tuple-element.25), channel_id=1, source_target_pairs={{0,3},{1,2},{2,1},{3,0},{4,7},{5,6},{6,5},{7,4},{8,11},{9,10},{10,... | collective-permute-start | bytes 98312 | tf_op jit(solution)/shard_map/ppermute | solution.py:29
  33.4 0.7 %collective-permute-start.11 = (f32[64,128]{1,0:T(8,128)S(1)}, f32[64,128]{1,0:T(8,128)S(1)}, u32[]{:S(2)}, u32[]{:S(2)}) collective-permute-start(f32[64,128]{1,0:T(8,128)S(1)} %get-tuple-element.26), channel_id=1, source_target_pairs={{0,1},{1,0},{2,3},{3,2},{4,5},{5,4},{6,7},{7,6},{8,9},{9,8},{10,11... | collective-permute-start | bytes 98312 | tf_op jit(solution)/shard_map/ppermute | solution.py:29
  34.0 2.0 %collective-permute-done.9.refs_1_ = f32[64,128]{1,0:T(8,128)S(1)} collective-permute-done((f32[64,128]{1,0:T(8,128)S(1)}, f32[64,128]{1,0:T(8,128)S(1)}, u32[]{:S(2)}, u32[]{:S(2)}) %collective-permute-start.9) | collective-permute-done | bytes 32800 | tf_op jit(solution)/shard_map/ppermute | solution.py:29
  36.2 0.7 %shard_map.52 = (f32[8,8,256]{2,1,0:T(8,128)S(1)}, f32[64,128]{1,0:T(8,128)S(1)}) custom-call(f32[64,128]{1,0:T(8,128)S(1)} %get-tuple-element.23.refs_0_, f32[64,128]{1,0:T(8,128)S(1)} %collective-permute-done.9.refs_1_, f32[64,128]{1,0:T(8,128)S(1)} %collective-permute-done.10.refs_2_, f32[64,128]{1,0:T(8,128)S(1)} %collective-permute-done.11.refs_3_, ...), custom_call_target="tpu_custom_call" | custom-call | tf_op jit(solution)/shard_map/pallas_call | solution.py:280
  36.9 8.4 %all_to_all.16.refs_1_ = f32[8,8,256]{2,1,0:T(8,128)S(1)} all-to-all(f32[8,8,256]{2,1,0:T(8,128)S(1)} %get-tuple-element.27), channel_id=1, replica_groups={{10,8,14,12,2,0,6,4},{11,9,15,13,3,1,7,5},{26,24,30,28,18,16,22,20},{27..., dimensions={0} | all-to-all | bytes 131072 | tf_op jit(solution)/shard_map/all_to_all | solution.py:365
  45.3 0.9 %shard_map.53 = f32[16,12,128]{2,1,0:T(8,128)S(1)} custom-call(f32[8,128]{1,0:T(8,128)S(1)} %get-tuple-element.17.refs_4_.refs_0_.info_ref, f32[8,8,256]{2,1,0:T(8,128)S(1)} %all_to_all.16.refs_1_, f32[64,128]{1,0:T(8,128)S(1)} %get-tuple-element.28.refs_2_, bf16[4,8,256,128]{3,2,1,0:T(8,128)(2,1)S(1)} %get-tuple-element.18.early_ref.refs_3_, ...), custom_call_target="tpu_custom_call" | custom-call | tf_op jit(solution)/shard_map/pallas_call | solution.py:280
  46.2 8.3 %all_to_all.17 = f32[16,12,128]{2,1,0:T(8,128)S(1)} all-to-all(f32[16,12,128]{2,1,0:T(8,128)S(1)} %shard_map.53), channel_id=1, replica_groups={{11,10,9,8,15,14,13,12,3,2,1,0,7,6,5,4},{27,26,25,24,31,30,29,28,19,18,..., dimensions={0} | all-to-all | bytes 196608 | tf_op jit(solution)/shard_map/all_to_all | solution.py:404
  54.6 0.6 %multiply_bitcast_fusion = f32[1536]{0:T(1024)} fusion(f32[12,128]{1,0:T(8,128)S(1)} %reduce_sum.9), kind=kLoop, calls=%fused_computation | loop fusion | flops 1536 | bytes 12288 | tf_op jit(solution)/shard_map/mul | solution.py:405
  (18 shorter events, 0.9 us)
Async XLA Ops:
  0.0 9.8 %copy-start = (f32[1536]{0:T(1024)S(1)}, f32[1536]{0:T(1024)}, u32[]{:S(2)}) copy-start(f32[1536]{0:T(1024)} %param.7) | copy-start | bytes 18436
  0.0 7.0 %collective-permute-start.2 = (f32[12,128]{1,0:T(8,128)}, f32[12,128]{1,0:T(8,128)S(1)}, u32[]{:S(2)}, u32[]{:S(2)}) collective-permute-start(f32[12,128]{1,0:T(8,128)} %bitcast.3), channel_id=1, source_target_pairs={{0,12},{1,13},{2,14},{3,15},{4,8},{5,9},{6,10},{7,11},{8,4},{9,5},... | collective-permute-start | bytes 18440 | tf_op jit(solution)/shard_map/ppermute | solution.py:29
  5.1 4.8 %collective-permute-start.1 = (f32[12,128]{1,0:T(8,128)}, f32[12,128]{1,0:T(8,128)S(1)}, u32[]{:S(2)}, u32[]{:S(2)}) collective-permute-start(f32[12,128]{1,0:T(8,128)} %bitcast.4), channel_id=1, source_target_pairs={{0,8},{1,9},{2,10},{3,11},{4,12},{5,13},{6,14},{7,15},{8,0},{9,1},... | collective-permute-start | bytes 18440 | tf_op jit(solution)/shard_map/ppermute | solution.py:29
  5.1 4.8 %collective-permute-start = (f32[12,128]{1,0:T(8,128)}, f32[12,128]{1,0:T(8,128)S(1)}, u32[]{:S(2)}, u32[]{:S(2)}) collective-permute-start(f32[12,128]{1,0:T(8,128)} %bitcast.5), channel_id=1, source_target_pairs={{0,5},{1,4},{2,7},{3,6},{4,1},{5,0},{6,3},{7,2},{8,13},{9,12},{10,... | collective-permute-start | bytes 18440 | tf_op jit(solution)/shard_map/ppermute | solution.py:29
  9.8 3.8 %collective-permute-start.5 = (f32[64,128]{1,0:T(8,128)S(1)}, f32[64,128]{1,0:T(8,128)S(1)}, u32[]{:S(2)}, u32[]{:S(2)}) collective-permute-start(f32[64,128]{1,0:T(8,128)S(1)} %shard_map.47.after_ref.refs_1_), channel_id=1, source_target_pairs={{0,3},{1,2},{2,1},{3,0},{4,7},{5,6},{6,5},{7,4},{8,11},{9,10},{10,... | collective-permute-start | bytes 98312 | tf_op jit(solution)/shard_map/ppermute | solution.py:29
  9.9 4.0 %collective-permute-start.4 = (f32[64,128]{1,0:T(8,128)S(1)}, f32[64,128]{1,0:T(8,128)S(1)}, u32[]{:S(2)}, u32[]{:S(2)}) collective-permute-start(f32[64,128]{1,0:T(8,128)S(1)} %shard_map.47.after_ref.refs_1_), channel_id=1, source_target_pairs={{0,2},{1,3},{2,0},{3,1},{4,6},{5,7},{6,4},{7,5},{8,10},{9,11},{10,... | collective-permute-start | bytes 98312 | tf_op jit(solution)/shard_map/ppermute | solution.py:29
  11.5 2.4 %collective-permute-start.3 = (f32[64,128]{1,0:T(8,128)S(1)}, f32[64,128]{1,0:T(8,128)S(1)}, u32[]{:S(2)}, u32[]{:S(2)}) collective-permute-start(f32[64,128]{1,0:T(8,128)S(1)} %shard_map.47.after_ref.refs_1_), channel_id=1, source_target_pairs={{0,1},{1,0},{2,3},{3,2},{4,5},{5,4},{6,7},{7,6},{8,9},{9,8},{10,11... | collective-permute-start | bytes 98312 | tf_op jit(solution)/shard_map/ppermute | solution.py:29
  25.0 5.5 %collective-permute-start.8 = (f32[72,128]{1,0:T(8,128)S(1)}, f32[72,128]{1,0:T(8,128)S(1)}, u32[]{:S(2)}, u32[]{:S(2)}) collective-permute-start(f32[72,128]{1,0:T(8,128)S(1)} %shard_map.50.refs_0_), channel_id=1, source_target_pairs={{0,13},{1,12},{2,15},{3,14},{4,9},{5,8},{6,11},{7,10},{8,5},{9,4},... | collective-permute-start | bytes 110600 | tf_op jit(solution)/shard_map/ppermute | solution.py:29
  25.4 6.1 %collective-permute-start.7 = (f32[72,128]{1,0:T(8,128)S(1)}, f32[72,128]{1,0:T(8,128)S(1)}, u32[]{:S(2)}, u32[]{:S(2)}) collective-permute-start(f32[72,128]{1,0:T(8,128)S(1)} %shard_map.50.refs_0_), channel_id=1, source_target_pairs={{0,8},{1,9},{2,10},{3,11},{4,12},{5,13},{6,14},{7,15},{8,0},{9,1},... | collective-permute-start | bytes 110600 | tf_op jit(solution)/shard_map/ppermute | solution.py:29
  26.3 5.2 %collective-permute-start.6 = (f32[72,128]{1,0:T(8,128)S(1)}, f32[72,128]{1,0:T(8,128)S(1)}, u32[]{:S(2)}, u32[]{:S(2)}) collective-permute-start(f32[72,128]{1,0:T(8,128)S(1)} %shard_map.50.refs_0_), channel_id=1, source_target_pairs={{0,4},{1,5},{2,6},{3,7},{4,0},{5,1},{6,2},{7,3},{8,12},{9,13},{10,... | collective-permute-start | bytes 110600 | tf_op jit(solution)/shard_map/ppermute | solution.py:29
  31.8 4.2 %collective-permute-start.9 = (f32[64,128]{1,0:T(8,128)S(1)}, f32[64,128]{1,0:T(8,128)S(1)}, u32[]{:S(2)}, u32[]{:S(2)}) collective-permute-start(f32[64,128]{1,0:T(8,128)S(1)} %get-tuple-element.24), channel_id=1, source_target_pairs={{0,2},{1,3},{2,0},{3,1},{4,6},{5,7},{6,4},{7,5},{8,10},{9,11},{10,... | collective-permute-start | bytes 98312 | tf_op jit(solution)/shard_map/ppermute | solution.py:29
  32.6 3.7 %collective-permute-start.10 = (f32[64,128]{1,0:T(8,128)S(1)}, f32[64,128]{1,0:T(8,128)S(1)}, u32[]{:S(2)}, u32[]{:S(2)}) collective-permute-start(f32[64,128]{1,0:T(8,128)S(1)} %get-tuple-element.25), channel_id=1, source_target_pairs={{0,3},{1,2},{2,1},{3,0},{4,7},{5,6},{6,5},{7,4},{8,11},{9,10},{10,... | collective-permute-start | bytes 98312 | tf_op jit(solution)/shard_map/ppermute | solution.py:29
  33.4 2.9 %collective-permute-start.11 = (f32[64,128]{1,0:T(8,128)S(1)}, f32[64,128]{1,0:T(8,128)S(1)}, u32[]{:S(2)}, u32[]{:S(2)}) collective-permute-start(f32[64,128]{1,0:T(8,128)S(1)} %get-tuple-element.26), channel_id=1, source_target_pairs={{0,1},{1,0},{2,3},{3,2},{4,5},{5,4},{6,7},{7,6},{8,9},{9,8},{10,11... | collective-permute-start | bytes 98312 | tf_op jit(solution)/shard_map/ppermute | solution.py:29

commit v17 on v15

--- a/solution.py
+++ b/solution.py
@@ -7,7 +7,7 @@
 
 ITERS = 2
 ALL = ("genome", "reads")
-TERMS = 16
+TERMS = 8
 ID_ROWS = 8
 CROSSED = (1,)
 LANES = 128
@@ -159,7 +159,7 @@
     return -(-(far * own_blocks + ID_ROWS) // 16) * 16
 
 
-def flip_kernel(after_ref, early_ref, lik_ref, late_ref, out_ref, sems):
+def flip_kernel(after_ref, info_ref, early_ref, lik_ref, late_ref, out_ref, pick_ref, count_ref, sems):
     early = early_ref.shape[0]
     copies = block_copies(lik_ref, late_ref, sems, early)
     for copy in copies:
@@ -172,6 +172,10 @@
         for s in range(slots):
             start = s % 2 * cols
             out_ref[b, s // 2, start : start + cols, :] = jnp.transpose(held_ref[s])
+    all_slots, picks = pick_ref.shape
+    pick_ref[...] = hot_rows(info_ref[1:2, :], picks)[:all_slots].astype(jnp.bfloat16)
+    block = lax.broadcasted_iota(jnp.int32, count_ref.shape, 0).astype(jnp.float32)
+    count_ref[...] = (block == info_ref[0:1, : count_ref.shape[1]]).astype(jnp.bfloat16)
 
 
 def block_copies(lik_ref, held_ref, sems, start):
@@ -203,11 +207,10 @@
             out_ref[i, b : b + 1, :] = row
 
 
-def first_row_kernel(near, info_ref, *refs):
+def first_row_kernel(near, pick_ref, *refs):
     pieces, (flip_ref, out_ref, picked_ref) = refs[:near], refs[near:]
     table = jnp.concatenate([piece[...] for piece in pieces], axis=0)
-    hot = hot_rows(info_ref[1:2, :], table.shape[0])
-    picked_ref[...] = select_rows(hot[: picked_ref.shape[0]], table)
+    picked_ref[...] = select_rows(pick_ref[...], table)
     row_sums(picked_ref, flip_ref, out_ref)
 
 
@@ -243,14 +246,11 @@
 
 
 def last_column_kernel(
-    order, info_ref, parts_ref, picked_ref, early_ref, late_ref, out_ref, inverse_ref, contrib_ref
+    order, count_ref, parts_ref, picked_ref, early_ref, late_ref, out_ref, inverse_ref, contrib_ref
 ):
     column_sums(parts_ref, picked_ref, (early_ref, late_ref), contrib_ref, inverse_ref)
     owners, own_blocks, cols = out_ref.shape
-    all_slots = contrib_ref.shape[0]
-    block = lax.broadcasted_iota(jnp.int32, (owners * own_blocks, all_slots), 0)
-    hot = (block.astype(jnp.float32) == info_ref[0:1, :all_slots]).astype(jnp.float32)
-    counts = select_rows(hot, contrib_ref[...])
+    counts = select_rows(count_ref[...], contrib_ref[...])
     for i, owner in enumerate(order):
         out_ref[i] = counts[owner * own_blocks : (owner + 1) * own_blocks, :]
 
@@ -315,7 +315,7 @@
     )(*in_hbm(likelihood, block_ids, slot_valid))
 
 
-def flip(after, held, likelihood):
+def flip(picks, blocks, after, info, held, likelihood):
     read_blocks, slots, reads, cols = likelihood.shape
     late = read_blocks - held.shape[0]
     return pl.pallas_call(
@@ -323,12 +323,14 @@
         out_shape=[
             pltpu.VMEM((late,) + likelihood.shape[1:], likelihood.dtype),
             pltpu.VMEM((read_blocks, slots // 2, 2 * cols, reads), likelihood.dtype),
+            pltpu.VMEM((read_blocks * slots, picks), jnp.bfloat16),
+            pltpu.VMEM((blocks, read_blocks * slots), jnp.bfloat16),
         ],
-        in_specs=[ANY, VMEM, ANY],
-        out_specs=[VMEM] * 2,
+        in_specs=[ANY, VMEM, VMEM, ANY],
+        out_specs=[VMEM] * 4,
         scratch_shapes=[pltpu.SemaphoreType.DMA((late,))],
         compiler_params=PARAMS,
-    )(after, held, *in_hbm(likelihood))
+    )(after, info, held, *in_hbm(likelihood))
 
 
 def local(likelihood, block_ids, slot_valid, start_weights):
@@ -346,7 +348,9 @@
     column = gather_far(own_weights, ALL, CROSSED)
     held, info = prepare(own_blocks, read_blocks // 2, likelihood, block_ids, slot_valid)
     (sent,) = call(join_kernel, [(near_rows(far, own_blocks), cols)], [], *column, info)
-    rest, flipped = flip(sent, held, likelihood)
+    rest, flipped, pick, count = flip(
+        near * sent.shape[0], n * own_blocks, sent, info, held, likelihood
+    )
     pieces = [sent] + [swap(sent, ALL, j) for j in range(1, near)]
     at = far * own_blocks
     wanted = [info] + [piece[at : at + ID_ROWS] for piece in pieces[1:]]
@@ -356,7 +360,7 @@
     for step in range(ITERS):
         if step == 0:
             row_parts, picked = call(
-                lambda *refs: first_row_kernel(near, *refs), row_shapes, [], info, *pieces, flipped
+                lambda *refs: first_row_kernel(near, *refs), row_shapes, [], pick, *pieces, flipped
             )
         else:
             row_parts, picked = call(
@@ -395,7 +399,7 @@
         lambda *refs: last_column_kernel(order, *refs),
         [(n, own_blocks, cols)],
         [inverse, (all_slots, cols)],
-        info,
+        count,
         row_parts,
         picked,
         held,

time: 55.6 us -> 55.6 us (level)
  no operation moved by 1% of the time
where the time goes in v17:
time: 55.6 us; the launch traced here: 55.1 us
  blocking collectives  26.4 us (47%)
  starting transfers between devices  12.5 us (22%)
  waiting for transfers between devices  8.59 us (15%)
  Pallas kernels  6.84 us (12%)
  other arithmetic  0.62 us (1%)
    all_to_all x2, blocking collectives, local(): lax.all_to_all(row_parts, 'genome', 0, 0, tiled=True, axis_index_groups=[...  18 us
    ppermute x12, starting transfers between devices, swap(): return lax.ppermute(x, axes, [(i, i ^ k) for i in range(n)])  12.5 us
    ppermute x12, waiting for transfers between devices, swap(): return lax.ppermute(x, axes, [(i, i ^ k) for i in range(n)])  8.59 us
    all_to_all x1, blocking collectives, local(): lax.all_to_all(counts, ALL, 0, 0, tiled=True, axis_index_groups=[order])  8.33 us
    pallas_call x6, Pallas kernels, call(): pl.pallas_call(kernel, out_shape=[jax.ShapeDtypeStruct(shape, jnp.float32...  3.37 us
    pallas_call x1, Pallas kernels, flip(): pl.pallas_call(flip_kernel, out_shape=[pltpu.VMEM((late,) + likelihood.sh...  1.87 us
    pallas_call x1, Pallas kernels, prepare(): pl.pallas_call(lambda *refs: prepare_kernel(own_blocks, *refs), out_shape...  1.6 us
  transfers between devices with their start and end apart: 12, of which 7 were waited for; matrix products, arithmetic and copies ran while one was open for 0% of the time, Pallas kernels for 6%

profile of v17, /device:TPU:0, one launch (start us, length us, event | category | flops | bytes accessed | tf_op | source)
XLA Modules:
  0.0 55.1 jit_solution(2802315363885004869)
XLA Ops:
  0.0 5.0 %collective-permute-start.2 = (f32[12,128]{1,0:T(8,128)}, f32[12,128]{1,0:T(8,128)S(1)}, u32[]{:S(2)}, u32[]{:S(2)}) collective-permute-start(f32[12,128]{1,0:T(8,128)} %bitcast.3), channel_id=1, source_target_pairs={{0,12},{1,13},{2,14},{3,15},{4,8},{5,9},{6,10},{7,11},{8,4},{9,5},... | collective-permute-start | bytes 18440 | tf_op jit(solution)/shard_map/ppermute | solution.py:29
  5.1 1.6 %shard_map.46 = (bf16[4,8,256,128]{3,2,1,0:T(8,128)(2,1)S(1)}, f32[8,128]{1,0:T(8,128)S(1)}) custom-call(bf16[8,8,256,128]{3,2,1,0:T(8,128)(2,1)} %lik_ref.1, s32[8,8]{1,0:T(8,128)} %refs_1_.1, s32[8,8]{1,0:T(8,128)} %refs_2_.1), custom_call_target="tpu_custom_call" | custom-call | tf_op jit(solution)/shard_map/pallas_call | solution.py:299
  6.7 0.3 collective-permute-done.2.refs_3_
  7.0 2.9 %collective-permute-done.1.refs_2_ = f32[12,128]{1,0:T(8,128)S(1)} collective-permute-done((f32[12,128]{1,0:T(8,128)}, f32[12,128]{1,0:T(8,128)S(1)}, u32[]{:S(2)}, u32[]{:S(2)}) %collective-permute-start.1) | collective-permute-done | bytes 6176 | tf_op jit(solution)/shard_map/ppermute | solution.py:29
  9.9 1.6 %collective-permute-start.4 = (f32[64,128]{1,0:T(8,128)S(1)}, f32[64,128]{1,0:T(8,128)S(1)}, u32[]{:S(2)}, u32[]{:S(2)}) collective-permute-start(f32[64,128]{1,0:T(8,128)S(1)} %shard_map.47.after_ref.refs_1_), channel_id=1, source_target_pairs={{0,2},{1,3},{2,0},{3,1},{4,6},{5,7},{6,4},{7,5},{8,10},{9,11},{10,... | collective-permute-start | bytes 98312 | tf_op jit(solution)/shard_map/ppermute | solution.py:29
  11.8 1.9 %shard_map.48 = (bf16[4,8,256,128]{3,2,1,0:T(8,128)(2,1)S(1)}, bf16[8,4,256,256]{3,2,1,0:T(8,128)(2,1)S(1)}, bf16[64,256]{1,0:T(8,128)(2,1)S(1)}, bf16[192,64]{1,0:T(8,128)(2,1)S(1)}) custom-call(f32[64,128]{1,0:T(8,128)S(1)} %shard_map.47.after_ref.refs_1_, f32[8,128]{1,0:T(8,128)S(1)} %get-tuple-element.19.refs_4_.info_ref, ...), custom_call_target="tpu_custom_call" | custom-call | tf_op jit(solution)/shard_map/pallas_call | solution.py:321
  13.6 0.3 collective-permute-done.4.refs_3_
  13.9 0.8 %shard_map.49 = (f32[8,8,256]{2,1,0:T(8,128)S(1)}, f32[64,128]{1,0:T(8,128)S(1)}) custom-call(bf16[64,256]{1,0:T(8,128)(2,1)S(1)} %get-tuple-element.22.refs_0_, f32[64,128]{1,0:T(8,128)S(1)} %shard_map.47.after_ref.refs_1_, f32[64,128]{1,0:T(8,128)S(1)} %collective-permute-done.3.refs_2_, f32[64,128]{1,0:T(8,128)S(1)} %collective-permute-done.4.refs_3_, ...), custom_call_target="tpu_custom_call" | custom-call | tf_op jit(solution)/shard_map/pallas_call | solution.py:280
  14.8 9.5 %all_to_all.15.parts_ref = f32[8,8,256]{2,1,0:T(8,128)S(1)} all-to-all(f32[8,8,256]{2,1,0:T(8,128)S(1)} %get-tuple-element.24), channel_id=1, replica_groups={{8,10,12,14,0,2,4,6},{9,11,13,15,1,3,5,7},{24,26,28,30,16,18,20,22},{25..., dimensions={0} | all-to-all | bytes 131072 | tf_op jit(solution)/shard_map/all_to_all | solution.py:369
  24.3 0.7 %shard_map.50.refs_0_ = f32[72,128]{1,0:T(8,128)S(1)} custom-call(f32[8,128]{1,0:T(8,128)S(1)} %get-tuple-element.19.refs_4_.info_ref, f32[8,8,256]{2,1,0:T(8,128)S(1)} %all_to_all.15.parts_ref, f32[64,128]{1,0:T(8,128)S(1)} %get-tuple-element.25.picked_ref, bf16[4,8,256,128]{3,2,1,0:T(8,128)(2,1)S(1)} %get-tuple-element.20.early_ref.refs_3_, ...), custom_call_target="tpu_custom_call" | custom-call | tf_op jit(solution)/shard_map/pallas_call | solution.py:280
  24.9 0.4 collective-permute-start.8
  25.3 1.4 %collective-permute-start.7 = (f32[72,128]{1,0:T(8,128)S(1)}, f32[72,128]{1,0:T(8,128)S(1)}, u32[]{:S(2)}, u32[]{:S(2)}) collective-permute-start(f32[72,128]{1,0:T(8,128)S(1)} %shard_map.50.refs_0_), channel_id=1, source_target_pairs={{0,9},{1,8},{2,11},{3,10},{4,13},{5,12},{6,15},{7,14},{8,1},{9,0},... | collective-permute-start | bytes 110600 | tf_op jit(solution)/shard_map/ppermute | solution.py:29
  26.7 0.9 %collective-permute-start.6 = (f32[72,128]{1,0:T(8,128)S(1)}, f32[72,128]{1,0:T(8,128)S(1)}, u32[]{:S(2)}, u32[]{:S(2)}) collective-permute-start(f32[72,128]{1,0:T(8,128)S(1)} %shard_map.50.refs_0_), channel_id=1, source_target_pairs={{0,5},{1,4},{2,7},{3,6},{4,1},{5,0},{6,3},{7,2},{8,13},{9,12},{10,... | collective-permute-start | bytes 110600 | tf_op jit(solution)/shard_map/ppermute | solution.py:29
  27.6 2.6 %collective-permute-done.8.refs_3_ = f32[72,128]{1,0:T(8,128)S(1)} collective-permute-done((f32[72,128]{1,0:T(8,128)S(1)}, f32[72,128]{1,0:T(8,128)S(1)}, u32[]{:S(2)}, u32[]{:S(2)}) %collective-permute-start.8) | collective-permute-done | bytes 36896 | tf_op jit(solution)/shard_map/ppermute | solution.py:29
  30.5 0.3 shard_map.51
  30.8 1.2 %collective-permute-start.9 = (f32[64,128]{1,0:T(8,128)S(1)}, f32[64,128]{1,0:T(8,128)S(1)}, u32[]{:S(2)}, u32[]{:S(2)}) collective-permute-start(f32[64,128]{1,0:T(8,128)S(1)} %get-tuple-element.28), channel_id=1, source_target_pairs={{0,3},{1,2},{2,1},{3,0},{4,7},{5,6},{6,5},{7,4},{8,11},{9,10},{10,... | collective-permute-start | bytes 98312 | tf_op jit(solution)/shard_map/ppermute | solution.py:29
  32.0 1.6 %collective-permute-start.10 = (f32[64,128]{1,0:T(8,128)S(1)}, f32[64,128]{1,0:T(8,128)S(1)}, u32[]{:S(2)}, u32[]{:S(2)}) collective-permute-start(f32[64,128]{1,0:T(8,128)S(1)} %get-tuple-element.29), channel_id=1, source_target_pairs={{0,2},{1,3},{2,0},{3,1},{4,6},{5,7},{6,4},{7,5},{8,10},{9,11},{10,... | collective-permute-start | bytes 98312 | tf_op jit(solution)/shard_map/ppermute | solution.py:29
  33.7 0.5 collective-permute-done.9.refs_1_
  34.2 1.7 %collective-permute-done.10.refs_2_ = f32[64,128]{1,0:T(8,128)S(1)} collective-permute-done((f32[64,128]{1,0:T(8,128)S(1)}, f32[64,128]{1,0:T(8,128)S(1)}, u32[]{:S(2)}, u32[]{:S(2)}) %collective-permute-start.10) | collective-permute-done | bytes 32800 | tf_op jit(solution)/shard_map/ppermute | solution.py:29
  36.0 0.7 %shard_map.52 = (f32[8,8,256]{2,1,0:T(8,128)S(1)}, f32[64,128]{1,0:T(8,128)S(1)}) custom-call(f32[64,128]{1,0:T(8,128)S(1)} %get-tuple-element.27.refs_0_, f32[64,128]{1,0:T(8,128)S(1)} %collective-permute-done.9.refs_1_, f32[64,128]{1,0:T(8,128)S(1)} %collective-permute-done.10.refs_2_, f32[64,128]{1,0:T(8,128)S(1)} %collective-permute-done.11.refs_3_, ...), custom_call_target="tpu_custom_call" | custom-call | tf_op jit(solution)/shard_map/pallas_call | solution.py:280
  36.6 8.5 %all_to_all.16.refs_1_ = f32[8,8,256]{2,1,0:T(8,128)S(1)} all-to-all(f32[8,8,256]{2,1,0:T(8,128)S(1)} %get-tuple-element.31), channel_id=1, replica_groups={{10,8,14,12,2,0,6,4},{11,9,15,13,3,1,7,5},{26,24,30,28,18,16,22,20},{27..., dimensions={0} | all-to-all | bytes 131072 | tf_op jit(solution)/shard_map/all_to_all | solution.py:369
  45.2 0.9 %shard_map.53 = f32[16,12,128]{2,1,0:T(8,128)S(1)} custom-call(bf16[192,64]{1,0:T(8,128)(2,1)S(1)} %get-tuple-element.21.refs_0_, f32[8,8,256]{2,1,0:T(8,128)S(1)} %all_to_all.16.refs_1_, f32[64,128]{1,0:T(8,128)S(1)} %get-tuple-element.32.refs_2_, bf16[4,8,256,128]{3,2,1,0:T(8,128)(2,1)S(1)} %get-tuple-element.20.early_ref.refs_3_, ...), custom_call_target="tpu_custom_call" | custom-call | tf_op jit(solution)/shard_map/pallas_call | solution.py:280
  46.1 8.3 %all_to_all.17 = f32[16,12,128]{2,1,0:T(8,128)S(1)} all-to-all(f32[16,12,128]{2,1,0:T(8,128)S(1)} %shard_map.53), channel_id=1, replica_groups={{11,10,9,8,15,14,13,12,3,2,1,0,7,6,5,4},{27,26,25,24,31,30,29,28,19,18,..., dimensions={0} | all-to-all | bytes 196608 | tf_op jit(solution)/shard_map/all_to_all | solution.py:408
  54.5 0.6 %multiply_bitcast_fusion = f32[1536]{0:T(1024)} fusion(f32[12,128]{1,0:T(8,128)S(1)} %reduce_sum.9), kind=kLoop, calls=%fused_computation | loop fusion | flops 1536 | bytes 12288 | tf_op jit(solution)/shard_map/mul | solution.py:409
  (18 shorter events, 0.6 us)
Async XLA Ops:
  0.0 9.8 %copy-start = (f32[1536]{0:T(1024)S(1)}, f32[1536]{0:T(1024)}, u32[]{:S(2)}) copy-start(f32[1536]{0:T(1024)} %param.7) | copy-start | bytes 18436
  0.0 7.0 %collective-permute-start.2 = (f32[12,128]{1,0:T(8,128)}, f32[12,128]{1,0:T(8,128)S(1)}, u32[]{:S(2)}, u32[]{:S(2)}) collective-permute-start(f32[12,128]{1,0:T(8,128)} %bitcast.3), channel_id=1, source_target_pairs={{0,12},{1,13},{2,14},{3,15},{4,8},{5,9},{6,10},{7,11},{8,4},{9,5},... | collective-permute-start | bytes 18440 | tf_op jit(solution)/shard_map/ppermute | solution.py:29
  5.1 4.8 %collective-permute-start.1 = (f32[12,128]{1,0:T(8,128)}, f32[12,128]{1,0:T(8,128)S(1)}, u32[]{:S(2)}, u32[]{:S(2)}) collective-permute-start(f32[12,128]{1,0:T(8,128)} %bitcast.4), channel_id=1, source_target_pairs={{0,8},{1,9},{2,10},{3,11},{4,12},{5,13},{6,14},{7,15},{8,0},{9,1},... | collective-permute-start | bytes 18440 | tf_op jit(solution)/shard_map/ppermute | solution.py:29
  5.1 4.8 %collective-permute-start = (f32[12,128]{1,0:T(8,128)}, f32[12,128]{1,0:T(8,128)S(1)}, u32[]{:S(2)}, u32[]{:S(2)}) collective-permute-start(f32[12,128]{1,0:T(8,128)} %bitcast.5), channel_id=1, source_target_pairs={{0,5},{1,4},{2,7},{3,6},{4,1},{5,0},{6,3},{7,2},{8,13},{9,12},{10,... | collective-permute-start | bytes 18440 | tf_op jit(solution)/shard_map/ppermute | solution.py:29
  9.8 3.8 %collective-permute-start.5 = (f32[64,128]{1,0:T(8,128)S(1)}, f32[64,128]{1,0:T(8,128)S(1)}, u32[]{:S(2)}, u32[]{:S(2)}) collective-permute-start(f32[64,128]{1,0:T(8,128)S(1)} %shard_map.47.after_ref.refs_1_), channel_id=1, source_target_pairs={{0,3},{1,2},{2,1},{3,0},{4,7},{5,6},{6,5},{7,4},{8,11},{9,10},{10,... | collective-permute-start | bytes 98312 | tf_op jit(solution)/shard_map/ppermute | solution.py:29
  9.9 4.0 %collective-permute-start.4 = (f32[64,128]{1,0:T(8,128)S(1)}, f32[64,128]{1,0:T(8,128)S(1)}, u32[]{:S(2)}, u32[]{:S(2)}) collective-permute-start(f32[64,128]{1,0:T(8,128)S(1)} %shard_map.47.after_ref.refs_1_), channel_id=1, source_target_pairs={{0,2},{1,3},{2,0},{3,1},{4,6},{5,7},{6,4},{7,5},{8,10},{9,11},{10,... | collective-permute-start | bytes 98312 | tf_op jit(solution)/shard_map/ppermute | solution.py:29
  11.5 2.4 %collective-permute-start.3 = (f32[64,128]{1,0:T(8,128)S(1)}, f32[64,128]{1,0:T(8,128)S(1)}, u32[]{:S(2)}, u32[]{:S(2)}) collective-permute-start(f32[64,128]{1,0:T(8,128)S(1)} %shard_map.47.after_ref.refs_1_), channel_id=1, source_target_pairs={{0,1},{1,0},{2,3},{3,2},{4,5},{5,4},{6,7},{7,6},{8,9},{9,8},{10,11... | collective-permute-start | bytes 98312 | tf_op jit(solution)/shard_map/ppermute | solution.py:29
  24.9 5.4 %collective-permute-start.8 = (f32[72,128]{1,0:T(8,128)S(1)}, f32[72,128]{1,0:T(8,128)S(1)}, u32[]{:S(2)}, u32[]{:S(2)}) collective-permute-start(f32[72,128]{1,0:T(8,128)S(1)} %shard_map.50.refs_0_), channel_id=1, source_target_pairs={{0,13},{1,12},{2,15},{3,14},{4,9},{5,8},{6,11},{7,10},{8,5},{9,4},... | collective-permute-start | bytes 110600 | tf_op jit(solution)/shard_map/ppermute | solution.py:29
  25.3 5.0 %collective-permute-start.7 = (f32[72,128]{1,0:T(8,128)S(1)}, f32[72,128]{1,0:T(8,128)S(1)}, u32[]{:S(2)}, u32[]{:S(2)}) collective-permute-start(f32[72,128]{1,0:T(8,128)S(1)} %shard_map.50.refs_0_), channel_id=1, source_target_pairs={{0,9},{1,8},{2,11},{3,10},{4,13},{5,12},{6,15},{7,14},{8,1},{9,0},... | collective-permute-start | bytes 110600 | tf_op jit(solution)/shard_map/ppermute | solution.py:29
  26.7 3.8 %collective-permute-start.6 = (f32[72,128]{1,0:T(8,128)S(1)}, f32[72,128]{1,0:T(8,128)S(1)}, u32[]{:S(2)}, u32[]{:S(2)}) collective-permute-start(f32[72,128]{1,0:T(8,128)S(1)} %shard_map.50.refs_0_), channel_id=1, source_target_pairs={{0,5},{1,4},{2,7},{3,6},{4,1},{5,0},{6,3},{7,2},{8,13},{9,12},{10,... | collective-permute-start | bytes 110600 | tf_op jit(solution)/shard_map/ppermute | solution.py:29
  30.8 3.4 %collective-permute-start.9 = (f32[64,128]{1,0:T(8,128)S(1)}, f32[64,128]{1,0:T(8,128)S(1)}, u32[]{:S(2)}, u32[]{:S(2)}) collective-permute-start(f32[64,128]{1,0:T(8,128)S(1)} %get-tuple-element.28), channel_id=1, source_target_pairs={{0,3},{1,2},{2,1},{3,0},{4,7},{5,6},{6,5},{7,4},{8,11},{9,10},{10,... | collective-permute-start | bytes 98312 | tf_op jit(solution)/shard_map/ppermute | solution.py:29
  32.0 3.9 %collective-permute-start.10 = (f32[64,128]{1,0:T(8,128)S(1)}, f32[64,128]{1,0:T(8,128)S(1)}, u32[]{:S(2)}, u32[]{:S(2)}) collective-permute-start(f32[64,128]{1,0:T(8,128)S(1)} %get-tuple-element.29), channel_id=1, source_target_pairs={{0,2},{1,3},{2,0},{3,1},{4,6},{5,7},{6,4},{7,5},{8,10},{9,11},{10,... | collective-permute-start | bytes 98312 | tf_op jit(solution)/shard_map/ppermute | solution.py:29
  33.7 2.3 %collective-permute-start.11 = (f32[64,128]{1,0:T(8,128)S(1)}, f32[64,128]{1,0:T(8,128)S(1)}, u32[]{:S(2)}, u32[]{:S(2)}) collective-permute-start(f32[64,128]{1,0:T(8,128)S(1)} %get-tuple-element.30), channel_id=1, source_target_pairs={{0,1},{1,0},{2,3},{3,2},{4,5},{5,4},{6,7},{7,6},{8,9},{9,8},{10,11... | collective-permute-start | bytes 98312 | tf_op jit(solution)/shard_map/ppermute | solution.py:29

commit v18 on v15

--- a/solution.py
+++ b/solution.py
@@ -30,7 +30,7 @@
 
 
 def middle_first(n, k):
-    return [i ^ k for i in range(n)]
+    return [k] + sorted((i for i in range(n) if i != k), key=lambda i: (-abs(i - k), i))
 
 
 def position(k, n):

time: 55.6 us -> 56.8 us (1.022)
  blocking collectives: 26.4 us -> 27.3 us
  waiting for transfers between devices: 8.63 us -> 9.29 us
    all_to_all x1, blocking collectives: 8.33 us -> 9.37 us  [local(): lax.all_to_all(counts, ALL, 0, 0, tiled=True, axis_index_groups=[order])]
    ppermute x12, waiting for transfers between devices: 8.63 us -> 9.29 us  [swap(): return lax.ppermute(x, axes, [(i, i ^ k) for i in range(n)])]
where the time goes in v18:
time: 56.8 us; the launch traced here: 56.5 us
  blocking collectives  27.3 us (48%)
  starting transfers between devices  12.3 us (22%)
  waiting for transfers between devices  9.29 us (16%)
  Pallas kernels  6.89 us (12%)
  other arithmetic  0.62 us (1%)
    all_to_all x2, blocking collectives, local(): lax.all_to_all(row_parts, 'genome', 0, 0, tiled=True, axis_index_groups=[...  17.9 us
    ppermute x12, starting transfers between devices, swap(): return lax.ppermute(x, axes, [(i, i ^ k) for i in range(n)])  12.3 us
    all_to_all x1, blocking collectives, local(): lax.all_to_all(counts, ALL, 0, 0, tiled=True, axis_index_groups=[order])  9.37 us
    ppermute x12, waiting for transfers between devices, swap(): return lax.ppermute(x, axes, [(i, i ^ k) for i in range(n)])  9.29 us
    pallas_call x6, Pallas kernels, call(): pl.pallas_call(kernel, out_shape=[jax.ShapeDtypeStruct(shape, jnp.float32...  3.46 us
    pallas_call x1, Pallas kernels, flip(): pl.pallas_call(flip_kernel, out_shape=[pltpu.VMEM((late,) + likelihood.sh...  1.84 us
    pallas_call x1, Pallas kernels, prepare(): pl.pallas_call(lambda *refs: prepare_kernel(own_blocks, *refs), out_shape...  1.6 us
  transfers between devices with their start and end apart: 12, of which 7 were waited for; matrix products, arithmetic and copies ran while one was open for 0% of the time, Pallas kernels for 6%

profile of v18, /device:TPU:0, one launch (start us, length us, event | category | flops | bytes accessed | tf_op | source)
XLA Modules:
  0.0 56.5 jit_solution(8680080762835035086)
XLA Ops:
  0.0 5.0 %collective-permute-start.2 = (f32[12,128]{1,0:T(8,128)}, f32[12,128]{1,0:T(8,128)S(1)}, u32[]{:S(2)}, u32[]{:S(2)}) collective-permute-start(f32[12,128]{1,0:T(8,128)} %bitcast.3), channel_id=1, source_target_pairs={{0,12},{1,13},{2,14},{3,15},{4,8},{5,9},{6,10},{7,11},{8,4},{9,5},... | collective-permute-start | bytes 18440 | tf_op jit(solution)/shard_map/ppermute | solution.py:29
  5.1 1.6 %shard_map.46 = (bf16[4,8,256,128]{3,2,1,0:T(8,128)(2,1)S(1)}, f32[8,128]{1,0:T(8,128)S(1)}) custom-call(bf16[8,8,256,128]{3,2,1,0:T(8,128)(2,1)} %lik_ref.1, s32[8,8]{1,0:T(8,128)} %refs_1_.1, s32[8,8]{1,0:T(8,128)} %refs_2_.1), custom_call_target="tpu_custom_call" | custom-call | tf_op jit(solution)/shard_map/pallas_call | solution.py:299
  6.7 0.3 collective-permute-done.2.refs_3_
  7.0 2.9 %collective-permute-done.1.refs_2_ = f32[12,128]{1,0:T(8,128)S(1)} collective-permute-done((f32[12,128]{1,0:T(8,128)}, f32[12,128]{1,0:T(8,128)S(1)}, u32[]{:S(2)}, u32[]{:S(2)}) %collective-permute-start.1) | collective-permute-done | bytes 6176 | tf_op jit(solution)/shard_map/ppermute | solution.py:29
  9.9 1.6 %collective-permute-start.4 = (f32[64,128]{1,0:T(8,128)S(1)}, f32[64,128]{1,0:T(8,128)S(1)}, u32[]{:S(2)}, u32[]{:S(2)}) collective-permute-start(f32[64,128]{1,0:T(8,128)S(1)} %shard_map.47.after_ref.refs_1_), channel_id=1, source_target_pairs={{0,2},{1,3},{2,0},{3,1},{4,6},{5,7},{6,4},{7,5},{8,10},{9,11},{10,... | collective-permute-start | bytes 98312 | tf_op jit(solution)/shard_map/ppermute | solution.py:29
  11.8 1.8 %shard_map.48 = (bf16[4,8,256,128]{3,2,1,0:T(8,128)(2,1)S(1)}, bf16[8,4,256,256]{3,2,1,0:T(8,128)(2,1)S(1)}) custom-call(f32[64,128]{1,0:T(8,128)S(1)} %shard_map.47.after_ref.refs_1_, bf16[4,8,256,128]{3,2,1,0:T(8,128)(2,1)S(1)} %get-tuple-element.18.early_ref.refs_3_, bf16[8,8,256,128]{3,2,1,0:T(8,128)(2,1)} %lik_ref.1), custom_call_target="tpu_custom_call" | custom-call | tf_op jit(solution)/shard_map/pallas_call | solution.py:321
  13.6 0.3 collective-permute-done.4.refs_3_
  13.9 0.9 %shard_map.49 = (f32[8,8,256]{2,1,0:T(8,128)S(1)}, f32[64,128]{1,0:T(8,128)S(1)}) custom-call(f32[8,128]{1,0:T(8,128)S(1)} %get-tuple-element.17.refs_4_.refs_0_.info_ref, f32[64,128]{1,0:T(8,128)S(1)} %shard_map.47.after_ref.refs_1_, f32[64,128]{1,0:T(8,128)S(1)} %collective-permute-done.3.refs_2_, f32[64,128]{1,0:T(8,128)S(1)} %collective-permute-done.4.refs_3_, ...), custom_call_target="tpu_custom_call" | custom-call | tf_op jit(solution)/shard_map/pallas_call | solution.py:280
  14.8 9.3 %all_to_all.15.parts_ref = f32[8,8,256]{2,1,0:T(8,128)S(1)} all-to-all(f32[8,8,256]{2,1,0:T(8,128)S(1)} %get-tuple-element.20), channel_id=1, replica_groups={{8,0,2,14,4,12,6,10},{9,1,3,15,5,13,7,11},{24,16,18,30,20,28,22,26},{25..., dimensions={0} | all-to-all | bytes 131072 | tf_op jit(solution)/shard_map/all_to_all | solution.py:365
  24.1 0.7 %shard_map.50.refs_0_ = f32[72,128]{1,0:T(8,128)S(1)} custom-call(f32[8,128]{1,0:T(8,128)S(1)} %get-tuple-element.17.refs_4_.refs_0_.info_ref, f32[8,8,256]{2,1,0:T(8,128)S(1)} %all_to_all.15.parts_ref, f32[64,128]{1,0:T(8,128)S(1)} %get-tuple-element.21.picked_ref, bf16[4,8,256,128]{3,2,1,0:T(8,128)(2,1)S(1)} %get-tuple-element.18.early_ref.refs_3_, ...), custom_call_target="tpu_custom_call" | custom-call | tf_op jit(solution)/shard_map/pallas_call | solution.py:280
  25.1 1.7 %collective-permute-start.7 = (f32[72,128]{1,0:T(8,128)S(1)}, f32[72,128]{1,0:T(8,128)S(1)}, u32[]{:S(2)}, u32[]{:S(2)}) collective-permute-start(f32[72,128]{1,0:T(8,128)S(1)} %shard_map.50.refs_0_), channel_id=1, source_target_pairs={{0,9},{1,8},{2,11},{3,10},{4,13},{5,12},{6,15},{7,14},{8,1},{9,0},... | collective-permute-start | bytes 110600 | tf_op jit(solution)/shard_map/ppermute | solution.py:29
  26.8 0.6 %collective-permute-start.6 = (f32[72,128]{1,0:T(8,128)S(1)}, f32[72,128]{1,0:T(8,128)S(1)}, u32[]{:S(2)}, u32[]{:S(2)}) collective-permute-start(f32[72,128]{1,0:T(8,128)S(1)} %shard_map.50.refs_0_), channel_id=1, source_target_pairs={{0,5},{1,4},{2,7},{3,6},{4,1},{5,0},{6,3},{7,2},{8,13},{9,12},{10,... | collective-permute-start | bytes 110600 | tf_op jit(solution)/shard_map/ppermute | solution.py:29
  27.4 2.6 %collective-permute-done.8.refs_3_ = f32[72,128]{1,0:T(8,128)S(1)} collective-permute-done((f32[72,128]{1,0:T(8,128)S(1)}, f32[72,128]{1,0:T(8,128)S(1)}, u32[]{:S(2)}, u32[]{:S(2)}) %collective-permute-start.8) | collective-permute-done | bytes 36896 | tf_op jit(solution)/shard_map/ppermute | solution.py:29
  30.1 0.4 collective-permute-done.6.refs_1_
  30.5 0.3 shard_map.51
  30.8 1.6 %collective-permute-start.9 = (f32[64,128]{1,0:T(8,128)S(1)}, f32[64,128]{1,0:T(8,128)S(1)}, u32[]{:S(2)}, u32[]{:S(2)}) collective-permute-start(f32[64,128]{1,0:T(8,128)S(1)} %get-tuple-element.24), channel_id=1, source_target_pairs={{0,3},{1,2},{2,1},{3,0},{4,7},{5,6},{6,5},{7,4},{8,11},{9,10},{10,... | collective-permute-start | bytes 98312 | tf_op jit(solution)/shard_map/ppermute | solution.py:29
  32.4 1.1 %collective-permute-start.10 = (f32[64,128]{1,0:T(8,128)S(1)}, f32[64,128]{1,0:T(8,128)S(1)}, u32[]{:S(2)}, u32[]{:S(2)}) collective-permute-start(f32[64,128]{1,0:T(8,128)S(1)} %get-tuple-element.25), channel_id=1, source_target_pairs={{0,2},{1,3},{2,0},{3,1},{4,6},{5,7},{6,4},{7,5},{8,10},{9,11},{10,... | collective-permute-start | bytes 98312 | tf_op jit(solution)/shard_map/ppermute | solution.py:29
  33.5 0.7 %collective-permute-done.9.refs_1_ = f32[64,128]{1,0:T(8,128)S(1)} collective-permute-done((f32[64,128]{1,0:T(8,128)S(1)}, f32[64,128]{1,0:T(8,128)S(1)}, u32[]{:S(2)}, u32[]{:S(2)}) %collective-permute-start.9) | collective-permute-done | bytes 32800 | tf_op jit(solution)/shard_map/ppermute | solution.py:29
  34.2 2.1 %collective-permute-done.10.refs_2_ = f32[64,128]{1,0:T(8,128)S(1)} collective-permute-done((f32[64,128]{1,0:T(8,128)S(1)}, f32[64,128]{1,0:T(8,128)S(1)}, u32[]{:S(2)}, u32[]{:S(2)}) %collective-permute-start.10) | collective-permute-done | bytes 32800 | tf_op jit(solution)/shard_map/ppermute | solution.py:29
  36.3 0.7 %shard_map.52 = (f32[8,8,256]{2,1,0:T(8,128)S(1)}, f32[64,128]{1,0:T(8,128)S(1)}) custom-call(f32[64,128]{1,0:T(8,128)S(1)} %get-tuple-element.23.refs_0_, f32[64,128]{1,0:T(8,128)S(1)} %collective-permute-done.9.refs_1_, f32[64,128]{1,0:T(8,128)S(1)} %collective-permute-done.10.refs_2_, f32[64,128]{1,0:T(8,128)S(1)} %collective-permute-done.11.refs_3_, ...), custom_call_target="tpu_custom_call" | custom-call | tf_op jit(solution)/shard_map/pallas_call | solution.py:280
  37.0 8.6 %all_to_all.16.refs_1_ = f32[8,8,256]{2,1,0:T(8,128)S(1)} all-to-all(f32[8,8,256]{2,1,0:T(8,128)S(1)} %get-tuple-element.27), channel_id=1, replica_groups={{10,0,2,4,6,14,8,12},{11,1,3,5,7,15,9,13},{26,16,18,20,22,30,24,28},{27..., dimensions={0} | all-to-all | bytes 131072 | tf_op jit(solution)/shard_map/all_to_all | solution.py:365
  45.6 0.9 %shard_map.53 = f32[16,12,128]{2,1,0:T(8,128)S(1)} custom-call(f32[8,128]{1,0:T(8,128)S(1)} %get-tuple-element.17.refs_4_.refs_0_.info_ref, f32[8,8,256]{2,1,0:T(8,128)S(1)} %all_to_all.16.refs_1_, f32[64,128]{1,0:T(8,128)S(1)} %get-tuple-element.28.refs_2_, bf16[4,8,256,128]{3,2,1,0:T(8,128)(2,1)S(1)} %get-tuple-element.18.early_ref.refs_3_, ...), custom_call_target="tpu_custom_call" | custom-call | tf_op jit(solution)/shard_map/pallas_call | solution.py:280
  46.5 9.4 %all_to_all.17 = f32[16,12,128]{2,1,0:T(8,128)S(1)} all-to-all(f32[16,12,128]{2,1,0:T(8,128)S(1)} %shard_map.53), channel_id=1, replica_groups={{11,0,1,2,3,4,5,6,7,15,8,14,9,13,10,12},{27,16,17,18,19,20,21,22,23,31,..., dimensions={0} | all-to-all | bytes 196608 | tf_op jit(solution)/shard_map/all_to_all | solution.py:404
  55.9 0.6 %multiply_bitcast_fusion = f32[1536]{0:T(1024)} fusion(f32[12,128]{1,0:T(8,128)S(1)} %reduce_sum.9), kind=kLoop, calls=%fused_computation | loop fusion | flops 1536 | bytes 12288 | tf_op jit(solution)/shard_map/mul | solution.py:405
  (18 shorter events, 0.7 us)
Async XLA Ops:
  0.0 9.8 %copy-start = (f32[1536]{0:T(1024)S(1)}, f32[1536]{0:T(1024)}, u32[]{:S(2)}) copy-start(f32[1536]{0:T(1024)} %param.7) | copy-start | bytes 18436
  0.0 7.0 %collective-permute-start.2 = (f32[12,128]{1,0:T(8,128)}, f32[12,128]{1,0:T(8,128)S(1)}, u32[]{:S(2)}, u32[]{:S(2)}) collective-permute-start(f32[12,128]{1,0:T(8,128)} %bitcast.3), channel_id=1, source_target_pairs={{0,12},{1,13},{2,14},{3,15},{4,8},{5,9},{6,10},{7,11},{8,4},{9,5},... | collective-permute-start | bytes 18440 | tf_op jit(solution)/shard_map/ppermute | solution.py:29
  5.1 4.8 %collective-permute-start.1 = (f32[12,128]{1,0:T(8,128)}, f32[12,128]{1,0:T(8,128)S(1)}, u32[]{:S(2)}, u32[]{:S(2)}) collective-permute-start(f32[12,128]{1,0:T(8,128)} %bitcast.4), channel_id=1, source_target_pairs={{0,8},{1,9},{2,10},{3,11},{4,12},{5,13},{6,14},{7,15},{8,0},{9,1},... | collective-permute-start | bytes 18440 | tf_op jit(solution)/shard_map/ppermute | solution.py:29
  5.1 4.8 %collective-permute-start = (f32[12,128]{1,0:T(8,128)}, f32[12,128]{1,0:T(8,128)S(1)}, u32[]{:S(2)}, u32[]{:S(2)}) collective-permute-start(f32[12,128]{1,0:T(8,128)} %bitcast.5), channel_id=1, source_target_pairs={{0,5},{1,4},{2,7},{3,6},{4,1},{5,0},{6,3},{7,2},{8,13},{9,12},{10,... | collective-permute-start | bytes 18440 | tf_op jit(solution)/shard_map/ppermute | solution.py:29
  9.8 3.8 %collective-permute-start.5 = (f32[64,128]{1,0:T(8,128)S(1)}, f32[64,128]{1,0:T(8,128)S(1)}, u32[]{:S(2)}, u32[]{:S(2)}) collective-permute-start(f32[64,128]{1,0:T(8,128)S(1)} %shard_map.47.after_ref.refs_1_), channel_id=1, source_target_pairs={{0,3},{1,2},{2,1},{3,0},{4,7},{5,6},{6,5},{7,4},{8,11},{9,10},{10,... | collective-permute-start | bytes 98312 | tf_op jit(solution)/shard_map/ppermute | solution.py:29
  9.9 4.0 %collective-permute-start.4 = (f32[64,128]{1,0:T(8,128)S(1)}, f32[64,128]{1,0:T(8,128)S(1)}, u32[]{:S(2)}, u32[]{:S(2)}) collective-permute-start(f32[64,128]{1,0:T(8,128)S(1)} %shard_map.47.after_ref.refs_1_), channel_id=1, source_target_pairs={{0,2},{1,3},{2,0},{3,1},{4,6},{5,7},{6,4},{7,5},{8,10},{9,11},{10,... | collective-permute-start | bytes 98312 | tf_op jit(solution)/shard_map/ppermute | solution.py:29
  11.5 2.4 %collective-permute-start.3 = (f32[64,128]{1,0:T(8,128)S(1)}, f32[64,128]{1,0:T(8,128)S(1)}, u32[]{:S(2)}, u32[]{:S(2)}) collective-permute-start(f32[64,128]{1,0:T(8,128)S(1)} %shard_map.47.after_ref.refs_1_), channel_id=1, source_target_pairs={{0,1},{1,0},{2,3},{3,2},{4,5},{5,4},{6,7},{7,6},{8,9},{9,8},{10,11... | collective-permute-start | bytes 98312 | tf_op jit(solution)/shard_map/ppermute | solution.py:29
  24.8 5.3 %collective-permute-start.8 = (f32[72,128]{1,0:T(8,128)S(1)}, f32[72,128]{1,0:T(8,128)S(1)}, u32[]{:S(2)}, u32[]{:S(2)}) collective-permute-start(f32[72,128]{1,0:T(8,128)S(1)} %shard_map.50.refs_0_), channel_id=1, source_target_pairs={{0,13},{1,12},{2,15},{3,14},{4,9},{5,8},{6,11},{7,10},{8,5},{9,4},... | collective-permute-start | bytes 110600 | tf_op jit(solution)/shard_map/ppermute | solution.py:29
  25.1 5.0 %collective-permute-start.7 = (f32[72,128]{1,0:T(8,128)S(1)}, f32[72,128]{1,0:T(8,128)S(1)}, u32[]{:S(2)}, u32[]{:S(2)}) collective-permute-start(f32[72,128]{1,0:T(8,128)S(1)} %shard_map.50.refs_0_), channel_id=1, source_target_pairs={{0,9},{1,8},{2,11},{3,10},{4,13},{5,12},{6,15},{7,14},{8,1},{9,0},... | collective-permute-start | bytes 110600 | tf_op jit(solution)/shard_map/ppermute | solution.py:29
  26.8 3.7 %collective-permute-start.6 = (f32[72,128]{1,0:T(8,128)S(1)}, f32[72,128]{1,0:T(8,128)S(1)}, u32[]{:S(2)}, u32[]{:S(2)}) collective-permute-start(f32[72,128]{1,0:T(8,128)S(1)} %shard_map.50.refs_0_), channel_id=1, source_target_pairs={{0,5},{1,4},{2,7},{3,6},{4,1},{5,0},{6,3},{7,2},{8,13},{9,12},{10,... | collective-permute-start | bytes 110600 | tf_op jit(solution)/shard_map/ppermute | solution.py:29
  30.8 3.4 %collective-permute-start.9 = (f32[64,128]{1,0:T(8,128)S(1)}, f32[64,128]{1,0:T(8,128)S(1)}, u32[]{:S(2)}, u32[]{:S(2)}) collective-permute-start(f32[64,128]{1,0:T(8,128)S(1)} %get-tuple-element.24), channel_id=1, source_target_pairs={{0,3},{1,2},{2,1},{3,0},{4,7},{5,6},{6,5},{7,4},{8,11},{9,10},{10,... | collective-permute-start | bytes 98312 | tf_op jit(solution)/shard_map/ppermute | solution.py:29
  32.4 3.9 %collective-permute-start.10 = (f32[64,128]{1,0:T(8,128)S(1)}, f32[64,128]{1,0:T(8,128)S(1)}, u32[]{:S(2)}, u32[]{:S(2)}) collective-permute-start(f32[64,128]{1,0:T(8,128)S(1)} %get-tuple-element.25), channel_id=1, source_target_pairs={{0,2},{1,3},{2,0},{3,1},{4,6},{5,7},{6,4},{7,5},{8,10},{9,11},{10,... | collective-permute-start | bytes 98312 | tf_op jit(solution)/shard_map/ppermute | solution.py:29
  33.5 2.8 %collective-permute-start.11 = (f32[64,128]{1,0:T(8,128)S(1)}, f32[64,128]{1,0:T(8,128)S(1)}, u32[]{:S(2)}, u32[]{:S(2)}) collective-permute-start(f32[64,128]{1,0:T(8,128)S(1)} %get-tuple-element.26), channel_id=1, source_target_pairs={{0,1},{1,0},{2,3},{3,2},{4,5},{5,4},{6,7},{7,6},{8,9},{9,8},{10,11... | collective-permute-start | bytes 98312 | tf_op jit(solution)/shard_map/ppermute | solution.py:29

commit v19 on v15

--- a/solution.py
+++ b/solution.py
@@ -31,6 +31,11 @@
 
 def middle_first(n, k):
     return [i ^ k for i in range(n)]
+
+
+def middle_then_up(n, k):
+    pairs = [k // 2] + [p for p in range(n // 2) if p != k // 2]
+    return [2 * p + (i ^ (k % 2)) for p in pairs for i in range(2)]
 
 
 def position(k, n):
@@ -368,7 +373,7 @@
             0,
             0,
             tiled=True,
-            axis_index_groups=[middle_first(chips, chips // 2 + step)],
+            axis_index_groups=[middle_then_up(chips, chips // 2 + step)],
         )
         if step + 1 < ITERS:
             (contrib,) = call(

time: 55.6 us -> 55.9 us (level)
  waiting for transfers between devices: 8.63 us -> 9.28 us
    ppermute x12, waiting for transfers between devices: 8.63 us -> 9.28 us  [swap(): return lax.ppermute(x, axes, [(i, i ^ k) for i in range(n)])]
where the time goes in v19:
time: 55.9 us; the launch traced here: 55.4 us
  blocking collectives  25.9 us (46%)
  starting transfers between devices  12.6 us (23%)
  waiting for transfers between devices  9.28 us (17%)
  Pallas kernels  6.9 us (12%)
  other arithmetic  0.62 us (1%)
    all_to_all x2, blocking collectives, local(): lax.all_to_all(row_parts, 'genome', 0, 0, tiled=True, axis_index_groups=[...  17.8 us
    ppermute x12, starting transfers between devices, swap(): return lax.ppermute(x, axes, [(i, i ^ k) for i in range(n)])  12.6 us
    ppermute x12, waiting for transfers between devices, swap(): return lax.ppermute(x, axes, [(i, i ^ k) for i in range(n)])  9.28 us
    all_to_all x1, blocking collectives, local(): lax.all_to_all(counts, ALL, 0, 0, tiled=True, axis_index_groups=[order])  8.15 us
    pallas_call x6, Pallas kernels, call(): pl.pallas_call(kernel, out_shape=[jax.ShapeDtypeStruct(shape, jnp.float32...  3.46 us
    pallas_call x1, Pallas kernels, flip(): pl.pallas_call(flip_kernel, out_shape=[pltpu.VMEM((late,) + likelihood.sh...  1.84 us
    pallas_call x1, Pallas kernels, prepare(): pl.pallas_call(lambda *refs: prepare_kernel(own_blocks, *refs), out_shape...  1.6 us
  transfers between devices with their start and end apart: 12, of which 7 were waited for; matrix products, arithmetic and copies ran while one was open for 0% of the time, Pallas kernels for 6%

profile of v19, /device:TPU:0, one launch (start us, length us, event | category | flops | bytes accessed | tf_op | source)
XLA Modules:
  0.0 55.4 jit_solution(17624753570125051610)
XLA Ops:
  0.0 5.0 %collective-permute-start.2 = (f32[12,128]{1,0:T(8,128)}, f32[12,128]{1,0:T(8,128)S(1)}, u32[]{:S(2)}, u32[]{:S(2)}) collective-permute-start(f32[12,128]{1,0:T(8,128)} %bitcast.3), channel_id=1, source_target_pairs={{0,12},{1,13},{2,14},{3,15},{4,8},{5,9},{6,10},{7,11},{8,4},{9,5},... | collective-permute-start | bytes 18440 | tf_op jit(solution)/shard_map/ppermute | solution.py:29
  5.1 1.6 %shard_map.46 = (bf16[4,8,256,128]{3,2,1,0:T(8,128)(2,1)S(1)}, f32[8,128]{1,0:T(8,128)S(1)}) custom-call(bf16[8,8,256,128]{3,2,1,0:T(8,128)(2,1)} %lik_ref.1, s32[8,8]{1,0:T(8,128)} %refs_1_.1, s32[8,8]{1,0:T(8,128)} %refs_2_.1), custom_call_target="tpu_custom_call" | custom-call | tf_op jit(solution)/shard_map/pallas_call | solution.py:304
  7.0 2.9 %collective-permute-done.1.refs_2_ = f32[12,128]{1,0:T(8,128)S(1)} collective-permute-done((f32[12,128]{1,0:T(8,128)}, f32[12,128]{1,0:T(8,128)S(1)}, u32[]{:S(2)}, u32[]{:S(2)}) %collective-permute-start.1) | collective-permute-done | bytes 6176 | tf_op jit(solution)/shard_map/ppermute | solution.py:29
  9.9 1.6 %collective-permute-start.4 = (f32[64,128]{1,0:T(8,128)S(1)}, f32[64,128]{1,0:T(8,128)S(1)}, u32[]{:S(2)}, u32[]{:S(2)}) collective-permute-start(f32[64,128]{1,0:T(8,128)S(1)} %shard_map.47.after_ref.refs_1_), channel_id=1, source_target_pairs={{0,2},{1,3},{2,0},{3,1},{4,6},{5,7},{6,4},{7,5},{8,10},{9,11},{10,... | collective-permute-start | bytes 98312 | tf_op jit(solution)/shard_map/ppermute | solution.py:29
  11.8 1.8 %shard_map.48 = (bf16[4,8,256,128]{3,2,1,0:T(8,128)(2,1)S(1)}, bf16[8,4,256,256]{3,2,1,0:T(8,128)(2,1)S(1)}) custom-call(f32[64,128]{1,0:T(8,128)S(1)} %shard_map.47.after_ref.refs_1_, bf16[4,8,256,128]{3,2,1,0:T(8,128)(2,1)S(1)} %get-tuple-element.18.early_ref.refs_3_, bf16[8,8,256,128]{3,2,1,0:T(8,128)(2,1)} %lik_ref.1), custom_call_target="tpu_custom_call" | custom-call | tf_op jit(solution)/shard_map/pallas_call | solution.py:326
  13.6 0.3 collective-permute-done.4.refs_3_
  13.9 0.9 %shard_map.49 = (f32[8,8,256]{2,1,0:T(8,128)S(1)}, f32[64,128]{1,0:T(8,128)S(1)}) custom-call(f32[8,128]{1,0:T(8,128)S(1)} %get-tuple-element.17.refs_4_.refs_0_.info_ref, f32[64,128]{1,0:T(8,128)S(1)} %shard_map.47.after_ref.refs_1_, f32[64,128]{1,0:T(8,128)S(1)} %collective-permute-done.3.refs_2_, f32[64,128]{1,0:T(8,128)S(1)} %collective-permute-done.4.refs_3_, ...), custom_call_target="tpu_custom_call" | custom-call | tf_op jit(solution)/shard_map/pallas_call | solution.py:285
  14.8 9.1 %all_to_all.15.parts_ref = f32[8,8,256]{2,1,0:T(8,128)S(1)} all-to-all(f32[8,8,256]{2,1,0:T(8,128)S(1)} %get-tuple-element.20), channel_id=1, replica_groups={{8,10,0,2,4,6,12,14},{9,11,1,3,5,7,13,15},{24,26,16,18,20,22,28,30},{25..., dimensions={0} | all-to-all | bytes 131072 | tf_op jit(solution)/shard_map/all_to_all | solution.py:370
  24.0 0.7 %shard_map.50.refs_0_ = f32[72,128]{1,0:T(8,128)S(1)} custom-call(f32[8,128]{1,0:T(8,128)S(1)} %get-tuple-element.17.refs_4_.refs_0_.info_ref, f32[8,8,256]{2,1,0:T(8,128)S(1)} %all_to_all.15.parts_ref, f32[64,128]{1,0:T(8,128)S(1)} %get-tuple-element.21.picked_ref, bf16[4,8,256,128]{3,2,1,0:T(8,128)(2,1)S(1)} %get-tuple-element.18.early_ref.refs_3_, ...), custom_call_target="tpu_custom_call" | custom-call | tf_op jit(solution)/shard_map/pallas_call | solution.py:285
  24.6 0.5 collective-permute-start.8
  25.1 1.7 %collective-permute-start.7 = (f32[72,128]{1,0:T(8,128)S(1)}, f32[72,128]{1,0:T(8,128)S(1)}, u32[]{:S(2)}, u32[]{:S(2)}) collective-permute-start(f32[72,128]{1,0:T(8,128)S(1)} %shard_map.50.refs_0_), channel_id=1, source_target_pairs={{0,9},{1,8},{2,11},{3,10},{4,13},{5,12},{6,15},{7,14},{8,1},{9,0},... | collective-permute-start | bytes 110600 | tf_op jit(solution)/shard_map/ppermute | solution.py:29
  26.8 0.6 %collective-permute-start.6 = (f32[72,128]{1,0:T(8,128)S(1)}, f32[72,128]{1,0:T(8,128)S(1)}, u32[]{:S(2)}, u32[]{:S(2)}) collective-permute-start(f32[72,128]{1,0:T(8,128)S(1)} %shard_map.50.refs_0_), channel_id=1, source_target_pairs={{0,5},{1,4},{2,7},{3,6},{4,1},{5,0},{6,3},{7,2},{8,13},{9,12},{10,... | collective-permute-start | bytes 110600 | tf_op jit(solution)/shard_map/ppermute | solution.py:29
  27.4 2.5 %collective-permute-done.8.refs_3_ = f32[72,128]{1,0:T(8,128)S(1)} collective-permute-done((f32[72,128]{1,0:T(8,128)S(1)}, f32[72,128]{1,0:T(8,128)S(1)}, u32[]{:S(2)}, u32[]{:S(2)}) %collective-permute-start.8) | collective-permute-done | bytes 36896 | tf_op jit(solution)/shard_map/ppermute | solution.py:29
  29.9 0.4 collective-permute-done.7.refs_2_
  30.4 0.3 shard_map.51
  30.7 1.8 %collective-permute-start.9 = (f32[64,128]{1,0:T(8,128)S(1)}, f32[64,128]{1,0:T(8,128)S(1)}, u32[]{:S(2)}, u32[]{:S(2)}) collective-permute-start(f32[64,128]{1,0:T(8,128)S(1)} %get-tuple-element.24), channel_id=1, source_target_pairs={{0,3},{1,2},{2,1},{3,0},{4,7},{5,6},{6,5},{7,4},{8,11},{9,10},{10,... | collective-permute-start | bytes 98312 | tf_op jit(solution)/shard_map/ppermute | solution.py:29
  32.5 1.0 %collective-permute-start.10 = (f32[64,128]{1,0:T(8,128)S(1)}, f32[64,128]{1,0:T(8,128)S(1)}, u32[]{:S(2)}, u32[]{:S(2)}) collective-permute-start(f32[64,128]{1,0:T(8,128)S(1)} %get-tuple-element.25), channel_id=1, source_target_pairs={{0,2},{1,3},{2,0},{3,1},{4,6},{5,7},{6,4},{7,5},{8,10},{9,11},{10,... | collective-permute-start | bytes 98312 | tf_op jit(solution)/shard_map/ppermute | solution.py:29
  33.5 0.6 %collective-permute-done.9.refs_1_ = f32[64,128]{1,0:T(8,128)S(1)} collective-permute-done((f32[64,128]{1,0:T(8,128)S(1)}, f32[64,128]{1,0:T(8,128)S(1)}, u32[]{:S(2)}, u32[]{:S(2)}) %collective-permute-start.9) | collective-permute-done | bytes 32800 | tf_op jit(solution)/shard_map/ppermute | solution.py:29
  34.1 2.3 %collective-permute-done.10.refs_2_ = f32[64,128]{1,0:T(8,128)S(1)} collective-permute-done((f32[64,128]{1,0:T(8,128)S(1)}, f32[64,128]{1,0:T(8,128)S(1)}, u32[]{:S(2)}, u32[]{:S(2)}) %collective-permute-start.10) | collective-permute-done | bytes 32800 | tf_op jit(solution)/shard_map/ppermute | solution.py:29
  36.4 0.7 %shard_map.52 = (f32[8,8,256]{2,1,0:T(8,128)S(1)}, f32[64,128]{1,0:T(8,128)S(1)}) custom-call(f32[64,128]{1,0:T(8,128)S(1)} %get-tuple-element.23.refs_0_, f32[64,128]{1,0:T(8,128)S(1)} %collective-permute-done.9.refs_1_, f32[64,128]{1,0:T(8,128)S(1)} %collective-permute-done.10.refs_2_, f32[64,128]{1,0:T(8,128)S(1)} %collective-permute-done.11.refs_3_, ...), custom_call_target="tpu_custom_call" | custom-call | tf_op jit(solution)/shard_map/pallas_call | solution.py:285
  37.1 8.6 %all_to_all.16.refs_1_ = f32[8,8,256]{2,1,0:T(8,128)S(1)} all-to-all(f32[8,8,256]{2,1,0:T(8,128)S(1)} %get-tuple-element.27), channel_id=1, replica_groups={{10,8,2,0,6,4,14,12},{11,9,3,1,7,5,15,13},{26,24,18,16,22,20,30,28},{27..., dimensions={0} | all-to-all | bytes 131072 | tf_op jit(solution)/shard_map/all_to_all | solution.py:370
  45.7 0.9 %shard_map.53 = f32[16,12,128]{2,1,0:T(8,128)S(1)} custom-call(f32[8,128]{1,0:T(8,128)S(1)} %get-tuple-element.17.refs_4_.refs_0_.info_ref, f32[8,8,256]{2,1,0:T(8,128)S(1)} %all_to_all.16.refs_1_, f32[64,128]{1,0:T(8,128)S(1)} %get-tuple-element.28.refs_2_, bf16[4,8,256,128]{3,2,1,0:T(8,128)(2,1)S(1)} %get-tuple-element.18.early_ref.refs_3_, ...), custom_call_target="tpu_custom_call" | custom-call | tf_op jit(solution)/shard_map/pallas_call | solution.py:285
  46.6 8.2 %all_to_all.17 = f32[16,12,128]{2,1,0:T(8,128)S(1)} all-to-all(f32[16,12,128]{2,1,0:T(8,128)S(1)} %shard_map.53), channel_id=1, replica_groups={{11,10,9,8,15,14,13,12,3,2,1,0,7,6,5,4},{27,26,25,24,31,30,29,28,19,18,..., dimensions={0} | all-to-all | bytes 196608 | tf_op jit(solution)/shard_map/all_to_all | solution.py:409
  54.8 0.6 %multiply_bitcast_fusion = f32[1536]{0:T(1024)} fusion(f32[12,128]{1,0:T(8,128)S(1)} %reduce_sum.9), kind=kLoop, calls=%fused_computation | loop fusion | flops 1536 | bytes 12288 | tf_op jit(solution)/shard_map/mul | solution.py:410
  (18 shorter events, 0.7 us)
Async XLA Ops:
  0.0 9.8 %copy-start = (f32[1536]{0:T(1024)S(1)}, f32[1536]{0:T(1024)}, u32[]{:S(2)}) copy-start(f32[1536]{0:T(1024)} %param.7) | copy-start | bytes 18436
  0.0 7.0 %collective-permute-start.2 = (f32[12,128]{1,0:T(8,128)}, f32[12,128]{1,0:T(8,128)S(1)}, u32[]{:S(2)}, u32[]{:S(2)}) collective-permute-start(f32[12,128]{1,0:T(8,128)} %bitcast.3), channel_id=1, source_target_pairs={{0,12},{1,13},{2,14},{3,15},{4,8},{5,9},{6,10},{7,11},{8,4},{9,5},... | collective-permute-start | bytes 18440 | tf_op jit(solution)/shard_map/ppermute | solution.py:29
  5.1 4.8 %collective-permute-start.1 = (f32[12,128]{1,0:T(8,128)}, f32[12,128]{1,0:T(8,128)S(1)}, u32[]{:S(2)}, u32[]{:S(2)}) collective-permute-start(f32[12,128]{1,0:T(8,128)} %bitcast.4), channel_id=1, source_target_pairs={{0,8},{1,9},{2,10},{3,11},{4,12},{5,13},{6,14},{7,15},{8,0},{9,1},... | collective-permute-start | bytes 18440 | tf_op jit(solution)/shard_map/ppermute | solution.py:29
  5.1 4.8 %collective-permute-start = (f32[12,128]{1,0:T(8,128)}, f32[12,128]{1,0:T(8,128)S(1)}, u32[]{:S(2)}, u32[]{:S(2)}) collective-permute-start(f32[12,128]{1,0:T(8,128)} %bitcast.5), channel_id=1, source_target_pairs={{0,5},{1,4},{2,7},{3,6},{4,1},{5,0},{6,3},{7,2},{8,13},{9,12},{10,... | collective-permute-start | bytes 18440 | tf_op jit(solution)/shard_map/ppermute | solution.py:29
  9.8 3.8 %collective-permute-start.5 = (f32[64,128]{1,0:T(8,128)S(1)}, f32[64,128]{1,0:T(8,128)S(1)}, u32[]{:S(2)}, u32[]{:S(2)}) collective-permute-start(f32[64,128]{1,0:T(8,128)S(1)} %shard_map.47.after_ref.refs_1_), channel_id=1, source_target_pairs={{0,3},{1,2},{2,1},{3,0},{4,7},{5,6},{6,5},{7,4},{8,11},{9,10},{10,... | collective-permute-start | bytes 98312 | tf_op jit(solution)/shard_map/ppermute | solution.py:29
  9.9 4.0 %collective-permute-start.4 = (f32[64,128]{1,0:T(8,128)S(1)}, f32[64,128]{1,0:T(8,128)S(1)}, u32[]{:S(2)}, u32[]{:S(2)}) collective-permute-start(f32[64,128]{1,0:T(8,128)S(1)} %shard_map.47.after_ref.refs_1_), channel_id=1, source_target_pairs={{0,2},{1,3},{2,0},{3,1},{4,6},{5,7},{6,4},{7,5},{8,10},{9,11},{10,... | collective-permute-start | bytes 98312 | tf_op jit(solution)/shard_map/ppermute | solution.py:29
  11.5 2.4 %collective-permute-start.3 = (f32[64,128]{1,0:T(8,128)S(1)}, f32[64,128]{1,0:T(8,128)S(1)}, u32[]{:S(2)}, u32[]{:S(2)}) collective-permute-start(f32[64,128]{1,0:T(8,128)S(1)} %shard_map.47.after_ref.refs_1_), channel_id=1, source_target_pairs={{0,1},{1,0},{2,3},{3,2},{4,5},{5,4},{6,7},{7,6},{8,9},{9,8},{10,11... | collective-permute-start | bytes 98312 | tf_op jit(solution)/shard_map/ppermute | solution.py:29
  24.6 5.3 %collective-permute-start.8 = (f32[72,128]{1,0:T(8,128)S(1)}, f32[72,128]{1,0:T(8,128)S(1)}, u32[]{:S(2)}, u32[]{:S(2)}) collective-permute-start(f32[72,128]{1,0:T(8,128)S(1)} %shard_map.50.refs_0_), channel_id=1, source_target_pairs={{0,13},{1,12},{2,15},{3,14},{4,9},{5,8},{6,11},{7,10},{8,5},{9,4},... | collective-permute-start | bytes 110600 | tf_op jit(solution)/shard_map/ppermute | solution.py:29
  25.1 5.2 %collective-permute-start.7 = (f32[72,128]{1,0:T(8,128)S(1)}, f32[72,128]{1,0:T(8,128)S(1)}, u32[]{:S(2)}, u32[]{:S(2)}) collective-permute-start(f32[72,128]{1,0:T(8,128)S(1)} %shard_map.50.refs_0_), channel_id=1, source_target_pairs={{0,9},{1,8},{2,11},{3,10},{4,13},{5,12},{6,15},{7,14},{8,1},{9,0},... | collective-permute-start | bytes 110600 | tf_op jit(solution)/shard_map/ppermute | solution.py:29
  26.8 3.5 %collective-permute-start.6 = (f32[72,128]{1,0:T(8,128)S(1)}, f32[72,128]{1,0:T(8,128)S(1)}, u32[]{:S(2)}, u32[]{:S(2)}) collective-permute-start(f32[72,128]{1,0:T(8,128)S(1)} %shard_map.50.refs_0_), channel_id=1, source_target_pairs={{0,5},{1,4},{2,7},{3,6},{4,1},{5,0},{6,3},{7,2},{8,13},{9,12},{10,... | collective-permute-start | bytes 110600 | tf_op jit(solution)/shard_map/ppermute | solution.py:29
  30.7 3.4 %collective-permute-start.9 = (f32[64,128]{1,0:T(8,128)S(1)}, f32[64,128]{1,0:T(8,128)S(1)}, u32[]{:S(2)}, u32[]{:S(2)}) collective-permute-start(f32[64,128]{1,0:T(8,128)S(1)} %get-tuple-element.24), channel_id=1, source_target_pairs={{0,3},{1,2},{2,1},{3,0},{4,7},{5,6},{6,5},{7,4},{8,11},{9,10},{10,... | collective-permute-start | bytes 98312 | tf_op jit(solution)/shard_map/ppermute | solution.py:29
  32.5 3.9 %collective-permute-start.10 = (f32[64,128]{1,0:T(8,128)S(1)}, f32[64,128]{1,0:T(8,128)S(1)}, u32[]{:S(2)}, u32[]{:S(2)}) collective-permute-start(f32[64,128]{1,0:T(8,128)S(1)} %get-tuple-element.25), channel_id=1, source_target_pairs={{0,2},{1,3},{2,0},{3,1},{4,6},{5,7},{6,4},{7,5},{8,10},{9,11},{10,... | collective-permute-start | bytes 98312 | tf_op jit(solution)/shard_map/ppermute | solution.py:29
  33.5 2.9 %collective-permute-start.11 = (f32[64,128]{1,0:T(8,128)S(1)}, f32[64,128]{1,0:T(8,128)S(1)}, u32[]{:S(2)}, u32[]{:S(2)}) collective-permute-start(f32[64,128]{1,0:T(8,128)S(1)} %get-tuple-element.26), channel_id=1, source_target_pairs={{0,1},{1,0},{2,3},{3,2},{4,5},{5,4},{6,7},{7,6},{8,9},{9,8},{10,11... | collective-permute-start | bytes 98312 | tf_op jit(solution)/shard_map/ppermute | solution.py:29

commit v20 on v15

--- a/solution.py
+++ b/solution.py
@@ -344,7 +344,7 @@
     scale = n * own_blocks * cols / total_reads
 
     column = gather_far(own_weights, ALL, CROSSED)
-    held, info = prepare(own_blocks, read_blocks // 2, likelihood, block_ids, slot_valid)
+    held, info = prepare(own_blocks, read_blocks // 4, likelihood, block_ids, slot_valid)
     (sent,) = call(join_kernel, [(near_rows(far, own_blocks), cols)], [], *column, info)
     rest, flipped = flip(sent, held, likelihood)
     pieces = [sent] + [swap(sent, ALL, j) for j in range(1, near)]

time: 55.6 us -> 55.7 us (level)
  transfers between devices with their start and end apart: 12 -> 12, of which waited for: 7 -> 6; matrix products, arithmetic and copies ran while one was open for 0% -> 0% of each run, Pallas kernels for 6% -> 6%
where the time goes in v20:
time: 55.7 us; the launch traced here: 55.2 us
  blocking collectives  26.4 us (47%)
  starting transfers between devices  12.5 us (22%)
  waiting for transfers between devices  8.65 us (16%)
  Pallas kernels  6.96 us (12%)
  other arithmetic  0.62 us (1%)
    all_to_all x2, blocking collectives, local(): lax.all_to_all(row_parts, 'genome', 0, 0, tiled=True, axis_index_groups=[...  18 us
    ppermute x12, starting transfers between devices, swap(): return lax.ppermute(x, axes, [(i, i ^ k) for i in range(n)])  12.5 us
    ppermute x12, waiting for transfers between devices, swap(): return lax.ppermute(x, axes, [(i, i ^ k) for i in range(n)])  8.65 us
    all_to_all x1, blocking collectives, local(): lax.all_to_all(counts, ALL, 0, 0, tiled=True, axis_index_groups=[order])  8.33 us
    pallas_call x6, Pallas kernels, call(): pl.pallas_call(kernel, out_shape=[jax.ShapeDtypeStruct(shape, jnp.float32...  3.45 us
    pallas_call x1, Pallas kernels, flip(): pl.pallas_call(flip_kernel, out_shape=[pltpu.VMEM((late,) + likelihood.sh...  2.24 us
    pallas_call x1, Pallas kernels, prepare(): pl.pallas_call(lambda *refs: prepare_kernel(own_blocks, *refs), out_shape...  1.27 us
  transfers between devices with their start and end apart: 12, of which 6 were waited for; matrix products, arithmetic and copies ran while one was open for 0% of the time, Pallas kernels for 6%

profile of v20, /device:TPU:0, one launch (start us, length us, event | category | flops | bytes accessed | tf_op | source)
XLA Modules:
  0.0 55.2 jit_solution(11249567545141115307)
XLA Ops:
  0.0 5.0 %collective-permute-start.2 = (f32[12,128]{1,0:T(8,128)}, f32[12,128]{1,0:T(8,128)S(1)}, u32[]{:S(2)}, u32[]{:S(2)}) collective-permute-start(f32[12,128]{1,0:T(8,128)} %bitcast.3), channel_id=1, source_target_pairs={{0,12},{1,13},{2,14},{3,15},{4,8},{5,9},{6,10},{7,11},{8,4},{9,5},... | collective-permute-start | bytes 18440 | tf_op jit(solution)/shard_map/ppermute | solution.py:29
  5.1 1.3 %shard_map.46 = (bf16[2,8,256,128]{3,2,1,0:T(8,128)(2,1)S(1)}, f32[8,128]{1,0:T(8,128)S(1)}) custom-call(bf16[8,8,256,128]{3,2,1,0:T(8,128)(2,1)} %lik_ref.1, s32[8,8]{1,0:T(8,128)} %refs_1_.1, s32[8,8]{1,0:T(8,128)} %refs_2_.1), custom_call_target="tpu_custom_call" | custom-call | tf_op jit(solution)/shard_map/pallas_call | solution.py:299
  6.3 0.6 %collective-permute-done.2.refs_3_ = f32[12,128]{1,0:T(8,128)S(1)} collective-permute-done((f32[12,128]{1,0:T(8,128)}, f32[12,128]{1,0:T(8,128)S(1)}, u32[]{:S(2)}, u32[]{:S(2)}) %collective-permute-start.2) | collective-permute-done | bytes 6176 | tf_op jit(solution)/shard_map/ppermute | solution.py:29
  7.0 2.9 %collective-permute-done.1.refs_2_ = f32[12,128]{1,0:T(8,128)S(1)} collective-permute-done((f32[12,128]{1,0:T(8,128)}, f32[12,128]{1,0:T(8,128)S(1)}, u32[]{:S(2)}, u32[]{:S(2)}) %collective-permute-start.1) | collective-permute-done | bytes 6176 | tf_op jit(solution)/shard_map/ppermute | solution.py:29
  9.9 1.6 %collective-permute-start.4 = (f32[64,128]{1,0:T(8,128)S(1)}, f32[64,128]{1,0:T(8,128)S(1)}, u32[]{:S(2)}, u32[]{:S(2)}) collective-permute-start(f32[64,128]{1,0:T(8,128)S(1)} %shard_map.47.after_ref.refs_1_), channel_id=1, source_target_pairs={{0,2},{1,3},{2,0},{3,1},{4,6},{5,7},{6,4},{7,5},{8,10},{9,11},{10,... | collective-permute-start | bytes 98312 | tf_op jit(solution)/shard_map/ppermute | solution.py:29
  11.5 0.3 collective-permute-start.3
  11.8 2.2 %shard_map.48 = (bf16[6,8,256,128]{3,2,1,0:T(8,128)(2,1)S(1)}, bf16[8,4,256,256]{3,2,1,0:T(8,128)(2,1)S(1)}) custom-call(f32[64,128]{1,0:T(8,128)S(1)} %shard_map.47.after_ref.refs_1_, bf16[2,8,256,128]{3,2,1,0:T(8,128)(2,1)S(1)} %get-tuple-element.18.early_ref.refs_3_, bf16[8,8,256,128]{3,2,1,0:T(8,128)(2,1)} %lik_ref.1), custom_call_target="tpu_custom_call" | custom-call | tf_op jit(solution)/shard_map/pallas_call | solution.py:321
  14.0 0.9 %shard_map.49 = (f32[8,8,256]{2,1,0:T(8,128)S(1)}, f32[64,128]{1,0:T(8,128)S(1)}) custom-call(f32[8,128]{1,0:T(8,128)S(1)} %get-tuple-element.17.refs_4_.refs_0_.info_ref, f32[64,128]{1,0:T(8,128)S(1)} %shard_map.47.after_ref.refs_1_, f32[64,128]{1,0:T(8,128)S(1)} %collective-permute-done.3.refs_2_, f32[64,128]{1,0:T(8,128)S(1)} %collective-permute-done.4.refs_3_, ...), custom_call_target="tpu_custom_call" | custom-call | tf_op jit(solution)/shard_map/pallas_call | solution.py:280
  14.9 9.5 %all_to_all.15.parts_ref = f32[8,8,256]{2,1,0:T(8,128)S(1)} all-to-all(f32[8,8,256]{2,1,0:T(8,128)S(1)} %get-tuple-element.20), channel_id=1, replica_groups={{8,10,12,14,0,2,4,6},{9,11,13,15,1,3,5,7},{24,26,28,30,16,18,20,22},{25..., dimensions={0} | all-to-all | bytes 131072 | tf_op jit(solution)/shard_map/all_to_all | solution.py:365
  24.4 0.7 %shard_map.50.refs_0_ = f32[72,128]{1,0:T(8,128)S(1)} custom-call(f32[8,128]{1,0:T(8,128)S(1)} %get-tuple-element.17.refs_4_.refs_0_.info_ref, f32[8,8,256]{2,1,0:T(8,128)S(1)} %all_to_all.15.parts_ref, f32[64,128]{1,0:T(8,128)S(1)} %get-tuple-element.21.picked_ref, bf16[2,8,256,128]{3,2,1,0:T(8,128)(2,1)S(1)} %get-tuple-element.18.early_ref.refs_3_, ...), custom_call_target="tpu_custom_call" | custom-call | tf_op jit(solution)/shard_map/pallas_call | solution.py:280
  25.1 0.5 collective-permute-start.8
  25.6 1.3 %collective-permute-start.7 = (f32[72,128]{1,0:T(8,128)S(1)}, f32[72,128]{1,0:T(8,128)S(1)}, u32[]{:S(2)}, u32[]{:S(2)}) collective-permute-start(f32[72,128]{1,0:T(8,128)S(1)} %shard_map.50.refs_0_), channel_id=1, source_target_pairs={{0,9},{1,8},{2,11},{3,10},{4,13},{5,12},{6,15},{7,14},{8,1},{9,0},... | collective-permute-start | bytes 110600 | tf_op jit(solution)/shard_map/ppermute | solution.py:29
  26.9 0.9 %collective-permute-start.6 = (f32[72,128]{1,0:T(8,128)S(1)}, f32[72,128]{1,0:T(8,128)S(1)}, u32[]{:S(2)}, u32[]{:S(2)}) collective-permute-start(f32[72,128]{1,0:T(8,128)S(1)} %shard_map.50.refs_0_), channel_id=1, source_target_pairs={{0,5},{1,4},{2,7},{3,6},{4,1},{5,0},{6,3},{7,2},{8,13},{9,12},{10,... | collective-permute-start | bytes 110600 | tf_op jit(solution)/shard_map/ppermute | solution.py:29
  27.8 2.6 %collective-permute-done.8.refs_3_ = f32[72,128]{1,0:T(8,128)S(1)} collective-permute-done((f32[72,128]{1,0:T(8,128)S(1)}, f32[72,128]{1,0:T(8,128)S(1)}, u32[]{:S(2)}, u32[]{:S(2)}) %collective-permute-start.8) | collective-permute-done | bytes 36896 | tf_op jit(solution)/shard_map/ppermute | solution.py:29
  30.7 0.3 shard_map.51
  31.0 1.2 %collective-permute-start.9 = (f32[64,128]{1,0:T(8,128)S(1)}, f32[64,128]{1,0:T(8,128)S(1)}, u32[]{:S(2)}, u32[]{:S(2)}) collective-permute-start(f32[64,128]{1,0:T(8,128)S(1)} %get-tuple-element.24), channel_id=1, source_target_pairs={{0,3},{1,2},{2,1},{3,0},{4,7},{5,6},{6,5},{7,4},{8,11},{9,10},{10,... | collective-permute-start | bytes 98312 | tf_op jit(solution)/shard_map/ppermute | solution.py:29
  32.2 1.6 %collective-permute-start.10 = (f32[64,128]{1,0:T(8,128)S(1)}, f32[64,128]{1,0:T(8,128)S(1)}, u32[]{:S(2)}, u32[]{:S(2)}) collective-permute-start(f32[64,128]{1,0:T(8,128)S(1)} %get-tuple-element.25), channel_id=1, source_target_pairs={{0,2},{1,3},{2,0},{3,1},{4,6},{5,7},{6,4},{7,5},{8,10},{9,11},{10,... | collective-permute-start | bytes 98312 | tf_op jit(solution)/shard_map/ppermute | solution.py:29
  33.9 0.6 %collective-permute-done.9.refs_1_ = f32[64,128]{1,0:T(8,128)S(1)} collective-permute-done((f32[64,128]{1,0:T(8,128)S(1)}, f32[64,128]{1,0:T(8,128)S(1)}, u32[]{:S(2)}, u32[]{:S(2)}) %collective-permute-start.9) | collective-permute-done | bytes 32800 | tf_op jit(solution)/shard_map/ppermute | solution.py:29
  34.4 1.7 %collective-permute-done.10.refs_2_ = f32[64,128]{1,0:T(8,128)S(1)} collective-permute-done((f32[64,128]{1,0:T(8,128)S(1)}, f32[64,128]{1,0:T(8,128)S(1)}, u32[]{:S(2)}, u32[]{:S(2)}) %collective-permute-start.10) | collective-permute-done | bytes 32800 | tf_op jit(solution)/shard_map/ppermute | solution.py:29
  36.1 0.7 %shard_map.52 = (f32[8,8,256]{2,1,0:T(8,128)S(1)}, f32[64,128]{1,0:T(8,128)S(1)}) custom-call(f32[64,128]{1,0:T(8,128)S(1)} %get-tuple-element.23.refs_0_, f32[64,128]{1,0:T(8,128)S(1)} %collective-permute-done.9.refs_1_, f32[64,128]{1,0:T(8,128)S(1)} %collective-permute-done.10.refs_2_, f32[64,128]{1,0:T(8,128)S(1)} %collective-permute-done.11.refs_3_, ...), custom_call_target="tpu_custom_call" | custom-call | tf_op jit(solution)/shard_map/pallas_call | solution.py:280
  36.8 8.5 %all_to_all.16.refs_1_ = f32[8,8,256]{2,1,0:T(8,128)S(1)} all-to-all(f32[8,8,256]{2,1,0:T(8,128)S(1)} %get-tuple-element.27), channel_id=1, replica_groups={{10,8,14,12,2,0,6,4},{11,9,15,13,3,1,7,5},{26,24,30,28,18,16,22,20},{27..., dimensions={0} | all-to-all | bytes 131072 | tf_op jit(solution)/shard_map/all_to_all | solution.py:365
  45.4 0.9 %shard_map.53 = f32[16,12,128]{2,1,0:T(8,128)S(1)} custom-call(f32[8,128]{1,0:T(8,128)S(1)} %get-tuple-element.17.refs_4_.refs_0_.info_ref, f32[8,8,256]{2,1,0:T(8,128)S(1)} %all_to_all.16.refs_1_, f32[64,128]{1,0:T(8,128)S(1)} %get-tuple-element.28.refs_2_, bf16[2,8,256,128]{3,2,1,0:T(8,128)(2,1)S(1)} %get-tuple-element.18.early_ref.refs_3_, ...), custom_call_target="tpu_custom_call" | custom-call | tf_op jit(solution)/shard_map/pallas_call | solution.py:280
  46.3 8.3 %all_to_all.17 = f32[16,12,128]{2,1,0:T(8,128)S(1)} all-to-all(f32[16,12,128]{2,1,0:T(8,128)S(1)} %shard_map.53), channel_id=1, replica_groups={{11,10,9,8,15,14,13,12,3,2,1,0,7,6,5,4},{27,26,25,24,31,30,29,28,19,18,..., dimensions={0} | all-to-all | bytes 196608 | tf_op jit(solution)/shard_map/all_to_all | solution.py:404
  54.6 0.6 %multiply_bitcast_fusion = f32[1536]{0:T(1024)} fusion(f32[12,128]{1,0:T(8,128)S(1)} %reduce_sum.9), kind=kLoop, calls=%fused_computation | loop fusion | flops 1536 | bytes 12288 | tf_op jit(solution)/shard_map/mul | solution.py:405
  (18 shorter events, 0.4 us)
Async XLA Ops:
  0.0 9.8 %copy-start = (f32[1536]{0:T(1024)S(1)}, f32[1536]{0:T(1024)}, u32[]{:S(2)}) copy-start(f32[1536]{0:T(1024)} %param.7) | copy-start | bytes 18436
  0.0 7.0 %collective-permute-start.2 = (f32[12,128]{1,0:T(8,128)}, f32[12,128]{1,0:T(8,128)S(1)}, u32[]{:S(2)}, u32[]{:S(2)}) collective-permute-start(f32[12,128]{1,0:T(8,128)} %bitcast.3), channel_id=1, source_target_pairs={{0,12},{1,13},{2,14},{3,15},{4,8},{5,9},{6,10},{7,11},{8,4},{9,5},... | collective-permute-start | bytes 18440 | tf_op jit(solution)/shard_map/ppermute | solution.py:29
  5.1 4.8 %collective-permute-start.1 = (f32[12,128]{1,0:T(8,128)}, f32[12,128]{1,0:T(8,128)S(1)}, u32[]{:S(2)}, u32[]{:S(2)}) collective-permute-start(f32[12,128]{1,0:T(8,128)} %bitcast.4), channel_id=1, source_target_pairs={{0,8},{1,9},{2,10},{3,11},{4,12},{5,13},{6,14},{7,15},{8,0},{9,1},... | collective-permute-start | bytes 18440 | tf_op jit(solution)/shard_map/ppermute | solution.py:29
  5.1 4.8 %collective-permute-start = (f32[12,128]{1,0:T(8,128)}, f32[12,128]{1,0:T(8,128)S(1)}, u32[]{:S(2)}, u32[]{:S(2)}) collective-permute-start(f32[12,128]{1,0:T(8,128)} %bitcast.5), channel_id=1, source_target_pairs={{0,5},{1,4},{2,7},{3,6},{4,1},{5,0},{6,3},{7,2},{8,13},{9,12},{10,... | collective-permute-start | bytes 18440 | tf_op jit(solution)/shard_map/ppermute | solution.py:29
  9.8 4.2 %collective-permute-start.5 = (f32[64,128]{1,0:T(8,128)S(1)}, f32[64,128]{1,0:T(8,128)S(1)}, u32[]{:S(2)}, u32[]{:S(2)}) collective-permute-start(f32[64,128]{1,0:T(8,128)S(1)} %shard_map.47.after_ref.refs_1_), channel_id=1, source_target_pairs={{0,3},{1,2},{2,1},{3,0},{4,7},{5,6},{6,5},{7,4},{8,11},{9,10},{10,... | collective-permute-start | bytes 98312 | tf_op jit(solution)/shard_map/ppermute | solution.py:29
  9.9 4.1 %collective-permute-start.4 = (f32[64,128]{1,0:T(8,128)S(1)}, f32[64,128]{1,0:T(8,128)S(1)}, u32[]{:S(2)}, u32[]{:S(2)}) collective-permute-start(f32[64,128]{1,0:T(8,128)S(1)} %shard_map.47.after_ref.refs_1_), channel_id=1, source_target_pairs={{0,2},{1,3},{2,0},{3,1},{4,6},{5,7},{6,4},{7,5},{8,10},{9,11},{10,... | collective-permute-start | bytes 98312 | tf_op jit(solution)/shard_map/ppermute | solution.py:29
  11.5 2.5 %collective-permute-start.3 = (f32[64,128]{1,0:T(8,128)S(1)}, f32[64,128]{1,0:T(8,128)S(1)}, u32[]{:S(2)}, u32[]{:S(2)}) collective-permute-start(f32[64,128]{1,0:T(8,128)S(1)} %shard_map.47.after_ref.refs_1_), channel_id=1, source_target_pairs={{0,1},{1,0},{2,3},{3,2},{4,5},{5,4},{6,7},{7,6},{8,9},{9,8},{10,11... | collective-permute-start | bytes 98312 | tf_op jit(solution)/shard_map/ppermute | solution.py:29
  25.1 5.4 %collective-permute-start.8 = (f32[72,128]{1,0:T(8,128)S(1)}, f32[72,128]{1,0:T(8,128)S(1)}, u32[]{:S(2)}, u32[]{:S(2)}) collective-permute-start(f32[72,128]{1,0:T(8,128)S(1)} %shard_map.50.refs_0_), channel_id=1, source_target_pairs={{0,13},{1,12},{2,15},{3,14},{4,9},{5,8},{6,11},{7,10},{8,5},{9,4},... | collective-permute-start | bytes 110600 | tf_op jit(solution)/shard_map/ppermute | solution.py:29
  25.6 4.8 %collective-permute-start.7 = (f32[72,128]{1,0:T(8,128)S(1)}, f32[72,128]{1,0:T(8,128)S(1)}, u32[]{:S(2)}, u32[]{:S(2)}) collective-permute-start(f32[72,128]{1,0:T(8,128)S(1)} %shard_map.50.refs_0_), channel_id=1, source_target_pairs={{0,9},{1,8},{2,11},{3,10},{4,13},{5,12},{6,15},{7,14},{8,1},{9,0},... | collective-permute-start | bytes 110600 | tf_op jit(solution)/shard_map/ppermute | solution.py:29
  26.9 3.8 %collective-permute-start.6 = (f32[72,128]{1,0:T(8,128)S(1)}, f32[72,128]{1,0:T(8,128)S(1)}, u32[]{:S(2)}, u32[]{:S(2)}) collective-permute-start(f32[72,128]{1,0:T(8,128)S(1)} %shard_map.50.refs_0_), channel_id=1, source_target_pairs={{0,5},{1,4},{2,7},{3,6},{4,1},{5,0},{6,3},{7,2},{8,13},{9,12},{10,... | collective-permute-start | bytes 110600 | tf_op jit(solution)/shard_map/ppermute | solution.py:29
  31.0 3.4 %collective-permute-start.9 = (f32[64,128]{1,0:T(8,128)S(1)}, f32[64,128]{1,0:T(8,128)S(1)}, u32[]{:S(2)}, u32[]{:S(2)}) collective-permute-start(f32[64,128]{1,0:T(8,128)S(1)} %get-tuple-element.24), channel_id=1, source_target_pairs={{0,3},{1,2},{2,1},{3,0},{4,7},{5,6},{6,5},{7,4},{8,11},{9,10},{10,... | collective-permute-start | bytes 98312 | tf_op jit(solution)/shard_map/ppermute | solution.py:29
  32.2 3.9 %collective-permute-start.10 = (f32[64,128]{1,0:T(8,128)S(1)}, f32[64,128]{1,0:T(8,128)S(1)}, u32[]{:S(2)}, u32[]{:S(2)}) collective-permute-start(f32[64,128]{1,0:T(8,128)S(1)} %get-tuple-element.25), channel_id=1, source_target_pairs={{0,2},{1,3},{2,0},{3,1},{4,6},{5,7},{6,4},{7,5},{8,10},{9,11},{10,... | collective-permute-start | bytes 98312 | tf_op jit(solution)/shard_map/ppermute | solution.py:29
  33.9 2.3 %collective-permute-start.11 = (f32[64,128]{1,0:T(8,128)S(1)}, f32[64,128]{1,0:T(8,128)S(1)}, u32[]{:S(2)}, u32[]{:S(2)}) collective-permute-start(f32[64,128]{1,0:T(8,128)S(1)} %get-tuple-element.26), channel_id=1, source_target_pairs={{0,1},{1,0},{2,3},{3,2},{4,5},{5,4},{6,7},{7,6},{8,9},{9,8},{10,11... | collective-permute-start | bytes 98312 | tf_op jit(solution)/shard_map/ppermute | solution.py:29

commit v21 on v20

--- a/solution.py
+++ b/solution.py
@@ -34,10 +34,14 @@
 
 
 def position(k, n):
-    place = 0
-    for r in radices(n):
+    first, *rest = radices(n)
+    n //= first
+    place = k % first * n
+    k = k // first
+    for r in rest:
         n //= r
-        place = place + (k % r) * n
+        digit = k % r
+        place = place + (digit ^ (digit >> 1)) * n
         k = k // r
     return place
 
@@ -48,7 +52,9 @@
     for r in radices(stride)[:0:-1]:
         stride //= r
         sent = parts[0] if len(parts) == 1 else jnp.concatenate(parts, axis=0)
-        parts = [sent] + [swap(sent, axes, j * stride + (j in crossed)) for j in range(1, r)]
+        parts = [sent] + [
+            swap(sent, axes, j * stride + (j in crossed)) for j in (1, 3, 2) if j < r
+        ]
     return parts
 
 
@@ -344,7 +350,7 @@
     scale = n * own_blocks * cols / total_reads
 
     column = gather_far(own_weights, ALL, CROSSED)
-    held, info = prepare(own_blocks, read_blocks // 4, likelihood, block_ids, slot_valid)
+    held, info = prepare(own_blocks, read_blocks * 3 // 8, likelihood, block_ids, slot_valid)
     (sent,) = call(join_kernel, [(near_rows(far, own_blocks), cols)], [], *column, info)
     rest, flipped = flip(sent, held, likelihood)
     pieces = [sent] + [swap(sent, ALL, j) for j in range(1, near)]

time: 55.7 us -> 56 us (level)
  waiting for transfers between devices: 8.65 us -> 9.65 us
    ppermute x12, waiting for transfers between devices: 8.65 us -> 9.65 us  [swap(): return lax.ppermute(x, axes, [(i, i ^ k) for i in range(n)])]
where the time goes in v21:
time: 56 us; the launch traced here: 55.5 us
  blocking collectives  26.2 us (47%)
  starting transfers between devices  12 us (21%)
  waiting for transfers between devices  9.65 us (17%)
  Pallas kernels  6.92 us (12%)
  other arithmetic  0.62 us (1%)
    all_to_all x2, blocking collectives, local(): lax.all_to_all(row_parts, 'genome', 0, 0, tiled=True, axis_index_groups=[...  17.9 us
    ppermute x12, starting transfers between devices, swap(): return lax.ppermute(x, axes, [(i, i ^ k) for i in range(n)])  12 us
    ppermute x12, waiting for transfers between devices, swap(): return lax.ppermute(x, axes, [(i, i ^ k) for i in range(n)])  9.65 us
    all_to_all x1, blocking collectives, local(): lax.all_to_all(counts, ALL, 0, 0, tiled=True, axis_index_groups=[order])  8.33 us
    pallas_call x6, Pallas kernels, call(): pl.pallas_call(kernel, out_shape=[jax.ShapeDtypeStruct(shape, jnp.float32...  3.45 us
    pallas_call x1, Pallas kernels, flip(): pl.pallas_call(flip_kernel, out_shape=[pltpu.VMEM((late,) + likelihood.sh...  2.04 us
    pallas_call x1, Pallas kernels, prepare(): pl.pallas_call(lambda *refs: prepare_kernel(own_blocks, *refs), out_shape...  1.43 us
  transfers between devices with their start and end apart: 12, of which 6 were waited for; matrix products, arithmetic and copies ran while one was open for 0% of the time, Pallas kernels for 6%

profile of v21, /device:TPU:0, one launch (start us, length us, event | category | flops | bytes accessed | tf_op | source)
XLA Modules:
  0.0 55.5 jit_solution(16091165100595452658)
XLA Ops:
  0.0 4.0 %collective-permute-start.2 = (f32[12,128]{1,0:T(8,128)}, f32[12,128]{1,0:T(8,128)S(1)}, u32[]{:S(2)}, u32[]{:S(2)}) collective-permute-start(f32[12,128]{1,0:T(8,128)} %bitcast.3), channel_id=1, source_target_pairs={{0,8},{1,9},{2,10},{3,11},{4,12},{5,13},{6,14},{7,15},{8,0},{9,1},... | collective-permute-start | bytes 18440 | tf_op jit(solution)/shard_map/ppermute | solution.py:29
  4.0 1.3 %collective-permute-start.1 = (f32[12,128]{1,0:T(8,128)}, f32[12,128]{1,0:T(8,128)S(1)}, u32[]{:S(2)}, u32[]{:S(2)}) collective-permute-start(f32[12,128]{1,0:T(8,128)} %bitcast.4), channel_id=1, source_target_pairs={{0,12},{1,13},{2,14},{3,15},{4,8},{5,9},{6,10},{7,11},{8,4},{9,5},... | collective-permute-start | bytes 18440 | tf_op jit(solution)/shard_map/ppermute | solution.py:29
  5.4 1.4 %shard_map.46 = (bf16[3,8,256,128]{3,2,1,0:T(8,128)(2,1)S(1)}, f32[8,128]{1,0:T(8,128)S(1)}) custom-call(bf16[8,8,256,128]{3,2,1,0:T(8,128)(2,1)} %lik_ref.1, s32[8,8]{1,0:T(8,128)} %refs_1_.1, s32[8,8]{1,0:T(8,128)} %refs_2_.1), custom_call_target="tpu_custom_call" | custom-call | tf_op jit(solution)/shard_map/pallas_call | solution.py:305
  6.8 2.9 %collective-permute-done.1.refs_2_ = f32[12,128]{1,0:T(8,128)S(1)} collective-permute-done((f32[12,128]{1,0:T(8,128)}, f32[12,128]{1,0:T(8,128)S(1)}, u32[]{:S(2)}, u32[]{:S(2)}) %collective-permute-start.1) | collective-permute-done | bytes 6176 | tf_op jit(solution)/shard_map/ppermute | solution.py:29
  9.8 1.6 %collective-permute-start.4 = (f32[64,128]{1,0:T(8,128)S(1)}, f32[64,128]{1,0:T(8,128)S(1)}, u32[]{:S(2)}, u32[]{:S(2)}) collective-permute-start(f32[64,128]{1,0:T(8,128)S(1)} %shard_map.47.after_ref.refs_1_), channel_id=1, source_target_pairs={{0,2},{1,3},{2,0},{3,1},{4,6},{5,7},{6,4},{7,5},{8,10},{9,11},{10,... | collective-permute-start | bytes 98312 | tf_op jit(solution)/shard_map/ppermute | solution.py:29
  11.4 0.3 collective-permute-start.3
  11.6 2.0 %shard_map.48 = (bf16[5,8,256,128]{3,2,1,0:T(8,128)(2,1)S(1)}, bf16[8,4,256,256]{3,2,1,0:T(8,128)(2,1)S(1)}) custom-call(f32[64,128]{1,0:T(8,128)S(1)} %shard_map.47.after_ref.refs_1_, bf16[3,8,256,128]{3,2,1,0:T(8,128)(2,1)S(1)} %get-tuple-element.18.early_ref.refs_3_, bf16[8,8,256,128]{3,2,1,0:T(8,128)(2,1)} %lik_ref.1), custom_call_target="tpu_custom_call" | custom-call | tf_op jit(solution)/shard_map/pallas_call | solution.py:327
  13.8 0.9 %shard_map.49 = (f32[8,8,256]{2,1,0:T(8,128)S(1)}, f32[64,128]{1,0:T(8,128)S(1)}) custom-call(f32[8,128]{1,0:T(8,128)S(1)} %get-tuple-element.17.refs_4_.refs_0_.info_ref, f32[64,128]{1,0:T(8,128)S(1)} %shard_map.47.after_ref.refs_1_, f32[64,128]{1,0:T(8,128)S(1)} %collective-permute-done.3.refs_2_, f32[64,128]{1,0:T(8,128)S(1)} %collective-permute-done.4.refs_3_, ...), custom_call_target="tpu_custom_call" | custom-call | tf_op jit(solution)/shard_map/pallas_call | solution.py:286
  14.7 9.5 %all_to_all.15.parts_ref = f32[8,8,256]{2,1,0:T(8,128)S(1)} all-to-all(f32[8,8,256]{2,1,0:T(8,128)S(1)} %get-tuple-element.20), channel_id=1, replica_groups={{8,10,12,14,0,2,4,6},{9,11,13,15,1,3,5,7},{24,26,28,30,16,18,20,22},{25..., dimensions={0} | all-to-all | bytes 131072 | tf_op jit(solution)/shard_map/all_to_all | solution.py:371
  24.2 0.7 %shard_map.50.refs_0_ = f32[72,128]{1,0:T(8,128)S(1)} custom-call(f32[8,128]{1,0:T(8,128)S(1)} %get-tuple-element.17.refs_4_.refs_0_.info_ref, f32[8,8,256]{2,1,0:T(8,128)S(1)} %all_to_all.15.parts_ref, f32[64,128]{1,0:T(8,128)S(1)} %get-tuple-element.21.picked_ref, bf16[3,8,256,128]{3,2,1,0:T(8,128)(2,1)S(1)} %get-tuple-element.18.early_ref.refs_3_, ...), custom_call_target="tpu_custom_call" | custom-call | tf_op jit(solution)/shard_map/pallas_call | solution.py:286
  25.0 2.6 %collective-permute-start.7 = (f32[72,128]{1,0:T(8,128)S(1)}, f32[72,128]{1,0:T(8,128)S(1)}, u32[]{:S(2)}, u32[]{:S(2)}) collective-permute-start(f32[72,128]{1,0:T(8,128)S(1)} %shard_map.50.refs_0_), channel_id=1, source_target_pairs={{0,13},{1,12},{2,15},{3,14},{4,9},{5,8},{6,11},{7,10},{8,5},{9,4},... | collective-permute-start | bytes 110600 | tf_op jit(solution)/shard_map/ppermute | solution.py:29
  27.6 2.7 %collective-permute-done.8.refs_3_ = f32[72,128]{1,0:T(8,128)S(1)} collective-permute-done((f32[72,128]{1,0:T(8,128)S(1)}, f32[72,128]{1,0:T(8,128)S(1)}, u32[]{:S(2)}, u32[]{:S(2)}) %collective-permute-start.8) | collective-permute-done | bytes 36896 | tf_op jit(solution)/shard_map/ppermute | solution.py:29
  30.3 1.4 %collective-permute-done.6.refs_1_ = f32[72,128]{1,0:T(8,128)S(1)} collective-permute-done((f32[72,128]{1,0:T(8,128)S(1)}, f32[72,128]{1,0:T(8,128)S(1)}, u32[]{:S(2)}, u32[]{:S(2)}) %collective-permute-start.6) | collective-permute-done | bytes 36896 | tf_op jit(solution)/shard_map/ppermute | solution.py:29
  31.8 0.3 shard_map.51
  32.1 0.3 collective-permute-start.9
  32.4 1.5 %collective-permute-start.10 = (f32[64,128]{1,0:T(8,128)S(1)}, f32[64,128]{1,0:T(8,128)S(1)}, u32[]{:S(2)}, u32[]{:S(2)}) collective-permute-start(f32[64,128]{1,0:T(8,128)S(1)} %get-tuple-element.25), channel_id=1, source_target_pairs={{0,2},{1,3},{2,0},{3,1},{4,6},{5,7},{6,4},{7,5},{8,10},{9,11},{10,... | collective-permute-start | bytes 98312 | tf_op jit(solution)/shard_map/ppermute | solution.py:29
  33.9 0.1 collective-permute-start.11
  34.0 1.5 %collective-permute-done.9.refs_1_ = f32[64,128]{1,0:T(8,128)S(1)} collective-permute-done((f32[64,128]{1,0:T(8,128)S(1)}, f32[64,128]{1,0:T(8,128)S(1)}, u32[]{:S(2)}, u32[]{:S(2)}) %collective-permute-start.9) | collective-permute-done | bytes 32800 | tf_op jit(solution)/shard_map/ppermute | solution.py:29
  35.5 1.0 %collective-permute-done.10.refs_2_ = f32[64,128]{1,0:T(8,128)S(1)} collective-permute-done((f32[64,128]{1,0:T(8,128)S(1)}, f32[64,128]{1,0:T(8,128)S(1)}, u32[]{:S(2)}, u32[]{:S(2)}) %collective-permute-start.10) | collective-permute-done | bytes 32800 | tf_op jit(solution)/shard_map/ppermute | solution.py:29
  36.5 0.7 %shard_map.52 = (f32[8,8,256]{2,1,0:T(8,128)S(1)}, f32[64,128]{1,0:T(8,128)S(1)}) custom-call(f32[64,128]{1,0:T(8,128)S(1)} %get-tuple-element.23.refs_0_, f32[64,128]{1,0:T(8,128)S(1)} %collective-permute-done.9.refs_1_, f32[64,128]{1,0:T(8,128)S(1)} %collective-permute-done.10.refs_2_, f32[64,128]{1,0:T(8,128)S(1)} %collective-permute-done.11.refs_3_, ...), custom_call_target="tpu_custom_call" | custom-call | tf_op jit(solution)/shard_map/pallas_call | solution.py:286
  37.2 8.4 %all_to_all.16.refs_1_ = f32[8,8,256]{2,1,0:T(8,128)S(1)} all-to-all(f32[8,8,256]{2,1,0:T(8,128)S(1)} %get-tuple-element.27), channel_id=1, replica_groups={{10,8,14,12,2,0,6,4},{11,9,15,13,3,1,7,5},{26,24,30,28,18,16,22,20},{27..., dimensions={0} | all-to-all | bytes 131072 | tf_op jit(solution)/shard_map/all_to_all | solution.py:371
  45.6 0.9 %shard_map.53 = f32[16,12,128]{2,1,0:T(8,128)S(1)} custom-call(f32[8,128]{1,0:T(8,128)S(1)} %get-tuple-element.17.refs_4_.refs_0_.info_ref, f32[8,8,256]{2,1,0:T(8,128)S(1)} %all_to_all.16.refs_1_, f32[64,128]{1,0:T(8,128)S(1)} %get-tuple-element.28.refs_2_, bf16[3,8,256,128]{3,2,1,0:T(8,128)(2,1)S(1)} %get-tuple-element.18.early_ref.refs_3_, ...), custom_call_target="tpu_custom_call" | custom-call | tf_op jit(solution)/shard_map/pallas_call | solution.py:286
  46.5 8.3 %all_to_all.17 = f32[16,12,128]{2,1,0:T(8,128)S(1)} all-to-all(f32[16,12,128]{2,1,0:T(8,128)S(1)} %shard_map.53), channel_id=1, replica_groups={{11,10,9,8,15,14,13,12,3,2,1,0,7,6,5,4},{27,26,25,24,31,30,29,28,19,18,..., dimensions={0} | all-to-all | bytes 196608 | tf_op jit(solution)/shard_map/all_to_all | solution.py:410
  54.9 0.6 %multiply_bitcast_fusion = f32[1536]{0:T(1024)} fusion(f32[12,128]{1,0:T(8,128)S(1)} %reduce_sum.9), kind=kLoop, calls=%fused_computation | loop fusion | flops 1536 | bytes 12288 | tf_op jit(solution)/shard_map/mul | solution.py:411
  (18 shorter events, 0.3 us)
Async XLA Ops:
  0.0 9.7 %copy-start = (f32[1536]{0:T(1024)S(1)}, f32[1536]{0:T(1024)}, u32[]{:S(2)}) copy-start(f32[1536]{0:T(1024)} %param.7) | copy-start | bytes 18436
  0.0 6.8 %collective-permute-start.2 = (f32[12,128]{1,0:T(8,128)}, f32[12,128]{1,0:T(8,128)S(1)}, u32[]{:S(2)}, u32[]{:S(2)}) collective-permute-start(f32[12,128]{1,0:T(8,128)} %bitcast.3), channel_id=1, source_target_pairs={{0,8},{1,9},{2,10},{3,11},{4,12},{5,13},{6,14},{7,15},{8,0},{9,1},... | collective-permute-start | bytes 18440 | tf_op jit(solution)/shard_map/ppermute | solution.py:29
  4.0 5.7 %collective-permute-start.1 = (f32[12,128]{1,0:T(8,128)}, f32[12,128]{1,0:T(8,128)S(1)}, u32[]{:S(2)}, u32[]{:S(2)}) collective-permute-start(f32[12,128]{1,0:T(8,128)} %bitcast.4), channel_id=1, source_target_pairs={{0,12},{1,13},{2,14},{3,15},{4,8},{5,9},{6,10},{7,11},{8,4},{9,5},... | collective-permute-start | bytes 18440 | tf_op jit(solution)/shard_map/ppermute | solution.py:29
  5.4 4.3 %collective-permute-start = (f32[12,128]{1,0:T(8,128)}, f32[12,128]{1,0:T(8,128)S(1)}, u32[]{:S(2)}, u32[]{:S(2)}) collective-permute-start(f32[12,128]{1,0:T(8,128)} %bitcast.5), channel_id=1, source_target_pairs={{0,5},{1,4},{2,7},{3,6},{4,1},{5,0},{6,3},{7,2},{8,13},{9,12},{10,... | collective-permute-start | bytes 18440 | tf_op jit(solution)/shard_map/ppermute | solution.py:29
  9.7 4.0 %collective-permute-start.5 = (f32[64,128]{1,0:T(8,128)S(1)}, f32[64,128]{1,0:T(8,128)S(1)}, u32[]{:S(2)}, u32[]{:S(2)}) collective-permute-start(f32[64,128]{1,0:T(8,128)S(1)} %shard_map.47.after_ref.refs_1_), channel_id=1, source_target_pairs={{0,3},{1,2},{2,1},{3,0},{4,7},{5,6},{6,5},{7,4},{8,11},{9,10},{10,... | collective-permute-start | bytes 98312 | tf_op jit(solution)/shard_map/ppermute | solution.py:29
  9.8 4.0 %collective-permute-start.4 = (f32[64,128]{1,0:T(8,128)S(1)}, f32[64,128]{1,0:T(8,128)S(1)}, u32[]{:S(2)}, u32[]{:S(2)}) collective-permute-start(f32[64,128]{1,0:T(8,128)S(1)} %shard_map.47.after_ref.refs_1_), channel_id=1, source_target_pairs={{0,2},{1,3},{2,0},{3,1},{4,6},{5,7},{6,4},{7,5},{8,10},{9,11},{10,... | collective-permute-start | bytes 98312 | tf_op jit(solution)/shard_map/ppermute | solution.py:29
  11.4 2.4 %collective-permute-start.3 = (f32[64,128]{1,0:T(8,128)S(1)}, f32[64,128]{1,0:T(8,128)S(1)}, u32[]{:S(2)}, u32[]{:S(2)}) collective-permute-start(f32[64,128]{1,0:T(8,128)S(1)} %shard_map.47.after_ref.refs_1_), channel_id=1, source_target_pairs={{0,1},{1,0},{2,3},{3,2},{4,5},{5,4},{6,7},{7,6},{8,9},{9,8},{10,11... | collective-permute-start | bytes 98312 | tf_op jit(solution)/shard_map/ppermute | solution.py:29
  24.9 5.5 %collective-permute-start.8 = (f32[72,128]{1,0:T(8,128)S(1)}, f32[72,128]{1,0:T(8,128)S(1)}, u32[]{:S(2)}, u32[]{:S(2)}) collective-permute-start(f32[72,128]{1,0:T(8,128)S(1)} %shard_map.50.refs_0_), channel_id=1, source_target_pairs={{0,9},{1,8},{2,11},{3,10},{4,13},{5,12},{6,15},{7,14},{8,1},{9,0},... | collective-permute-start | bytes 110600 | tf_op jit(solution)/shard_map/ppermute | solution.py:29
  25.0 5.4 %collective-permute-start.7 = (f32[72,128]{1,0:T(8,128)S(1)}, f32[72,128]{1,0:T(8,128)S(1)}, u32[]{:S(2)}, u32[]{:S(2)}) collective-permute-start(f32[72,128]{1,0:T(8,128)S(1)} %shard_map.50.refs_0_), channel_id=1, source_target_pairs={{0,13},{1,12},{2,15},{3,14},{4,9},{5,8},{6,11},{7,10},{8,5},{9,4},... | collective-permute-start | bytes 110600 | tf_op jit(solution)/shard_map/ppermute | solution.py:29
  27.6 4.2 %collective-permute-start.6 = (f32[72,128]{1,0:T(8,128)S(1)}, f32[72,128]{1,0:T(8,128)S(1)}, u32[]{:S(2)}, u32[]{:S(2)}) collective-permute-start(f32[72,128]{1,0:T(8,128)S(1)} %shard_map.50.refs_0_), channel_id=1, source_target_pairs={{0,5},{1,4},{2,7},{3,6},{4,1},{5,0},{6,3},{7,2},{8,13},{9,12},{10,... | collective-permute-start | bytes 110600 | tf_op jit(solution)/shard_map/ppermute | solution.py:29
  32.1 3.5 %collective-permute-start.9 = (f32[64,128]{1,0:T(8,128)S(1)}, f32[64,128]{1,0:T(8,128)S(1)}, u32[]{:S(2)}, u32[]{:S(2)}) collective-permute-start(f32[64,128]{1,0:T(8,128)S(1)} %get-tuple-element.24), channel_id=1, source_target_pairs={{0,3},{1,2},{2,1},{3,0},{4,7},{5,6},{6,5},{7,4},{8,11},{9,10},{10,... | collective-permute-start | bytes 98312 | tf_op jit(solution)/shard_map/ppermute | solution.py:29
  32.4 4.1 %collective-permute-start.10 = (f32[64,128]{1,0:T(8,128)S(1)}, f32[64,128]{1,0:T(8,128)S(1)}, u32[]{:S(2)}, u32[]{:S(2)}) collective-permute-start(f32[64,128]{1,0:T(8,128)S(1)} %get-tuple-element.25), channel_id=1, source_target_pairs={{0,2},{1,3},{2,0},{3,1},{4,6},{5,7},{6,4},{7,5},{8,10},{9,11},{10,... | collective-permute-start | bytes 98312 | tf_op jit(solution)/shard_map/ppermute | solution.py:29
  33.9 2.6 %collective-permute-start.11 = (f32[64,128]{1,0:T(8,128)S(1)}, f32[64,128]{1,0:T(8,128)S(1)}, u32[]{:S(2)}, u32[]{:S(2)}) collective-permute-start(f32[64,128]{1,0:T(8,128)S(1)} %get-tuple-element.26), channel_id=1, source_target_pairs={{0,1},{1,0},{2,3},{3,2},{4,5},{5,4},{6,7},{7,6},{8,9},{9,8},{10,11... | collective-permute-start | bytes 98312 | tf_op jit(solution)/shard_map/ppermute | solution.py:29

commit v22 on v16

--- a/solution.py
+++ b/solution.py
@@ -9,7 +9,7 @@
 ALL = ("genome", "reads")
 TERMS = 16
 ID_ROWS = 8
-CROSSED = (1,)
+CROSSED = (3,)
 LANES = 128
 VMEM = pl.BlockSpec(memory_space=pltpu.VMEM)
 ANY = pl.BlockSpec(memory_space=pl.ANY)
@@ -344,7 +344,7 @@
     scale = n * own_blocks * cols / total_reads
 
     column = gather_far(own_weights, ALL, CROSSED)
-    held, info = prepare(own_blocks, read_blocks // 2, likelihood, block_ids, slot_valid)
+    held, info = prepare(own_blocks, read_blocks * 3 // 8, likelihood, block_ids, slot_valid)
     (sent,) = call(join_kernel, [(near_rows(far, own_blocks), cols)], [], *column, info)
     rest, flipped = flip(sent, held, likelihood)
     pieces = [sent] + [swap(sent, ALL, j) for j in range(1, near)]
@@ -381,7 +381,7 @@
                 held,
                 rest,
             )
-            given = gather_far(contrib, ALL, (3,))
+            given = gather_far(contrib, ALL, (1, 3))
             sums = call(
                 lambda *refs: wanted_kernel(near, all_slots, len(given), *refs),
                 [(all_slots, cols)] * near,

time: 55.7 us -> 55.3 us (level)
  starting transfers between devices: 12.2 us -> 13.7 us
  waiting for transfers between devices: 9.2 us -> 7.95 us
  blocking collectives: 26.2 us -> 25.5 us
    ppermute x12, starting transfers between devices: 12.2 us -> 13.7 us  [swap(): return lax.ppermute(x, axes, [(i, i ^ k) for i in range(n)])]
    ppermute x12, waiting for transfers between devices: 9.2 us -> 7.95 us  [swap(): return lax.ppermute(x, axes, [(i, i ^ k) for i in range(n)])]
    all_to_all x2, blocking collectives: 17.9 us -> 17.2 us  [local(): lax.all_to_all(row_parts, 'genome', 0, 0, tiled=True, axis_index_groups=[...]
  transfers between devices with their start and end apart: 12 -> 12, of which waited for: 7 -> 6; matrix products, arithmetic and copies ran while one was open for 0% -> 0% of each run, Pallas kernels for 6% -> 6%
where the time goes in v22:
time: 55.3 us; the launch traced here: 54.8 us
  blocking collectives  25.5 us (46%)
  starting transfers between devices  13.7 us (25%)
  waiting for transfers between devices  7.95 us (14%)
  Pallas kernels  6.93 us (13%)
  other arithmetic  0.62 us (1%)
    all_to_all x2, blocking collectives, local(): lax.all_to_all(row_parts, 'genome', 0, 0, tiled=True, axis_index_groups=[...  17.2 us
    ppermute x12, starting transfers between devices, swap(): return lax.ppermute(x, axes, [(i, i ^ k) for i in range(n)])  13.7 us
    all_to_all x1, blocking collectives, local(): lax.all_to_all(counts, ALL, 0, 0, tiled=True, axis_index_groups=[order])  8.33 us
    ppermute x12, waiting for transfers between devices, swap(): return lax.ppermute(x, axes, [(i, i ^ k) for i in range(n)])  7.95 us
    pallas_call x6, Pallas kernels, call(): pl.pallas_call(kernel, out_shape=[jax.ShapeDtypeStruct(shape, jnp.float32...  3.46 us
    pallas_call x1, Pallas kernels, flip(): pl.pallas_call(flip_kernel, out_shape=[pltpu.VMEM((late,) + likelihood.sh...  2.04 us
    pallas_call x1, Pallas kernels, prepare(): pl.pallas_call(lambda *refs: prepare_kernel(own_blocks, *refs), out_shape...  1.43 us
  transfers between devices with their start and end apart: 12, of which 6 were waited for; matrix products, arithmetic and copies ran while one was open for 0% of the time, Pallas kernels for 6%

profile of v22, /device:TPU:0, one launch (start us, length us, event | category | flops | bytes accessed | tf_op | source)
XLA Modules:
  0.0 54.8 jit_solution(2945578450323566888)
XLA Ops:
  0.0 4.5 %collective-permute-start.2 = (f32[12,128]{1,0:T(8,128)}, f32[12,128]{1,0:T(8,128)S(1)}, u32[]{:S(2)}, u32[]{:S(2)}) collective-permute-start(f32[12,128]{1,0:T(8,128)} %bitcast.3), channel_id=1, source_target_pairs={{0,13},{1,12},{2,15},{3,14},{4,9},{5,8},{6,11},{7,10},{8,5},{9,4},... | collective-permute-start | bytes 18440 | tf_op jit(solution)/shard_map/ppermute | solution.py:29
  4.5 1.2 %collective-permute-start = (f32[12,128]{1,0:T(8,128)}, f32[12,128]{1,0:T(8,128)S(1)}, u32[]{:S(2)}, u32[]{:S(2)}) collective-permute-start(f32[12,128]{1,0:T(8,128)} %bitcast.5), channel_id=1, source_target_pairs={{0,4},{1,5},{2,6},{3,7},{4,0},{5,1},{6,2},{7,3},{8,12},{9,13},{10,... | collective-permute-start | bytes 18440 | tf_op jit(solution)/shard_map/ppermute | solution.py:29
  5.7 1.4 %shard_map.46 = (bf16[3,8,256,128]{3,2,1,0:T(8,128)(2,1)S(1)}, f32[8,128]{1,0:T(8,128)S(1)}) custom-call(bf16[8,8,256,128]{3,2,1,0:T(8,128)(2,1)} %lik_ref.1, s32[8,8]{1,0:T(8,128)} %refs_1_.1, s32[8,8]{1,0:T(8,128)} %refs_2_.1), custom_call_target="tpu_custom_call" | custom-call | tf_op jit(solution)/shard_map/pallas_call | solution.py:299
  7.1 2.1 %collective-permute-done.1.refs_2_ = f32[12,128]{1,0:T(8,128)S(1)} collective-permute-done((f32[12,128]{1,0:T(8,128)}, f32[12,128]{1,0:T(8,128)S(1)}, u32[]{:S(2)}, u32[]{:S(2)}) %collective-permute-start.1) | collective-permute-done | bytes 6176 | tf_op jit(solution)/shard_map/ppermute | solution.py:29
  9.3 0.7 %collective-permute-start.5 = (f32[64,128]{1,0:T(8,128)S(1)}, f32[64,128]{1,0:T(8,128)S(1)}, u32[]{:S(2)}, u32[]{:S(2)}) collective-permute-start(f32[64,128]{1,0:T(8,128)S(1)} %shard_map.47.after_ref.refs_1_), channel_id=1, source_target_pairs={{0,3},{1,2},{2,1},{3,0},{4,7},{5,6},{6,5},{7,4},{8,11},{9,10},{10,... | collective-permute-start | bytes 98312 | tf_op jit(solution)/shard_map/ppermute | solution.py:29
  10.0 0.9 %collective-permute-start.4 = (f32[64,128]{1,0:T(8,128)S(1)}, f32[64,128]{1,0:T(8,128)S(1)}, u32[]{:S(2)}, u32[]{:S(2)}) collective-permute-start(f32[64,128]{1,0:T(8,128)S(1)} %shard_map.47.after_ref.refs_1_), channel_id=1, source_target_pairs={{0,2},{1,3},{2,0},{3,1},{4,6},{5,7},{6,4},{7,5},{8,10},{9,11},{10,... | collective-permute-start | bytes 98312 | tf_op jit(solution)/shard_map/ppermute | solution.py:29
  11.2 2.0 %shard_map.48 = (bf16[5,8,256,128]{3,2,1,0:T(8,128)(2,1)S(1)}, bf16[8,4,256,256]{3,2,1,0:T(8,128)(2,1)S(1)}) custom-call(f32[64,128]{1,0:T(8,128)S(1)} %shard_map.47.after_ref.refs_1_, bf16[3,8,256,128]{3,2,1,0:T(8,128)(2,1)S(1)} %get-tuple-element.18.early_ref.refs_3_, bf16[8,8,256,128]{3,2,1,0:T(8,128)(2,1)} %lik_ref.1), custom_call_target="tpu_custom_call" | custom-call | tf_op jit(solution)/shard_map/pallas_call | solution.py:321
  13.2 1.0 %collective-permute-done.4.refs_3_ = f32[64,128]{1,0:T(8,128)S(1)} collective-permute-done((f32[64,128]{1,0:T(8,128)S(1)}, f32[64,128]{1,0:T(8,128)S(1)}, u32[]{:S(2)}, u32[]{:S(2)}) %collective-permute-start.4) | collective-permute-done | bytes 32800 | tf_op jit(solution)/shard_map/ppermute | solution.py:29
  14.2 0.9 %shard_map.49 = (f32[8,8,256]{2,1,0:T(8,128)S(1)}, f32[64,128]{1,0:T(8,128)S(1)}) custom-call(f32[8,128]{1,0:T(8,128)S(1)} %get-tuple-element.17.refs_4_.refs_0_.info_ref, f32[64,128]{1,0:T(8,128)S(1)} %shard_map.47.after_ref.refs_1_, f32[64,128]{1,0:T(8,128)S(1)} %collective-permute-done.3.refs_2_, f32[64,128]{1,0:T(8,128)S(1)} %collective-permute-done.4.refs_3_, ...), custom_call_target="tpu_custom_call" | custom-call | tf_op jit(solution)/shard_map/pallas_call | solution.py:280
  15.1 8.7 %all_to_all.15.parts_ref = f32[8,8,256]{2,1,0:T(8,128)S(1)} all-to-all(f32[8,8,256]{2,1,0:T(8,128)S(1)} %get-tuple-element.20), channel_id=1, replica_groups={{8,10,12,14,0,2,4,6},{9,11,13,15,1,3,5,7},{24,26,28,30,16,18,20,22},{25..., dimensions={0} | all-to-all | bytes 131072 | tf_op jit(solution)/shard_map/all_to_all | solution.py:365
  23.8 0.7 %shard_map.50.refs_0_ = f32[72,128]{1,0:T(8,128)S(1)} custom-call(f32[8,128]{1,0:T(8,128)S(1)} %get-tuple-element.17.refs_4_.refs_0_.info_ref, f32[8,8,256]{2,1,0:T(8,128)S(1)} %all_to_all.15.parts_ref, f32[64,128]{1,0:T(8,128)S(1)} %get-tuple-element.21.picked_ref, bf16[3,8,256,128]{3,2,1,0:T(8,128)(2,1)S(1)} %get-tuple-element.18.early_ref.refs_3_, ...), custom_call_target="tpu_custom_call" | custom-call | tf_op jit(solution)/shard_map/pallas_call | solution.py:280
  24.5 0.8 %collective-permute-start.8 = (f32[72,128]{1,0:T(8,128)S(1)}, f32[72,128]{1,0:T(8,128)S(1)}, u32[]{:S(2)}, u32[]{:S(2)}) collective-permute-start(f32[72,128]{1,0:T(8,128)S(1)} %shard_map.50.refs_0_), channel_id=1, source_target_pairs={{0,13},{1,12},{2,15},{3,14},{4,9},{5,8},{6,11},{7,10},{8,5},{9,4},... | collective-permute-start | bytes 110600 | tf_op jit(solution)/shard_map/ppermute | solution.py:29
  25.3 0.5 collective-permute-start.7
  25.7 2.6 %collective-permute-start.6 = (f32[72,128]{1,0:T(8,128)S(1)}, f32[72,128]{1,0:T(8,128)S(1)}, u32[]{:S(2)}, u32[]{:S(2)}) collective-permute-start(f32[72,128]{1,0:T(8,128)S(1)} %shard_map.50.refs_0_), channel_id=1, source_target_pairs={{0,5},{1,4},{2,7},{3,6},{4,1},{5,0},{6,3},{7,2},{8,13},{9,12},{10,... | collective-permute-start | bytes 110600 | tf_op jit(solution)/shard_map/ppermute | solution.py:29
  28.4 1.6 %collective-permute-done.8.refs_3_ = f32[72,128]{1,0:T(8,128)S(1)} collective-permute-done((f32[72,128]{1,0:T(8,128)S(1)}, f32[72,128]{1,0:T(8,128)S(1)}, u32[]{:S(2)}, u32[]{:S(2)}) %collective-permute-start.8) | collective-permute-done | bytes 36896 | tf_op jit(solution)/shard_map/ppermute | solution.py:29
  30.0 1.0 %collective-permute-done.7.refs_2_ = f32[72,128]{1,0:T(8,128)S(1)} collective-permute-done((f32[72,128]{1,0:T(8,128)S(1)}, f32[72,128]{1,0:T(8,128)S(1)}, u32[]{:S(2)}, u32[]{:S(2)}) %collective-permute-start.7) | collective-permute-done | bytes 36896 | tf_op jit(solution)/shard_map/ppermute | solution.py:29
  32.1 1.1 %collective-permute-start.10 = (f32[64,128]{1,0:T(8,128)S(1)}, f32[64,128]{1,0:T(8,128)S(1)}, u32[]{:S(2)}, u32[]{:S(2)}) collective-permute-start(f32[64,128]{1,0:T(8,128)S(1)} %get-tuple-element.25), channel_id=1, source_target_pairs={{0,3},{1,2},{2,1},{3,0},{4,7},{5,6},{6,5},{7,4},{8,11},{9,10},{10,... | collective-permute-start | bytes 98312 | tf_op jit(solution)/shard_map/ppermute | solution.py:29
  33.1 0.7 %collective-permute-start.11 = (f32[64,128]{1,0:T(8,128)S(1)}, f32[64,128]{1,0:T(8,128)S(1)}, u32[]{:S(2)}, u32[]{:S(2)}) collective-permute-start(f32[64,128]{1,0:T(8,128)S(1)} %get-tuple-element.26), channel_id=1, source_target_pairs={{0,1},{1,0},{2,3},{3,2},{4,5},{5,4},{6,7},{7,6},{8,9},{9,8},{10,11... | collective-permute-start | bytes 98312 | tf_op jit(solution)/shard_map/ppermute | solution.py:29
  33.8 2.0 %collective-permute-done.9.refs_1_ = f32[64,128]{1,0:T(8,128)S(1)} collective-permute-done((f32[64,128]{1,0:T(8,128)S(1)}, f32[64,128]{1,0:T(8,128)S(1)}, u32[]{:S(2)}, u32[]{:S(2)}) %collective-permute-start.9) | collective-permute-done | bytes 32800 | tf_op jit(solution)/shard_map/ppermute | solution.py:29
  35.8 0.7 %shard_map.52 = (f32[8,8,256]{2,1,0:T(8,128)S(1)}, f32[64,128]{1,0:T(8,128)S(1)}) custom-call(f32[64,128]{1,0:T(8,128)S(1)} %get-tuple-element.23.refs_0_, f32[64,128]{1,0:T(8,128)S(1)} %collective-permute-done.9.refs_1_, f32[64,128]{1,0:T(8,128)S(1)} %collective-permute-done.10.refs_2_, f32[64,128]{1,0:T(8,128)S(1)} %collective-permute-done.11.refs_3_, ...), custom_call_target="tpu_custom_call" | custom-call | tf_op jit(solution)/shard_map/pallas_call | solution.py:280
  36.4 8.5 %all_to_all.16.refs_1_ = f32[8,8,256]{2,1,0:T(8,128)S(1)} all-to-all(f32[8,8,256]{2,1,0:T(8,128)S(1)} %get-tuple-element.27), channel_id=1, replica_groups={{10,8,14,12,2,0,6,4},{11,9,15,13,3,1,7,5},{26,24,30,28,18,16,22,20},{27..., dimensions={0} | all-to-all | bytes 131072 | tf_op jit(solution)/shard_map/all_to_all | solution.py:365
  44.9 0.9 %shard_map.53 = f32[16,12,128]{2,1,0:T(8,128)S(1)} custom-call(f32[8,128]{1,0:T(8,128)S(1)} %get-tuple-element.17.refs_4_.refs_0_.info_ref, f32[8,8,256]{2,1,0:T(8,128)S(1)} %all_to_all.16.refs_1_, f32[64,128]{1,0:T(8,128)S(1)} %get-tuple-element.28.refs_2_, bf16[3,8,256,128]{3,2,1,0:T(8,128)(2,1)S(1)} %get-tuple-element.18.early_ref.refs_3_, ...), custom_call_target="tpu_custom_call" | custom-call | tf_op jit(solution)/shard_map/pallas_call | solution.py:280
  45.9 8.3 %all_to_all.17 = f32[16,12,128]{2,1,0:T(8,128)S(1)} all-to-all(f32[16,12,128]{2,1,0:T(8,128)S(1)} %shard_map.53), channel_id=1, replica_groups={{11,10,9,8,15,14,13,12,3,2,1,0,7,6,5,4},{27,26,25,24,31,30,29,28,19,18,..., dimensions={0} | all-to-all | bytes 196608 | tf_op jit(solution)/shard_map/all_to_all | solution.py:404
  54.2 0.6 %multiply_bitcast_fusion = f32[1536]{0:T(1024)} fusion(f32[12,128]{1,0:T(8,128)S(1)} %reduce_sum.9), kind=kLoop, calls=%fused_computation | loop fusion | flops 1536 | bytes 12288 | tf_op jit(solution)/shard_map/mul | solution.py:405
  (18 shorter events, 1.4 us)
Async XLA Ops:
  0.0 9.3 %copy-start = (f32[1536]{0:T(1024)S(1)}, f32[1536]{0:T(1024)}, u32[]{:S(2)}) copy-start(f32[1536]{0:T(1024)} %param.7) | copy-start | bytes 18436
  0.0 7.1 %collective-permute-start.2 = (f32[12,128]{1,0:T(8,128)}, f32[12,128]{1,0:T(8,128)S(1)}, u32[]{:S(2)}, u32[]{:S(2)}) collective-permute-start(f32[12,128]{1,0:T(8,128)} %bitcast.3), channel_id=1, source_target_pairs={{0,13},{1,12},{2,15},{3,14},{4,9},{5,8},{6,11},{7,10},{8,5},{9,4},... | collective-permute-start | bytes 18440 | tf_op jit(solution)/shard_map/ppermute | solution.py:29
  4.5 4.8 %collective-permute-start.1 = (f32[12,128]{1,0:T(8,128)}, f32[12,128]{1,0:T(8,128)S(1)}, u32[]{:S(2)}, u32[]{:S(2)}) collective-permute-start(f32[12,128]{1,0:T(8,128)} %bitcast.4), channel_id=1, source_target_pairs={{0,8},{1,9},{2,10},{3,11},{4,12},{5,13},{6,14},{7,15},{8,0},{9,1},... | collective-permute-start | bytes 18440 | tf_op jit(solution)/shard_map/ppermute | solution.py:29
  4.5 4.8 %collective-permute-start = (f32[12,128]{1,0:T(8,128)}, f32[12,128]{1,0:T(8,128)S(1)}, u32[]{:S(2)}, u32[]{:S(2)}) collective-permute-start(f32[12,128]{1,0:T(8,128)} %bitcast.5), channel_id=1, source_target_pairs={{0,4},{1,5},{2,6},{3,7},{4,0},{5,1},{6,2},{7,3},{8,12},{9,13},{10,... | collective-permute-start | bytes 18440 | tf_op jit(solution)/shard_map/ppermute | solution.py:29
  9.3 4.0 %collective-permute-start.5 = (f32[64,128]{1,0:T(8,128)S(1)}, f32[64,128]{1,0:T(8,128)S(1)}, u32[]{:S(2)}, u32[]{:S(2)}) collective-permute-start(f32[64,128]{1,0:T(8,128)S(1)} %shard_map.47.after_ref.refs_1_), channel_id=1, source_target_pairs={{0,3},{1,2},{2,1},{3,0},{4,7},{5,6},{6,5},{7,4},{8,11},{9,10},{10,... | collective-permute-start | bytes 98312 | tf_op jit(solution)/shard_map/ppermute | solution.py:29
  10.0 4.2 %collective-permute-start.4 = (f32[64,128]{1,0:T(8,128)S(1)}, f32[64,128]{1,0:T(8,128)S(1)}, u32[]{:S(2)}, u32[]{:S(2)}) collective-permute-start(f32[64,128]{1,0:T(8,128)S(1)} %shard_map.47.after_ref.refs_1_), channel_id=1, source_target_pairs={{0,2},{1,3},{2,0},{3,1},{4,6},{5,7},{6,4},{7,5},{8,10},{9,11},{10,... | collective-permute-start | bytes 98312 | tf_op jit(solution)/shard_map/ppermute | solution.py:29
  10.9 3.3 %collective-permute-start.3 = (f32[64,128]{1,0:T(8,128)S(1)}, f32[64,128]{1,0:T(8,128)S(1)}, u32[]{:S(2)}, u32[]{:S(2)}) collective-permute-start(f32[64,128]{1,0:T(8,128)S(1)} %shard_map.47.after_ref.refs_1_), channel_id=1, source_target_pairs={{0,1},{1,0},{2,3},{3,2},{4,5},{5,4},{6,7},{7,6},{8,9},{9,8},{10,11... | collective-permute-start | bytes 98312 | tf_op jit(solution)/shard_map/ppermute | solution.py:29
  24.5 5.5 %collective-permute-start.8 = (f32[72,128]{1,0:T(8,128)S(1)}, f32[72,128]{1,0:T(8,128)S(1)}, u32[]{:S(2)}, u32[]{:S(2)}) collective-permute-start(f32[72,128]{1,0:T(8,128)S(1)} %shard_map.50.refs_0_), channel_id=1, source_target_pairs={{0,13},{1,12},{2,15},{3,14},{4,9},{5,8},{6,11},{7,10},{8,5},{9,4},... | collective-permute-start | bytes 110600 | tf_op jit(solution)/shard_map/ppermute | solution.py:29
  25.3 5.7 %collective-permute-start.7 = (f32[72,128]{1,0:T(8,128)S(1)}, f32[72,128]{1,0:T(8,128)S(1)}, u32[]{:S(2)}, u32[]{:S(2)}) collective-permute-start(f32[72,128]{1,0:T(8,128)S(1)} %shard_map.50.refs_0_), channel_id=1, source_target_pairs={{0,8},{1,9},{2,10},{3,11},{4,12},{5,13},{6,14},{7,15},{8,0},{9,1},... | collective-permute-start | bytes 110600 | tf_op jit(solution)/shard_map/ppermute | solution.py:29
  25.7 5.5 %collective-permute-start.6 = (f32[72,128]{1,0:T(8,128)S(1)}, f32[72,128]{1,0:T(8,128)S(1)}, u32[]{:S(2)}, u32[]{:S(2)}) collective-permute-start(f32[72,128]{1,0:T(8,128)S(1)} %shard_map.50.refs_0_), channel_id=1, source_target_pairs={{0,5},{1,4},{2,7},{3,6},{4,1},{5,0},{6,3},{7,2},{8,13},{9,12},{10,... | collective-permute-start | bytes 110600 | tf_op jit(solution)/shard_map/ppermute | solution.py:29
  31.6 4.2 %collective-permute-start.9 = (f32[64,128]{1,0:T(8,128)S(1)}, f32[64,128]{1,0:T(8,128)S(1)}, u32[]{:S(2)}, u32[]{:S(2)}) collective-permute-start(f32[64,128]{1,0:T(8,128)S(1)} %get-tuple-element.24), channel_id=1, source_target_pairs={{0,2},{1,3},{2,0},{3,1},{4,6},{5,7},{6,4},{7,5},{8,10},{9,11},{10,... | collective-permute-start | bytes 98312 | tf_op jit(solution)/shard_map/ppermute | solution.py:29
  32.1 3.7 %collective-permute-start.10 = (f32[64,128]{1,0:T(8,128)S(1)}, f32[64,128]{1,0:T(8,128)S(1)}, u32[]{:S(2)}, u32[]{:S(2)}) collective-permute-start(f32[64,128]{1,0:T(8,128)S(1)} %get-tuple-element.25), channel_id=1, source_target_pairs={{0,3},{1,2},{2,1},{3,0},{4,7},{5,6},{6,5},{7,4},{8,11},{9,10},{10,... | collective-permute-start | bytes 98312 | tf_op jit(solution)/shard_map/ppermute | solution.py:29
  33.1 2.6 %collective-permute-start.11 = (f32[64,128]{1,0:T(8,128)S(1)}, f32[64,128]{1,0:T(8,128)S(1)}, u32[]{:S(2)}, u32[]{:S(2)}) collective-permute-start(f32[64,128]{1,0:T(8,128)S(1)} %get-tuple-element.26), channel_id=1, source_target_pairs={{0,1},{1,0},{2,3},{3,2},{4,5},{5,4},{6,7},{7,6},{8,9},{9,8},{10,11... | collective-permute-start | bytes 98312 | tf_op jit(solution)/shard_map/ppermute | solution.py:29

commit v23 on v22

--- a/solution.py
+++ b/solution.py
@@ -9,7 +9,7 @@
 ALL = ("genome", "reads")
 TERMS = 16
 ID_ROWS = 8
-CROSSED = (3,)
+CROSSED = (1, 2, 3)
 LANES = 128
 VMEM = pl.BlockSpec(memory_space=pltpu.VMEM)
 ANY = pl.BlockSpec(memory_space=pl.ANY)
@@ -33,22 +33,28 @@
     return [i ^ k for i in range(n)]
 
 
+GRAY = (0, 1, 3, 2)
+
+
 def position(k, n):
     place = 0
     for r in radices(n):
         n //= r
-        place = place + (k % r) * n
+        digit = k % r
+        place = place + (digit ^ (digit >> 1)) * n
         k = k // r
     return place
 
 
-def gather_far(x, axes, crossed):
+def gather_far(x, axes, crossed, order):
     parts = [x]
     stride = lax.axis_size(axes)
     for r in radices(stride)[:0:-1]:
         stride //= r
         sent = parts[0] if len(parts) == 1 else jnp.concatenate(parts, axis=0)
-        parts = [sent] + [swap(sent, axes, j * stride + (j in crossed)) for j in range(1, r)]
+        parts = [sent] + [
+            swap(sent, axes, j * stride + (j in crossed)) for j in order[1:] if j < r
+        ]
     return parts
 
 
@@ -343,13 +349,13 @@
     total_reads = read_blocks * lax.axis_size("reads") * reads
     scale = n * own_blocks * cols / total_reads
 
-    column = gather_far(own_weights, ALL, CROSSED)
+    column = gather_far(own_weights, ALL, CROSSED, GRAY)
     held, info = prepare(own_blocks, read_blocks * 3 // 8, likelihood, block_ids, slot_valid)
     (sent,) = call(join_kernel, [(near_rows(far, own_blocks), cols)], [], *column, info)
     rest, flipped = flip(sent, held, likelihood)
-    pieces = [sent] + [swap(sent, ALL, j) for j in range(1, near)]
+    pieces = [sent] + [swap(sent, ALL, j) for j in GRAY[1:]]
     at = far * own_blocks
-    wanted = [info] + [piece[at : at + ID_ROWS] for piece in pieces[1:]]
+    wanted = [info] + [pieces[GRAY[j]][at : at + ID_ROWS] for j in range(1, near)]
 
     row_shapes = [(chips, read_blocks, reads), (all_slots, cols)]
     inverse = (read_blocks, reads)
@@ -381,7 +387,7 @@
                 held,
                 rest,
             )
-            given = gather_far(contrib, ALL, (1, 3))
+            given = gather_far(contrib, ALL, (1, 3), range(4))
             sums = call(
                 lambda *refs: wanted_kernel(near, all_slots, len(given), *refs),
                 [(all_slots, cols)] * near,

time: 55.3 us -> 54.9 us (level)
  no operation moved by 1% of the time
where the time goes in v23:
time: 54.9 us; the launch traced here: 54.4 us
  blocking collectives  25.7 us (47%)
  starting transfers between devices  13.6 us (25%)
  waiting for transfers between devices  7.42 us (14%)
  Pallas kernels  6.92 us (13%)
  other arithmetic  0.62 us (1%)
    all_to_all x2, blocking collectives, local(): lax.all_to_all(row_parts, 'genome', 0, 0, tiled=True, axis_index_groups=[...  17.4 us
    ppermute x12, starting transfers between devices, swap(): return lax.ppermute(x, axes, [(i, i ^ k) for i in range(n)])  13.6 us
    all_to_all x1, blocking collectives, local(): lax.all_to_all(counts, ALL, 0, 0, tiled=True, axis_index_groups=[order])  8.33 us
    ppermute x12, waiting for transfers between devices, swap(): return lax.ppermute(x, axes, [(i, i ^ k) for i in range(n)])  7.42 us
    pallas_call x6, Pallas kernels, call(): pl.pallas_call(kernel, out_shape=[jax.ShapeDtypeStruct(shape, jnp.float32...  3.45 us
    pallas_call x1, Pallas kernels, flip(): pl.pallas_call(flip_kernel, out_shape=[pltpu.VMEM((late,) + likelihood.sh...  2.04 us
    pallas_call x1, Pallas kernels, prepare(): pl.pallas_call(lambda *refs: prepare_kernel(own_blocks, *refs), out_shape...  1.43 us
  transfers between devices with their start and end apart: 12, of which 6 were waited for; matrix products, arithmetic and copies ran while one was open for 0% of the time, Pallas kernels for 6%

profile of v23, /device:TPU:0, one launch (start us, length us, event | category | flops | bytes accessed | tf_op | source)
XLA Modules:
  0.0 54.4 jit_solution(4059861993230352714)
XLA Ops:
  0.0 3.5 %collective-permute-start.2 = (f32[12,128]{1,0:T(8,128)}, f32[12,128]{1,0:T(8,128)S(1)}, u32[]{:S(2)}, u32[]{:S(2)}) collective-permute-start(f32[12,128]{1,0:T(8,128)} %bitcast.3), channel_id=1, source_target_pairs={{0,9},{1,8},{2,11},{3,10},{4,13},{5,12},{6,15},{7,14},{8,1},{9,0},... | collective-permute-start | bytes 18440 | tf_op jit(solution)/shard_map/ppermute | solution.py:29
  3.5 1.6 %collective-permute-start.1 = (f32[12,128]{1,0:T(8,128)}, f32[12,128]{1,0:T(8,128)S(1)}, u32[]{:S(2)}, u32[]{:S(2)}) collective-permute-start(f32[12,128]{1,0:T(8,128)} %bitcast.4), channel_id=1, source_target_pairs={{0,13},{1,12},{2,15},{3,14},{4,9},{5,8},{6,11},{7,10},{8,5},{9,4},... | collective-permute-start | bytes 18440 | tf_op jit(solution)/shard_map/ppermute | solution.py:29
  5.3 1.4 %shard_map.46 = (bf16[3,8,256,128]{3,2,1,0:T(8,128)(2,1)S(1)}, f32[8,128]{1,0:T(8,128)S(1)}) custom-call(bf16[8,8,256,128]{3,2,1,0:T(8,128)(2,1)} %lik_ref.1, s32[8,8]{1,0:T(8,128)} %refs_1_.1, s32[8,8]{1,0:T(8,128)} %refs_2_.1), custom_call_target="tpu_custom_call" | custom-call | tf_op jit(solution)/shard_map/pallas_call | solution.py:305
  6.8 1.8 %collective-permute-done.1.refs_2_ = f32[12,128]{1,0:T(8,128)S(1)} collective-permute-done((f32[12,128]{1,0:T(8,128)}, f32[12,128]{1,0:T(8,128)S(1)}, u32[]{:S(2)}, u32[]{:S(2)}) %collective-permute-start.1) | collective-permute-done | bytes 6176 | tf_op jit(solution)/shard_map/ppermute | solution.py:29
  8.6 1.6 %collective-permute-start.5 = (f32[64,128]{1,0:T(8,128)S(1)}, f32[64,128]{1,0:T(8,128)S(1)}, u32[]{:S(2)}, u32[]{:S(2)}) collective-permute-start(f32[64,128]{1,0:T(8,128)S(1)} %shard_map.47.after_ref.refs_1_), channel_id=1, source_target_pairs={{0,2},{1,3},{2,0},{3,1},{4,6},{5,7},{6,4},{7,5},{8,10},{9,11},{10,... | collective-permute-start | bytes 98312 | tf_op jit(solution)/shard_map/ppermute | solution.py:29
  10.2 0.5 collective-permute-start.4
  10.8 2.0 %shard_map.48 = (bf16[5,8,256,128]{3,2,1,0:T(8,128)(2,1)S(1)}, bf16[8,4,256,256]{3,2,1,0:T(8,128)(2,1)S(1)}) custom-call(f32[64,128]{1,0:T(8,128)S(1)} %shard_map.47.after_ref.refs_1_, bf16[3,8,256,128]{3,2,1,0:T(8,128)(2,1)S(1)} %get-tuple-element.18.early_ref.refs_3_, bf16[8,8,256,128]{3,2,1,0:T(8,128)(2,1)} %lik_ref.1), custom_call_target="tpu_custom_call" | custom-call | tf_op jit(solution)/shard_map/pallas_call | solution.py:327
  12.8 0.7 %collective-permute-done.4.refs_3_ = f32[64,128]{1,0:T(8,128)S(1)} collective-permute-done((f32[64,128]{1,0:T(8,128)S(1)}, f32[64,128]{1,0:T(8,128)S(1)}, u32[]{:S(2)}, u32[]{:S(2)}) %collective-permute-start.4) | collective-permute-done | bytes 32800 | tf_op jit(solution)/shard_map/ppermute | solution.py:29
  13.5 0.9 %shard_map.49 = (f32[8,8,256]{2,1,0:T(8,128)S(1)}, f32[64,128]{1,0:T(8,128)S(1)}) custom-call(f32[8,128]{1,0:T(8,128)S(1)} %get-tuple-element.17.refs_4_.refs_0_.info_ref, f32[64,128]{1,0:T(8,128)S(1)} %shard_map.47.after_ref.refs_1_, f32[64,128]{1,0:T(8,128)S(1)} %collective-permute-done.3.refs_2_, f32[64,128]{1,0:T(8,128)S(1)} %collective-permute-done.4.refs_3_, ...), custom_call_target="tpu_custom_call" | custom-call | tf_op jit(solution)/shard_map/pallas_call | solution.py:286
  14.4 9.0 %all_to_all.15.parts_ref = f32[8,8,256]{2,1,0:T(8,128)S(1)} all-to-all(f32[8,8,256]{2,1,0:T(8,128)S(1)} %get-tuple-element.20), channel_id=1, replica_groups={{8,10,12,14,0,2,4,6},{9,11,13,15,1,3,5,7},{24,26,28,30,16,18,20,22},{25..., dimensions={0} | all-to-all | bytes 131072 | tf_op jit(solution)/shard_map/all_to_all | solution.py:371
  23.4 0.7 %shard_map.50.refs_0_ = f32[72,128]{1,0:T(8,128)S(1)} custom-call(f32[8,128]{1,0:T(8,128)S(1)} %get-tuple-element.17.refs_4_.refs_0_.info_ref, f32[8,8,256]{2,1,0:T(8,128)S(1)} %all_to_all.15.parts_ref, f32[64,128]{1,0:T(8,128)S(1)} %get-tuple-element.21.picked_ref, bf16[3,8,256,128]{3,2,1,0:T(8,128)(2,1)S(1)} %get-tuple-element.18.early_ref.refs_3_, ...), custom_call_target="tpu_custom_call" | custom-call | tf_op jit(solution)/shard_map/pallas_call | solution.py:286
  24.1 0.8 %collective-permute-start.8 = (f32[72,128]{1,0:T(8,128)S(1)}, f32[72,128]{1,0:T(8,128)S(1)}, u32[]{:S(2)}, u32[]{:S(2)}) collective-permute-start(f32[72,128]{1,0:T(8,128)S(1)} %shard_map.50.refs_0_), channel_id=1, source_target_pairs={{0,13},{1,12},{2,15},{3,14},{4,9},{5,8},{6,11},{7,10},{8,5},{9,4},... | collective-permute-start | bytes 110600 | tf_op jit(solution)/shard_map/ppermute | solution.py:29
  25.3 2.6 %collective-permute-start.6 = (f32[72,128]{1,0:T(8,128)S(1)}, f32[72,128]{1,0:T(8,128)S(1)}, u32[]{:S(2)}, u32[]{:S(2)}) collective-permute-start(f32[72,128]{1,0:T(8,128)S(1)} %shard_map.50.refs_0_), channel_id=1, source_target_pairs={{0,5},{1,4},{2,7},{3,6},{4,1},{5,0},{6,3},{7,2},{8,13},{9,12},{10,... | collective-permute-start | bytes 110600 | tf_op jit(solution)/shard_map/ppermute | solution.py:29
  28.0 1.6 %collective-permute-done.8.refs_3_ = f32[72,128]{1,0:T(8,128)S(1)} collective-permute-done((f32[72,128]{1,0:T(8,128)S(1)}, f32[72,128]{1,0:T(8,128)S(1)}, u32[]{:S(2)}, u32[]{:S(2)}) %collective-permute-start.8) | collective-permute-done | bytes 36896 | tf_op jit(solution)/shard_map/ppermute | solution.py:29
  29.6 1.0 %collective-permute-done.7.refs_2_ = f32[72,128]{1,0:T(8,128)S(1)} collective-permute-done((f32[72,128]{1,0:T(8,128)S(1)}, f32[72,128]{1,0:T(8,128)S(1)}, u32[]{:S(2)}, u32[]{:S(2)}) %collective-permute-start.7) | collective-permute-done | bytes 36896 | tf_op jit(solution)/shard_map/ppermute | solution.py:29
  31.2 0.6 %collective-permute-start.9 = (f32[64,128]{1,0:T(8,128)S(1)}, f32[64,128]{1,0:T(8,128)S(1)}, u32[]{:S(2)}, u32[]{:S(2)}) collective-permute-start(f32[64,128]{1,0:T(8,128)S(1)} %get-tuple-element.24), channel_id=1, source_target_pairs={{0,2},{1,3},{2,0},{3,1},{4,6},{5,7},{6,4},{7,5},{8,10},{9,11},{10,... | collective-permute-start | bytes 98312 | tf_op jit(solution)/shard_map/ppermute | solution.py:29
  31.8 0.9 %collective-permute-start.10 = (f32[64,128]{1,0:T(8,128)S(1)}, f32[64,128]{1,0:T(8,128)S(1)}, u32[]{:S(2)}, u32[]{:S(2)}) collective-permute-start(f32[64,128]{1,0:T(8,128)S(1)} %get-tuple-element.25), channel_id=1, source_target_pairs={{0,3},{1,2},{2,1},{3,0},{4,7},{5,6},{6,5},{7,4},{8,11},{9,10},{10,... | collective-permute-start | bytes 98312 | tf_op jit(solution)/shard_map/ppermute | solution.py:29
  32.7 0.7 %collective-permute-start.11 = (f32[64,128]{1,0:T(8,128)S(1)}, f32[64,128]{1,0:T(8,128)S(1)}, u32[]{:S(2)}, u32[]{:S(2)}) collective-permute-start(f32[64,128]{1,0:T(8,128)S(1)} %get-tuple-element.26), channel_id=1, source_target_pairs={{0,1},{1,0},{2,3},{3,2},{4,5},{5,4},{6,7},{7,6},{8,9},{9,8},{10,11... | collective-permute-start | bytes 98312 | tf_op jit(solution)/shard_map/ppermute | solution.py:29
  33.4 2.1 %collective-permute-done.9.refs_1_ = f32[64,128]{1,0:T(8,128)S(1)} collective-permute-done((f32[64,128]{1,0:T(8,128)S(1)}, f32[64,128]{1,0:T(8,128)S(1)}, u32[]{:S(2)}, u32[]{:S(2)}) %collective-permute-start.9) | collective-permute-done | bytes 32800 | tf_op jit(solution)/shard_map/ppermute | solution.py:29
  35.5 0.7 %shard_map.52 = (f32[8,8,256]{2,1,0:T(8,128)S(1)}, f32[64,128]{1,0:T(8,128)S(1)}) custom-call(f32[64,128]{1,0:T(8,128)S(1)} %get-tuple-element.23.refs_0_, f32[64,128]{1,0:T(8,128)S(1)} %collective-permute-done.9.refs_1_, f32[64,128]{1,0:T(8,128)S(1)} %collective-permute-done.10.refs_2_, f32[64,128]{1,0:T(8,128)S(1)} %collective-permute-done.11.refs_3_, ...), custom_call_target="tpu_custom_call" | custom-call | tf_op jit(solution)/shard_map/pallas_call | solution.py:286
  36.2 8.4 %all_to_all.16.refs_1_ = f32[8,8,256]{2,1,0:T(8,128)S(1)} all-to-all(f32[8,8,256]{2,1,0:T(8,128)S(1)} %get-tuple-element.27), channel_id=1, replica_groups={{10,8,14,12,2,0,6,4},{11,9,15,13,3,1,7,5},{26,24,30,28,18,16,22,20},{27..., dimensions={0} | all-to-all | bytes 131072 | tf_op jit(solution)/shard_map/all_to_all | solution.py:371
  44.5 0.9 %shard_map.53 = f32[16,12,128]{2,1,0:T(8,128)S(1)} custom-call(f32[8,128]{1,0:T(8,128)S(1)} %get-tuple-element.17.refs_4_.refs_0_.info_ref, f32[8,8,256]{2,1,0:T(8,128)S(1)} %all_to_all.16.refs_1_, f32[64,128]{1,0:T(8,128)S(1)} %get-tuple-element.28.refs_2_, bf16[3,8,256,128]{3,2,1,0:T(8,128)(2,1)S(1)} %get-tuple-element.18.early_ref.refs_3_, ...), custom_call_target="tpu_custom_call" | custom-call | tf_op jit(solution)/shard_map/pallas_call | solution.py:286
  45.5 8.3 %all_to_all.17 = f32[16,12,128]{2,1,0:T(8,128)S(1)} all-to-all(f32[16,12,128]{2,1,0:T(8,128)S(1)} %shard_map.53), channel_id=1, replica_groups={{11,10,9,8,15,14,13,12,3,2,1,0,7,6,5,4},{27,26,25,24,31,30,29,28,19,18,..., dimensions={0} | all-to-all | bytes 196608 | tf_op jit(solution)/shard_map/all_to_all | solution.py:410
  53.8 0.6 %multiply_bitcast_fusion = f32[1536]{0:T(1024)} fusion(f32[12,128]{1,0:T(8,128)S(1)} %reduce_sum.9), kind=kLoop, calls=%fused_computation | loop fusion | flops 1536 | bytes 12288 | tf_op jit(solution)/shard_map/mul | solution.py:411
  (18 shorter events, 1.4 us)
Async XLA Ops:
  0.0 8.6 %copy-start = (f32[1536]{0:T(1024)S(1)}, f32[1536]{0:T(1024)}, u32[]{:S(2)}) copy-start(f32[1536]{0:T(1024)} %param.7) | copy-start | bytes 18436
  0.0 6.8 %collective-permute-start.2 = (f32[12,128]{1,0:T(8,128)}, f32[12,128]{1,0:T(8,128)S(1)}, u32[]{:S(2)}, u32[]{:S(2)}) collective-permute-start(f32[12,128]{1,0:T(8,128)} %bitcast.3), channel_id=1, source_target_pairs={{0,9},{1,8},{2,11},{3,10},{4,13},{5,12},{6,15},{7,14},{8,1},{9,0},... | collective-permute-start | bytes 18440 | tf_op jit(solution)/shard_map/ppermute | solution.py:29
  3.5 5.1 %collective-permute-start.1 = (f32[12,128]{1,0:T(8,128)}, f32[12,128]{1,0:T(8,128)S(1)}, u32[]{:S(2)}, u32[]{:S(2)}) collective-permute-start(f32[12,128]{1,0:T(8,128)} %bitcast.4), channel_id=1, source_target_pairs={{0,13},{1,12},{2,15},{3,14},{4,9},{5,8},{6,11},{7,10},{8,5},{9,4},... | collective-permute-start | bytes 18440 | tf_op jit(solution)/shard_map/ppermute | solution.py:29
  5.1 3.5 %collective-permute-start = (f32[12,128]{1,0:T(8,128)}, f32[12,128]{1,0:T(8,128)S(1)}, u32[]{:S(2)}, u32[]{:S(2)}) collective-permute-start(f32[12,128]{1,0:T(8,128)} %bitcast.5), channel_id=1, source_target_pairs={{0,5},{1,4},{2,7},{3,6},{4,1},{5,0},{6,3},{7,2},{8,13},{9,12},{10,... | collective-permute-start | bytes 18440 | tf_op jit(solution)/shard_map/ppermute | solution.py:29
  8.6 4.3 %collective-permute-start.5 = (f32[64,128]{1,0:T(8,128)S(1)}, f32[64,128]{1,0:T(8,128)S(1)}, u32[]{:S(2)}, u32[]{:S(2)}) collective-permute-start(f32[64,128]{1,0:T(8,128)S(1)} %shard_map.47.after_ref.refs_1_), channel_id=1, source_target_pairs={{0,2},{1,3},{2,0},{3,1},{4,6},{5,7},{6,4},{7,5},{8,10},{9,11},{10,... | collective-permute-start | bytes 98312 | tf_op jit(solution)/shard_map/ppermute | solution.py:29
  10.2 3.3 %collective-permute-start.4 = (f32[64,128]{1,0:T(8,128)S(1)}, f32[64,128]{1,0:T(8,128)S(1)}, u32[]{:S(2)}, u32[]{:S(2)}) collective-permute-start(f32[64,128]{1,0:T(8,128)S(1)} %shard_map.47.after_ref.refs_1_), channel_id=1, source_target_pairs={{0,3},{1,2},{2,1},{3,0},{4,7},{5,6},{6,5},{7,4},{8,11},{9,10},{10,... | collective-permute-start | bytes 98312 | tf_op jit(solution)/shard_map/ppermute | solution.py:29
  10.7 2.8 %collective-permute-start.3 = (f32[64,128]{1,0:T(8,128)S(1)}, f32[64,128]{1,0:T(8,128)S(1)}, u32[]{:S(2)}, u32[]{:S(2)}) collective-permute-start(f32[64,128]{1,0:T(8,128)S(1)} %shard_map.47.after_ref.refs_1_), channel_id=1, source_target_pairs={{0,1},{1,0},{2,3},{3,2},{4,5},{5,4},{6,7},{7,6},{8,9},{9,8},{10,11... | collective-permute-start | bytes 98312 | tf_op jit(solution)/shard_map/ppermute | solution.py:29
  24.1 5.5 %collective-permute-start.8 = (f32[72,128]{1,0:T(8,128)S(1)}, f32[72,128]{1,0:T(8,128)S(1)}, u32[]{:S(2)}, u32[]{:S(2)}) collective-permute-start(f32[72,128]{1,0:T(8,128)S(1)} %shard_map.50.refs_0_), channel_id=1, source_target_pairs={{0,13},{1,12},{2,15},{3,14},{4,9},{5,8},{6,11},{7,10},{8,5},{9,4},... | collective-permute-start | bytes 110600 | tf_op jit(solution)/shard_map/ppermute | solution.py:29
  24.9 5.7 %collective-permute-start.7 = (f32[72,128]{1,0:T(8,128)S(1)}, f32[72,128]{1,0:T(8,128)S(1)}, u32[]{:S(2)}, u32[]{:S(2)}) collective-permute-start(f32[72,128]{1,0:T(8,128)S(1)} %shard_map.50.refs_0_), channel_id=1, source_target_pairs={{0,8},{1,9},{2,10},{3,11},{4,12},{5,13},{6,14},{7,15},{8,0},{9,1},... | collective-permute-start | bytes 110600 | tf_op jit(solution)/shard_map/ppermute | solution.py:29
  25.3 5.5 %collective-permute-start.6 = (f32[72,128]{1,0:T(8,128)S(1)}, f32[72,128]{1,0:T(8,128)S(1)}, u32[]{:S(2)}, u32[]{:S(2)}) collective-permute-start(f32[72,128]{1,0:T(8,128)S(1)} %shard_map.50.refs_0_), channel_id=1, source_target_pairs={{0,5},{1,4},{2,7},{3,6},{4,1},{5,0},{6,3},{7,2},{8,13},{9,12},{10,... | collective-permute-start | bytes 110600 | tf_op jit(solution)/shard_map/ppermute | solution.py:29
  31.2 4.3 %collective-permute-start.9 = (f32[64,128]{1,0:T(8,128)S(1)}, f32[64,128]{1,0:T(8,128)S(1)}, u32[]{:S(2)}, u32[]{:S(2)}) collective-permute-start(f32[64,128]{1,0:T(8,128)S(1)} %get-tuple-element.24), channel_id=1, source_target_pairs={{0,2},{1,3},{2,0},{3,1},{4,6},{5,7},{6,4},{7,5},{8,10},{9,11},{10,... | collective-permute-start | bytes 98312 | tf_op jit(solution)/shard_map/ppermute | solution.py:29
  31.8 3.7 %collective-permute-start.10 = (f32[64,128]{1,0:T(8,128)S(1)}, f32[64,128]{1,0:T(8,128)S(1)}, u32[]{:S(2)}, u32[]{:S(2)}) collective-permute-start(f32[64,128]{1,0:T(8,128)S(1)} %get-tuple-element.25), channel_id=1, source_target_pairs={{0,3},{1,2},{2,1},{3,0},{4,7},{5,6},{6,5},{7,4},{8,11},{9,10},{10,... | collective-permute-start | bytes 98312 | tf_op jit(solution)/shard_map/ppermute | solution.py:29
  32.7 2.8 %collective-permute-start.11 = (f32[64,128]{1,0:T(8,128)S(1)}, f32[64,128]{1,0:T(8,128)S(1)}, u32[]{:S(2)}, u32[]{:S(2)}) collective-permute-start(f32[64,128]{1,0:T(8,128)S(1)} %get-tuple-element.26), channel_id=1, source_target_pairs={{0,1},{1,0},{2,3},{3,2},{4,5},{5,4},{6,7},{7,6},{8,9},{9,8},{10,11... | collective-permute-start | bytes 98312 | tf_op jit(solution)/shard_map/ppermute | solution.py:29

commit v24 on v23

--- a/solution.py
+++ b/solution.py
@@ -262,7 +262,8 @@
 
 
 def wanted_kernel(near, all_slots, pieces, *refs):
-    given_refs, wanted, outs = refs[:pieces], refs[pieces : pieces + near], refs[pieces + near :]
+    given_refs, wanted, refs = refs[:pieces], refs[pieces : pieces + near], refs[pieces + near :]
+    before, outs = refs[:-near], refs[-near:]
     rows = all_slots + ID_ROWS
     half = LANES // 2
     lane = lax.broadcasted_iota(jnp.int32, (1, LANES), 1)
@@ -271,15 +272,19 @@
         for at in range(0, ref.shape[0], rows):
             ids.append(ref[at + all_slots : at + all_slots + 1, :])
             values.append(ref[at : at + all_slots, :])
+    if len(ids) % 2:
+        ids.append(jnp.full_like(ids[0], -2.0))
+        values.append(jnp.zeros_like(values[0]))
     pairs = [
         jnp.where(lane < half, a, pltpu.roll(b, half, 1)) for a, b in zip(ids[::2], ids[1::2])
     ]
-    given = terms(jnp.concatenate(values, axis=0))
-    for ids_ref, out_ref in zip(wanted, outs):
-        column = down(ids_ref[0:1, :])[:all_slots]
-        hot = jnp.concatenate([(column == pair).astype(jnp.float32) for pair in pairs], axis=1)
-        hot = hot.astype(jnp.bfloat16)
-        out_ref[...] = dot(hot, given[0]) + dot(hot, given[1]) + dot(hot, given[2])
+    columns = [down(ids_ref[0:1, :])[:all_slots] for ids_ref in wanted]
+    column = jnp.concatenate(columns, axis=0)
+    hot = jnp.concatenate([(column == pair).astype(jnp.float32) for pair in pairs], axis=1)
+    sums = select_rows(hot, jnp.concatenate(values, axis=0))
+    for j, out_ref in enumerate(outs):
+        part = sums[j * all_slots : (j + 1) * all_slots]
+        out_ref[...] = part + before[j][...] if before else part
 
 
 def call(kernel, outs, scratch, *operands):
@@ -387,14 +392,17 @@
                 held,
                 rest,
             )
-            given = gather_far(contrib, ALL, (1, 3), range(4))
-            sums = call(
-                lambda *refs: wanted_kernel(near, all_slots, len(given), *refs),
-                [(all_slots, cols)] * near,
-                [],
-                *given,
-                *wanted,
-            )
+            first, last, *others = gather_far(contrib, ALL, (1, 3), range(4))
+            sums = []
+            for given in ([first] + others, [last]):
+                sums = call(
+                    lambda *refs: wanted_kernel(near, all_slots, len(given), *refs),
+                    [(all_slots, cols)] * near,
+                    [],
+                    *given,
+                    *wanted,
+                    *sums,
+                )
             parts = [sums[0]] + [swap(sums[j], ALL, j) for j in list(range(2, near)) + [1]]
     order = middle_first(n, n // 2 + 3)
     (counts,) = call(

time: 54.9 us -> 55.2 us (level)
    pallas_call x6 -> x7, Pallas kernels: 3.45 us -> 3.73 us  [call(): pl.pallas_call(kernel, out_shape=[jax.ShapeDtypeStruct(shape, jnp.float32...]
  transfers between devices with their start and end apart: 12 -> 12, of which waited for: 6 -> 6; matrix products, arithmetic and copies ran while one was open for 0% -> 0% of each run, Pallas kernels for 6% -> 7%
where the time goes in v24:
time: 55.2 us; the launch traced here: 54.7 us
  blocking collectives  25.7 us (47%)
  starting transfers between devices  13.6 us (25%)
  waiting for transfers between devices  7.41 us (13%)
  Pallas kernels  7.19 us (13%)
  other arithmetic  0.62 us (1%)
    all_to_all x2, blocking collectives, local(): lax.all_to_all(row_parts, 'genome', 0, 0, tiled=True, axis_index_groups=[...  17.4 us
    ppermute x12, starting transfers between devices, swap(): return lax.ppermute(x, axes, [(i, i ^ k) for i in range(n)])  13.6 us
    all_to_all x1, blocking collectives, local(): lax.all_to_all(counts, ALL, 0, 0, tiled=True, axis_index_groups=[order])  8.33 us
    ppermute x12, waiting for transfers between devices, swap(): return lax.ppermute(x, axes, [(i, i ^ k) for i in range(n)])  7.41 us
    pallas_call x7, Pallas kernels, call(): pl.pallas_call(kernel, out_shape=[jax.ShapeDtypeStruct(shape, jnp.float32...  3.73 us
    pallas_call x1, Pallas kernels, flip(): pl.pallas_call(flip_kernel, out_shape=[pltpu.VMEM((late,) + likelihood.sh...  2.04 us
    pallas_call x1, Pallas kernels, prepare(): pl.pallas_call(lambda *refs: prepare_kernel(own_blocks, *refs), out_shape...  1.43 us
  transfers between devices with their start and end apart: 12, of which 6 were waited for; matrix products, arithmetic and copies ran while one was open for 0% of the time, Pallas kernels for 7%

profile of v24, /device:TPU:0, one launch (start us, length us, event | category | flops | bytes accessed | tf_op | source)
XLA Modules:
  0.0 54.7 jit_solution(9526533986539005809)
XLA Ops:
  0.0 3.5 %collective-permute-start.2 = (f32[12,128]{1,0:T(8,128)}, f32[12,128]{1,0:T(8,128)S(1)}, u32[]{:S(2)}, u32[]{:S(2)}) collective-permute-start(f32[12,128]{1,0:T(8,128)} %bitcast.3), channel_id=1, source_target_pairs={{0,9},{1,8},{2,11},{3,10},{4,13},{5,12},{6,15},{7,14},{8,1},{9,0},... | collective-permute-start | bytes 18440 | tf_op jit(solution)/shard_map/ppermute | solution.py:29
  3.5 1.6 %collective-permute-start.1 = (f32[12,128]{1,0:T(8,128)}, f32[12,128]{1,0:T(8,128)S(1)}, u32[]{:S(2)}, u32[]{:S(2)}) collective-permute-start(f32[12,128]{1,0:T(8,128)} %bitcast.4), channel_id=1, source_target_pairs={{0,13},{1,12},{2,15},{3,14},{4,9},{5,8},{6,11},{7,10},{8,5},{9,4},... | collective-permute-start | bytes 18440 | tf_op jit(solution)/shard_map/ppermute | solution.py:29
  5.3 1.4 %shard_map.46 = (bf16[3,8,256,128]{3,2,1,0:T(8,128)(2,1)S(1)}, f32[8,128]{1,0:T(8,128)S(1)}) custom-call(bf16[8,8,256,128]{3,2,1,0:T(8,128)(2,1)} %lik_ref.1, s32[8,8]{1,0:T(8,128)} %refs_1_.1, s32[8,8]{1,0:T(8,128)} %refs_2_.1), custom_call_target="tpu_custom_call" | custom-call | tf_op jit(solution)/shard_map/pallas_call | solution.py:310
  6.8 1.8 %collective-permute-done.1.refs_2_ = f32[12,128]{1,0:T(8,128)S(1)} collective-permute-done((f32[12,128]{1,0:T(8,128)}, f32[12,128]{1,0:T(8,128)S(1)}, u32[]{:S(2)}, u32[]{:S(2)}) %collective-permute-start.1) | collective-permute-done | bytes 6176 | tf_op jit(solution)/shard_map/ppermute | solution.py:29
  8.6 1.6 %collective-permute-start.5 = (f32[64,128]{1,0:T(8,128)S(1)}, f32[64,128]{1,0:T(8,128)S(1)}, u32[]{:S(2)}, u32[]{:S(2)}) collective-permute-start(f32[64,128]{1,0:T(8,128)S(1)} %shard_map.47.after_ref.refs_1_), channel_id=1, source_target_pairs={{0,2},{1,3},{2,0},{3,1},{4,6},{5,7},{6,4},{7,5},{8,10},{9,11},{10,... | collective-permute-start | bytes 98312 | tf_op jit(solution)/shard_map/ppermute | solution.py:29
  10.2 0.5 collective-permute-start.4
  10.8 2.0 %shard_map.48 = (bf16[5,8,256,128]{3,2,1,0:T(8,128)(2,1)S(1)}, bf16[8,4,256,256]{3,2,1,0:T(8,128)(2,1)S(1)}) custom-call(f32[64,128]{1,0:T(8,128)S(1)} %shard_map.47.after_ref.refs_1_, bf16[3,8,256,128]{3,2,1,0:T(8,128)(2,1)S(1)} %get-tuple-element.22.early_ref.refs_3_, bf16[8,8,256,128]{3,2,1,0:T(8,128)(2,1)} %lik_ref.1), custom_call_target="tpu_custom_call" | custom-call | tf_op jit(solution)/shard_map/pallas_call | solution.py:332
  12.8 0.7 %collective-permute-done.4.refs_3_ = f32[64,128]{1,0:T(8,128)S(1)} collective-permute-done((f32[64,128]{1,0:T(8,128)S(1)}, f32[64,128]{1,0:T(8,128)S(1)}, u32[]{:S(2)}, u32[]{:S(2)}) %collective-permute-start.4) | collective-permute-done | bytes 32800 | tf_op jit(solution)/shard_map/ppermute | solution.py:29
  13.5 0.9 %shard_map.49 = (f32[8,8,256]{2,1,0:T(8,128)S(1)}, f32[64,128]{1,0:T(8,128)S(1)}) custom-call(f32[8,128]{1,0:T(8,128)S(1)} %get-tuple-element.21.refs_4_.refs_0_.info_ref.refs_3_.refs_1_, f32[64,128]{1,0:T(8,128)S(1)} %shard_map.47.after_ref.refs_1_, f32[64,128]{1,0:T(8,128)S(1)} %collective-permute-done.3.refs_2_, ...), custom_call_target="tpu_custom_call" | custom-call | tf_op jit(solution)/shard_map/pallas_call | solution.py:291
  14.4 9.0 %all_to_all.15.parts_ref = f32[8,8,256]{2,1,0:T(8,128)S(1)} all-to-all(f32[8,8,256]{2,1,0:T(8,128)S(1)} %get-tuple-element.24), channel_id=1, replica_groups={{8,10,12,14,0,2,4,6},{9,11,13,15,1,3,5,7},{24,26,28,30,16,18,20,22},{25..., dimensions={0} | all-to-all | bytes 131072 | tf_op jit(solution)/shard_map/all_to_all | solution.py:376
  23.4 0.7 %shard_map.50.refs_0_ = f32[72,128]{1,0:T(8,128)S(1)} custom-call(f32[8,128]{1,0:T(8,128)S(1)} %get-tuple-element.21.refs_4_.refs_0_.info_ref.refs_3_.refs_1_, f32[8,8,256]{2,1,0:T(8,128)S(1)} %all_to_all.15.parts_ref, f32[64,128]{1,0:T(8,128)S(1)} %get-tuple-element.25.picked_ref, bf16[3,8,256,128]{3,2,1,0:T(8,128)(2,1)S(1)} %get-tuple-element.22.early_ref.refs_3_, ...), custom_call_target="tpu_custom_call" | custom-call | tf_op jit(solution)/shard_map/pallas_call | solution.py:291
  24.1 0.8 %collective-permute-start.8 = (f32[72,128]{1,0:T(8,128)S(1)}, f32[72,128]{1,0:T(8,128)S(1)}, u32[]{:S(2)}, u32[]{:S(2)}) collective-permute-start(f32[72,128]{1,0:T(8,128)S(1)} %shard_map.50.refs_0_), channel_id=1, source_target_pairs={{0,13},{1,12},{2,15},{3,14},{4,9},{5,8},{6,11},{7,10},{8,5},{9,4},... | collective-permute-start | bytes 110600 | tf_op jit(solution)/shard_map/ppermute | solution.py:29
  25.3 2.6 %collective-permute-start.6 = (f32[72,128]{1,0:T(8,128)S(1)}, f32[72,128]{1,0:T(8,128)S(1)}, u32[]{:S(2)}, u32[]{:S(2)}) collective-permute-start(f32[72,128]{1,0:T(8,128)S(1)} %shard_map.50.refs_0_), channel_id=1, source_target_pairs={{0,5},{1,4},{2,7},{3,6},{4,1},{5,0},{6,3},{7,2},{8,13},{9,12},{10,... | collective-permute-start | bytes 110600 | tf_op jit(solution)/shard_map/ppermute | solution.py:29
  28.0 1.6 %collective-permute-done.8.refs_2_ = f32[72,128]{1,0:T(8,128)S(1)} collective-permute-done((f32[72,128]{1,0:T(8,128)S(1)}, f32[72,128]{1,0:T(8,128)S(1)}, u32[]{:S(2)}, u32[]{:S(2)}) %collective-permute-start.8) | collective-permute-done | bytes 36896 | tf_op jit(solution)/shard_map/ppermute | solution.py:29
  29.6 1.0 %collective-permute-done.7.refs_1_ = f32[72,128]{1,0:T(8,128)S(1)} collective-permute-done((f32[72,128]{1,0:T(8,128)S(1)}, f32[72,128]{1,0:T(8,128)S(1)}, u32[]{:S(2)}, u32[]{:S(2)}) %collective-permute-start.7) | collective-permute-done | bytes 36896 | tf_op jit(solution)/shard_map/ppermute | solution.py:29
  31.2 0.9 %collective-permute-start.9 = (f32[64,128]{1,0:T(8,128)S(1)}, f32[64,128]{1,0:T(8,128)S(1)}, u32[]{:S(2)}, u32[]{:S(2)}) collective-permute-start(f32[64,128]{1,0:T(8,128)S(1)} %get-tuple-element.32), channel_id=1, source_target_pairs={{0,2},{1,3},{2,0},{3,1},{4,6},{5,7},{6,4},{7,5},{8,10},{9,11},{10,... | collective-permute-start | bytes 98312 | tf_op jit(solution)/shard_map/ppermute | solution.py:29
  32.1 0.6 %collective-permute-start.10 = (f32[64,128]{1,0:T(8,128)S(1)}, f32[64,128]{1,0:T(8,128)S(1)}, u32[]{:S(2)}, u32[]{:S(2)}) collective-permute-start(f32[64,128]{1,0:T(8,128)S(1)} %get-tuple-element.33), channel_id=1, source_target_pairs={{0,3},{1,2},{2,1},{3,0},{4,7},{5,6},{6,5},{7,4},{8,11},{9,10},{10,... | collective-permute-start | bytes 98312 | tf_op jit(solution)/shard_map/ppermute | solution.py:29
  32.7 0.7 %collective-permute-start.11 = (f32[64,128]{1,0:T(8,128)S(1)}, f32[64,128]{1,0:T(8,128)S(1)}, u32[]{:S(2)}, u32[]{:S(2)}) collective-permute-start(f32[64,128]{1,0:T(8,128)S(1)} %get-tuple-element.34), channel_id=1, source_target_pairs={{0,1},{1,0},{2,3},{3,2},{4,5},{5,4},{6,7},{7,6},{8,9},{9,8},{10,11... | collective-permute-start | bytes 98312 | tf_op jit(solution)/shard_map/ppermute | solution.py:29
  33.4 1.9 %collective-permute-done.9.refs_1_ = f32[64,128]{1,0:T(8,128)S(1)} collective-permute-done((f32[64,128]{1,0:T(8,128)S(1)}, f32[64,128]{1,0:T(8,128)S(1)}, u32[]{:S(2)}, u32[]{:S(2)}) %collective-permute-start.9) | collective-permute-done | bytes 32800 | tf_op jit(solution)/shard_map/ppermute | solution.py:29
  35.8 0.7 %shard_map.53 = (f32[8,8,256]{2,1,0:T(8,128)S(1)}, f32[64,128]{1,0:T(8,128)S(1)}) custom-call(f32[64,128]{1,0:T(8,128)S(1)} %get-tuple-element.31.refs_0_, f32[64,128]{1,0:T(8,128)S(1)} %collective-permute-done.9.refs_1_, f32[64,128]{1,0:T(8,128)S(1)} %collective-permute-done.10.refs_2_, f32[64,128]{1,0:T(8,128)S(1)} %collective-permute-done.11.refs_3_, ...), custom_call_target="tpu_custom_call" | custom-call | tf_op jit(solution)/shard_map/pallas_call | solution.py:291
  36.5 8.4 %all_to_all.16.refs_1_ = f32[8,8,256]{2,1,0:T(8,128)S(1)} all-to-all(f32[8,8,256]{2,1,0:T(8,128)S(1)} %get-tuple-element.35), channel_id=1, replica_groups={{10,8,14,12,2,0,6,4},{11,9,15,13,3,1,7,5},{26,24,30,28,18,16,22,20},{27..., dimensions={0} | all-to-all | bytes 131072 | tf_op jit(solution)/shard_map/all_to_all | solution.py:376
  44.8 0.9 %shard_map.54 = f32[16,12,128]{2,1,0:T(8,128)S(1)} custom-call(f32[8,128]{1,0:T(8,128)S(1)} %get-tuple-element.21.refs_4_.refs_0_.info_ref.refs_3_.refs_1_, f32[8,8,256]{2,1,0:T(8,128)S(1)} %all_to_all.16.refs_1_, f32[64,128]{1,0:T(8,128)S(1)} %get-tuple-element.36.refs_2_, bf16[3,8,256,128]{3,2,1,0:T(8,128)(2,1)S(1)} %get-tuple-element.22.early_ref.refs_3_, ...), custom_call_target="tpu_custom_call" | custom-call | tf_op jit(solution)/shard_map/pallas_call | solution.py:291
  45.7 8.3 %all_to_all.17 = f32[16,12,128]{2,1,0:T(8,128)S(1)} all-to-all(f32[16,12,128]{2,1,0:T(8,128)S(1)} %shard_map.54), channel_id=1, replica_groups={{11,10,9,8,15,14,13,12,3,2,1,0,7,6,5,4},{27,26,25,24,31,30,29,28,19,18,..., dimensions={0} | all-to-all | bytes 196608 | tf_op jit(solution)/shard_map/all_to_all | solution.py:418
  54.1 0.6 %multiply_bitcast_fusion = f32[1536]{0:T(1024)} fusion(f32[12,128]{1,0:T(8,128)S(1)} %reduce_sum.9), kind=kLoop, calls=%fused_computation | loop fusion | flops 1536 | bytes 12288 | tf_op jit(solution)/shard_map/mul | solution.py:419
  (19 shorter events, 1.9 us)
Async XLA Ops:
  0.0 8.6 %copy-start = (f32[1536]{0:T(1024)S(1)}, f32[1536]{0:T(1024)}, u32[]{:S(2)}) copy-start(f32[1536]{0:T(1024)} %param.7) | copy-start | bytes 18436
  0.0 6.8 %collective-permute-start.2 = (f32[12,128]{1,0:T(8,128)}, f32[12,128]{1,0:T(8,128)S(1)}, u32[]{:S(2)}, u32[]{:S(2)}) collective-permute-start(f32[12,128]{1,0:T(8,128)} %bitcast.3), channel_id=1, source_target_pairs={{0,9},{1,8},{2,11},{3,10},{4,13},{5,12},{6,15},{7,14},{8,1},{9,0},... | collective-permute-start | bytes 18440 | tf_op jit(solution)/shard_map/ppermute | solution.py:29
  3.5 5.1 %collective-permute-start.1 = (f32[12,128]{1,0:T(8,128)}, f32[12,128]{1,0:T(8,128)S(1)}, u32[]{:S(2)}, u32[]{:S(2)}) collective-permute-start(f32[12,128]{1,0:T(8,128)} %bitcast.4), channel_id=1, source_target_pairs={{0,13},{1,12},{2,15},{3,14},{4,9},{5,8},{6,11},{7,10},{8,5},{9,4},... | collective-permute-start | bytes 18440 | tf_op jit(solution)/shard_map/ppermute | solution.py:29
  5.1 3.5 %collective-permute-start = (f32[12,128]{1,0:T(8,128)}, f32[12,128]{1,0:T(8,128)S(1)}, u32[]{:S(2)}, u32[]{:S(2)}) collective-permute-start(f32[12,128]{1,0:T(8,128)} %bitcast.5), channel_id=1, source_target_pairs={{0,5},{1,4},{2,7},{3,6},{4,1},{5,0},{6,3},{7,2},{8,13},{9,12},{10,... | collective-permute-start | bytes 18440 | tf_op jit(solution)/shard_map/ppermute | solution.py:29
  8.6 4.3 %collective-permute-start.5 = (f32[64,128]{1,0:T(8,128)S(1)}, f32[64,128]{1,0:T(8,128)S(1)}, u32[]{:S(2)}, u32[]{:S(2)}) collective-permute-start(f32[64,128]{1,0:T(8,128)S(1)} %shard_map.47.after_ref.refs_1_), channel_id=1, source_target_pairs={{0,2},{1,3},{2,0},{3,1},{4,6},{5,7},{6,4},{7,5},{8,10},{9,11},{10,... | collective-permute-start | bytes 98312 | tf_op jit(solution)/shard_map/ppermute | solution.py:29
  10.2 3.3 %collective-permute-start.4 = (f32[64,128]{1,0:T(8,128)S(1)}, f32[64,128]{1,0:T(8,128)S(1)}, u32[]{:S(2)}, u32[]{:S(2)}) collective-permute-start(f32[64,128]{1,0:T(8,128)S(1)} %shard_map.47.after_ref.refs_1_), channel_id=1, source_target_pairs={{0,3},{1,2},{2,1},{3,0},{4,7},{5,6},{6,5},{7,4},{8,11},{9,10},{10,... | collective-permute-start | bytes 98312 | tf_op jit(solution)/shard_map/ppermute | solution.py:29
  10.7 2.8 %collective-permute-start.3 = (f32[64,128]{1,0:T(8,128)S(1)}, f32[64,128]{1,0:T(8,128)S(1)}, u32[]{:S(2)}, u32[]{:S(2)}) collective-permute-start(f32[64,128]{1,0:T(8,128)S(1)} %shard_map.47.after_ref.refs_1_), channel_id=1, source_target_pairs={{0,1},{1,0},{2,3},{3,2},{4,5},{5,4},{6,7},{7,6},{8,9},{9,8},{10,11... | collective-permute-start | bytes 98312 | tf_op jit(solution)/shard_map/ppermute | solution.py:29
  24.1 5.5 %collective-permute-start.8 = (f32[72,128]{1,0:T(8,128)S(1)}, f32[72,128]{1,0:T(8,128)S(1)}, u32[]{:S(2)}, u32[]{:S(2)}) collective-permute-start(f32[72,128]{1,0:T(8,128)S(1)} %shard_map.50.refs_0_), channel_id=1, source_target_pairs={{0,13},{1,12},{2,15},{3,14},{4,9},{5,8},{6,11},{7,10},{8,5},{9,4},... | collective-permute-start | bytes 110600 | tf_op jit(solution)/shard_map/ppermute | solution.py:29
  24.9 5.7 %collective-permute-start.7 = (f32[72,128]{1,0:T(8,128)S(1)}, f32[72,128]{1,0:T(8,128)S(1)}, u32[]{:S(2)}, u32[]{:S(2)}) collective-permute-start(f32[72,128]{1,0:T(8,128)S(1)} %shard_map.50.refs_0_), channel_id=1, source_target_pairs={{0,8},{1,9},{2,10},{3,11},{4,12},{5,13},{6,14},{7,15},{8,0},{9,1},... | collective-permute-start | bytes 110600 | tf_op jit(solution)/shard_map/ppermute | solution.py:29
  25.3 5.6 %collective-permute-start.6 = (f32[72,128]{1,0:T(8,128)S(1)}, f32[72,128]{1,0:T(8,128)S(1)}, u32[]{:S(2)}, u32[]{:S(2)}) collective-permute-start(f32[72,128]{1,0:T(8,128)S(1)} %shard_map.50.refs_0_), channel_id=1, source_target_pairs={{0,5},{1,4},{2,7},{3,6},{4,1},{5,0},{6,3},{7,2},{8,13},{9,12},{10,... | collective-permute-start | bytes 110600 | tf_op jit(solution)/shard_map/ppermute | solution.py:29
  31.2 4.1 %collective-permute-start.9 = (f32[64,128]{1,0:T(8,128)S(1)}, f32[64,128]{1,0:T(8,128)S(1)}, u32[]{:S(2)}, u32[]{:S(2)}) collective-permute-start(f32[64,128]{1,0:T(8,128)S(1)} %get-tuple-element.32), channel_id=1, source_target_pairs={{0,2},{1,3},{2,0},{3,1},{4,6},{5,7},{6,4},{7,5},{8,10},{9,11},{10,... | collective-permute-start | bytes 98312 | tf_op jit(solution)/shard_map/ppermute | solution.py:29
  32.1 3.7 %collective-permute-start.10 = (f32[64,128]{1,0:T(8,128)S(1)}, f32[64,128]{1,0:T(8,128)S(1)}, u32[]{:S(2)}, u32[]{:S(2)}) collective-permute-start(f32[64,128]{1,0:T(8,128)S(1)} %get-tuple-element.33), channel_id=1, source_target_pairs={{0,3},{1,2},{2,1},{3,0},{4,7},{5,6},{6,5},{7,4},{8,11},{9,10},{10,... | collective-permute-start | bytes 98312 | tf_op jit(solution)/shard_map/ppermute | solution.py:29
  32.7 3.1 %collective-permute-start.11 = (f32[64,128]{1,0:T(8,128)S(1)}, f32[64,128]{1,0:T(8,128)S(1)}, u32[]{:S(2)}, u32[]{:S(2)}) collective-permute-start(f32[64,128]{1,0:T(8,128)S(1)} %get-tuple-element.34), channel_id=1, source_target_pairs={{0,1},{1,0},{2,3},{3,2},{4,5},{5,4},{6,7},{7,6},{8,9},{9,8},{10,11... | collective-permute-start | bytes 98312 | tf_op jit(solution)/shard_map/ppermute | solution.py:29

commit v25 on v23

--- a/solution.py
+++ b/solution.py
@@ -387,7 +387,7 @@
                 held,
                 rest,
             )
-            given = gather_far(contrib, ALL, (1, 3), range(4))
+            given = gather_far(contrib, ALL, (1, 2), GRAY)
             sums = call(
                 lambda *refs: wanted_kernel(near, all_slots, len(given), *refs),
                 [(all_slots, cols)] * near,

time: 54.9 us -> 54.9 us (level)
  starting transfers between devices: 13.6 us -> 12.7 us
  waiting for transfers between devices: 7.42 us -> 7.99 us
    ppermute x12, starting transfers between devices: 13.6 us -> 12.7 us  [swap(): return lax.ppermute(x, axes, [(i, i ^ k) for i in range(n)])]
    ppermute x12, waiting for transfers between devices: 7.42 us -> 7.99 us  [swap(): return lax.ppermute(x, axes, [(i, i ^ k) for i in range(n)])]
where the time goes in v25:
time: 54.9 us; the launch traced here: 54.4 us
  blocking collectives  26 us (47%)
  starting transfers between devices  12.7 us (23%)
  waiting for transfers between devices  7.99 us (15%)
  Pallas kernels  6.92 us (13%)
  other arithmetic  0.62 us (1%)
    all_to_all x2, blocking collectives, local(): lax.all_to_all(row_parts, 'genome', 0, 0, tiled=True, axis_index_groups=[...  17.7 us
    ppermute x12, starting transfers between devices, swap(): return lax.ppermute(x, axes, [(i, i ^ k) for i in range(n)])  12.7 us
    all_to_all x1, blocking collectives, local(): lax.all_to_all(counts, ALL, 0, 0, tiled=True, axis_index_groups=[order])  8.33 us
    ppermute x12, waiting for transfers between devices, swap(): return lax.ppermute(x, axes, [(i, i ^ k) for i in range(n)])  7.99 us
    pallas_call x6, Pallas kernels, call(): pl.pallas_call(kernel, out_shape=[jax.ShapeDtypeStruct(shape, jnp.float32...  3.45 us
    pallas_call x1, Pallas kernels, flip(): pl.pallas_call(flip_kernel, out_shape=[pltpu.VMEM((late,) + likelihood.sh...  2.04 us
    pallas_call x1, Pallas kernels, prepare(): pl.pallas_call(lambda *refs: prepare_kernel(own_blocks, *refs), out_shape...  1.43 us
  transfers between devices with their start and end apart: 12, of which 6 were waited for; matrix products, arithmetic and copies ran while one was open for 0% of the time, Pallas kernels for 6%

profile of v25, /device:TPU:0, one launch (start us, length us, event | category | flops | bytes accessed | tf_op | source)
XLA Modules:
  0.0 54.4 jit_solution(7209042317453417917)
XLA Ops:
  0.0 3.5 %collective-permute-start.2 = (f32[12,128]{1,0:T(8,128)}, f32[12,128]{1,0:T(8,128)S(1)}, u32[]{:S(2)}, u32[]{:S(2)}) collective-permute-start(f32[12,128]{1,0:T(8,128)} %bitcast.3), channel_id=1, source_target_pairs={{0,9},{1,8},{2,11},{3,10},{4,13},{5,12},{6,15},{7,14},{8,1},{9,0},... | collective-permute-start | bytes 18440 | tf_op jit(solution)/shard_map/ppermute | solution.py:29
  3.5 1.6 %collective-permute-start.1 = (f32[12,128]{1,0:T(8,128)}, f32[12,128]{1,0:T(8,128)S(1)}, u32[]{:S(2)}, u32[]{:S(2)}) collective-permute-start(f32[12,128]{1,0:T(8,128)} %bitcast.4), channel_id=1, source_target_pairs={{0,13},{1,12},{2,15},{3,14},{4,9},{5,8},{6,11},{7,10},{8,5},{9,4},... | collective-permute-start | bytes 18440 | tf_op jit(solution)/shard_map/ppermute | solution.py:29
  5.3 1.4 %shard_map.46 = (bf16[3,8,256,128]{3,2,1,0:T(8,128)(2,1)S(1)}, f32[8,128]{1,0:T(8,128)S(1)}) custom-call(bf16[8,8,256,128]{3,2,1,0:T(8,128)(2,1)} %lik_ref.1, s32[8,8]{1,0:T(8,128)} %refs_1_.1, s32[8,8]{1,0:T(8,128)} %refs_2_.1), custom_call_target="tpu_custom_call" | custom-call | tf_op jit(solution)/shard_map/pallas_call | solution.py:305
  6.8 1.8 %collective-permute-done.1.refs_2_ = f32[12,128]{1,0:T(8,128)S(1)} collective-permute-done((f32[12,128]{1,0:T(8,128)}, f32[12,128]{1,0:T(8,128)S(1)}, u32[]{:S(2)}, u32[]{:S(2)}) %collective-permute-start.1) | collective-permute-done | bytes 6176 | tf_op jit(solution)/shard_map/ppermute | solution.py:29
  8.6 1.6 %collective-permute-start.5 = (f32[64,128]{1,0:T(8,128)S(1)}, f32[64,128]{1,0:T(8,128)S(1)}, u32[]{:S(2)}, u32[]{:S(2)}) collective-permute-start(f32[64,128]{1,0:T(8,128)S(1)} %shard_map.47.after_ref.refs_1_), channel_id=1, source_target_pairs={{0,2},{1,3},{2,0},{3,1},{4,6},{5,7},{6,4},{7,5},{8,10},{9,11},{10,... | collective-permute-start | bytes 98312 | tf_op jit(solution)/shard_map/ppermute | solution.py:29
  10.2 0.5 collective-permute-start.4
  10.8 2.0 %shard_map.48 = (bf16[5,8,256,128]{3,2,1,0:T(8,128)(2,1)S(1)}, bf16[8,4,256,256]{3,2,1,0:T(8,128)(2,1)S(1)}) custom-call(f32[64,128]{1,0:T(8,128)S(1)} %shard_map.47.after_ref.refs_1_, bf16[3,8,256,128]{3,2,1,0:T(8,128)(2,1)S(1)} %get-tuple-element.18.early_ref.refs_3_, bf16[8,8,256,128]{3,2,1,0:T(8,128)(2,1)} %lik_ref.1), custom_call_target="tpu_custom_call" | custom-call | tf_op jit(solution)/shard_map/pallas_call | solution.py:327
  12.8 0.7 %collective-permute-done.4.refs_3_ = f32[64,128]{1,0:T(8,128)S(1)} collective-permute-done((f32[64,128]{1,0:T(8,128)S(1)}, f32[64,128]{1,0:T(8,128)S(1)}, u32[]{:S(2)}, u32[]{:S(2)}) %collective-permute-start.4) | collective-permute-done | bytes 32800 | tf_op jit(solution)/shard_map/ppermute | solution.py:29
  13.5 0.9 %shard_map.49 = (f32[8,8,256]{2,1,0:T(8,128)S(1)}, f32[64,128]{1,0:T(8,128)S(1)}) custom-call(f32[8,128]{1,0:T(8,128)S(1)} %get-tuple-element.17.refs_4_.refs_0_.info_ref, f32[64,128]{1,0:T(8,128)S(1)} %shard_map.47.after_ref.refs_1_, f32[64,128]{1,0:T(8,128)S(1)} %collective-permute-done.3.refs_2_, f32[64,128]{1,0:T(8,128)S(1)} %collective-permute-done.4.refs_3_, ...), custom_call_target="tpu_custom_call" | custom-call | tf_op jit(solution)/shard_map/pallas_call | solution.py:286
  14.4 9.0 %all_to_all.15.parts_ref = f32[8,8,256]{2,1,0:T(8,128)S(1)} all-to-all(f32[8,8,256]{2,1,0:T(8,128)S(1)} %get-tuple-element.20), channel_id=1, replica_groups={{8,10,12,14,0,2,4,6},{9,11,13,15,1,3,5,7},{24,26,28,30,16,18,20,22},{25..., dimensions={0} | all-to-all | bytes 131072 | tf_op jit(solution)/shard_map/all_to_all | solution.py:371
  23.4 0.7 %shard_map.50.refs_0_ = f32[72,128]{1,0:T(8,128)S(1)} custom-call(f32[8,128]{1,0:T(8,128)S(1)} %get-tuple-element.17.refs_4_.refs_0_.info_ref, f32[8,8,256]{2,1,0:T(8,128)S(1)} %all_to_all.15.parts_ref, f32[64,128]{1,0:T(8,128)S(1)} %get-tuple-element.21.picked_ref, bf16[3,8,256,128]{3,2,1,0:T(8,128)(2,1)S(1)} %get-tuple-element.18.early_ref.refs_3_, ...), custom_call_target="tpu_custom_call" | custom-call | tf_op jit(solution)/shard_map/pallas_call | solution.py:286
  24.2 2.3 %collective-permute-start.7 = (f32[72,128]{1,0:T(8,128)S(1)}, f32[72,128]{1,0:T(8,128)S(1)}, u32[]{:S(2)}, u32[]{:S(2)}) collective-permute-start(f32[72,128]{1,0:T(8,128)S(1)} %shard_map.50.refs_0_), channel_id=1, source_target_pairs={{0,12},{1,13},{2,14},{3,15},{4,8},{5,9},{6,10},{7,11},{8,4},{9,5},... | collective-permute-start | bytes 110600 | tf_op jit(solution)/shard_map/ppermute | solution.py:29
  26.5 0.6 %collective-permute-start.6 = (f32[72,128]{1,0:T(8,128)S(1)}, f32[72,128]{1,0:T(8,128)S(1)}, u32[]{:S(2)}, u32[]{:S(2)}) collective-permute-start(f32[72,128]{1,0:T(8,128)S(1)} %shard_map.50.refs_0_), channel_id=1, source_target_pairs={{0,5},{1,4},{2,7},{3,6},{4,1},{5,0},{6,3},{7,2},{8,13},{9,12},{10,... | collective-permute-start | bytes 110600 | tf_op jit(solution)/shard_map/ppermute | solution.py:29
  27.1 2.4 %collective-permute-done.8.refs_3_ = f32[72,128]{1,0:T(8,128)S(1)} collective-permute-done((f32[72,128]{1,0:T(8,128)S(1)}, f32[72,128]{1,0:T(8,128)S(1)}, u32[]{:S(2)}, u32[]{:S(2)}) %collective-permute-start.8) | collective-permute-done | bytes 36896 | tf_op jit(solution)/shard_map/ppermute | solution.py:29
  29.5 0.8 %collective-permute-done.7.refs_2_ = f32[72,128]{1,0:T(8,128)S(1)} collective-permute-done((f32[72,128]{1,0:T(8,128)S(1)}, f32[72,128]{1,0:T(8,128)S(1)}, u32[]{:S(2)}, u32[]{:S(2)}) %collective-permute-start.7) | collective-permute-done | bytes 36896 | tf_op jit(solution)/shard_map/ppermute | solution.py:29
  30.3 0.5 collective-permute-done.6.refs_1_
  31.2 1.5 %collective-permute-start.10 = (f32[64,128]{1,0:T(8,128)S(1)}, f32[64,128]{1,0:T(8,128)S(1)}, u32[]{:S(2)}, u32[]{:S(2)}) collective-permute-start(f32[64,128]{1,0:T(8,128)S(1)} %get-tuple-element.25), channel_id=1, source_target_pairs={{0,3},{1,2},{2,1},{3,0},{4,7},{5,6},{6,5},{7,4},{8,11},{9,10},{10,... | collective-permute-start | bytes 98312 | tf_op jit(solution)/shard_map/ppermute | solution.py:29
  32.7 0.7 %collective-permute-start.11 = (f32[64,128]{1,0:T(8,128)S(1)}, f32[64,128]{1,0:T(8,128)S(1)}, u32[]{:S(2)}, u32[]{:S(2)}) collective-permute-start(f32[64,128]{1,0:T(8,128)S(1)} %get-tuple-element.26), channel_id=1, source_target_pairs={{0,1},{1,0},{2,3},{3,2},{4,5},{5,4},{6,7},{7,6},{8,9},{9,8},{10,11... | collective-permute-start | bytes 98312 | tf_op jit(solution)/shard_map/ppermute | solution.py:29
  33.4 1.8 %collective-permute-done.9.refs_1_ = f32[64,128]{1,0:T(8,128)S(1)} collective-permute-done((f32[64,128]{1,0:T(8,128)S(1)}, f32[64,128]{1,0:T(8,128)S(1)}, u32[]{:S(2)}, u32[]{:S(2)}) %collective-permute-start.9) | collective-permute-done | bytes 32800 | tf_op jit(solution)/shard_map/ppermute | solution.py:29
  35.2 0.7 %shard_map.52 = (f32[8,8,256]{2,1,0:T(8,128)S(1)}, f32[64,128]{1,0:T(8,128)S(1)}) custom-call(f32[64,128]{1,0:T(8,128)S(1)} %get-tuple-element.23.refs_0_, f32[64,128]{1,0:T(8,128)S(1)} %collective-permute-done.9.refs_1_, f32[64,128]{1,0:T(8,128)S(1)} %collective-permute-done.10.refs_2_, f32[64,128]{1,0:T(8,128)S(1)} %collective-permute-done.11.refs_3_, ...), custom_call_target="tpu_custom_call" | custom-call | tf_op jit(solution)/shard_map/pallas_call | solution.py:286
  35.8 8.7 %all_to_all.16.refs_1_ = f32[8,8,256]{2,1,0:T(8,128)S(1)} all-to-all(f32[8,8,256]{2,1,0:T(8,128)S(1)} %get-tuple-element.27), channel_id=1, replica_groups={{10,8,14,12,2,0,6,4},{11,9,15,13,3,1,7,5},{26,24,30,28,18,16,22,20},{27..., dimensions={0} | all-to-all | bytes 131072 | tf_op jit(solution)/shard_map/all_to_all | solution.py:371
  44.5 0.9 %shard_map.53 = f32[16,12,128]{2,1,0:T(8,128)S(1)} custom-call(f32[8,128]{1,0:T(8,128)S(1)} %get-tuple-element.17.refs_4_.refs_0_.info_ref, f32[8,8,256]{2,1,0:T(8,128)S(1)} %all_to_all.16.refs_1_, f32[64,128]{1,0:T(8,128)S(1)} %get-tuple-element.28.refs_2_, bf16[3,8,256,128]{3,2,1,0:T(8,128)(2,1)S(1)} %get-tuple-element.18.early_ref.refs_3_, ...), custom_call_target="tpu_custom_call" | custom-call | tf_op jit(solution)/shard_map/pallas_call | solution.py:286
  45.4 8.3 %all_to_all.17 = f32[16,12,128]{2,1,0:T(8,128)S(1)} all-to-all(f32[16,12,128]{2,1,0:T(8,128)S(1)} %shard_map.53), channel_id=1, replica_groups={{11,10,9,8,15,14,13,12,3,2,1,0,7,6,5,4},{27,26,25,24,31,30,29,28,19,18,..., dimensions={0} | all-to-all | bytes 196608 | tf_op jit(solution)/shard_map/all_to_all | solution.py:410
  53.8 0.6 %multiply_bitcast_fusion = f32[1536]{0:T(1024)} fusion(f32[12,128]{1,0:T(8,128)S(1)} %reduce_sum.9), kind=kLoop, calls=%fused_computation | loop fusion | flops 1536 | bytes 12288 | tf_op jit(solution)/shard_map/mul | solution.py:411
  (18 shorter events, 0.8 us)
Async XLA Ops:
  0.0 8.6 %copy-start = (f32[1536]{0:T(1024)S(1)}, f32[1536]{0:T(1024)}, u32[]{:S(2)}) copy-start(f32[1536]{0:T(1024)} %param.7) | copy-start | bytes 18436
  0.0 6.8 %collective-permute-start.2 = (f32[12,128]{1,0:T(8,128)}, f32[12,128]{1,0:T(8,128)S(1)}, u32[]{:S(2)}, u32[]{:S(2)}) collective-permute-start(f32[12,128]{1,0:T(8,128)} %bitcast.3), channel_id=1, source_target_pairs={{0,9},{1,8},{2,11},{3,10},{4,13},{5,12},{6,15},{7,14},{8,1},{9,0},... | collective-permute-start | bytes 18440 | tf_op jit(solution)/shard_map/ppermute | solution.py:29
  3.5 5.1 %collective-permute-start.1 = (f32[12,128]{1,0:T(8,128)}, f32[12,128]{1,0:T(8,128)S(1)}, u32[]{:S(2)}, u32[]{:S(2)}) collective-permute-start(f32[12,128]{1,0:T(8,128)} %bitcast.4), channel_id=1, source_target_pairs={{0,13},{1,12},{2,15},{3,14},{4,9},{5,8},{6,11},{7,10},{8,5},{9,4},... | collective-permute-start | bytes 18440 | tf_op jit(solution)/shard_map/ppermute | solution.py:29
  5.1 3.5 %collective-permute-start = (f32[12,128]{1,0:T(8,128)}, f32[12,128]{1,0:T(8,128)S(1)}, u32[]{:S(2)}, u32[]{:S(2)}) collective-permute-start(f32[12,128]{1,0:T(8,128)} %bitcast.5), channel_id=1, source_target_pairs={{0,5},{1,4},{2,7},{3,6},{4,1},{5,0},{6,3},{7,2},{8,13},{9,12},{10,... | collective-permute-start | bytes 18440 | tf_op jit(solution)/shard_map/ppermute | solution.py:29
  8.6 4.3 %collective-permute-start.5 = (f32[64,128]{1,0:T(8,128)S(1)}, f32[64,128]{1,0:T(8,128)S(1)}, u32[]{:S(2)}, u32[]{:S(2)}) collective-permute-start(f32[64,128]{1,0:T(8,128)S(1)} %shard_map.47.after_ref.refs_1_), channel_id=1, source_target_pairs={{0,2},{1,3},{2,0},{3,1},{4,6},{5,7},{6,4},{7,5},{8,10},{9,11},{10,... | collective-permute-start | bytes 98312 | tf_op jit(solution)/shard_map/ppermute | solution.py:29
  10.2 3.3 %collective-permute-start.4 = (f32[64,128]{1,0:T(8,128)S(1)}, f32[64,128]{1,0:T(8,128)S(1)}, u32[]{:S(2)}, u32[]{:S(2)}) collective-permute-start(f32[64,128]{1,0:T(8,128)S(1)} %shard_map.47.after_ref.refs_1_), channel_id=1, source_target_pairs={{0,3},{1,2},{2,1},{3,0},{4,7},{5,6},{6,5},{7,4},{8,11},{9,10},{10,... | collective-permute-start | bytes 98312 | tf_op jit(solution)/shard_map/ppermute | solution.py:29
  10.7 2.8 %collective-permute-start.3 = (f32[64,128]{1,0:T(8,128)S(1)}, f32[64,128]{1,0:T(8,128)S(1)}, u32[]{:S(2)}, u32[]{:S(2)}) collective-permute-start(f32[64,128]{1,0:T(8,128)S(1)} %shard_map.47.after_ref.refs_1_), channel_id=1, source_target_pairs={{0,1},{1,0},{2,3},{3,2},{4,5},{5,4},{6,7},{7,6},{8,9},{9,8},{10,11... | collective-permute-start | bytes 98312 | tf_op jit(solution)/shard_map/ppermute | solution.py:29
  24.1 5.4 %collective-permute-start.8 = (f32[72,128]{1,0:T(8,128)S(1)}, f32[72,128]{1,0:T(8,128)S(1)}, u32[]{:S(2)}, u32[]{:S(2)}) collective-permute-start(f32[72,128]{1,0:T(8,128)S(1)} %shard_map.50.refs_0_), channel_id=1, source_target_pairs={{0,9},{1,8},{2,11},{3,10},{4,13},{5,12},{6,15},{7,14},{8,1},{9,0},... | collective-permute-start | bytes 110600 | tf_op jit(solution)/shard_map/ppermute | solution.py:29
  24.2 6.2 %collective-permute-start.7 = (f32[72,128]{1,0:T(8,128)S(1)}, f32[72,128]{1,0:T(8,128)S(1)}, u32[]{:S(2)}, u32[]{:S(2)}) collective-permute-start(f32[72,128]{1,0:T(8,128)S(1)} %shard_map.50.refs_0_), channel_id=1, source_target_pairs={{0,12},{1,13},{2,14},{3,15},{4,8},{5,9},{6,10},{7,11},{8,4},{9,5},... | collective-permute-start | bytes 110600 | tf_op jit(solution)/shard_map/ppermute | solution.py:29
  26.5 4.3 %collective-permute-start.6 = (f32[72,128]{1,0:T(8,128)S(1)}, f32[72,128]{1,0:T(8,128)S(1)}, u32[]{:S(2)}, u32[]{:S(2)}) collective-permute-start(f32[72,128]{1,0:T(8,128)S(1)} %shard_map.50.refs_0_), channel_id=1, source_target_pairs={{0,5},{1,4},{2,7},{3,6},{4,1},{5,0},{6,3},{7,2},{8,13},{9,12},{10,... | collective-permute-start | bytes 110600 | tf_op jit(solution)/shard_map/ppermute | solution.py:29
  31.2 4.0 %collective-permute-start.9 = (f32[64,128]{1,0:T(8,128)S(1)}, f32[64,128]{1,0:T(8,128)S(1)}, u32[]{:S(2)}, u32[]{:S(2)}) collective-permute-start(f32[64,128]{1,0:T(8,128)S(1)} %get-tuple-element.24), channel_id=1, source_target_pairs={{0,2},{1,3},{2,0},{3,1},{4,6},{5,7},{6,4},{7,5},{8,10},{9,11},{10,... | collective-permute-start | bytes 98312 | tf_op jit(solution)/shard_map/ppermute | solution.py:29
  31.2 3.9 %collective-permute-start.10 = (f32[64,128]{1,0:T(8,128)S(1)}, f32[64,128]{1,0:T(8,128)S(1)}, u32[]{:S(2)}, u32[]{:S(2)}) collective-permute-start(f32[64,128]{1,0:T(8,128)S(1)} %get-tuple-element.25), channel_id=1, source_target_pairs={{0,3},{1,2},{2,1},{3,0},{4,7},{5,6},{6,5},{7,4},{8,11},{9,10},{10,... | collective-permute-start | bytes 98312 | tf_op jit(solution)/shard_map/ppermute | solution.py:29
  32.7 2.5 %collective-permute-start.11 = (f32[64,128]{1,0:T(8,128)S(1)}, f32[64,128]{1,0:T(8,128)S(1)}, u32[]{:S(2)}, u32[]{:S(2)}) collective-permute-start(f32[64,128]{1,0:T(8,128)S(1)} %get-tuple-element.26), channel_id=1, source_target_pairs={{0,1},{1,0},{2,3},{3,2},{4,5},{5,4},{6,7},{7,6},{8,9},{9,8},{10,11... | collective-permute-start | bytes 98312 | tf_op jit(solution)/shard_map/ppermute | solution.py:29

commit v26 on v23

--- a/solution.py
+++ b/solution.py
@@ -350,7 +350,7 @@
     scale = n * own_blocks * cols / total_reads
 
     column = gather_far(own_weights, ALL, CROSSED, GRAY)
-    held, info = prepare(own_blocks, read_blocks * 3 // 8, likelihood, block_ids, slot_valid)
+    held, info = prepare(own_blocks, read_blocks // 2, likelihood, block_ids, slot_valid)
     (sent,) = call(join_kernel, [(near_rows(far, own_blocks), cols)], [], *column, info)
     rest, flipped = flip(sent, held, likelihood)
     pieces = [sent] + [swap(sent, ALL, j) for j in GRAY[1:]]

time: 54.9 us -> 54.9 us (level)
  no operation moved by 1% of the time
where the time goes in v26:
time: 54.9 us; the launch traced here: 54.4 us
  blocking collectives  25.7 us (47%)
  starting transfers between devices  13.6 us (25%)
  waiting for transfers between devices  7.46 us (14%)
  Pallas kernels  6.89 us (13%)
  other arithmetic  0.62 us (1%)
    all_to_all x2, blocking collectives, local(): lax.all_to_all(row_parts, 'genome', 0, 0, tiled=True, axis_index_groups=[...  17.4 us
    ppermute x12, starting transfers between devices, swap(): return lax.ppermute(x, axes, [(i, i ^ k) for i in range(n)])  13.6 us
    all_to_all x1, blocking collectives, local(): lax.all_to_all(counts, ALL, 0, 0, tiled=True, axis_index_groups=[order])  8.33 us
    ppermute x12, waiting for transfers between devices, swap(): return lax.ppermute(x, axes, [(i, i ^ k) for i in range(n)])  7.46 us
    pallas_call x6, Pallas kernels, call(): pl.pallas_call(kernel, out_shape=[jax.ShapeDtypeStruct(shape, jnp.float32...  3.46 us
    pallas_call x1, Pallas kernels, flip(): pl.pallas_call(flip_kernel, out_shape=[pltpu.VMEM((late,) + likelihood.sh...  1.84 us
    pallas_call x1, Pallas kernels, prepare(): pl.pallas_call(lambda *refs: prepare_kernel(own_blocks, *refs), out_shape...  1.6 us
  transfers between devices with their start and end apart: 12, of which 6 were waited for; matrix products, arithmetic and copies ran while one was open for 0% of the time, Pallas kernels for 6%

profile of v26, /device:TPU:0, one launch (start us, length us, event | category | flops | bytes accessed | tf_op | source)
XLA Modules:
  0.0 54.4 jit_solution(5991686854953601694)
XLA Ops:
  0.0 3.5 %collective-permute-start.2 = (f32[12,128]{1,0:T(8,128)}, f32[12,128]{1,0:T(8,128)S(1)}, u32[]{:S(2)}, u32[]{:S(2)}) collective-permute-start(f32[12,128]{1,0:T(8,128)} %bitcast.3), channel_id=1, source_target_pairs={{0,9},{1,8},{2,11},{3,10},{4,13},{5,12},{6,15},{7,14},{8,1},{9,0},... | collective-permute-start | bytes 18440 | tf_op jit(solution)/shard_map/ppermute | solution.py:29
  3.5 1.6 %collective-permute-start.1 = (f32[12,128]{1,0:T(8,128)}, f32[12,128]{1,0:T(8,128)S(1)}, u32[]{:S(2)}, u32[]{:S(2)}) collective-permute-start(f32[12,128]{1,0:T(8,128)} %bitcast.4), channel_id=1, source_target_pairs={{0,13},{1,12},{2,15},{3,14},{4,9},{5,8},{6,11},{7,10},{8,5},{9,4},... | collective-permute-start | bytes 18440 | tf_op jit(solution)/shard_map/ppermute | solution.py:29
  5.3 1.6 %shard_map.46 = (bf16[4,8,256,128]{3,2,1,0:T(8,128)(2,1)S(1)}, f32[8,128]{1,0:T(8,128)S(1)}) custom-call(bf16[8,8,256,128]{3,2,1,0:T(8,128)(2,1)} %lik_ref.1, s32[8,8]{1,0:T(8,128)} %refs_1_.1, s32[8,8]{1,0:T(8,128)} %refs_2_.1), custom_call_target="tpu_custom_call" | custom-call | tf_op jit(solution)/shard_map/pallas_call | solution.py:305
  7.0 1.6 %collective-permute-done.1.refs_2_ = f32[12,128]{1,0:T(8,128)S(1)} collective-permute-done((f32[12,128]{1,0:T(8,128)}, f32[12,128]{1,0:T(8,128)S(1)}, u32[]{:S(2)}, u32[]{:S(2)}) %collective-permute-start.1) | collective-permute-done | bytes 6176 | tf_op jit(solution)/shard_map/ppermute | solution.py:29
  8.6 1.6 %collective-permute-start.5 = (f32[64,128]{1,0:T(8,128)S(1)}, f32[64,128]{1,0:T(8,128)S(1)}, u32[]{:S(2)}, u32[]{:S(2)}) collective-permute-start(f32[64,128]{1,0:T(8,128)S(1)} %shard_map.47.after_ref.refs_1_), channel_id=1, source_target_pairs={{0,2},{1,3},{2,0},{3,1},{4,6},{5,7},{6,4},{7,5},{8,10},{9,11},{10,... | collective-permute-start | bytes 98312 | tf_op jit(solution)/shard_map/ppermute | solution.py:29
  10.2 0.5 collective-permute-start.4
  10.8 1.8 %shard_map.48 = (bf16[4,8,256,128]{3,2,1,0:T(8,128)(2,1)S(1)}, bf16[8,4,256,256]{3,2,1,0:T(8,128)(2,1)S(1)}) custom-call(f32[64,128]{1,0:T(8,128)S(1)} %shard_map.47.after_ref.refs_1_, bf16[4,8,256,128]{3,2,1,0:T(8,128)(2,1)S(1)} %get-tuple-element.18.early_ref.refs_3_, bf16[8,8,256,128]{3,2,1,0:T(8,128)(2,1)} %lik_ref.1), custom_call_target="tpu_custom_call" | custom-call | tf_op jit(solution)/shard_map/pallas_call | solution.py:327
  12.6 0.9 %collective-permute-done.4.refs_3_ = f32[64,128]{1,0:T(8,128)S(1)} collective-permute-done((f32[64,128]{1,0:T(8,128)S(1)}, f32[64,128]{1,0:T(8,128)S(1)}, u32[]{:S(2)}, u32[]{:S(2)}) %collective-permute-start.4) | collective-permute-done | bytes 32800 | tf_op jit(solution)/shard_map/ppermute | solution.py:29
  13.5 0.9 %shard_map.49 = (f32[8,8,256]{2,1,0:T(8,128)S(1)}, f32[64,128]{1,0:T(8,128)S(1)}) custom-call(f32[8,128]{1,0:T(8,128)S(1)} %get-tuple-element.17.refs_4_.refs_0_.info_ref, f32[64,128]{1,0:T(8,128)S(1)} %shard_map.47.after_ref.refs_1_, f32[64,128]{1,0:T(8,128)S(1)} %collective-permute-done.3.refs_2_, f32[64,128]{1,0:T(8,128)S(1)} %collective-permute-done.4.refs_3_, ...), custom_call_target="tpu_custom_call" | custom-call | tf_op jit(solution)/shard_map/pallas_call | solution.py:286
  14.4 9.0 %all_to_all.15.parts_ref = f32[8,8,256]{2,1,0:T(8,128)S(1)} all-to-all(f32[8,8,256]{2,1,0:T(8,128)S(1)} %get-tuple-element.20), channel_id=1, replica_groups={{8,10,12,14,0,2,4,6},{9,11,13,15,1,3,5,7},{24,26,28,30,16,18,20,22},{25..., dimensions={0} | all-to-all | bytes 131072 | tf_op jit(solution)/shard_map/all_to_all | solution.py:371
  23.4 0.7 %shard_map.50.refs_0_ = f32[72,128]{1,0:T(8,128)S(1)} custom-call(f32[8,128]{1,0:T(8,128)S(1)} %get-tuple-element.17.refs_4_.refs_0_.info_ref, f32[8,8,256]{2,1,0:T(8,128)S(1)} %all_to_all.15.parts_ref, f32[64,128]{1,0:T(8,128)S(1)} %get-tuple-element.21.picked_ref, bf16[4,8,256,128]{3,2,1,0:T(8,128)(2,1)S(1)} %get-tuple-element.18.early_ref.refs_3_, ...), custom_call_target="tpu_custom_call" | custom-call | tf_op jit(solution)/shard_map/pallas_call | solution.py:286
  24.1 0.7 %collective-permute-start.8 = (f32[72,128]{1,0:T(8,128)S(1)}, f32[72,128]{1,0:T(8,128)S(1)}, u32[]{:S(2)}, u32[]{:S(2)}) collective-permute-start(f32[72,128]{1,0:T(8,128)S(1)} %shard_map.50.refs_0_), channel_id=1, source_target_pairs={{0,13},{1,12},{2,15},{3,14},{4,9},{5,8},{6,11},{7,10},{8,5},{9,4},... | collective-permute-start | bytes 110600 | tf_op jit(solution)/shard_map/ppermute | solution.py:29
  25.3 2.6 %collective-permute-start.6 = (f32[72,128]{1,0:T(8,128)S(1)}, f32[72,128]{1,0:T(8,128)S(1)}, u32[]{:S(2)}, u32[]{:S(2)}) collective-permute-start(f32[72,128]{1,0:T(8,128)S(1)} %shard_map.50.refs_0_), channel_id=1, source_target_pairs={{0,5},{1,4},{2,7},{3,6},{4,1},{5,0},{6,3},{7,2},{8,13},{9,12},{10,... | collective-permute-start | bytes 110600 | tf_op jit(solution)/shard_map/ppermute | solution.py:29
  28.0 1.6 %collective-permute-done.8.refs_3_ = f32[72,128]{1,0:T(8,128)S(1)} collective-permute-done((f32[72,128]{1,0:T(8,128)S(1)}, f32[72,128]{1,0:T(8,128)S(1)}, u32[]{:S(2)}, u32[]{:S(2)}) %collective-permute-start.8) | collective-permute-done | bytes 36896 | tf_op jit(solution)/shard_map/ppermute | solution.py:29
  29.6 1.0 %collective-permute-done.7.refs_2_ = f32[72,128]{1,0:T(8,128)S(1)} collective-permute-done((f32[72,128]{1,0:T(8,128)S(1)}, f32[72,128]{1,0:T(8,128)S(1)}, u32[]{:S(2)}, u32[]{:S(2)}) %collective-permute-start.7) | collective-permute-done | bytes 36896 | tf_op jit(solution)/shard_map/ppermute | solution.py:29
  31.2 0.6 %collective-permute-start.9 = (f32[64,128]{1,0:T(8,128)S(1)}, f32[64,128]{1,0:T(8,128)S(1)}, u32[]{:S(2)}, u32[]{:S(2)}) collective-permute-start(f32[64,128]{1,0:T(8,128)S(1)} %get-tuple-element.24), channel_id=1, source_target_pairs={{0,2},{1,3},{2,0},{3,1},{4,6},{5,7},{6,4},{7,5},{8,10},{9,11},{10,... | collective-permute-start | bytes 98312 | tf_op jit(solution)/shard_map/ppermute | solution.py:29
  31.8 0.9 %collective-permute-start.10 = (f32[64,128]{1,0:T(8,128)S(1)}, f32[64,128]{1,0:T(8,128)S(1)}, u32[]{:S(2)}, u32[]{:S(2)}) collective-permute-start(f32[64,128]{1,0:T(8,128)S(1)} %get-tuple-element.25), channel_id=1, source_target_pairs={{0,3},{1,2},{2,1},{3,0},{4,7},{5,6},{6,5},{7,4},{8,11},{9,10},{10,... | collective-permute-start | bytes 98312 | tf_op jit(solution)/shard_map/ppermute | solution.py:29
  32.7 0.7 %collective-permute-start.11 = (f32[64,128]{1,0:T(8,128)S(1)}, f32[64,128]{1,0:T(8,128)S(1)}, u32[]{:S(2)}, u32[]{:S(2)}) collective-permute-start(f32[64,128]{1,0:T(8,128)S(1)} %get-tuple-element.26), channel_id=1, source_target_pairs={{0,1},{1,0},{2,3},{3,2},{4,5},{5,4},{6,7},{7,6},{8,9},{9,8},{10,11... | collective-permute-start | bytes 98312 | tf_op jit(solution)/shard_map/ppermute | solution.py:29
  33.4 2.1 %collective-permute-done.9.refs_1_ = f32[64,128]{1,0:T(8,128)S(1)} collective-permute-done((f32[64,128]{1,0:T(8,128)S(1)}, f32[64,128]{1,0:T(8,128)S(1)}, u32[]{:S(2)}, u32[]{:S(2)}) %collective-permute-start.9) | collective-permute-done | bytes 32800 | tf_op jit(solution)/shard_map/ppermute | solution.py:29
  35.5 0.7 %shard_map.52 = (f32[8,8,256]{2,1,0:T(8,128)S(1)}, f32[64,128]{1,0:T(8,128)S(1)}) custom-call(f32[64,128]{1,0:T(8,128)S(1)} %get-tuple-element.23.refs_0_, f32[64,128]{1,0:T(8,128)S(1)} %collective-permute-done.9.refs_1_, f32[64,128]{1,0:T(8,128)S(1)} %collective-permute-done.10.refs_2_, f32[64,128]{1,0:T(8,128)S(1)} %collective-permute-done.11.refs_3_, ...), custom_call_target="tpu_custom_call" | custom-call | tf_op jit(solution)/shard_map/pallas_call | solution.py:286
  36.2 8.4 %all_to_all.16.refs_1_ = f32[8,8,256]{2,1,0:T(8,128)S(1)} all-to-all(f32[8,8,256]{2,1,0:T(8,128)S(1)} %get-tuple-element.27), channel_id=1, replica_groups={{10,8,14,12,2,0,6,4},{11,9,15,13,3,1,7,5},{26,24,30,28,18,16,22,20},{27..., dimensions={0} | all-to-all | bytes 131072 | tf_op jit(solution)/shard_map/all_to_all | solution.py:371
  44.5 0.9 %shard_map.53 = f32[16,12,128]{2,1,0:T(8,128)S(1)} custom-call(f32[8,128]{1,0:T(8,128)S(1)} %get-tuple-element.17.refs_4_.refs_0_.info_ref, f32[8,8,256]{2,1,0:T(8,128)S(1)} %all_to_all.16.refs_1_, f32[64,128]{1,0:T(8,128)S(1)} %get-tuple-element.28.refs_2_, bf16[4,8,256,128]{3,2,1,0:T(8,128)(2,1)S(1)} %get-tuple-element.18.early_ref.refs_3_, ...), custom_call_target="tpu_custom_call" | custom-call | tf_op jit(solution)/shard_map/pallas_call | solution.py:286
  45.5 8.3 %all_to_all.17 = f32[16,12,128]{2,1,0:T(8,128)S(1)} all-to-all(f32[16,12,128]{2,1,0:T(8,128)S(1)} %shard_map.53), channel_id=1, replica_groups={{11,10,9,8,15,14,13,12,3,2,1,0,7,6,5,4},{27,26,25,24,31,30,29,28,19,18,..., dimensions={0} | all-to-all | bytes 196608 | tf_op jit(solution)/shard_map/all_to_all | solution.py:410
  53.8 0.6 %multiply_bitcast_fusion = f32[1536]{0:T(1024)} fusion(f32[12,128]{1,0:T(8,128)S(1)} %reduce_sum.9), kind=kLoop, calls=%fused_computation | loop fusion | flops 1536 | bytes 12288 | tf_op jit(solution)/shard_map/mul | solution.py:411
  (18 shorter events, 1.5 us)
Async XLA Ops:
  0.0 8.6 %copy-start = (f32[1536]{0:T(1024)S(1)}, f32[1536]{0:T(1024)}, u32[]{:S(2)}) copy-start(f32[1536]{0:T(1024)} %param.7) | copy-start | bytes 18436
  0.0 6.9 %collective-permute-start.2 = (f32[12,128]{1,0:T(8,128)}, f32[12,128]{1,0:T(8,128)S(1)}, u32[]{:S(2)}, u32[]{:S(2)}) collective-permute-start(f32[12,128]{1,0:T(8,128)} %bitcast.3), channel_id=1, source_target_pairs={{0,9},{1,8},{2,11},{3,10},{4,13},{5,12},{6,15},{7,14},{8,1},{9,0},... | collective-permute-start | bytes 18440 | tf_op jit(solution)/shard_map/ppermute | solution.py:29
  3.5 5.1 %collective-permute-start.1 = (f32[12,128]{1,0:T(8,128)}, f32[12,128]{1,0:T(8,128)S(1)}, u32[]{:S(2)}, u32[]{:S(2)}) collective-permute-start(f32[12,128]{1,0:T(8,128)} %bitcast.4), channel_id=1, source_target_pairs={{0,13},{1,12},{2,15},{3,14},{4,9},{5,8},{6,11},{7,10},{8,5},{9,4},... | collective-permute-start | bytes 18440 | tf_op jit(solution)/shard_map/ppermute | solution.py:29
  5.1 3.5 %collective-permute-start = (f32[12,128]{1,0:T(8,128)}, f32[12,128]{1,0:T(8,128)S(1)}, u32[]{:S(2)}, u32[]{:S(2)}) collective-permute-start(f32[12,128]{1,0:T(8,128)} %bitcast.5), channel_id=1, source_target_pairs={{0,5},{1,4},{2,7},{3,6},{4,1},{5,0},{6,3},{7,2},{8,13},{9,12},{10,... | collective-permute-start | bytes 18440 | tf_op jit(solution)/shard_map/ppermute | solution.py:29
  8.6 4.1 %collective-permute-start.5 = (f32[64,128]{1,0:T(8,128)S(1)}, f32[64,128]{1,0:T(8,128)S(1)}, u32[]{:S(2)}, u32[]{:S(2)}) collective-permute-start(f32[64,128]{1,0:T(8,128)S(1)} %shard_map.47.after_ref.refs_1_), channel_id=1, source_target_pairs={{0,2},{1,3},{2,0},{3,1},{4,6},{5,7},{6,4},{7,5},{8,10},{9,11},{10,... | collective-permute-start | bytes 98312 | tf_op jit(solution)/shard_map/ppermute | solution.py:29
  10.2 3.3 %collective-permute-start.4 = (f32[64,128]{1,0:T(8,128)S(1)}, f32[64,128]{1,0:T(8,128)S(1)}, u32[]{:S(2)}, u32[]{:S(2)}) collective-permute-start(f32[64,128]{1,0:T(8,128)S(1)} %shard_map.47.after_ref.refs_1_), channel_id=1, source_target_pairs={{0,3},{1,2},{2,1},{3,0},{4,7},{5,6},{6,5},{7,4},{8,11},{9,10},{10,... | collective-permute-start | bytes 98312 | tf_op jit(solution)/shard_map/ppermute | solution.py:29
  10.7 2.8 %collective-permute-start.3 = (f32[64,128]{1,0:T(8,128)S(1)}, f32[64,128]{1,0:T(8,128)S(1)}, u32[]{:S(2)}, u32[]{:S(2)}) collective-permute-start(f32[64,128]{1,0:T(8,128)S(1)} %shard_map.47.after_ref.refs_1_), channel_id=1, source_target_pairs={{0,1},{1,0},{2,3},{3,2},{4,5},{5,4},{6,7},{7,6},{8,9},{9,8},{10,11... | collective-permute-start | bytes 98312 | tf_op jit(solution)/shard_map/ppermute | solution.py:29
  24.1 5.5 %collective-permute-start.8 = (f32[72,128]{1,0:T(8,128)S(1)}, f32[72,128]{1,0:T(8,128)S(1)}, u32[]{:S(2)}, u32[]{:S(2)}) collective-permute-start(f32[72,128]{1,0:T(8,128)S(1)} %shard_map.50.refs_0_), channel_id=1, source_target_pairs={{0,13},{1,12},{2,15},{3,14},{4,9},{5,8},{6,11},{7,10},{8,5},{9,4},... | collective-permute-start | bytes 110600 | tf_op jit(solution)/shard_map/ppermute | solution.py:29
  24.8 5.7 %collective-permute-start.7 = (f32[72,128]{1,0:T(8,128)S(1)}, f32[72,128]{1,0:T(8,128)S(1)}, u32[]{:S(2)}, u32[]{:S(2)}) collective-permute-start(f32[72,128]{1,0:T(8,128)S(1)} %shard_map.50.refs_0_), channel_id=1, source_target_pairs={{0,8},{1,9},{2,10},{3,11},{4,12},{5,13},{6,14},{7,15},{8,0},{9,1},... | collective-permute-start | bytes 110600 | tf_op jit(solution)/shard_map/ppermute | solution.py:29
  25.3 5.5 %collective-permute-start.6 = (f32[72,128]{1,0:T(8,128)S(1)}, f32[72,128]{1,0:T(8,128)S(1)}, u32[]{:S(2)}, u32[]{:S(2)}) collective-permute-start(f32[72,128]{1,0:T(8,128)S(1)} %shard_map.50.refs_0_), channel_id=1, source_target_pairs={{0,5},{1,4},{2,7},{3,6},{4,1},{5,0},{6,3},{7,2},{8,13},{9,12},{10,... | collective-permute-start | bytes 110600 | tf_op jit(solution)/shard_map/ppermute | solution.py:29
  31.2 4.3 %collective-permute-start.9 = (f32[64,128]{1,0:T(8,128)S(1)}, f32[64,128]{1,0:T(8,128)S(1)}, u32[]{:S(2)}, u32[]{:S(2)}) collective-permute-start(f32[64,128]{1,0:T(8,128)S(1)} %get-tuple-element.24), channel_id=1, source_target_pairs={{0,2},{1,3},{2,0},{3,1},{4,6},{5,7},{6,4},{7,5},{8,10},{9,11},{10,... | collective-permute-start | bytes 98312 | tf_op jit(solution)/shard_map/ppermute | solution.py:29
  31.8 3.7 %collective-permute-start.10 = (f32[64,128]{1,0:T(8,128)S(1)}, f32[64,128]{1,0:T(8,128)S(1)}, u32[]{:S(2)}, u32[]{:S(2)}) collective-permute-start(f32[64,128]{1,0:T(8,128)S(1)} %get-tuple-element.25), channel_id=1, source_target_pairs={{0,3},{1,2},{2,1},{3,0},{4,7},{5,6},{6,5},{7,4},{8,11},{9,10},{10,... | collective-permute-start | bytes 98312 | tf_op jit(solution)/shard_map/ppermute | solution.py:29
  32.7 2.8 %collective-permute-start.11 = (f32[64,128]{1,0:T(8,128)S(1)}, f32[64,128]{1,0:T(8,128)S(1)}, u32[]{:S(2)}, u32[]{:S(2)}) collective-permute-start(f32[64,128]{1,0:T(8,128)S(1)} %get-tuple-element.26), channel_id=1, source_target_pairs={{0,1},{1,0},{2,3},{3,2},{4,5},{5,4},{6,7},{7,6},{8,9},{9,8},{10,11... | collective-permute-start | bytes 98312 | tf_op jit(solution)/shard_map/ppermute | solution.py:29

commit v27 on v23

--- a/solution.py
+++ b/solution.py
@@ -162,7 +162,7 @@
 
 
 def near_rows(far, own_blocks):
-    return -(-(far * own_blocks + ID_ROWS) // 16) * 16
+    return -(-(far * own_blocks + ID_ROWS) // 8) * 8
 
 
 def flip_kernel(after_ref, early_ref, lik_ref, late_ref, out_ref, sems):

time: 54.9 us -> 54.8 us (level)
  no operation moved by 1% of the time
where the time goes in v27:
time: 54.8 us; the launch traced here: 54.3 us
  blocking collectives  25.6 us (47%)
  starting transfers between devices  13.6 us (25%)
  waiting for transfers between devices  7.36 us (13%)
  Pallas kernels  6.98 us (13%)
  other arithmetic  0.62 us (1%)
    all_to_all x2, blocking collectives, local(): lax.all_to_all(row_parts, 'genome', 0, 0, tiled=True, axis_index_groups=[...  17.3 us
    ppermute x12, starting transfers between devices, swap(): return lax.ppermute(x, axes, [(i, i ^ k) for i in range(n)])  13.6 us
    all_to_all x1, blocking collectives, local(): lax.all_to_all(counts, ALL, 0, 0, tiled=True, axis_index_groups=[order])  8.33 us
    ppermute x12, waiting for transfers between devices, swap(): return lax.ppermute(x, axes, [(i, i ^ k) for i in range(n)])  7.36 us
    pallas_call x6, Pallas kernels, call(): pl.pallas_call(kernel, out_shape=[jax.ShapeDtypeStruct(shape, jnp.float32...  3.51 us
    pallas_call x1, Pallas kernels, flip(): pl.pallas_call(flip_kernel, out_shape=[pltpu.VMEM((late,) + likelihood.sh...  2.04 us
    pallas_call x1, Pallas kernels, prepare(): pl.pallas_call(lambda *refs: prepare_kernel(own_blocks, *refs), out_shape...  1.43 us
  transfers between devices with their start and end apart: 12, of which 6 were waited for; matrix products, arithmetic and copies ran while one was open for 0% of the time, Pallas kernels for 6%

profile of v27, /device:TPU:0, one launch (start us, length us, event | category | flops | bytes accessed | tf_op | source)
XLA Modules:
  0.0 54.3 jit_solution(10252091487054831943)
XLA Ops:
  0.0 3.5 %collective-permute-start.2 = (f32[12,128]{1,0:T(8,128)}, f32[12,128]{1,0:T(8,128)S(1)}, u32[]{:S(2)}, u32[]{:S(2)}) collective-permute-start(f32[12,128]{1,0:T(8,128)} %bitcast.3), channel_id=1, source_target_pairs={{0,9},{1,8},{2,11},{3,10},{4,13},{5,12},{6,15},{7,14},{8,1},{9,0},... | collective-permute-start | bytes 18440 | tf_op jit(solution)/shard_map/ppermute | solution.py:29
  3.5 1.6 %collective-permute-start.1 = (f32[12,128]{1,0:T(8,128)}, f32[12,128]{1,0:T(8,128)S(1)}, u32[]{:S(2)}, u32[]{:S(2)}) collective-permute-start(f32[12,128]{1,0:T(8,128)} %bitcast.4), channel_id=1, source_target_pairs={{0,13},{1,12},{2,15},{3,14},{4,9},{5,8},{6,11},{7,10},{8,5},{9,4},... | collective-permute-start | bytes 18440 | tf_op jit(solution)/shard_map/ppermute | solution.py:29
  5.3 1.4 %shard_map.46 = (bf16[3,8,256,128]{3,2,1,0:T(8,128)(2,1)S(1)}, f32[8,128]{1,0:T(8,128)S(1)}) custom-call(bf16[8,8,256,128]{3,2,1,0:T(8,128)(2,1)} %lik_ref.1, s32[8,8]{1,0:T(8,128)} %refs_1_.1, s32[8,8]{1,0:T(8,128)} %refs_2_.1), custom_call_target="tpu_custom_call" | custom-call | tf_op jit(solution)/shard_map/pallas_call | solution.py:305
  6.8 1.8 %collective-permute-done.1.refs_2_ = f32[12,128]{1,0:T(8,128)S(1)} collective-permute-done((f32[12,128]{1,0:T(8,128)}, f32[12,128]{1,0:T(8,128)S(1)}, u32[]{:S(2)}, u32[]{:S(2)}) %collective-permute-start.1) | collective-permute-done | bytes 6176 | tf_op jit(solution)/shard_map/ppermute | solution.py:29
  8.6 1.6 %collective-permute-start.5 = (f32[56,128]{1,0:T(8,128)S(1)}, f32[56,128]{1,0:T(8,128)S(1)}, u32[]{:S(2)}, u32[]{:S(2)}) collective-permute-start(f32[56,128]{1,0:T(8,128)S(1)} %shard_map.47.after_ref.refs_1_), channel_id=1, source_target_pairs={{0,2},{1,3},{2,0},{3,1},{4,6},{5,7},{6,4},{7,5},{8,10},{9,11},{10,... | collective-permute-start | bytes 86024 | tf_op jit(solution)/shard_map/ppermute | solution.py:29
  10.2 0.5 collective-permute-start.4
  10.8 2.0 %shard_map.48 = (bf16[5,8,256,128]{3,2,1,0:T(8,128)(2,1)S(1)}, bf16[8,4,256,256]{3,2,1,0:T(8,128)(2,1)S(1)}) custom-call(f32[56,128]{1,0:T(8,128)S(1)} %shard_map.47.after_ref.refs_1_, bf16[3,8,256,128]{3,2,1,0:T(8,128)(2,1)S(1)} %get-tuple-element.18.early_ref.refs_3_, bf16[8,8,256,128]{3,2,1,0:T(8,128)(2,1)} %lik_ref.1), custom_call_target="tpu_custom_call" | custom-call | tf_op jit(solution)/shard_map/pallas_call | solution.py:327
  12.8 0.6 %collective-permute-done.4.refs_3_ = f32[56,128]{1,0:T(8,128)S(1)} collective-permute-done((f32[56,128]{1,0:T(8,128)S(1)}, f32[56,128]{1,0:T(8,128)S(1)}, u32[]{:S(2)}, u32[]{:S(2)}) %collective-permute-start.4) | collective-permute-done | bytes 28704 | tf_op jit(solution)/shard_map/ppermute | solution.py:29
  13.5 0.9 %shard_map.49 = (f32[8,8,256]{2,1,0:T(8,128)S(1)}, f32[64,128]{1,0:T(8,128)S(1)}) custom-call(f32[8,128]{1,0:T(8,128)S(1)} %get-tuple-element.17.refs_4_.refs_0_.info_ref, f32[56,128]{1,0:T(8,128)S(1)} %shard_map.47.after_ref.refs_1_, f32[56,128]{1,0:T(8,128)S(1)} %collective-permute-done.3.refs_2_, f32[56,128]{1,0:T(8,128)S(1)} %collective-permute-done.4.refs_3_, ...), custom_call_target="tpu_custom_call" | custom-call | tf_op jit(solution)/shard_map/pallas_call | solution.py:286
  14.4 8.9 %all_to_all.15.parts_ref = f32[8,8,256]{2,1,0:T(8,128)S(1)} all-to-all(f32[8,8,256]{2,1,0:T(8,128)S(1)} %get-tuple-element.20), channel_id=1, replica_groups={{8,10,12,14,0,2,4,6},{9,11,13,15,1,3,5,7},{24,26,28,30,16,18,20,22},{25..., dimensions={0} | all-to-all | bytes 131072 | tf_op jit(solution)/shard_map/all_to_all | solution.py:371
  23.3 0.7 %shard_map.50.refs_0_ = f32[72,128]{1,0:T(8,128)S(1)} custom-call(f32[8,128]{1,0:T(8,128)S(1)} %get-tuple-element.17.refs_4_.refs_0_.info_ref, f32[8,8,256]{2,1,0:T(8,128)S(1)} %all_to_all.15.parts_ref, f32[64,128]{1,0:T(8,128)S(1)} %get-tuple-element.21.picked_ref, bf16[3,8,256,128]{3,2,1,0:T(8,128)(2,1)S(1)} %get-tuple-element.18.early_ref.refs_3_, ...), custom_call_target="tpu_custom_call" | custom-call | tf_op jit(solution)/shard_map/pallas_call | solution.py:286
  24.0 1.0 %collective-permute-start.8 = (f32[72,128]{1,0:T(8,128)S(1)}, f32[72,128]{1,0:T(8,128)S(1)}, u32[]{:S(2)}, u32[]{:S(2)}) collective-permute-start(f32[72,128]{1,0:T(8,128)S(1)} %shard_map.50.refs_0_), channel_id=1, source_target_pairs={{0,13},{1,12},{2,15},{3,14},{4,9},{5,8},{6,11},{7,10},{8,5},{9,4},... | collective-permute-start | bytes 110600 | tf_op jit(solution)/shard_map/ppermute | solution.py:29
  25.2 2.6 %collective-permute-start.6 = (f32[72,128]{1,0:T(8,128)S(1)}, f32[72,128]{1,0:T(8,128)S(1)}, u32[]{:S(2)}, u32[]{:S(2)}) collective-permute-start(f32[72,128]{1,0:T(8,128)S(1)} %shard_map.50.refs_0_), channel_id=1, source_target_pairs={{0,5},{1,4},{2,7},{3,6},{4,1},{5,0},{6,3},{7,2},{8,13},{9,12},{10,... | collective-permute-start | bytes 110600 | tf_op jit(solution)/shard_map/ppermute | solution.py:29
  27.9 1.6 %collective-permute-done.8.refs_3_ = f32[72,128]{1,0:T(8,128)S(1)} collective-permute-done((f32[72,128]{1,0:T(8,128)S(1)}, f32[72,128]{1,0:T(8,128)S(1)}, u32[]{:S(2)}, u32[]{:S(2)}) %collective-permute-start.8) | collective-permute-done | bytes 36896 | tf_op jit(solution)/shard_map/ppermute | solution.py:29
  29.5 1.0 %collective-permute-done.7.refs_2_ = f32[72,128]{1,0:T(8,128)S(1)} collective-permute-done((f32[72,128]{1,0:T(8,128)S(1)}, f32[72,128]{1,0:T(8,128)S(1)}, u32[]{:S(2)}, u32[]{:S(2)}) %collective-permute-start.7) | collective-permute-done | bytes 36896 | tf_op jit(solution)/shard_map/ppermute | solution.py:29
  31.1 0.6 %collective-permute-start.9 = (f32[64,128]{1,0:T(8,128)S(1)}, f32[64,128]{1,0:T(8,128)S(1)}, u32[]{:S(2)}, u32[]{:S(2)}) collective-permute-start(f32[64,128]{1,0:T(8,128)S(1)} %get-tuple-element.24), channel_id=1, source_target_pairs={{0,2},{1,3},{2,0},{3,1},{4,6},{5,7},{6,4},{7,5},{8,10},{9,11},{10,... | collective-permute-start | bytes 98312 | tf_op jit(solution)/shard_map/ppermute | solution.py:29
  31.7 0.9 %collective-permute-start.10 = (f32[64,128]{1,0:T(8,128)S(1)}, f32[64,128]{1,0:T(8,128)S(1)}, u32[]{:S(2)}, u32[]{:S(2)}) collective-permute-start(f32[64,128]{1,0:T(8,128)S(1)} %get-tuple-element.25), channel_id=1, source_target_pairs={{0,3},{1,2},{2,1},{3,0},{4,7},{5,6},{6,5},{7,4},{8,11},{9,10},{10,... | collective-permute-start | bytes 98312 | tf_op jit(solution)/shard_map/ppermute | solution.py:29
  32.6 0.7 %collective-permute-start.11 = (f32[64,128]{1,0:T(8,128)S(1)}, f32[64,128]{1,0:T(8,128)S(1)}, u32[]{:S(2)}, u32[]{:S(2)}) collective-permute-start(f32[64,128]{1,0:T(8,128)S(1)} %get-tuple-element.26), channel_id=1, source_target_pairs={{0,1},{1,0},{2,3},{3,2},{4,5},{5,4},{6,7},{7,6},{8,9},{9,8},{10,11... | collective-permute-start | bytes 98312 | tf_op jit(solution)/shard_map/ppermute | solution.py:29
  33.3 2.1 %collective-permute-done.9.refs_1_ = f32[64,128]{1,0:T(8,128)S(1)} collective-permute-done((f32[64,128]{1,0:T(8,128)S(1)}, f32[64,128]{1,0:T(8,128)S(1)}, u32[]{:S(2)}, u32[]{:S(2)}) %collective-permute-start.9) | collective-permute-done | bytes 32800 | tf_op jit(solution)/shard_map/ppermute | solution.py:29
  35.4 0.7 %shard_map.52 = (f32[8,8,256]{2,1,0:T(8,128)S(1)}, f32[64,128]{1,0:T(8,128)S(1)}) custom-call(f32[64,128]{1,0:T(8,128)S(1)} %get-tuple-element.23.refs_0_, f32[64,128]{1,0:T(8,128)S(1)} %collective-permute-done.9.refs_1_, f32[64,128]{1,0:T(8,128)S(1)} %collective-permute-done.10.refs_2_, f32[64,128]{1,0:T(8,128)S(1)} %collective-permute-done.11.refs_3_, ...), custom_call_target="tpu_custom_call" | custom-call | tf_op jit(solution)/shard_map/pallas_call | solution.py:286
  36.1 8.4 %all_to_all.16.refs_1_ = f32[8,8,256]{2,1,0:T(8,128)S(1)} all-to-all(f32[8,8,256]{2,1,0:T(8,128)S(1)} %get-tuple-element.27), channel_id=1, replica_groups={{10,8,14,12,2,0,6,4},{11,9,15,13,3,1,7,5},{26,24,30,28,18,16,22,20},{27..., dimensions={0} | all-to-all | bytes 131072 | tf_op jit(solution)/shard_map/all_to_all | solution.py:371
  44.4 0.9 %shard_map.53 = f32[16,12,128]{2,1,0:T(8,128)S(1)} custom-call(f32[8,128]{1,0:T(8,128)S(1)} %get-tuple-element.17.refs_4_.refs_0_.info_ref, f32[8,8,256]{2,1,0:T(8,128)S(1)} %all_to_all.16.refs_1_, f32[64,128]{1,0:T(8,128)S(1)} %get-tuple-element.28.refs_2_, bf16[3,8,256,128]{3,2,1,0:T(8,128)(2,1)S(1)} %get-tuple-element.18.early_ref.refs_3_, ...), custom_call_target="tpu_custom_call" | custom-call | tf_op jit(solution)/shard_map/pallas_call | solution.py:286
  45.3 8.3 %all_to_all.17 = f32[16,12,128]{2,1,0:T(8,128)S(1)} all-to-all(f32[16,12,128]{2,1,0:T(8,128)S(1)} %shard_map.53), channel_id=1, replica_groups={{11,10,9,8,15,14,13,12,3,2,1,0,7,6,5,4},{27,26,25,24,31,30,29,28,19,18,..., dimensions={0} | all-to-all | bytes 196608 | tf_op jit(solution)/shard_map/all_to_all | solution.py:410
  53.7 0.6 %multiply_bitcast_fusion = f32[1536]{0:T(1024)} fusion(f32[12,128]{1,0:T(8,128)S(1)} %reduce_sum.9), kind=kLoop, calls=%fused_computation | loop fusion | flops 1536 | bytes 12288 | tf_op jit(solution)/shard_map/mul | solution.py:411
  (18 shorter events, 1.2 us)
Async XLA Ops:
  0.0 8.6 %copy-start = (f32[1536]{0:T(1024)S(1)}, f32[1536]{0:T(1024)}, u32[]{:S(2)}) copy-start(f32[1536]{0:T(1024)} %param.7) | copy-start | bytes 18436
  0.0 6.8 %collective-permute-start.2 = (f32[12,128]{1,0:T(8,128)}, f32[12,128]{1,0:T(8,128)S(1)}, u32[]{:S(2)}, u32[]{:S(2)}) collective-permute-start(f32[12,128]{1,0:T(8,128)} %bitcast.3), channel_id=1, source_target_pairs={{0,9},{1,8},{2,11},{3,10},{4,13},{5,12},{6,15},{7,14},{8,1},{9,0},... | collective-permute-start | bytes 18440 | tf_op jit(solution)/shard_map/ppermute | solution.py:29
  3.5 5.1 %collective-permute-start.1 = (f32[12,128]{1,0:T(8,128)}, f32[12,128]{1,0:T(8,128)S(1)}, u32[]{:S(2)}, u32[]{:S(2)}) collective-permute-start(f32[12,128]{1,0:T(8,128)} %bitcast.4), channel_id=1, source_target_pairs={{0,13},{1,12},{2,15},{3,14},{4,9},{5,8},{6,11},{7,10},{8,5},{9,4},... | collective-permute-start | bytes 18440 | tf_op jit(solution)/shard_map/ppermute | solution.py:29
  5.1 3.5 %collective-permute-start = (f32[12,128]{1,0:T(8,128)}, f32[12,128]{1,0:T(8,128)S(1)}, u32[]{:S(2)}, u32[]{:S(2)}) collective-permute-start(f32[12,128]{1,0:T(8,128)} %bitcast.5), channel_id=1, source_target_pairs={{0,5},{1,4},{2,7},{3,6},{4,1},{5,0},{6,3},{7,2},{8,13},{9,12},{10,... | collective-permute-start | bytes 18440 | tf_op jit(solution)/shard_map/ppermute | solution.py:29
  8.6 4.3 %collective-permute-start.5 = (f32[56,128]{1,0:T(8,128)S(1)}, f32[56,128]{1,0:T(8,128)S(1)}, u32[]{:S(2)}, u32[]{:S(2)}) collective-permute-start(f32[56,128]{1,0:T(8,128)S(1)} %shard_map.47.after_ref.refs_1_), channel_id=1, source_target_pairs={{0,2},{1,3},{2,0},{3,1},{4,6},{5,7},{6,4},{7,5},{8,10},{9,11},{10,... | collective-permute-start | bytes 86024 | tf_op jit(solution)/shard_map/ppermute | solution.py:29
  10.2 3.3 %collective-permute-start.4 = (f32[56,128]{1,0:T(8,128)S(1)}, f32[56,128]{1,0:T(8,128)S(1)}, u32[]{:S(2)}, u32[]{:S(2)}) collective-permute-start(f32[56,128]{1,0:T(8,128)S(1)} %shard_map.47.after_ref.refs_1_), channel_id=1, source_target_pairs={{0,3},{1,2},{2,1},{3,0},{4,7},{5,6},{6,5},{7,4},{8,11},{9,10},{10,... | collective-permute-start | bytes 86024 | tf_op jit(solution)/shard_map/ppermute | solution.py:29
  10.7 2.8 %collective-permute-start.3 = (f32[56,128]{1,0:T(8,128)S(1)}, f32[56,128]{1,0:T(8,128)S(1)}, u32[]{:S(2)}, u32[]{:S(2)}) collective-permute-start(f32[56,128]{1,0:T(8,128)S(1)} %shard_map.47.after_ref.refs_1_), channel_id=1, source_target_pairs={{0,1},{1,0},{2,3},{3,2},{4,5},{5,4},{6,7},{7,6},{8,9},{9,8},{10,11... | collective-permute-start | bytes 86024 | tf_op jit(solution)/shard_map/ppermute | solution.py:29
  24.0 5.5 %collective-permute-start.8 = (f32[72,128]{1,0:T(8,128)S(1)}, f32[72,128]{1,0:T(8,128)S(1)}, u32[]{:S(2)}, u32[]{:S(2)}) collective-permute-start(f32[72,128]{1,0:T(8,128)S(1)} %shard_map.50.refs_0_), channel_id=1, source_target_pairs={{0,13},{1,12},{2,15},{3,14},{4,9},{5,8},{6,11},{7,10},{8,5},{9,4},... | collective-permute-start | bytes 110600 | tf_op jit(solution)/shard_map/ppermute | solution.py:29
  25.0 5.5 %collective-permute-start.7 = (f32[72,128]{1,0:T(8,128)S(1)}, f32[72,128]{1,0:T(8,128)S(1)}, u32[]{:S(2)}, u32[]{:S(2)}) collective-permute-start(f32[72,128]{1,0:T(8,128)S(1)} %shard_map.50.refs_0_), channel_id=1, source_target_pairs={{0,8},{1,9},{2,10},{3,11},{4,12},{5,13},{6,14},{7,15},{8,0},{9,1},... | collective-permute-start | bytes 110600 | tf_op jit(solution)/shard_map/ppermute | solution.py:29
  25.2 5.5 %collective-permute-start.6 = (f32[72,128]{1,0:T(8,128)S(1)}, f32[72,128]{1,0:T(8,128)S(1)}, u32[]{:S(2)}, u32[]{:S(2)}) collective-permute-start(f32[72,128]{1,0:T(8,128)S(1)} %shard_map.50.refs_0_), channel_id=1, source_target_pairs={{0,5},{1,4},{2,7},{3,6},{4,1},{5,0},{6,3},{7,2},{8,13},{9,12},{10,... | collective-permute-start | bytes 110600 | tf_op jit(solution)/shard_map/ppermute | solution.py:29
  31.1 4.3 %collective-permute-start.9 = (f32[64,128]{1,0:T(8,128)S(1)}, f32[64,128]{1,0:T(8,128)S(1)}, u32[]{:S(2)}, u32[]{:S(2)}) collective-permute-start(f32[64,128]{1,0:T(8,128)S(1)} %get-tuple-element.24), channel_id=1, source_target_pairs={{0,2},{1,3},{2,0},{3,1},{4,6},{5,7},{6,4},{7,5},{8,10},{9,11},{10,... | collective-permute-start | bytes 98312 | tf_op jit(solution)/shard_map/ppermute | solution.py:29
  31.7 3.7 %collective-permute-start.10 = (f32[64,128]{1,0:T(8,128)S(1)}, f32[64,128]{1,0:T(8,128)S(1)}, u32[]{:S(2)}, u32[]{:S(2)}) collective-permute-start(f32[64,128]{1,0:T(8,128)S(1)} %get-tuple-element.25), channel_id=1, source_target_pairs={{0,3},{1,2},{2,1},{3,0},{4,7},{5,6},{6,5},{7,4},{8,11},{9,10},{10,... | collective-permute-start | bytes 98312 | tf_op jit(solution)/shard_map/ppermute | solution.py:29
  32.6 2.8 %collective-permute-start.11 = (f32[64,128]{1,0:T(8,128)S(1)}, f32[64,128]{1,0:T(8,128)S(1)}, u32[]{:S(2)}, u32[]{:S(2)}) collective-permute-start(f32[64,128]{1,0:T(8,128)S(1)} %get-tuple-element.26), channel_id=1, source_target_pairs={{0,1},{1,0},{2,3},{3,2},{4,5},{5,4},{6,7},{7,6},{8,9},{9,8},{10,11... | collective-permute-start | bytes 98312 | tf_op jit(solution)/shard_map/ppermute | solution.py:29

commit v28 on v27

--- a/solution.py
+++ b/solution.py
@@ -64,15 +64,13 @@
 
 def terms(x):
     hi = x.astype(jnp.bfloat16)
-    rest = x - hi.astype(jnp.float32)
-    mid = rest.astype(jnp.bfloat16)
-    return hi, mid, (rest - mid.astype(jnp.float32)).astype(jnp.bfloat16)
+    return hi, (x - hi.astype(jnp.float32)).astype(jnp.bfloat16)
 
 
 def select_rows(hot, x):
-    hi, mid, low = terms(x)
+    hi, low = terms(x)
     hot = hot.astype(jnp.bfloat16)
-    return dot(hot, hi) + dot(hot, mid) + dot(hot, low)
+    return dot(hot, hi) + dot(hot, low)
 
 
 def split(row):
@@ -279,7 +277,7 @@
         column = down(ids_ref[0:1, :])[:all_slots]
         hot = jnp.concatenate([(column == pair).astype(jnp.float32) for pair in pairs], axis=1)
         hot = hot.astype(jnp.bfloat16)
-        out_ref[...] = dot(hot, given[0]) + dot(hot, given[1]) + dot(hot, given[2])
+        out_ref[...] = dot(hot, given[0]) + dot(hot, given[1])
 
 
 def call(kernel, outs, scratch, *operands):

time: 54.8 us -> 54.6 us (level)
  no operation moved by 1% of the time
where the time goes in v28:
time: 54.6 us; the launch traced here: 54.1 us
  blocking collectives  25.6 us (47%)
  starting transfers between devices  13.6 us (25%)
  waiting for transfers between devices  7.35 us (13%)
  Pallas kernels  6.77 us (12%)
  other arithmetic  0.62 us (1%)
    all_to_all x2, blocking collectives, local(): lax.all_to_all(row_parts, 'genome', 0, 0, tiled=True, axis_index_groups=[...  17.3 us
    ppermute x12, starting transfers between devices, swap(): return lax.ppermute(x, axes, [(i, i ^ k) for i in range(n)])  13.6 us
    all_to_all x1, blocking collectives, local(): lax.all_to_all(counts, ALL, 0, 0, tiled=True, axis_index_groups=[order])  8.33 us
    ppermute x12, waiting for transfers between devices, swap(): return lax.ppermute(x, axes, [(i, i ^ k) for i in range(n)])  7.35 us
    pallas_call x6, Pallas kernels, call(): pl.pallas_call(kernel, out_shape=[jax.ShapeDtypeStruct(shape, jnp.float32...  3.3 us
    pallas_call x1, Pallas kernels, flip(): pl.pallas_call(flip_kernel, out_shape=[pltpu.VMEM((late,) + likelihood.sh...  2.04 us
    pallas_call x1, Pallas kernels, prepare(): pl.pallas_call(lambda *refs: prepare_kernel(own_blocks, *refs), out_shape...  1.43 us
  transfers between devices with their start and end apart: 12, of which 6 were waited for; matrix products, arithmetic and copies ran while one was open for 0% of the time, Pallas kernels for 6%

profile of v28, /device:TPU:0, one launch (start us, length us, event | category | flops | bytes accessed | tf_op | source)
XLA Modules:
  0.0 54.1 jit_solution(12516247340491718227)
XLA Ops:
  0.0 3.5 %collective-permute-start.2 = (f32[12,128]{1,0:T(8,128)}, f32[12,128]{1,0:T(8,128)S(1)}, u32[]{:S(2)}, u32[]{:S(2)}) collective-permute-start(f32[12,128]{1,0:T(8,128)} %bitcast.3), channel_id=1, source_target_pairs={{0,9},{1,8},{2,11},{3,10},{4,13},{5,12},{6,15},{7,14},{8,1},{9,0},... | collective-permute-start | bytes 18440 | tf_op jit(solution)/shard_map/ppermute | solution.py:29
  3.5 1.6 %collective-permute-start.1 = (f32[12,128]{1,0:T(8,128)}, f32[12,128]{1,0:T(8,128)S(1)}, u32[]{:S(2)}, u32[]{:S(2)}) collective-permute-start(f32[12,128]{1,0:T(8,128)} %bitcast.4), channel_id=1, source_target_pairs={{0,13},{1,12},{2,15},{3,14},{4,9},{5,8},{6,11},{7,10},{8,5},{9,4},... | collective-permute-start | bytes 18440 | tf_op jit(solution)/shard_map/ppermute | solution.py:29
  5.3 1.4 %shard_map.46 = (bf16[3,8,256,128]{3,2,1,0:T(8,128)(2,1)S(1)}, f32[8,128]{1,0:T(8,128)S(1)}) custom-call(bf16[8,8,256,128]{3,2,1,0:T(8,128)(2,1)} %lik_ref.1, s32[8,8]{1,0:T(8,128)} %refs_1_.1, s32[8,8]{1,0:T(8,128)} %refs_2_.1), custom_call_target="tpu_custom_call" | custom-call | tf_op jit(solution)/shard_map/pallas_call | solution.py:303
  6.8 1.8 %collective-permute-done.1.refs_2_ = f32[12,128]{1,0:T(8,128)S(1)} collective-permute-done((f32[12,128]{1,0:T(8,128)}, f32[12,128]{1,0:T(8,128)S(1)}, u32[]{:S(2)}, u32[]{:S(2)}) %collective-permute-start.1) | collective-permute-done | bytes 6176 | tf_op jit(solution)/shard_map/ppermute | solution.py:29
  8.6 1.6 %collective-permute-start.5 = (f32[56,128]{1,0:T(8,128)S(1)}, f32[56,128]{1,0:T(8,128)S(1)}, u32[]{:S(2)}, u32[]{:S(2)}) collective-permute-start(f32[56,128]{1,0:T(8,128)S(1)} %shard_map.47.after_ref.refs_1_), channel_id=1, source_target_pairs={{0,2},{1,3},{2,0},{3,1},{4,6},{5,7},{6,4},{7,5},{8,10},{9,11},{10,... | collective-permute-start | bytes 86024 | tf_op jit(solution)/shard_map/ppermute | solution.py:29
  10.2 0.5 collective-permute-start.4
  10.8 2.0 %shard_map.48 = (bf16[5,8,256,128]{3,2,1,0:T(8,128)(2,1)S(1)}, bf16[8,4,256,256]{3,2,1,0:T(8,128)(2,1)S(1)}) custom-call(f32[56,128]{1,0:T(8,128)S(1)} %shard_map.47.after_ref.refs_1_, bf16[3,8,256,128]{3,2,1,0:T(8,128)(2,1)S(1)} %get-tuple-element.18.early_ref.refs_3_, bf16[8,8,256,128]{3,2,1,0:T(8,128)(2,1)} %lik_ref.1), custom_call_target="tpu_custom_call" | custom-call | tf_op jit(solution)/shard_map/pallas_call | solution.py:325
  12.8 0.6 %collective-permute-done.4.refs_3_ = f32[56,128]{1,0:T(8,128)S(1)} collective-permute-done((f32[56,128]{1,0:T(8,128)S(1)}, f32[56,128]{1,0:T(8,128)S(1)}, u32[]{:S(2)}, u32[]{:S(2)}) %collective-permute-start.4) | collective-permute-done | bytes 28704 | tf_op jit(solution)/shard_map/ppermute | solution.py:29
  13.5 0.8 %shard_map.49 = (f32[8,8,256]{2,1,0:T(8,128)S(1)}, f32[64,128]{1,0:T(8,128)S(1)}) custom-call(f32[8,128]{1,0:T(8,128)S(1)} %get-tuple-element.17.refs_4_.refs_0_.info_ref, f32[56,128]{1,0:T(8,128)S(1)} %shard_map.47.after_ref.refs_1_, f32[56,128]{1,0:T(8,128)S(1)} %collective-permute-done.3.refs_2_, f32[56,128]{1,0:T(8,128)S(1)} %collective-permute-done.4.refs_3_, ...), custom_call_target="tpu_custom_call" | custom-call | tf_op jit(solution)/shard_map/pallas_call | solution.py:284
  14.3 8.9 %all_to_all.15.parts_ref = f32[8,8,256]{2,1,0:T(8,128)S(1)} all-to-all(f32[8,8,256]{2,1,0:T(8,128)S(1)} %get-tuple-element.20), channel_id=1, replica_groups={{8,10,12,14,0,2,4,6},{9,11,13,15,1,3,5,7},{24,26,28,30,16,18,20,22},{25..., dimensions={0} | all-to-all | bytes 131072 | tf_op jit(solution)/shard_map/all_to_all | solution.py:369
  23.2 0.7 %shard_map.50.refs_0_ = f32[72,128]{1,0:T(8,128)S(1)} custom-call(f32[8,128]{1,0:T(8,128)S(1)} %get-tuple-element.17.refs_4_.refs_0_.info_ref, f32[8,8,256]{2,1,0:T(8,128)S(1)} %all_to_all.15.parts_ref, f32[64,128]{1,0:T(8,128)S(1)} %get-tuple-element.21.picked_ref, bf16[3,8,256,128]{3,2,1,0:T(8,128)(2,1)S(1)} %get-tuple-element.18.early_ref.refs_3_, ...), custom_call_target="tpu_custom_call" | custom-call | tf_op jit(solution)/shard_map/pallas_call | solution.py:284
  23.9 1.0 %collective-permute-start.8 = (f32[72,128]{1,0:T(8,128)S(1)}, f32[72,128]{1,0:T(8,128)S(1)}, u32[]{:S(2)}, u32[]{:S(2)}) collective-permute-start(f32[72,128]{1,0:T(8,128)S(1)} %shard_map.50.refs_0_), channel_id=1, source_target_pairs={{0,13},{1,12},{2,15},{3,14},{4,9},{5,8},{6,11},{7,10},{8,5},{9,4},... | collective-permute-start | bytes 110600 | tf_op jit(solution)/shard_map/ppermute | solution.py:29
  25.1 2.6 %collective-permute-start.6 = (f32[72,128]{1,0:T(8,128)S(1)}, f32[72,128]{1,0:T(8,128)S(1)}, u32[]{:S(2)}, u32[]{:S(2)}) collective-permute-start(f32[72,128]{1,0:T(8,128)S(1)} %shard_map.50.refs_0_), channel_id=1, source_target_pairs={{0,5},{1,4},{2,7},{3,6},{4,1},{5,0},{6,3},{7,2},{8,13},{9,12},{10,... | collective-permute-start | bytes 110600 | tf_op jit(solution)/shard_map/ppermute | solution.py:29
  27.8 1.6 %collective-permute-done.8.refs_3_ = f32[72,128]{1,0:T(8,128)S(1)} collective-permute-done((f32[72,128]{1,0:T(8,128)S(1)}, f32[72,128]{1,0:T(8,128)S(1)}, u32[]{:S(2)}, u32[]{:S(2)}) %collective-permute-start.8) | collective-permute-done | bytes 36896 | tf_op jit(solution)/shard_map/ppermute | solution.py:29
  29.4 1.0 %collective-permute-done.7.refs_2_ = f32[72,128]{1,0:T(8,128)S(1)} collective-permute-done((f32[72,128]{1,0:T(8,128)S(1)}, f32[72,128]{1,0:T(8,128)S(1)}, u32[]{:S(2)}, u32[]{:S(2)}) %collective-permute-start.7) | collective-permute-done | bytes 36896 | tf_op jit(solution)/shard_map/ppermute | solution.py:29
  30.9 0.6 %collective-permute-start.9 = (f32[64,128]{1,0:T(8,128)S(1)}, f32[64,128]{1,0:T(8,128)S(1)}, u32[]{:S(2)}, u32[]{:S(2)}) collective-permute-start(f32[64,128]{1,0:T(8,128)S(1)} %get-tuple-element.24), channel_id=1, source_target_pairs={{0,2},{1,3},{2,0},{3,1},{4,6},{5,7},{6,4},{7,5},{8,10},{9,11},{10,... | collective-permute-start | bytes 98312 | tf_op jit(solution)/shard_map/ppermute | solution.py:29
  31.5 0.9 %collective-permute-start.10 = (f32[64,128]{1,0:T(8,128)S(1)}, f32[64,128]{1,0:T(8,128)S(1)}, u32[]{:S(2)}, u32[]{:S(2)}) collective-permute-start(f32[64,128]{1,0:T(8,128)S(1)} %get-tuple-element.25), channel_id=1, source_target_pairs={{0,3},{1,2},{2,1},{3,0},{4,7},{5,6},{6,5},{7,4},{8,11},{9,10},{10,... | collective-permute-start | bytes 98312 | tf_op jit(solution)/shard_map/ppermute | solution.py:29
  32.5 0.7 %collective-permute-start.11 = (f32[64,128]{1,0:T(8,128)S(1)}, f32[64,128]{1,0:T(8,128)S(1)}, u32[]{:S(2)}, u32[]{:S(2)}) collective-permute-start(f32[64,128]{1,0:T(8,128)S(1)} %get-tuple-element.26), channel_id=1, source_target_pairs={{0,1},{1,0},{2,3},{3,2},{4,5},{5,4},{6,7},{7,6},{8,9},{9,8},{10,11... | collective-permute-start | bytes 98312 | tf_op jit(solution)/shard_map/ppermute | solution.py:29
  33.1 2.1 %collective-permute-done.9.refs_1_ = f32[64,128]{1,0:T(8,128)S(1)} collective-permute-done((f32[64,128]{1,0:T(8,128)S(1)}, f32[64,128]{1,0:T(8,128)S(1)}, u32[]{:S(2)}, u32[]{:S(2)}) %collective-permute-start.9) | collective-permute-done | bytes 32800 | tf_op jit(solution)/shard_map/ppermute | solution.py:29
  35.2 0.7 %shard_map.52 = (f32[8,8,256]{2,1,0:T(8,128)S(1)}, f32[64,128]{1,0:T(8,128)S(1)}) custom-call(f32[64,128]{1,0:T(8,128)S(1)} %get-tuple-element.23.refs_0_, f32[64,128]{1,0:T(8,128)S(1)} %collective-permute-done.9.refs_1_, f32[64,128]{1,0:T(8,128)S(1)} %collective-permute-done.10.refs_2_, f32[64,128]{1,0:T(8,128)S(1)} %collective-permute-done.11.refs_3_, ...), custom_call_target="tpu_custom_call" | custom-call | tf_op jit(solution)/shard_map/pallas_call | solution.py:284
  35.9 8.4 %all_to_all.16.refs_1_ = f32[8,8,256]{2,1,0:T(8,128)S(1)} all-to-all(f32[8,8,256]{2,1,0:T(8,128)S(1)} %get-tuple-element.27), channel_id=1, replica_groups={{10,8,14,12,2,0,6,4},{11,9,15,13,3,1,7,5},{26,24,30,28,18,16,22,20},{27..., dimensions={0} | all-to-all | bytes 131072 | tf_op jit(solution)/shard_map/all_to_all | solution.py:369
  44.3 0.8 %shard_map.53 = f32[16,12,128]{2,1,0:T(8,128)S(1)} custom-call(f32[8,128]{1,0:T(8,128)S(1)} %get-tuple-element.17.refs_4_.refs_0_.info_ref, f32[8,8,256]{2,1,0:T(8,128)S(1)} %all_to_all.16.refs_1_, f32[64,128]{1,0:T(8,128)S(1)} %get-tuple-element.28.refs_2_, bf16[3,8,256,128]{3,2,1,0:T(8,128)(2,1)S(1)} %get-tuple-element.18.early_ref.refs_3_, ...), custom_call_target="tpu_custom_call" | custom-call | tf_op jit(solution)/shard_map/pallas_call | solution.py:284
  45.1 8.3 %all_to_all.17 = f32[16,12,128]{2,1,0:T(8,128)S(1)} all-to-all(f32[16,12,128]{2,1,0:T(8,128)S(1)} %shard_map.53), channel_id=1, replica_groups={{11,10,9,8,15,14,13,12,3,2,1,0,7,6,5,4},{27,26,25,24,31,30,29,28,19,18,..., dimensions={0} | all-to-all | bytes 196608 | tf_op jit(solution)/shard_map/all_to_all | solution.py:408
  53.5 0.6 %multiply_bitcast_fusion = f32[1536]{0:T(1024)} fusion(f32[12,128]{1,0:T(8,128)S(1)} %reduce_sum.9), kind=kLoop, calls=%fused_computation | loop fusion | flops 1536 | bytes 12288 | tf_op jit(solution)/shard_map/mul | solution.py:409
  (18 shorter events, 1.2 us)
Async XLA Ops:
  0.0 8.6 %copy-start = (f32[1536]{0:T(1024)S(1)}, f32[1536]{0:T(1024)}, u32[]{:S(2)}) copy-start(f32[1536]{0:T(1024)} %param.7) | copy-start | bytes 18436
  0.0 6.8 %collective-permute-start.2 = (f32[12,128]{1,0:T(8,128)}, f32[12,128]{1,0:T(8,128)S(1)}, u32[]{:S(2)}, u32[]{:S(2)}) collective-permute-start(f32[12,128]{1,0:T(8,128)} %bitcast.3), channel_id=1, source_target_pairs={{0,9},{1,8},{2,11},{3,10},{4,13},{5,12},{6,15},{7,14},{8,1},{9,0},... | collective-permute-start | bytes 18440 | tf_op jit(solution)/shard_map/ppermute | solution.py:29
  3.5 5.1 %collective-permute-start.1 = (f32[12,128]{1,0:T(8,128)}, f32[12,128]{1,0:T(8,128)S(1)}, u32[]{:S(2)}, u32[]{:S(2)}) collective-permute-start(f32[12,128]{1,0:T(8,128)} %bitcast.4), channel_id=1, source_target_pairs={{0,13},{1,12},{2,15},{3,14},{4,9},{5,8},{6,11},{7,10},{8,5},{9,4},... | collective-permute-start | bytes 18440 | tf_op jit(solution)/shard_map/ppermute | solution.py:29
  5.1 3.5 %collective-permute-start = (f32[12,128]{1,0:T(8,128)}, f32[12,128]{1,0:T(8,128)S(1)}, u32[]{:S(2)}, u32[]{:S(2)}) collective-permute-start(f32[12,128]{1,0:T(8,128)} %bitcast.5), channel_id=1, source_target_pairs={{0,5},{1,4},{2,7},{3,6},{4,1},{5,0},{6,3},{7,2},{8,13},{9,12},{10,... | collective-permute-start | bytes 18440 | tf_op jit(solution)/shard_map/ppermute | solution.py:29
  8.6 4.3 %collective-permute-start.5 = (f32[56,128]{1,0:T(8,128)S(1)}, f32[56,128]{1,0:T(8,128)S(1)}, u32[]{:S(2)}, u32[]{:S(2)}) collective-permute-start(f32[56,128]{1,0:T(8,128)S(1)} %shard_map.47.after_ref.refs_1_), channel_id=1, source_target_pairs={{0,2},{1,3},{2,0},{3,1},{4,6},{5,7},{6,4},{7,5},{8,10},{9,11},{10,... | collective-permute-start | bytes 86024 | tf_op jit(solution)/shard_map/ppermute | solution.py:29
  10.2 3.3 %collective-permute-start.4 = (f32[56,128]{1,0:T(8,128)S(1)}, f32[56,128]{1,0:T(8,128)S(1)}, u32[]{:S(2)}, u32[]{:S(2)}) collective-permute-start(f32[56,128]{1,0:T(8,128)S(1)} %shard_map.47.after_ref.refs_1_), channel_id=1, source_target_pairs={{0,3},{1,2},{2,1},{3,0},{4,7},{5,6},{6,5},{7,4},{8,11},{9,10},{10,... | collective-permute-start | bytes 86024 | tf_op jit(solution)/shard_map/ppermute | solution.py:29
  10.7 2.8 %collective-permute-start.3 = (f32[56,128]{1,0:T(8,128)S(1)}, f32[56,128]{1,0:T(8,128)S(1)}, u32[]{:S(2)}, u32[]{:S(2)}) collective-permute-start(f32[56,128]{1,0:T(8,128)S(1)} %shard_map.47.after_ref.refs_1_), channel_id=1, source_target_pairs={{0,1},{1,0},{2,3},{3,2},{4,5},{5,4},{6,7},{7,6},{8,9},{9,8},{10,11... | collective-permute-start | bytes 86024 | tf_op jit(solution)/shard_map/ppermute | solution.py:29
  23.9 5.5 %collective-permute-start.8 = (f32[72,128]{1,0:T(8,128)S(1)}, f32[72,128]{1,0:T(8,128)S(1)}, u32[]{:S(2)}, u32[]{:S(2)}) collective-permute-start(f32[72,128]{1,0:T(8,128)S(1)} %shard_map.50.refs_0_), channel_id=1, source_target_pairs={{0,13},{1,12},{2,15},{3,14},{4,9},{5,8},{6,11},{7,10},{8,5},{9,4},... | collective-permute-start | bytes 110600 | tf_op jit(solution)/shard_map/ppermute | solution.py:29
  24.9 5.5 %collective-permute-start.7 = (f32[72,128]{1,0:T(8,128)S(1)}, f32[72,128]{1,0:T(8,128)S(1)}, u32[]{:S(2)}, u32[]{:S(2)}) collective-permute-start(f32[72,128]{1,0:T(8,128)S(1)} %shard_map.50.refs_0_), channel_id=1, source_target_pairs={{0,8},{1,9},{2,10},{3,11},{4,12},{5,13},{6,14},{7,15},{8,0},{9,1},... | collective-permute-start | bytes 110600 | tf_op jit(solution)/shard_map/ppermute | solution.py:29
  25.1 5.5 %collective-permute-start.6 = (f32[72,128]{1,0:T(8,128)S(1)}, f32[72,128]{1,0:T(8,128)S(1)}, u32[]{:S(2)}, u32[]{:S(2)}) collective-permute-start(f32[72,128]{1,0:T(8,128)S(1)} %shard_map.50.refs_0_), channel_id=1, source_target_pairs={{0,5},{1,4},{2,7},{3,6},{4,1},{5,0},{6,3},{7,2},{8,13},{9,12},{10,... | collective-permute-start | bytes 110600 | tf_op jit(solution)/shard_map/ppermute | solution.py:29
  30.9 4.3 %collective-permute-start.9 = (f32[64,128]{1,0:T(8,128)S(1)}, f32[64,128]{1,0:T(8,128)S(1)}, u32[]{:S(2)}, u32[]{:S(2)}) collective-permute-start(f32[64,128]{1,0:T(8,128)S(1)} %get-tuple-element.24), channel_id=1, source_target_pairs={{0,2},{1,3},{2,0},{3,1},{4,6},{5,7},{6,4},{7,5},{8,10},{9,11},{10,... | collective-permute-start | bytes 98312 | tf_op jit(solution)/shard_map/ppermute | solution.py:29
  31.5 3.7 %collective-permute-start.10 = (f32[64,128]{1,0:T(8,128)S(1)}, f32[64,128]{1,0:T(8,128)S(1)}, u32[]{:S(2)}, u32[]{:S(2)}) collective-permute-start(f32[64,128]{1,0:T(8,128)S(1)} %get-tuple-element.25), channel_id=1, source_target_pairs={{0,3},{1,2},{2,1},{3,0},{4,7},{5,6},{6,5},{7,4},{8,11},{9,10},{10,... | collective-permute-start | bytes 98312 | tf_op jit(solution)/shard_map/ppermute | solution.py:29
  32.5 2.8 %collective-permute-start.11 = (f32[64,128]{1,0:T(8,128)S(1)}, f32[64,128]{1,0:T(8,128)S(1)}, u32[]{:S(2)}, u32[]{:S(2)}) collective-permute-start(f32[64,128]{1,0:T(8,128)S(1)} %get-tuple-element.26), channel_id=1, source_target_pairs={{0,1},{1,0},{2,3},{3,2},{4,5},{5,4},{6,7},{7,6},{8,9},{9,8},{10,11... | collective-permute-start | bytes 98312 | tf_op jit(solution)/shard_map/ppermute | solution.py:29

commit v29 on v28

--- a/solution.py
+++ b/solution.py
@@ -273,11 +273,12 @@
         jnp.where(lane < half, a, pltpu.roll(b, half, 1)) for a, b in zip(ids[::2], ids[1::2])
     ]
     given = terms(jnp.concatenate(values, axis=0))
-    for ids_ref, out_ref in zip(wanted, outs):
-        column = down(ids_ref[0:1, :])[:all_slots]
-        hot = jnp.concatenate([(column == pair).astype(jnp.float32) for pair in pairs], axis=1)
-        hot = hot.astype(jnp.bfloat16)
-        out_ref[...] = dot(hot, given[0]) + dot(hot, given[1])
+    column = jnp.concatenate([down(ids_ref[0:1, :])[:all_slots] for ids_ref in wanted], axis=0)
+    hot = jnp.concatenate([(column == pair).astype(jnp.float32) for pair in pairs], axis=1)
+    hot = hot.astype(jnp.bfloat16)
+    sums = dot(hot, given[0]) + dot(hot, given[1])
+    for j, out_ref in enumerate(outs):
+        out_ref[...] = sums[j * all_slots : (j + 1) * all_slots]
 
 
 def call(kernel, outs, scratch, *operands):

time: 54.6 us -> 54.6 us (level)
  no operation moved by 1% of the time
where the time goes in v29:
time: 54.6 us; the launch traced here: 54.1 us
  blocking collectives  25.6 us (47%)
  starting transfers between devices  13.6 us (25%)
  waiting for transfers between devices  7.35 us (13%)
  Pallas kernels  6.77 us (12%)
  other arithmetic  0.62 us (1%)
    all_to_all x2, blocking collectives, local(): lax.all_to_all(row_parts, 'genome', 0, 0, tiled=True, axis_index_groups=[...  17.3 us
    ppermute x12, starting transfers between devices, swap(): return lax.ppermute(x, axes, [(i, i ^ k) for i in range(n)])  13.6 us
    all_to_all x1, blocking collectives, local(): lax.all_to_all(counts, ALL, 0, 0, tiled=True, axis_index_groups=[order])  8.33 us
    ppermute x12, waiting for transfers between devices, swap(): return lax.ppermute(x, axes, [(i, i ^ k) for i in range(n)])  7.35 us
    pallas_call x6, Pallas kernels, call(): pl.pallas_call(kernel, out_shape=[jax.ShapeDtypeStruct(shape, jnp.float32...  3.3 us
    pallas_call x1, Pallas kernels, flip(): pl.pallas_call(flip_kernel, out_shape=[pltpu.VMEM((late,) + likelihood.sh...  2.04 us
    pallas_call x1, Pallas kernels, prepare(): pl.pallas_call(lambda *refs: prepare_kernel(own_blocks, *refs), out_shape...  1.43 us
  transfers between devices with their start and end apart: 12, of which 6 were waited for; matrix products, arithmetic and copies ran while one was open for 0% of the time, Pallas kernels for 6%

profile of v29, /device:TPU:0, one launch (start us, length us, event | category | flops | bytes accessed | tf_op | source)
XLA Modules:
  0.0 54.1 jit_solution(12156529157901029038)
XLA Ops:
  0.0 3.5 %collective-permute-start.2 = (f32[12,128]{1,0:T(8,128)}, f32[12,128]{1,0:T(8,128)S(1)}, u32[]{:S(2)}, u32[]{:S(2)}) collective-permute-start(f32[12,128]{1,0:T(8,128)} %bitcast.3), channel_id=1, source_target_pairs={{0,9},{1,8},{2,11},{3,10},{4,13},{5,12},{6,15},{7,14},{8,1},{9,0},... | collective-permute-start | bytes 18440 | tf_op jit(solution)/shard_map/ppermute | solution.py:29
  3.5 1.6 %collective-permute-start.1 = (f32[12,128]{1,0:T(8,128)}, f32[12,128]{1,0:T(8,128)S(1)}, u32[]{:S(2)}, u32[]{:S(2)}) collective-permute-start(f32[12,128]{1,0:T(8,128)} %bitcast.4), channel_id=1, source_target_pairs={{0,13},{1,12},{2,15},{3,14},{4,9},{5,8},{6,11},{7,10},{8,5},{9,4},... | collective-permute-start | bytes 18440 | tf_op jit(solution)/shard_map/ppermute | solution.py:29
  5.3 1.4 %shard_map.46 = (bf16[3,8,256,128]{3,2,1,0:T(8,128)(2,1)S(1)}, f32[8,128]{1,0:T(8,128)S(1)}) custom-call(bf16[8,8,256,128]{3,2,1,0:T(8,128)(2,1)} %lik_ref.1, s32[8,8]{1,0:T(8,128)} %refs_1_.1, s32[8,8]{1,0:T(8,128)} %refs_2_.1), custom_call_target="tpu_custom_call" | custom-call | tf_op jit(solution)/shard_map/pallas_call | solution.py:304
  6.8 1.8 %collective-permute-done.1.refs_2_ = f32[12,128]{1,0:T(8,128)S(1)} collective-permute-done((f32[12,128]{1,0:T(8,128)}, f32[12,128]{1,0:T(8,128)S(1)}, u32[]{:S(2)}, u32[]{:S(2)}) %collective-permute-start.1) | collective-permute-done | bytes 6176 | tf_op jit(solution)/shard_map/ppermute | solution.py:29
  8.6 1.6 %collective-permute-start.5 = (f32[56,128]{1,0:T(8,128)S(1)}, f32[56,128]{1,0:T(8,128)S(1)}, u32[]{:S(2)}, u32[]{:S(2)}) collective-permute-start(f32[56,128]{1,0:T(8,128)S(1)} %shard_map.47.after_ref.refs_1_), channel_id=1, source_target_pairs={{0,2},{1,3},{2,0},{3,1},{4,6},{5,7},{6,4},{7,5},{8,10},{9,11},{10,... | collective-permute-start | bytes 86024 | tf_op jit(solution)/shard_map/ppermute | solution.py:29
  10.2 0.5 collective-permute-start.4
  10.8 2.0 %shard_map.48 = (bf16[5,8,256,128]{3,2,1,0:T(8,128)(2,1)S(1)}, bf16[8,4,256,256]{3,2,1,0:T(8,128)(2,1)S(1)}) custom-call(f32[56,128]{1,0:T(8,128)S(1)} %shard_map.47.after_ref.refs_1_, bf16[3,8,256,128]{3,2,1,0:T(8,128)(2,1)S(1)} %get-tuple-element.18.early_ref.refs_3_, bf16[8,8,256,128]{3,2,1,0:T(8,128)(2,1)} %lik_ref.1), custom_call_target="tpu_custom_call" | custom-call | tf_op jit(solution)/shard_map/pallas_call | solution.py:326
  12.8 0.6 %collective-permute-done.4.refs_3_ = f32[56,128]{1,0:T(8,128)S(1)} collective-permute-done((f32[56,128]{1,0:T(8,128)S(1)}, f32[56,128]{1,0:T(8,128)S(1)}, u32[]{:S(2)}, u32[]{:S(2)}) %collective-permute-start.4) | collective-permute-done | bytes 28704 | tf_op jit(solution)/shard_map/ppermute | solution.py:29
  13.5 0.8 %shard_map.49 = (f32[8,8,256]{2,1,0:T(8,128)S(1)}, f32[64,128]{1,0:T(8,128)S(1)}) custom-call(f32[8,128]{1,0:T(8,128)S(1)} %get-tuple-element.17.refs_4_.refs_0_.info_ref, f32[56,128]{1,0:T(8,128)S(1)} %shard_map.47.after_ref.refs_1_, f32[56,128]{1,0:T(8,128)S(1)} %collective-permute-done.3.refs_2_, f32[56,128]{1,0:T(8,128)S(1)} %collective-permute-done.4.refs_3_, ...), custom_call_target="tpu_custom_call" | custom-call | tf_op jit(solution)/shard_map/pallas_call | solution.py:285
  14.3 8.9 %all_to_all.15.parts_ref = f32[8,8,256]{2,1,0:T(8,128)S(1)} all-to-all(f32[8,8,256]{2,1,0:T(8,128)S(1)} %get-tuple-element.20), channel_id=1, replica_groups={{8,10,12,14,0,2,4,6},{9,11,13,15,1,3,5,7},{24,26,28,30,16,18,20,22},{25..., dimensions={0} | all-to-all | bytes 131072 | tf_op jit(solution)/shard_map/all_to_all | solution.py:370
  23.2 0.7 %shard_map.50.refs_0_ = f32[72,128]{1,0:T(8,128)S(1)} custom-call(f32[8,128]{1,0:T(8,128)S(1)} %get-tuple-element.17.refs_4_.refs_0_.info_ref, f32[8,8,256]{2,1,0:T(8,128)S(1)} %all_to_all.15.parts_ref, f32[64,128]{1,0:T(8,128)S(1)} %get-tuple-element.21.picked_ref, bf16[3,8,256,128]{3,2,1,0:T(8,128)(2,1)S(1)} %get-tuple-element.18.early_ref.refs_3_, ...), custom_call_target="tpu_custom_call" | custom-call | tf_op jit(solution)/shard_map/pallas_call | solution.py:285
  23.9 1.0 %collective-permute-start.8 = (f32[72,128]{1,0:T(8,128)S(1)}, f32[72,128]{1,0:T(8,128)S(1)}, u32[]{:S(2)}, u32[]{:S(2)}) collective-permute-start(f32[72,128]{1,0:T(8,128)S(1)} %shard_map.50.refs_0_), channel_id=1, source_target_pairs={{0,13},{1,12},{2,15},{3,14},{4,9},{5,8},{6,11},{7,10},{8,5},{9,4},... | collective-permute-start | bytes 110600 | tf_op jit(solution)/shard_map/ppermute | solution.py:29
  25.1 2.6 %collective-permute-start.6 = (f32[72,128]{1,0:T(8,128)S(1)}, f32[72,128]{1,0:T(8,128)S(1)}, u32[]{:S(2)}, u32[]{:S(2)}) collective-permute-start(f32[72,128]{1,0:T(8,128)S(1)} %shard_map.50.refs_0_), channel_id=1, source_target_pairs={{0,5},{1,4},{2,7},{3,6},{4,1},{5,0},{6,3},{7,2},{8,13},{9,12},{10,... | collective-permute-start | bytes 110600 | tf_op jit(solution)/shard_map/ppermute | solution.py:29
  27.8 1.6 %collective-permute-done.8.refs_3_ = f32[72,128]{1,0:T(8,128)S(1)} collective-permute-done((f32[72,128]{1,0:T(8,128)S(1)}, f32[72,128]{1,0:T(8,128)S(1)}, u32[]{:S(2)}, u32[]{:S(2)}) %collective-permute-start.8) | collective-permute-done | bytes 36896 | tf_op jit(solution)/shard_map/ppermute | solution.py:29
  29.4 1.0 %collective-permute-done.7.refs_2_ = f32[72,128]{1,0:T(8,128)S(1)} collective-permute-done((f32[72,128]{1,0:T(8,128)S(1)}, f32[72,128]{1,0:T(8,128)S(1)}, u32[]{:S(2)}, u32[]{:S(2)}) %collective-permute-start.7) | collective-permute-done | bytes 36896 | tf_op jit(solution)/shard_map/ppermute | solution.py:29
  30.9 0.6 %collective-permute-start.9 = (f32[64,128]{1,0:T(8,128)S(1)}, f32[64,128]{1,0:T(8,128)S(1)}, u32[]{:S(2)}, u32[]{:S(2)}) collective-permute-start(f32[64,128]{1,0:T(8,128)S(1)} %get-tuple-element.24), channel_id=1, source_target_pairs={{0,2},{1,3},{2,0},{3,1},{4,6},{5,7},{6,4},{7,5},{8,10},{9,11},{10,... | collective-permute-start | bytes 98312 | tf_op jit(solution)/shard_map/ppermute | solution.py:29
  31.5 0.9 %collective-permute-start.10 = (f32[64,128]{1,0:T(8,128)S(1)}, f32[64,128]{1,0:T(8,128)S(1)}, u32[]{:S(2)}, u32[]{:S(2)}) collective-permute-start(f32[64,128]{1,0:T(8,128)S(1)} %get-tuple-element.25), channel_id=1, source_target_pairs={{0,3},{1,2},{2,1},{3,0},{4,7},{5,6},{6,5},{7,4},{8,11},{9,10},{10,... | collective-permute-start | bytes 98312 | tf_op jit(solution)/shard_map/ppermute | solution.py:29
  32.4 0.7 %collective-permute-start.11 = (f32[64,128]{1,0:T(8,128)S(1)}, f32[64,128]{1,0:T(8,128)S(1)}, u32[]{:S(2)}, u32[]{:S(2)}) collective-permute-start(f32[64,128]{1,0:T(8,128)S(1)} %get-tuple-element.26), channel_id=1, source_target_pairs={{0,1},{1,0},{2,3},{3,2},{4,5},{5,4},{6,7},{7,6},{8,9},{9,8},{10,11... | collective-permute-start | bytes 98312 | tf_op jit(solution)/shard_map/ppermute | solution.py:29
  33.1 2.1 %collective-permute-done.9.refs_1_ = f32[64,128]{1,0:T(8,128)S(1)} collective-permute-done((f32[64,128]{1,0:T(8,128)S(1)}, f32[64,128]{1,0:T(8,128)S(1)}, u32[]{:S(2)}, u32[]{:S(2)}) %collective-permute-start.9) | collective-permute-done | bytes 32800 | tf_op jit(solution)/shard_map/ppermute | solution.py:29
  35.2 0.7 %shard_map.52 = (f32[8,8,256]{2,1,0:T(8,128)S(1)}, f32[64,128]{1,0:T(8,128)S(1)}) custom-call(f32[64,128]{1,0:T(8,128)S(1)} %get-tuple-element.23.refs_0_, f32[64,128]{1,0:T(8,128)S(1)} %collective-permute-done.9.refs_1_, f32[64,128]{1,0:T(8,128)S(1)} %collective-permute-done.10.refs_2_, f32[64,128]{1,0:T(8,128)S(1)} %collective-permute-done.11.refs_3_, ...), custom_call_target="tpu_custom_call" | custom-call | tf_op jit(solution)/shard_map/pallas_call | solution.py:285
  35.9 8.4 %all_to_all.16.refs_1_ = f32[8,8,256]{2,1,0:T(8,128)S(1)} all-to-all(f32[8,8,256]{2,1,0:T(8,128)S(1)} %get-tuple-element.27), channel_id=1, replica_groups={{10,8,14,12,2,0,6,4},{11,9,15,13,3,1,7,5},{26,24,30,28,18,16,22,20},{27..., dimensions={0} | all-to-all | bytes 131072 | tf_op jit(solution)/shard_map/all_to_all | solution.py:370
  44.3 0.8 %shard_map.53 = f32[16,12,128]{2,1,0:T(8,128)S(1)} custom-call(f32[8,128]{1,0:T(8,128)S(1)} %get-tuple-element.17.refs_4_.refs_0_.info_ref, f32[8,8,256]{2,1,0:T(8,128)S(1)} %all_to_all.16.refs_1_, f32[64,128]{1,0:T(8,128)S(1)} %get-tuple-element.28.refs_2_, bf16[3,8,256,128]{3,2,1,0:T(8,128)(2,1)S(1)} %get-tuple-element.18.early_ref.refs_3_, ...), custom_call_target="tpu_custom_call" | custom-call | tf_op jit(solution)/shard_map/pallas_call | solution.py:285
  45.1 8.3 %all_to_all.17 = f32[16,12,128]{2,1,0:T(8,128)S(1)} all-to-all(f32[16,12,128]{2,1,0:T(8,128)S(1)} %shard_map.53), channel_id=1, replica_groups={{11,10,9,8,15,14,13,12,3,2,1,0,7,6,5,4},{27,26,25,24,31,30,29,28,19,18,..., dimensions={0} | all-to-all | bytes 196608 | tf_op jit(solution)/shard_map/all_to_all | solution.py:409
  53.5 0.6 %multiply_bitcast_fusion = f32[1536]{0:T(1024)} fusion(f32[12,128]{1,0:T(8,128)S(1)} %reduce_sum.9), kind=kLoop, calls=%fused_computation | loop fusion | flops 1536 | bytes 12288 | tf_op jit(solution)/shard_map/mul | solution.py:410
  (18 shorter events, 1.2 us)
Async XLA Ops:
  0.0 8.6 %copy-start = (f32[1536]{0:T(1024)S(1)}, f32[1536]{0:T(1024)}, u32[]{:S(2)}) copy-start(f32[1536]{0:T(1024)} %param.7) | copy-start | bytes 18436
  0.0 6.8 %collective-permute-start.2 = (f32[12,128]{1,0:T(8,128)}, f32[12,128]{1,0:T(8,128)S(1)}, u32[]{:S(2)}, u32[]{:S(2)}) collective-permute-start(f32[12,128]{1,0:T(8,128)} %bitcast.3), channel_id=1, source_target_pairs={{0,9},{1,8},{2,11},{3,10},{4,13},{5,12},{6,15},{7,14},{8,1},{9,0},... | collective-permute-start | bytes 18440 | tf_op jit(solution)/shard_map/ppermute | solution.py:29
  3.5 5.1 %collective-permute-start.1 = (f32[12,128]{1,0:T(8,128)}, f32[12,128]{1,0:T(8,128)S(1)}, u32[]{:S(2)}, u32[]{:S(2)}) collective-permute-start(f32[12,128]{1,0:T(8,128)} %bitcast.4), channel_id=1, source_target_pairs={{0,13},{1,12},{2,15},{3,14},{4,9},{5,8},{6,11},{7,10},{8,5},{9,4},... | collective-permute-start | bytes 18440 | tf_op jit(solution)/shard_map/ppermute | solution.py:29
  5.1 3.5 %collective-permute-start = (f32[12,128]{1,0:T(8,128)}, f32[12,128]{1,0:T(8,128)S(1)}, u32[]{:S(2)}, u32[]{:S(2)}) collective-permute-start(f32[12,128]{1,0:T(8,128)} %bitcast.5), channel_id=1, source_target_pairs={{0,5},{1,4},{2,7},{3,6},{4,1},{5,0},{6,3},{7,2},{8,13},{9,12},{10,... | collective-permute-start | bytes 18440 | tf_op jit(solution)/shard_map/ppermute | solution.py:29
  8.6 4.3 %collective-permute-start.5 = (f32[56,128]{1,0:T(8,128)S(1)}, f32[56,128]{1,0:T(8,128)S(1)}, u32[]{:S(2)}, u32[]{:S(2)}) collective-permute-start(f32[56,128]{1,0:T(8,128)S(1)} %shard_map.47.after_ref.refs_1_), channel_id=1, source_target_pairs={{0,2},{1,3},{2,0},{3,1},{4,6},{5,7},{6,4},{7,5},{8,10},{9,11},{10,... | collective-permute-start | bytes 86024 | tf_op jit(solution)/shard_map/ppermute | solution.py:29
  10.2 3.3 %collective-permute-start.4 = (f32[56,128]{1,0:T(8,128)S(1)}, f32[56,128]{1,0:T(8,128)S(1)}, u32[]{:S(2)}, u32[]{:S(2)}) collective-permute-start(f32[56,128]{1,0:T(8,128)S(1)} %shard_map.47.after_ref.refs_1_), channel_id=1, source_target_pairs={{0,3},{1,2},{2,1},{3,0},{4,7},{5,6},{6,5},{7,4},{8,11},{9,10},{10,... | collective-permute-start | bytes 86024 | tf_op jit(solution)/shard_map/ppermute | solution.py:29
  10.7 2.8 %collective-permute-start.3 = (f32[56,128]{1,0:T(8,128)S(1)}, f32[56,128]{1,0:T(8,128)S(1)}, u32[]{:S(2)}, u32[]{:S(2)}) collective-permute-start(f32[56,128]{1,0:T(8,128)S(1)} %shard_map.47.after_ref.refs_1_), channel_id=1, source_target_pairs={{0,1},{1,0},{2,3},{3,2},{4,5},{5,4},{6,7},{7,6},{8,9},{9,8},{10,11... | collective-permute-start | bytes 86024 | tf_op jit(solution)/shard_map/ppermute | solution.py:29
  23.9 5.5 %collective-permute-start.8 = (f32[72,128]{1,0:T(8,128)S(1)}, f32[72,128]{1,0:T(8,128)S(1)}, u32[]{:S(2)}, u32[]{:S(2)}) collective-permute-start(f32[72,128]{1,0:T(8,128)S(1)} %shard_map.50.refs_0_), channel_id=1, source_target_pairs={{0,13},{1,12},{2,15},{3,14},{4,9},{5,8},{6,11},{7,10},{8,5},{9,4},... | collective-permute-start | bytes 110600 | tf_op jit(solution)/shard_map/ppermute | solution.py:29
  24.9 5.5 %collective-permute-start.7 = (f32[72,128]{1,0:T(8,128)S(1)}, f32[72,128]{1,0:T(8,128)S(1)}, u32[]{:S(2)}, u32[]{:S(2)}) collective-permute-start(f32[72,128]{1,0:T(8,128)S(1)} %shard_map.50.refs_0_), channel_id=1, source_target_pairs={{0,8},{1,9},{2,10},{3,11},{4,12},{5,13},{6,14},{7,15},{8,0},{9,1},... | collective-permute-start | bytes 110600 | tf_op jit(solution)/shard_map/ppermute | solution.py:29
  25.1 5.5 %collective-permute-start.6 = (f32[72,128]{1,0:T(8,128)S(1)}, f32[72,128]{1,0:T(8,128)S(1)}, u32[]{:S(2)}, u32[]{:S(2)}) collective-permute-start(f32[72,128]{1,0:T(8,128)S(1)} %shard_map.50.refs_0_), channel_id=1, source_target_pairs={{0,5},{1,4},{2,7},{3,6},{4,1},{5,0},{6,3},{7,2},{8,13},{9,12},{10,... | collective-permute-start | bytes 110600 | tf_op jit(solution)/shard_map/ppermute | solution.py:29
  30.9 4.3 %collective-permute-start.9 = (f32[64,128]{1,0:T(8,128)S(1)}, f32[64,128]{1,0:T(8,128)S(1)}, u32[]{:S(2)}, u32[]{:S(2)}) collective-permute-start(f32[64,128]{1,0:T(8,128)S(1)} %get-tuple-element.24), channel_id=1, source_target_pairs={{0,2},{1,3},{2,0},{3,1},{4,6},{5,7},{6,4},{7,5},{8,10},{9,11},{10,... | collective-permute-start | bytes 98312 | tf_op jit(solution)/shard_map/ppermute | solution.py:29
  31.5 3.7 %collective-permute-start.10 = (f32[64,128]{1,0:T(8,128)S(1)}, f32[64,128]{1,0:T(8,128)S(1)}, u32[]{:S(2)}, u32[]{:S(2)}) collective-permute-start(f32[64,128]{1,0:T(8,128)S(1)} %get-tuple-element.25), channel_id=1, source_target_pairs={{0,3},{1,2},{2,1},{3,0},{4,7},{5,6},{6,5},{7,4},{8,11},{9,10},{10,... | collective-permute-start | bytes 98312 | tf_op jit(solution)/shard_map/ppermute | solution.py:29
  32.4 2.8 %collective-permute-start.11 = (f32[64,128]{1,0:T(8,128)S(1)}, f32[64,128]{1,0:T(8,128)S(1)}, u32[]{:S(2)}, u32[]{:S(2)}) collective-permute-start(f32[64,128]{1,0:T(8,128)S(1)} %get-tuple-element.26), channel_id=1, source_target_pairs={{0,1},{1,0},{2,3},{3,2},{4,5},{5,4},{6,7},{7,6},{8,9},{9,8},{10,11... | collective-permute-start | bytes 98312 | tf_op jit(solution)/shard_map/ppermute | solution.py:29

commit v30 on v29

--- a/solution.py
+++ b/solution.py
@@ -349,7 +349,7 @@
     scale = n * own_blocks * cols / total_reads
 
     column = gather_far(own_weights, ALL, CROSSED, GRAY)
-    held, info = prepare(own_blocks, read_blocks * 3 // 8, likelihood, block_ids, slot_valid)
+    held, info = prepare(own_blocks, read_blocks // 2, likelihood, block_ids, slot_valid)
     (sent,) = call(join_kernel, [(near_rows(far, own_blocks), cols)], [], *column, info)
     rest, flipped = flip(sent, held, likelihood)
     pieces = [sent] + [swap(sent, ALL, j) for j in GRAY[1:]]

time: 54.6 us -> 54.6 us (level)
  no operation moved by 1% of the time
where the time goes in v30:
time: 54.6 us; the launch traced here: 54.1 us
  blocking collectives  25.6 us (47%)
  starting transfers between devices  13.6 us (25%)
  waiting for transfers between devices  7.4 us (14%)
  Pallas kernels  6.74 us (12%)
  other arithmetic  0.62 us (1%)
    all_to_all x2, blocking collectives, local(): lax.all_to_all(row_parts, 'genome', 0, 0, tiled=True, axis_index_groups=[...  17.2 us
    ppermute x12, starting transfers between devices, swap(): return lax.ppermute(x, axes, [(i, i ^ k) for i in range(n)])  13.6 us
    all_to_all x1, blocking collectives, local(): lax.all_to_all(counts, ALL, 0, 0, tiled=True, axis_index_groups=[order])  8.33 us
    ppermute x12, waiting for transfers between devices, swap(): return lax.ppermute(x, axes, [(i, i ^ k) for i in range(n)])  7.4 us
    pallas_call x6, Pallas kernels, call(): pl.pallas_call(kernel, out_shape=[jax.ShapeDtypeStruct(shape, jnp.float32...  3.31 us
    pallas_call x1, Pallas kernels, flip(): pl.pallas_call(flip_kernel, out_shape=[pltpu.VMEM((late,) + likelihood.sh...  1.84 us
    pallas_call x1, Pallas kernels, prepare(): pl.pallas_call(lambda *refs: prepare_kernel(own_blocks, *refs), out_shape...  1.6 us
  transfers between devices with their start and end apart: 12, of which 6 were waited for; matrix products, arithmetic and copies ran while one was open for 0% of the time, Pallas kernels for 6%

profile of v30, /device:TPU:0, one launch (start us, length us, event | category | flops | bytes accessed | tf_op | source)
XLA Modules:
  0.0 54.1 jit_solution(8553109539367341445)
XLA Ops:
  0.0 3.5 %collective-permute-start.2 = (f32[12,128]{1,0:T(8,128)}, f32[12,128]{1,0:T(8,128)S(1)}, u32[]{:S(2)}, u32[]{:S(2)}) collective-permute-start(f32[12,128]{1,0:T(8,128)} %bitcast.3), channel_id=1, source_target_pairs={{0,9},{1,8},{2,11},{3,10},{4,13},{5,12},{6,15},{7,14},{8,1},{9,0},... | collective-permute-start | bytes 18440 | tf_op jit(solution)/shard_map/ppermute | solution.py:29
  3.5 1.6 %collective-permute-start.1 = (f32[12,128]{1,0:T(8,128)}, f32[12,128]{1,0:T(8,128)S(1)}, u32[]{:S(2)}, u32[]{:S(2)}) collective-permute-start(f32[12,128]{1,0:T(8,128)} %bitcast.4), channel_id=1, source_target_pairs={{0,13},{1,12},{2,15},{3,14},{4,9},{5,8},{6,11},{7,10},{8,5},{9,4},... | collective-permute-start | bytes 18440 | tf_op jit(solution)/shard_map/ppermute | solution.py:29
  5.3 1.6 %shard_map.46 = (bf16[4,8,256,128]{3,2,1,0:T(8,128)(2,1)S(1)}, f32[8,128]{1,0:T(8,128)S(1)}) custom-call(bf16[8,8,256,128]{3,2,1,0:T(8,128)(2,1)} %lik_ref.1, s32[8,8]{1,0:T(8,128)} %refs_1_.1, s32[8,8]{1,0:T(8,128)} %refs_2_.1), custom_call_target="tpu_custom_call" | custom-call | tf_op jit(solution)/shard_map/pallas_call | solution.py:304
  7.0 1.6 %collective-permute-done.1.refs_2_ = f32[12,128]{1,0:T(8,128)S(1)} collective-permute-done((f32[12,128]{1,0:T(8,128)}, f32[12,128]{1,0:T(8,128)S(1)}, u32[]{:S(2)}, u32[]{:S(2)}) %collective-permute-start.1) | collective-permute-done | bytes 6176 | tf_op jit(solution)/shard_map/ppermute | solution.py:29
  8.6 1.6 %collective-permute-start.5 = (f32[56,128]{1,0:T(8,128)S(1)}, f32[56,128]{1,0:T(8,128)S(1)}, u32[]{:S(2)}, u32[]{:S(2)}) collective-permute-start(f32[56,128]{1,0:T(8,128)S(1)} %shard_map.47.after_ref.refs_1_), channel_id=1, source_target_pairs={{0,2},{1,3},{2,0},{3,1},{4,6},{5,7},{6,4},{7,5},{8,10},{9,11},{10,... | collective-permute-start | bytes 86024 | tf_op jit(solution)/shard_map/ppermute | solution.py:29
  10.2 0.5 collective-permute-start.4
  10.8 1.8 %shard_map.48 = (bf16[4,8,256,128]{3,2,1,0:T(8,128)(2,1)S(1)}, bf16[8,4,256,256]{3,2,1,0:T(8,128)(2,1)S(1)}) custom-call(f32[56,128]{1,0:T(8,128)S(1)} %shard_map.47.after_ref.refs_1_, bf16[4,8,256,128]{3,2,1,0:T(8,128)(2,1)S(1)} %get-tuple-element.18.early_ref.refs_3_, bf16[8,8,256,128]{3,2,1,0:T(8,128)(2,1)} %lik_ref.1), custom_call_target="tpu_custom_call" | custom-call | tf_op jit(solution)/shard_map/pallas_call | solution.py:326
  12.6 0.8 %collective-permute-done.4.refs_3_ = f32[56,128]{1,0:T(8,128)S(1)} collective-permute-done((f32[56,128]{1,0:T(8,128)S(1)}, f32[56,128]{1,0:T(8,128)S(1)}, u32[]{:S(2)}, u32[]{:S(2)}) %collective-permute-start.4) | collective-permute-done | bytes 28704 | tf_op jit(solution)/shard_map/ppermute | solution.py:29
  13.5 0.8 %shard_map.49 = (f32[8,8,256]{2,1,0:T(8,128)S(1)}, f32[64,128]{1,0:T(8,128)S(1)}) custom-call(f32[8,128]{1,0:T(8,128)S(1)} %get-tuple-element.17.refs_4_.refs_0_.info_ref, f32[56,128]{1,0:T(8,128)S(1)} %shard_map.47.after_ref.refs_1_, f32[56,128]{1,0:T(8,128)S(1)} %collective-permute-done.3.refs_2_, f32[56,128]{1,0:T(8,128)S(1)} %collective-permute-done.4.refs_3_, ...), custom_call_target="tpu_custom_call" | custom-call | tf_op jit(solution)/shard_map/pallas_call | solution.py:285
  14.3 8.9 %all_to_all.15.parts_ref = f32[8,8,256]{2,1,0:T(8,128)S(1)} all-to-all(f32[8,8,256]{2,1,0:T(8,128)S(1)} %get-tuple-element.20), channel_id=1, replica_groups={{8,10,12,14,0,2,4,6},{9,11,13,15,1,3,5,7},{24,26,28,30,16,18,20,22},{25..., dimensions={0} | all-to-all | bytes 131072 | tf_op jit(solution)/shard_map/all_to_all | solution.py:370
  23.2 0.7 %shard_map.50.refs_0_ = f32[72,128]{1,0:T(8,128)S(1)} custom-call(f32[8,128]{1,0:T(8,128)S(1)} %get-tuple-element.17.refs_4_.refs_0_.info_ref, f32[8,8,256]{2,1,0:T(8,128)S(1)} %all_to_all.15.parts_ref, f32[64,128]{1,0:T(8,128)S(1)} %get-tuple-element.21.picked_ref, bf16[4,8,256,128]{3,2,1,0:T(8,128)(2,1)S(1)} %get-tuple-element.18.early_ref.refs_3_, ...), custom_call_target="tpu_custom_call" | custom-call | tf_op jit(solution)/shard_map/pallas_call | solution.py:285
  23.9 0.8 %collective-permute-start.8 = (f32[72,128]{1,0:T(8,128)S(1)}, f32[72,128]{1,0:T(8,128)S(1)}, u32[]{:S(2)}, u32[]{:S(2)}) collective-permute-start(f32[72,128]{1,0:T(8,128)S(1)} %shard_map.50.refs_0_), channel_id=1, source_target_pairs={{0,13},{1,12},{2,15},{3,14},{4,9},{5,8},{6,11},{7,10},{8,5},{9,4},... | collective-permute-start | bytes 110600 | tf_op jit(solution)/shard_map/ppermute | solution.py:29
  25.1 2.6 %collective-permute-start.6 = (f32[72,128]{1,0:T(8,128)S(1)}, f32[72,128]{1,0:T(8,128)S(1)}, u32[]{:S(2)}, u32[]{:S(2)}) collective-permute-start(f32[72,128]{1,0:T(8,128)S(1)} %shard_map.50.refs_0_), channel_id=1, source_target_pairs={{0,5},{1,4},{2,7},{3,6},{4,1},{5,0},{6,3},{7,2},{8,13},{9,12},{10,... | collective-permute-start | bytes 110600 | tf_op jit(solution)/shard_map/ppermute | solution.py:29
  27.8 1.6 %collective-permute-done.8.refs_3_ = f32[72,128]{1,0:T(8,128)S(1)} collective-permute-done((f32[72,128]{1,0:T(8,128)S(1)}, f32[72,128]{1,0:T(8,128)S(1)}, u32[]{:S(2)}, u32[]{:S(2)}) %collective-permute-start.8) | collective-permute-done | bytes 36896 | tf_op jit(solution)/shard_map/ppermute | solution.py:29
  29.4 1.0 %collective-permute-done.7.refs_2_ = f32[72,128]{1,0:T(8,128)S(1)} collective-permute-done((f32[72,128]{1,0:T(8,128)S(1)}, f32[72,128]{1,0:T(8,128)S(1)}, u32[]{:S(2)}, u32[]{:S(2)}) %collective-permute-start.7) | collective-permute-done | bytes 36896 | tf_op jit(solution)/shard_map/ppermute | solution.py:29
  30.9 0.6 %collective-permute-start.9 = (f32[64,128]{1,0:T(8,128)S(1)}, f32[64,128]{1,0:T(8,128)S(1)}, u32[]{:S(2)}, u32[]{:S(2)}) collective-permute-start(f32[64,128]{1,0:T(8,128)S(1)} %get-tuple-element.24), channel_id=1, source_target_pairs={{0,2},{1,3},{2,0},{3,1},{4,6},{5,7},{6,4},{7,5},{8,10},{9,11},{10,... | collective-permute-start | bytes 98312 | tf_op jit(solution)/shard_map/ppermute | solution.py:29
  31.5 0.9 %collective-permute-start.10 = (f32[64,128]{1,0:T(8,128)S(1)}, f32[64,128]{1,0:T(8,128)S(1)}, u32[]{:S(2)}, u32[]{:S(2)}) collective-permute-start(f32[64,128]{1,0:T(8,128)S(1)} %get-tuple-element.25), channel_id=1, source_target_pairs={{0,3},{1,2},{2,1},{3,0},{4,7},{5,6},{6,5},{7,4},{8,11},{9,10},{10,... | collective-permute-start | bytes 98312 | tf_op jit(solution)/shard_map/ppermute | solution.py:29
  32.5 0.7 %collective-permute-start.11 = (f32[64,128]{1,0:T(8,128)S(1)}, f32[64,128]{1,0:T(8,128)S(1)}, u32[]{:S(2)}, u32[]{:S(2)}) collective-permute-start(f32[64,128]{1,0:T(8,128)S(1)} %get-tuple-element.26), channel_id=1, source_target_pairs={{0,1},{1,0},{2,3},{3,2},{4,5},{5,4},{6,7},{7,6},{8,9},{9,8},{10,11... | collective-permute-start | bytes 98312 | tf_op jit(solution)/shard_map/ppermute | solution.py:29
  33.1 2.1 %collective-permute-done.9.refs_1_ = f32[64,128]{1,0:T(8,128)S(1)} collective-permute-done((f32[64,128]{1,0:T(8,128)S(1)}, f32[64,128]{1,0:T(8,128)S(1)}, u32[]{:S(2)}, u32[]{:S(2)}) %collective-permute-start.9) | collective-permute-done | bytes 32800 | tf_op jit(solution)/shard_map/ppermute | solution.py:29
  35.2 0.7 %shard_map.52 = (f32[8,8,256]{2,1,0:T(8,128)S(1)}, f32[64,128]{1,0:T(8,128)S(1)}) custom-call(f32[64,128]{1,0:T(8,128)S(1)} %get-tuple-element.23.refs_0_, f32[64,128]{1,0:T(8,128)S(1)} %collective-permute-done.9.refs_1_, f32[64,128]{1,0:T(8,128)S(1)} %collective-permute-done.10.refs_2_, f32[64,128]{1,0:T(8,128)S(1)} %collective-permute-done.11.refs_3_, ...), custom_call_target="tpu_custom_call" | custom-call | tf_op jit(solution)/shard_map/pallas_call | solution.py:285
  35.9 8.4 %all_to_all.16.refs_1_ = f32[8,8,256]{2,1,0:T(8,128)S(1)} all-to-all(f32[8,8,256]{2,1,0:T(8,128)S(1)} %get-tuple-element.27), channel_id=1, replica_groups={{10,8,14,12,2,0,6,4},{11,9,15,13,3,1,7,5},{26,24,30,28,18,16,22,20},{27..., dimensions={0} | all-to-all | bytes 131072 | tf_op jit(solution)/shard_map/all_to_all | solution.py:370
  44.3 0.8 %shard_map.53 = f32[16,12,128]{2,1,0:T(8,128)S(1)} custom-call(f32[8,128]{1,0:T(8,128)S(1)} %get-tuple-element.17.refs_4_.refs_0_.info_ref, f32[8,8,256]{2,1,0:T(8,128)S(1)} %all_to_all.16.refs_1_, f32[64,128]{1,0:T(8,128)S(1)} %get-tuple-element.28.refs_2_, bf16[4,8,256,128]{3,2,1,0:T(8,128)(2,1)S(1)} %get-tuple-element.18.early_ref.refs_3_, ...), custom_call_target="tpu_custom_call" | custom-call | tf_op jit(solution)/shard_map/pallas_call | solution.py:285
  45.1 8.3 %all_to_all.17 = f32[16,12,128]{2,1,0:T(8,128)S(1)} all-to-all(f32[16,12,128]{2,1,0:T(8,128)S(1)} %shard_map.53), channel_id=1, replica_groups={{11,10,9,8,15,14,13,12,3,2,1,0,7,6,5,4},{27,26,25,24,31,30,29,28,19,18,..., dimensions={0} | all-to-all | bytes 196608 | tf_op jit(solution)/shard_map/all_to_all | solution.py:409
  53.5 0.6 %multiply_bitcast_fusion = f32[1536]{0:T(1024)} fusion(f32[12,128]{1,0:T(8,128)S(1)} %reduce_sum.9), kind=kLoop, calls=%fused_computation | loop fusion | flops 1536 | bytes 12288 | tf_op jit(solution)/shard_map/mul | solution.py:410
  (18 shorter events, 1.4 us)
Async XLA Ops:
  0.0 8.6 %copy-start = (f32[1536]{0:T(1024)S(1)}, f32[1536]{0:T(1024)}, u32[]{:S(2)}) copy-start(f32[1536]{0:T(1024)} %param.7) | copy-start | bytes 18436
  0.0 6.9 %collective-permute-start.2 = (f32[12,128]{1,0:T(8,128)}, f32[12,128]{1,0:T(8,128)S(1)}, u32[]{:S(2)}, u32[]{:S(2)}) collective-permute-start(f32[12,128]{1,0:T(8,128)} %bitcast.3), channel_id=1, source_target_pairs={{0,9},{1,8},{2,11},{3,10},{4,13},{5,12},{6,15},{7,14},{8,1},{9,0},... | collective-permute-start | bytes 18440 | tf_op jit(solution)/shard_map/ppermute | solution.py:29
  3.5 5.1 %collective-permute-start.1 = (f32[12,128]{1,0:T(8,128)}, f32[12,128]{1,0:T(8,128)S(1)}, u32[]{:S(2)}, u32[]{:S(2)}) collective-permute-start(f32[12,128]{1,0:T(8,128)} %bitcast.4), channel_id=1, source_target_pairs={{0,13},{1,12},{2,15},{3,14},{4,9},{5,8},{6,11},{7,10},{8,5},{9,4},... | collective-permute-start | bytes 18440 | tf_op jit(solution)/shard_map/ppermute | solution.py:29
  5.1 3.5 %collective-permute-start = (f32[12,128]{1,0:T(8,128)}, f32[12,128]{1,0:T(8,128)S(1)}, u32[]{:S(2)}, u32[]{:S(2)}) collective-permute-start(f32[12,128]{1,0:T(8,128)} %bitcast.5), channel_id=1, source_target_pairs={{0,5},{1,4},{2,7},{3,6},{4,1},{5,0},{6,3},{7,2},{8,13},{9,12},{10,... | collective-permute-start | bytes 18440 | tf_op jit(solution)/shard_map/ppermute | solution.py:29
  8.6 4.1 %collective-permute-start.5 = (f32[56,128]{1,0:T(8,128)S(1)}, f32[56,128]{1,0:T(8,128)S(1)}, u32[]{:S(2)}, u32[]{:S(2)}) collective-permute-start(f32[56,128]{1,0:T(8,128)S(1)} %shard_map.47.after_ref.refs_1_), channel_id=1, source_target_pairs={{0,2},{1,3},{2,0},{3,1},{4,6},{5,7},{6,4},{7,5},{8,10},{9,11},{10,... | collective-permute-start | bytes 86024 | tf_op jit(solution)/shard_map/ppermute | solution.py:29
  10.2 3.3 %collective-permute-start.4 = (f32[56,128]{1,0:T(8,128)S(1)}, f32[56,128]{1,0:T(8,128)S(1)}, u32[]{:S(2)}, u32[]{:S(2)}) collective-permute-start(f32[56,128]{1,0:T(8,128)S(1)} %shard_map.47.after_ref.refs_1_), channel_id=1, source_target_pairs={{0,3},{1,2},{2,1},{3,0},{4,7},{5,6},{6,5},{7,4},{8,11},{9,10},{10,... | collective-permute-start | bytes 86024 | tf_op jit(solution)/shard_map/ppermute | solution.py:29
  10.7 2.8 %collective-permute-start.3 = (f32[56,128]{1,0:T(8,128)S(1)}, f32[56,128]{1,0:T(8,128)S(1)}, u32[]{:S(2)}, u32[]{:S(2)}) collective-permute-start(f32[56,128]{1,0:T(8,128)S(1)} %shard_map.47.after_ref.refs_1_), channel_id=1, source_target_pairs={{0,1},{1,0},{2,3},{3,2},{4,5},{5,4},{6,7},{7,6},{8,9},{9,8},{10,11... | collective-permute-start | bytes 86024 | tf_op jit(solution)/shard_map/ppermute | solution.py:29
  23.9 5.5 %collective-permute-start.8 = (f32[72,128]{1,0:T(8,128)S(1)}, f32[72,128]{1,0:T(8,128)S(1)}, u32[]{:S(2)}, u32[]{:S(2)}) collective-permute-start(f32[72,128]{1,0:T(8,128)S(1)} %shard_map.50.refs_0_), channel_id=1, source_target_pairs={{0,13},{1,12},{2,15},{3,14},{4,9},{5,8},{6,11},{7,10},{8,5},{9,4},... | collective-permute-start | bytes 110600 | tf_op jit(solution)/shard_map/ppermute | solution.py:29
  24.6 5.7 %collective-permute-start.7 = (f32[72,128]{1,0:T(8,128)S(1)}, f32[72,128]{1,0:T(8,128)S(1)}, u32[]{:S(2)}, u32[]{:S(2)}) collective-permute-start(f32[72,128]{1,0:T(8,128)S(1)} %shard_map.50.refs_0_), channel_id=1, source_target_pairs={{0,8},{1,9},{2,10},{3,11},{4,12},{5,13},{6,14},{7,15},{8,0},{9,1},... | collective-permute-start | bytes 110600 | tf_op jit(solution)/shard_map/ppermute | solution.py:29
  25.1 5.5 %collective-permute-start.6 = (f32[72,128]{1,0:T(8,128)S(1)}, f32[72,128]{1,0:T(8,128)S(1)}, u32[]{:S(2)}, u32[]{:S(2)}) collective-permute-start(f32[72,128]{1,0:T(8,128)S(1)} %shard_map.50.refs_0_), channel_id=1, source_target_pairs={{0,5},{1,4},{2,7},{3,6},{4,1},{5,0},{6,3},{7,2},{8,13},{9,12},{10,... | collective-permute-start | bytes 110600 | tf_op jit(solution)/shard_map/ppermute | solution.py:29
  30.9 4.3 %collective-permute-start.9 = (f32[64,128]{1,0:T(8,128)S(1)}, f32[64,128]{1,0:T(8,128)S(1)}, u32[]{:S(2)}, u32[]{:S(2)}) collective-permute-start(f32[64,128]{1,0:T(8,128)S(1)} %get-tuple-element.24), channel_id=1, source_target_pairs={{0,2},{1,3},{2,0},{3,1},{4,6},{5,7},{6,4},{7,5},{8,10},{9,11},{10,... | collective-permute-start | bytes 98312 | tf_op jit(solution)/shard_map/ppermute | solution.py:29
  31.5 3.7 %collective-permute-start.10 = (f32[64,128]{1,0:T(8,128)S(1)}, f32[64,128]{1,0:T(8,128)S(1)}, u32[]{:S(2)}, u32[]{:S(2)}) collective-permute-start(f32[64,128]{1,0:T(8,128)S(1)} %get-tuple-element.25), channel_id=1, source_target_pairs={{0,3},{1,2},{2,1},{3,0},{4,7},{5,6},{6,5},{7,4},{8,11},{9,10},{10,... | collective-permute-start | bytes 98312 | tf_op jit(solution)/shard_map/ppermute | solution.py:29
  32.5 2.8 %collective-permute-start.11 = (f32[64,128]{1,0:T(8,128)S(1)}, f32[64,128]{1,0:T(8,128)S(1)}, u32[]{:S(2)}, u32[]{:S(2)}) collective-permute-start(f32[64,128]{1,0:T(8,128)S(1)} %get-tuple-element.26), channel_id=1, source_target_pairs={{0,1},{1,0},{2,3},{3,2},{4,5},{5,4},{6,7},{7,6},{8,9},{9,8},{10,11... | collective-permute-start | bytes 98312 | tf_op jit(solution)/shard_map/ppermute | solution.py:29
